TPU v7x, 32 devices: a whole 2x2x4 slice. The times are simulated.
32 devices in a mesh: fsdp: 2 (over y), ep: 8 (over z, x), tp: 2 (over core).
Axes of the slice: x: 2, y: 2, z: 4, core: 2. Of those that a mesh axis runs over, the one named last changes fastest.
Arguments:
- tokens: bfloat16 [2048, 2048], P(('fsdp', 'ep')), may hold values from -6 to 6
- routes: int32 [2048, 8], P(('fsdp', 'ep')), may hold values from 0 to 23, all different within a row; in each aligned block of 128 rows (0 to 127, 128 to 255, ...) at most 85 rows name the same one
- places: int32 [2048], replicated, may hold values from 0 to 2047, as said below
- piece_starts: int32 [2, 2], replicated, may hold values from 0 to 768, as said below
- attn_gain: float32 [2048], replicated, may hold values from 0.5 to 1.5
- query_proj: bfloat16 [2048, 4096], P('fsdp', 'tp'), may hold values from -0.125 to 0.125
- key_matrix: bfloat16 [2048, 512], P('fsdp', 'tp'), may hold values from -0.125 to 0.125
- value_matrix: bfloat16 [2048, 512], P('fsdp', 'tp'), may hold values from -0.125 to 0.125
- out_proj: bfloat16 [2048, 4096], P('fsdp', 'tp'), may hold values from -4 to 4
- query_gain: float32 [128], replicated, may hold values from 0.1 to 1.9
- key_gain: float32 [128], replicated, may hold values from 0.1 to 1.9
- ffn_gain: float32 [2048], replicated, may hold values from 0.5 to 1.5
- router: bfloat16 [2048, 24], P('fsdp'), may hold values from -0.0625 to 0.0625
- gate_proj: bfloat16 [24, 2048, 768], P('ep', None, 'tp'), may hold values from -0.125 to 0.125
- up_proj: bfloat16 [24, 2048, 768], P('ep', None, 'tp'), may hold values from -0.125 to 0.125
- down_proj: bfloat16 [24, 768, 2048], P('ep', 'tp'), may hold values from -0.875 to 0.875
- out_grad: bfloat16 [2048, 2048], P(('fsdp', 'ep')), may hold values from -6 to 6
Outputs:
- layer_out: bfloat16 [2048, 2048], P(('fsdp', 'ep'))
- tokens_grad: float32 [2048, 2048], P(('fsdp', 'ep'))
- attn_gain_grad: float32 [2048], replicated
- query_proj_grad: float32 [2048, 4096], P('fsdp', 'tp')
- key_proj_grad: float32 [2048, 512], P('fsdp', 'tp')
- value_proj_grad: float32 [2048, 512], P('fsdp', 'tp')
- out_proj_grad: float32 [2048, 4096], P('fsdp', 'tp')
- query_gain_grad: float32 [128], replicated
- key_gain_grad: float32 [128], replicated
- ffn_gain_grad: float32 [2048], replicated
- router_grad: float32 [2048, 24], P('fsdp')
- gate_proj_grad: float32 [24, 2048, 768], P('ep', None, 'tp')
- up_proj_grad: float32 [24, 2048, 768], P('ep', None, 'tp')
- down_proj_grad: float32 [24, 768, 2048], P('ep', 'tp')
Inputs may be any that keep to these rules, and one draw needn't show every extreme that they name: Rows r * 1024 to (r + 1) * 1024 - 1 hold sequence r, each of its positions once: places[t] // 1024 = t // 1024. `routes`: the rows of one device name each expert at most 85 times; some expert is named exactly 85 times by some device's rows. `piece_starts`: piece k of a sequence lies within positions k * (512) to (k + 1) * 512 - 1.
All inputs are finite; a program needn't handle non-finite values.
Results may differ from a plain program's by a relative error of at most 0.018.
Values may be sent and summed in bfloat16 or wider, within the bound.
No kernel may reach another device: no remote copies, remote signals or barrier semaphores. Data moves between devices by JAX's collectives and lax.ppermute only.
A program may use at most 320 MiB of HBM per device.

v0:
```python
import math

import jax
import jax.numpy as jnp
from jax import lax
from jax.sharding import PartitionSpec as P

PIECE = 256


EPSILON = 1e-06
LOG_THETA = math.log(1000000.0)
MASKED_SCORE = -1e30


def inverse_norm(values):
    return lax.rsqrt(jnp.mean(values * values, axis=-1, keepdims=True) + EPSILON)


def rotate(vectors, angles):
    half_dim = vectors.shape[-1] // 2
    cosine = jnp.cos(angles)[:, None, :]
    sine = jnp.sin(angles)[:, None, :]
    leading = vectors[..., :half_dim]
    trailing = vectors[..., half_dim:]
    return jnp.concatenate(
        [leading * cosine - trailing * sine, trailing * cosine + leading * sine], axis=-1
    )


def rotary_angles(place_ids, seq_len, head_dim):
    half_dim = head_dim // 2
    freqs = jnp.exp(jnp.arange(half_dim, dtype=jnp.float32) * (-2.0 * LOG_THETA / head_dim))
    return (place_ids % seq_len).astype(jnp.float32)[:, None] * freqs[None, :]


def piece_numbers(place_ids, piece_starts, seq_len, piece_len):
    seq_index = place_ids // seq_len
    position = place_ids % seq_len
    seq_total, piece_total = piece_starts.shape
    matches = seq_index[:, None] == jnp.arange(seq_total, dtype=jnp.int32)[None, :]
    begins = piece_starts[None, :, :]
    inside = (
        matches[:, :, None]
        & (begins <= position[:, None, None])
        & (position[:, None, None] < begins + piece_len)
    )
    numbers = jnp.arange(1, piece_total + 1, dtype=jnp.int32)
    return jnp.sum(jnp.where(inside, numbers[None, None, :], 0), axis=(1, 2))


def norm_backward(grad_rot, unit, inverse, gain, angles):
    grad_normed = rotate(grad_rot, -angles)
    gain_part = jnp.sum(grad_normed * unit, axis=(0, 1))
    unit_grad = grad_normed * gain
    raw_grad = inverse * (unit_grad - unit * jnp.mean(unit_grad * unit, axis=-1, keepdims=True))
    return (raw_grad, gain_part)


def contract_rows(left, right):
    return lax.dot_general(
        left, right, (((0,), (0,)), ((), ())), preferred_element_type=jnp.float32
    )


def contract_cols(left, right):
    return lax.dot_general(
        left, right, (((1,), (1,)), ((), ())), preferred_element_type=jnp.float32
    )


def body(
    tokens,
    routes,
    places,
    piece_starts,
    attn_gain,
    query_proj,
    key_matrix,
    value_matrix,
    out_proj,
    query_gain,
    key_gain,
    ffn_gain,
    router,
    gate_proj,
    up_proj,
    down_proj,
    out_grad,
):
    local_rows, model_width = tokens.shape
    head_dim = query_gain.shape[0]
    heads_here = query_proj.shape[1] // head_dim
    kv_here = key_matrix.shape[1] // head_dim
    queries_each_key_head = heads_here // kv_here
    experts_here = gate_proj.shape[0]
    owners = lax.axis_size("ep")
    halves = lax.axis_size("tp")
    expert_count = experts_here * owners
    picks = routes.shape[1]
    capacity = min(local_rows, 2 * local_rows * picks // expert_count)
    slot_count = expert_count * capacity
    seq_len = local_rows * owners
    key_block = min(512, seq_len)
    key_blocks = seq_len // key_block
    score_scale = head_dim ** (-0.5)
    device = lax.axis_index(("fsdp", "ep"))
    group_start = lax.axis_index("fsdp") * seq_len
    own_places = lax.dynamic_slice_in_dim(places, device * local_rows, local_rows)
    all_pieces = piece_numbers(places, piece_starts, seq_len, PIECE)
    own_pieces = lax.dynamic_slice_in_dim(all_pieces, device * local_rows, local_rows)
    own_pos = own_places % seq_len
    key_pos = lax.dynamic_slice_in_dim(places, group_start, seq_len) % seq_len
    key_pieces = lax.dynamic_slice_in_dim(all_pieces, group_start, seq_len)
    angles = rotary_angles(own_places, seq_len, head_dim)
    whole_query, whole_key, whole_value, whole_out, whole_router = (
        lax.all_gather(query_proj, "fsdp", axis=0, tiled=True),
        lax.all_gather(key_matrix, "fsdp", axis=0, tiled=True),
        lax.all_gather(value_matrix, "fsdp", axis=0, tiled=True),
        lax.all_gather(out_proj, "fsdp", axis=0, tiled=True),
        lax.all_gather(router, "fsdp", axis=0, tiled=True),
    )
    stream = tokens.astype(jnp.float32)
    first_inverse = inverse_norm(stream)
    normed = stream * first_inverse
    attention_input = (normed * attn_gain).astype(jnp.bfloat16)
    q_raw = jnp.dot(attention_input, whole_query, preferred_element_type=jnp.float32).reshape(
        local_rows, heads_here, head_dim
    )
    key_unrotated = jnp.dot(attention_input, whole_key, preferred_element_type=jnp.float32).reshape(
        local_rows, kv_here, head_dim
    )
    v_raw = jnp.dot(attention_input, whole_value, preferred_element_type=jnp.float32)
    q_inverse = inverse_norm(q_raw)
    q_unit = q_raw * q_inverse
    k_inverse = inverse_norm(key_unrotated)
    k_unit = key_unrotated * k_inverse
    query_low = (
        rotate(q_unit * query_gain, angles)
        .astype(jnp.bfloat16)
        .reshape(local_rows, kv_here, queries_each_key_head, head_dim)
    )
    key_low = (
        rotate(k_unit * key_gain, angles)
        .astype(jnp.bfloat16)
        .reshape(local_rows, kv_here * head_dim)
    )
    value_low = v_raw.astype(jnp.bfloat16)
    keys_all, values_all = (
        lax.all_gather(key_low, "ep", axis=0, tiled=True),
        lax.all_gather(value_low, "ep", axis=0, tiled=True),
    )

    def key_block_parts(block_index):
        begin_row = block_index * key_block
        key_rows = lax.dynamic_slice_in_dim(keys_all, begin_row, key_block).reshape(
            key_block, kv_here, head_dim
        )
        value_rows = lax.dynamic_slice_in_dim(values_all, begin_row, key_block).reshape(
            key_block, kv_here, head_dim
        )
        pos_rows = lax.dynamic_slice_in_dim(key_pos, begin_row, key_block)
        piece_rows = lax.dynamic_slice_in_dim(key_pieces, begin_row, key_block)
        allowed = (pos_rows[None, :] <= own_pos[:, None]) | (
            own_pieces[:, None] == piece_rows[None, :]
        ) & (own_pieces[:, None] > 0)
        scores = (
            jnp.einsum("thgd,khd->hgtk", query_low, key_rows, preferred_element_type=jnp.float32)
            * score_scale
        )
        return (key_rows, value_rows, allowed[None, None], scores)

    def stats_step(block_index, state_pair):
        row_max, row_total = state_pair
        _, _, allowed, scores = key_block_parts(block_index)
        masked = jnp.where(allowed, scores, MASKED_SCORE)
        new_max = jnp.maximum(row_max, jnp.max(masked, axis=-1))
        fresh = jnp.where(allowed, jnp.exp(masked - new_max[..., None]), 0.0)
        return (new_max, row_total * jnp.exp(row_max - new_max) + jnp.sum(fresh, axis=-1))

    stat_shape = (kv_here, queries_each_key_head, local_rows)
    row_max, row_total = lax.fori_loop(
        0,
        key_blocks,
        stats_step,
        (jnp.full(stat_shape, MASKED_SCORE, jnp.float32), jnp.zeros(stat_shape, jnp.float32)),
    )

    def probabilities(allowed, scores):
        return (
            jnp.exp(jnp.where(allowed, scores - row_max[..., None], MASKED_SCORE))
            / row_total[..., None]
        )

    def output_step(block_index, summed):
        _, value_rows, allowed, scores = key_block_parts(block_index)
        probs_low = probabilities(allowed, scores).astype(jnp.bfloat16)
        return summed + jnp.einsum(
            "hgtk,khd->thgd", probs_low, value_rows, preferred_element_type=jnp.float32
        )

    attn_vals = lax.fori_loop(
        0,
        key_blocks,
        output_step,
        jnp.zeros((local_rows, kv_here, queries_each_key_head, head_dim), jnp.float32),
    )
    attn_low = attn_vals.astype(jnp.bfloat16).reshape(local_rows, heads_here * head_dim)
    branch = lax.psum(contract_cols(attn_low, whole_out), "tp")
    residual = stream + branch
    second_inverse = inverse_norm(residual)
    mid_normed = residual * second_inverse
    ffn_in = (mid_normed * ffn_gain).astype(jnp.bfloat16)
    logits = jnp.dot(ffn_in, whole_router, preferred_element_type=jnp.float32)
    chosen = routes[:, :, None] == jnp.arange(expert_count, dtype=jnp.int32)[None, None, :]
    picked = jnp.sum(jnp.where(chosen, logits[:, None, :], 0.0), axis=-1)
    gates = jax.nn.softmax(picked, axis=-1)
    flat_hits = chosen.reshape(local_rows * picks, expert_count).astype(jnp.int32)
    before = jnp.cumsum(flat_hits, axis=0) - flat_hits
    slot_index = jnp.sum(before * flat_hits, axis=1)
    target = routes.reshape(local_rows * picks) * capacity + slot_index
    pick_table = (target[None, :] == jnp.arange(slot_count, dtype=jnp.int32)[:, None]).reshape(
        slot_count, local_rows, picks
    )
    dispatch_matrix = jnp.any(pick_table, axis=2).astype(jnp.bfloat16)
    outgoing = (
        jnp.dot(dispatch_matrix, ffn_in, preferred_element_type=jnp.float32)
        .astype(jnp.bfloat16)
        .reshape(owners, experts_here, capacity, model_width)
    )
    arrived = lax.all_to_all(outgoing, "ep", split_axis=0, concat_axis=0, tiled=True)
    gate_val = jnp.einsum("secd,edf->secf", arrived, gate_proj, preferred_element_type=jnp.float32)
    up_val = jnp.einsum("secd,edf->secf", arrived, up_proj, preferred_element_type=jnp.float32)
    act_low = (jax.nn.silu(gate_val) * up_val).astype(jnp.bfloat16)
    half_out = jnp.einsum(
        "secf,efd->secd", act_low, down_proj, preferred_element_type=jnp.float32
    ).astype(jnp.bfloat16)
    spread_out = jnp.broadcast_to(
        half_out[:, None], (owners, halves, experts_here, capacity, model_width)
    ).reshape(owners * halves, experts_here, capacity, model_width)
    returned = lax.all_to_all(spread_out, ("ep", "tp"), split_axis=0, concat_axis=0, tiled=True)
    expert_rows = jnp.sum(
        returned.reshape(owners, halves, experts_here, capacity, model_width).astype(jnp.float32),
        axis=1,
    ).reshape(slot_count, model_width)
    routed = jnp.take(expert_rows, target, axis=0).reshape(local_rows, picks, model_width)
    layer_val = residual + jnp.sum(gates[..., None] * routed, axis=1)
    layer_out = layer_val.astype(jnp.bfloat16)
    grad_stream = out_grad.astype(jnp.float32)
    slot_grad = (
        (gates[..., None] * grad_stream[:, None, :])
        .astype(jnp.bfloat16)
        .reshape(local_rows * picks, model_width)
    )
    grad_slots = (
        jnp.zeros((slot_count, model_width), jnp.bfloat16)
        .at[target]
        .set(slot_grad)
        .reshape(owners, experts_here, capacity, model_width)
    )
    grad_arrived = lax.all_to_all(grad_slots, "ep", split_axis=0, concat_axis=0, tiled=True)
    gate_grad_rows = jnp.sum(grad_stream[:, None, :] * routed, axis=-1)
    picked_grad = gates * (gate_grad_rows - jnp.sum(gates * gate_grad_rows, axis=-1, keepdims=True))
    logit_grad = jnp.sum(jnp.where(chosen, picked_grad[:, :, None], 0.0), axis=1).astype(
        jnp.bfloat16
    )
    act_grad = jnp.einsum(
        "secd,efd->secf", grad_arrived, down_proj, preferred_element_type=jnp.float32
    )
    down_grad = jnp.einsum(
        "secf,secd->efd", act_low, grad_arrived, preferred_element_type=jnp.float32
    )
    sigmoid_val = jax.nn.sigmoid(gate_val)
    gate_low = (act_grad * up_val * sigmoid_val * (1.0 + gate_val * (1.0 - sigmoid_val))).astype(
        jnp.bfloat16
    )
    up_low = (act_grad * jax.nn.silu(gate_val)).astype(jnp.bfloat16)
    gate_grad = jnp.einsum("secd,secf->edf", arrived, gate_low, preferred_element_type=jnp.float32)
    up_grad = jnp.einsum("secd,secf->edf", arrived, up_low, preferred_element_type=jnp.float32)
    input_part = jnp.einsum(
        "secf,edf->secd", gate_low, gate_proj, preferred_element_type=jnp.float32
    ) + jnp.einsum("secf,edf->secd", up_low, up_proj, preferred_element_type=jnp.float32)
    spread_grad = jnp.broadcast_to(
        input_part[:, None], (owners, halves, experts_here, capacity, model_width)
    ).reshape(owners * halves, experts_here, capacity, model_width)
    came_back = lax.all_to_all(spread_grad, ("ep", "tp"), split_axis=0, concat_axis=0, tiled=True)
    row_grads = jnp.sum(
        came_back.reshape(owners, halves, experts_here, capacity, model_width), axis=1
    )
    row_grads = row_grads.reshape(slot_count, model_width)
    ffn_in_grad = jnp.sum(
        jnp.take(row_grads, target, axis=0).reshape(local_rows, picks, model_width), axis=1
    ) + contract_cols(logit_grad, whole_router)
    router_grad = contract_rows(ffn_in, logit_grad)
    ffn_gain_part = jnp.sum(ffn_in_grad * mid_normed, axis=0)
    second_normed_grad = ffn_in_grad * ffn_gain
    mid_grad = grad_stream + second_inverse * (
        second_normed_grad
        - mid_normed * jnp.mean(second_normed_grad * mid_normed, axis=-1, keepdims=True)
    )
    branch_grad = mid_grad.astype(jnp.bfloat16)
    out_proj_full = contract_rows(branch_grad, attn_low)
    value_grad_in = (
        jnp.dot(branch_grad, whole_out, preferred_element_type=jnp.float32)
        .astype(jnp.bfloat16)
        .reshape(local_rows, kv_here, queries_each_key_head, head_dim)
    )

    def delta_step(block_index, summed):
        _, value_rows, allowed, scores = key_block_parts(block_index)
        prob_grad = jnp.einsum(
            "thgd,khd->hgtk", value_grad_in, value_rows, preferred_element_type=jnp.float32
        )
        return summed + jnp.sum(probabilities(allowed, scores) * prob_grad, axis=-1)

    delta = lax.fori_loop(0, key_blocks, delta_step, jnp.zeros(stat_shape, jnp.float32))

    def grad_step(block_index, state_triple):
        query_acc, key_acc, value_acc = state_triple
        key_rows, value_rows, allowed, scores = key_block_parts(block_index)
        probs_full = probabilities(allowed, scores)
        prob_grad = jnp.einsum(
            "thgd,khd->hgtk", value_grad_in, value_rows, preferred_element_type=jnp.float32
        )
        score_grad = (probs_full * (prob_grad - delta[..., None])).astype(jnp.bfloat16)
        query_acc = query_acc + jnp.einsum(
            "hgtk,khd->thgd", score_grad, key_rows, preferred_element_type=jnp.float32
        )
        key_part = (
            jnp.einsum("hgtk,thgd->khd", score_grad, query_low, preferred_element_type=jnp.float32)
            * score_scale
        )
        value_part = jnp.einsum(
            "hgtk,thgd->khd",
            probs_full.astype(jnp.bfloat16),
            value_grad_in,
            preferred_element_type=jnp.float32,
        )
        key_acc = lax.dynamic_update_slice_in_dim(
            key_acc, key_part.reshape(key_block, kv_here * head_dim), block_index * key_block, 0
        )
        value_acc = lax.dynamic_update_slice_in_dim(
            value_acc, value_part.reshape(key_block, kv_here * head_dim), block_index * key_block, 0
        )
        return (query_acc, key_acc, value_acc)

    grad_shape = (seq_len, kv_here * head_dim)
    query_acc, key_acc, value_acc = lax.fori_loop(
        0,
        key_blocks,
        grad_step,
        (
            jnp.zeros((local_rows, kv_here, queries_each_key_head, head_dim), jnp.float32),
            jnp.zeros(grad_shape, jnp.float32),
            jnp.zeros(grad_shape, jnp.float32),
        ),
    )
    key_sum, value_sum = (
        lax.psum_scatter(key_acc, "ep", scatter_dimension=0, tiled=True),
        lax.psum_scatter(value_acc, "ep", scatter_dimension=0, tiled=True),
    )
    q_raw_grad, query_gain_part = norm_backward(
        (query_acc * score_scale).reshape(local_rows, heads_here, head_dim),
        q_unit,
        q_inverse,
        query_gain,
        angles,
    )
    k_raw_grad, key_gain_part = norm_backward(
        key_sum.reshape(local_rows, kv_here, head_dim), k_unit, k_inverse, key_gain, angles
    )
    q_grad_low = q_raw_grad.reshape(local_rows, heads_here * head_dim).astype(jnp.bfloat16)
    k_grad_low = k_raw_grad.reshape(local_rows, kv_here * head_dim).astype(jnp.bfloat16)
    v_grad_low = value_sum.astype(jnp.bfloat16)
    in_part = (
        contract_cols(q_grad_low, whole_query)
        + contract_cols(k_grad_low, whole_key)
        + contract_cols(v_grad_low, whole_value)
    )
    query_full = contract_rows(attention_input, q_grad_low)
    key_full = contract_rows(attention_input, k_grad_low)
    value_full = contract_rows(attention_input, v_grad_low)
    attn_in_grad, query_gain_sum, key_gain_sum = lax.psum(
        (in_part, query_gain_part, key_gain_part), "tp"
    )
    attn_gain_part = jnp.sum(attn_in_grad * normed, axis=0)
    first_normed_grad = attn_in_grad * attn_gain
    tokens_grad = mid_grad + first_inverse * (
        first_normed_grad - normed * jnp.mean(first_normed_grad * normed, axis=-1, keepdims=True)
    )
    (
        gate_total,
        up_total,
        down_total,
        attn_gain_fsdp,
        ffn_gain_fsdp,
        query_gain_fsdp,
        key_gain_fsdp,
    ) = lax.psum(
        (
            gate_grad,
            up_grad,
            down_grad,
            attn_gain_part,
            ffn_gain_part,
            query_gain_sum,
            key_gain_sum,
        ),
        "fsdp",
    )
    query_share, key_share, value_share, out_share, router_share = (
        lax.psum_scatter(query_full, "fsdp", scatter_dimension=0, tiled=True),
        lax.psum_scatter(key_full, "fsdp", scatter_dimension=0, tiled=True),
        lax.psum_scatter(value_full, "fsdp", scatter_dimension=0, tiled=True),
        lax.psum_scatter(out_proj_full, "fsdp", scatter_dimension=0, tiled=True),
        lax.psum_scatter(router_grad, "fsdp", scatter_dimension=0, tiled=True),
    )
    (
        query_fin,
        key_fin,
        value_fin,
        out_fin,
        router_fin,
        attn_gain_fin,
        ffn_gain_fin,
        query_gain_fin,
        key_gain_fin,
    ) = lax.psum(
        (
            query_share,
            key_share,
            value_share,
            out_share,
            router_share,
            attn_gain_fsdp,
            ffn_gain_fsdp,
            query_gain_fsdp,
            key_gain_fsdp,
        ),
        "ep",
    )
    return (
        layer_out,
        tokens_grad,
        attn_gain_fin,
        query_fin,
        key_fin,
        value_fin,
        out_fin,
        query_gain_fin,
        key_gain_fin,
        ffn_gain_fin,
        router_fin,
        gate_total,
        up_total,
        down_total,
    )


def solution(mesh):
    return jax.shard_map(
        body,
        mesh=mesh,
        in_specs=(
            P(("fsdp", "ep"), None),
            P(("fsdp", "ep"), None),
            P(),
            P(),
            P(),
            P("fsdp", "tp"),
            P("fsdp", "tp"),
            P("fsdp", "tp"),
            P("fsdp", "tp"),
            P(),
            P(),
            P(),
            P("fsdp", None),
            P("ep", None, "tp"),
            P("ep", None, "tp"),
            P("ep", "tp", None),
            P(("fsdp", "ep"), None),
        ),
        out_specs=(
            P(("fsdp", "ep"), None),
            P(("fsdp", "ep"), None),
            P(),
            P("fsdp", "tp"),
            P("fsdp", "tp"),
            P("fsdp", "tp"),
            P("fsdp", "tp"),
            P(),
            P(),
            P(),
            P("fsdp", None),
            P("ep", None, "tp"),
            P("ep", None, "tp"),
            P("ep", "tp", None),
        ),
        check_vma=False,
    )
```

profile of v0, /device:TPU:0, one launch (start us, length us, event | category | flops | bytes accessed | tf_op | source)
XLA Modules:
  0.0 3990.8 jit_solution(1820541770285202204)
XLA Ops:
  11.9 21.8 all-gather.7.cloned.1.call-done
  35.8 20.7 all-gather.5.cloned.1.call-done
  58.2 31.3 all_gather.22
  91.0 27.1 all_gather.24
  118.1 44.1 %all-gather.9.cloned.1.call-done = bf16[2048,2048]{1,0:T(8,128)(2,1)} async-done(((bf16[1024,2048]{1,0:T(8,128)(2,1)}), bf16[2048,2048]{1,0:T(8,128)(2,1)}) %all-gather.9.cloned.1.call-update) | async-done | bytes 8388624 | tf_op jit(solution)/shard_map/all_gather | solution.py:117
  162.2 4.7 fusion.110
  173.0 13.5 while.62
  186.5 6.3 while.63
  193.0 74.6 %all-gather.11.cloned.1.call-done = bf16[2048,2048]{1,0:T(8,128)(2,1)} async-done(((bf16[1024,2048]{1,0:T(8,128)(2,1)}), bf16[2048,2048]{1,0:T(8,128)(2,1)}) %all-gather.11.cloned.1.call-update) | async-done | bytes 8388624 | tf_op jit(solution)/shard_map/all_gather | solution.py:120
  267.6 7.3 fusion.120
  275.3 6.8 reduce-window.6
  282.7 7.9 fusion.27
  290.6 4.3 all-reduce.10.cloned.1.call-done
  297.5 5.7 convolution_convert_fusion
  303.2 8.9 reshape.824
  312.1 195.1 %all_to_all.20 = bf16[8,3,85,2048]{3,2,1,0:T(8,128)(2,1)S(1)} all-to-all(bf16[8,3,85,2048]{3,2,1,0:T(8,128)(2,1)} %reshape.824), channel_id=1, replica_groups=mesh['fsdp'=2,'ep'=8,'tp'=2] {'ep'}, dimensions={0} | all-to-all | bytes 16711680 | tf_op jit(solution)/shard_map/all_to_all | solution.py:231
  507.3 6.4 fusion.34
  513.7 9.1 fusion.55
  524.0 9.3 convert_bitcast_fusion
  533.2 8.7 copy.250
  542.0 11.0 broadcast_in_dim.303
  553.0 5.3 all-to-all-start.1
  558.5 4.8 all_gather.27
  564.0 300.1 %all-to-all-done.1 = bf16[16,3,85,2048]{3,2,1,0:T(8,128)(2,1)} async-done(((bf16[16,3,85,2048]{3,2,1,0:T(8,128)(2,1)}), bf16[16,3,85,2048]{3,2,1,0:T(8,128)(2,1)}, u32[]{:S(2)}, u32[]{:S(2)}) %all-to-all-start.1) | async-done | bytes 16711712 | tf_op jit(solution)/shard_map/all_to_all | solution.py:241
  864.1 14.7 convert_reduce_fusion
  878.8 17.1 reshape.826
  896.0 14.6 gather_fusion
  910.6 4.2 fusion.25
  915.1 11.8 scatter_custom_fusion
  926.9 8.8 reshape.828
  935.8 262.5 %all_to_all.21 = bf16[8,3,85,2048]{3,2,1,0:T(8,128)(2,1)} all-to-all(bf16[8,3,85,2048]{3,2,1,0:T(8,128)(2,1)} %reshape.828), channel_id=1, replica_groups=mesh['fsdp'=2,'ep'=8,'tp'=2] {'ep'}, dimensions={0} | all-to-all | bytes 16711680 | tf_op jit(solution)/shard_map/all_to_all | solution.py:261
  1198.3 12.3 fusion.54
  1210.6 11.9 fusion.38
  1222.6 13.2 add_bitcast_fusion
  1235.8 6.7 copy.255
  1242.5 11.8 broadcast_in_dim.305
  1254.2 6.0 all-to-all-start.3
  1260.3 607.0 %all-to-all-done.3 = f32[16,3,85,2048]{3,2,1,0:T(8,128)} async-done(((f32[16,3,85,2048]{3,2,1,0:T(8,128)}), f32[16,3,85,2048]{3,2,1,0:T(8,128)}, u32[]{:S(2)}, u32[]{:S(2)}) %all-to-all-start.3) | async-done | bytes 33423392 | tf_op jit(solution)/shard_map/all_to_all | solution.py:286
  1867.3 20.1 bitcast_reduce_fusion
  1887.4 17.1 reshape.831
  1904.5 14.6 gather_fusion.1
  1919.1 10.3 bitcast_reduce_fusion.1
  1931.8 5.0 fusion.66
  1937.6 11.4 while.64
  1951.2 31.5 while.65
  1986.2 197.7 %reduce-scatter.8.cloned.1.call-done = f32[128,256]{0,1:T(8,128)} async-done(((f32[1024,256]{0,1:T(8,128)}), f32[128,256]{0,1:T(8,128)}) %reduce-scatter.8.cloned.1.call-update) | async-done | bytes 131088 | tf_op jit(solution)/shard_map/reduce_scatter | solution.py:359
  2189.9 60.4 %reduce-scatter.10.cloned.1.call-done = f32[128,256]{0,1:T(8,128)} async-done(((f32[1024,256]{0,1:T(8,128)}), f32[128,256]{0,1:T(8,128)}) %reduce-scatter.10.cloned.1.call-update) | async-done | bytes 131088 | tf_op jit(solution)/shard_map/reduce_scatter | solution.py:360
  2262.1 8.2 fusion.108
  2272.0 8.3 fusion.78
  2280.6 10.6 convolution_bitcast_fusion.3
  2291.2 6.5 fusion.122
  2299.8 10.2 convolution_bitcast_fusion.2
  2310.0 11.2 fusion.43
  2321.3 10.6 reduce-scatter.16.cloned.1.call-done
  2331.9 191.6 %reduce-scatter.12.cloned.1.call-done = f32[1024,2048]{1,0:T(8,128)} async-done(((f32[2048,2048]{1,0:T(8,128)}), f32[1024,2048]{1,0:T(8,128)}) %reduce-scatter.12.cloned.1.call-update) | async-done | bytes 8388624 | tf_op jit(solution)/shard_map/reduce_scatter | solution.py:412
  2523.5 191.3 %reduce-scatter.18.cloned.1.call-done = f32[1024,2048]{1,0:T(8,128)} async-done(((f32[2048,2048]{1,0:T(8,128)}), f32[1024,2048]{1,0:T(8,128)}) %reduce-scatter.18.cloned.1.call-update) | async-done | bytes 8388624 | tf_op jit(solution)/shard_map/reduce_scatter | solution.py:415
  2717.6 19.9 all-reduce.12.cloned.1.call-done
  2739.1 8.5 all-reduce.3
  2747.6 37.7 all-reduce
  2787.8 582.0 %all-reduce.16.cloned.1.call-done = (f32[3,2048,384]{2,1,0:T(8,128)}, f32[3,2048,384]{2,1,0:T(8,128)}, f32[3,384,2048]{2,1,0:T(8,128)}) async-done(((f32[3,2048,384]{2,1,0:T(8,128)}, f32[3,2048,384]{2,1,0:T(8,128)}, f32[3,384,2048]{2,1,0:T(8,128)}), (f32[3,2048,384]{2,1,0:T(8,128)}, f32[3,2048,384]{2,1,0:T(8,128)}, f32[3,384,2048]{2,1,0:T(8,128)})) %all-reduce.16.cloned.1.call-update) | async-done | bytes 28311568 | tf_op jit(solution)/shard_map/psum | solution.py:399
  3369.9 581.7 %all-reduce.14.cloned.1.call-done = (f32[1024,2048]{1,0:T(8,128)}, f32[1024,256]{1,0:T(8,128)}, f32[1024,256]{1,0:T(8,128)}, f32[1024,2048]{1,0:T(8,128)}, f32[1024,24]{0,1:T(8,128)}) async-done(((f32[1024,2048]{1,0:T(8,128)}, f32[1024,256]{1,0:T(8,128)}, f32[1024,256]{1,0:T(8,128)}, f32[1024,2048]{1,0:T(8,128)}, f32[1024,24]{0,1:T(8,128)}), (f32[1024,2048]{1,0:T(8,128)}, f32[1024,256]{1,0:T(8,128)}, ...) | async-done | bytes 18972688 | tf_op jit(solution)/shard_map/psum | solution.py:428
  3951.6 8.4 copy.393
  3962.0 4.3 copy.396
  3966.9 9.3 copy.398
  (427 shorter events, 131.0 us)
Async XLA Ops:
  7.2 26.5 all-gather.7.cloned.1.call-start
  7.9 48.6 %all-gather.5.cloned.1.call-start = ((), (), s32[]{:S(2)}) async-start(), calls=%async_computation.11 | async-start | bytes 1572864 | tf_op jit(solution)/shard_map/all_gather | solution.py:119
  8.7 25.0 copy-start.44
  8.7 153.4 %all-gather.9.cloned.1.call-start = ((), (), s32[]{:S(2)}) async-start(), calls=%async_computation.13 | async-start | bytes 12582912 | tf_op jit(solution)/shard_map/all_gather | solution.py:117
  9.4 26.2 copy-start.78
  9.5 258.1 %all-gather.11.cloned.1.call-start = ((), (), s32[]{:S(2)}) async-start(), calls=%async_computation.14 | async-start | bytes 12582912 | tf_op jit(solution)/shard_map/all_gather | solution.py:120
  10.0 284.9 %all-reduce.10.cloned.1.call-start = ((), (), s32[]{:S(2)}) async-start(), calls=%async_computation.15 | async-start | bytes 2097152 | tf_op jit(solution)/shard_map/psum | solution.py:209
  10.4 156.5 %copy-start.52 = (s32[2048]{0:T(1024)}, s32[2048]{0:T(1024)S(1)}, u32[]{:S(2)}) copy-start(s32[2048]{0:T(1024)S(1)} %fusion.91) | copy-start | bytes 24580
  10.7 156.2 %copy-start.69 = (f32[128]{0:T(128)}, f32[128]{0:T(128)S(1)}, u32[]{:S(2)}) copy-start(f32[128]{0:T(128)S(1)} %add_rsqrt_fusion.3) | copy-start | bytes 1540
  35.3 131.6 %copy-start.49 = (f32[128,256]{1,0:T(8,128)}, f32[128,256]{1,0:T(8,128)S(1)}, u32[]{:S(2)}) copy-start(f32[128,256]{1,0:T(8,128)S(1)} %fusion.112) | copy-start | bytes 393220
  35.4 21.2 copy-start.27
  35.6 21.0 copy-start.36
  118.1 50.7 %copy-start.73 = (f32[128]{0:T(128)S(1)}, f32[128]{0:T(128)}, u32[]{:S(2)}) copy-start(f32[128]{0:T(128)} %param.36) | copy-start | bytes 1540
  192.8 82.0 %copy-start.2 = (bf16[128,2,8,128]{3,0,2,1:T(8,128)(2,1)}, bf16[128,2,8,128]{3,0,2,1:T(8,128)(2,1)S(1)}, u32[]{:S(2)}) copy-start(bf16[128,2,8,128]{3,0,2,1:T(8,128)(2,1)S(1)} %get-tuple-element.1951) | copy-start | bytes 1572868
  192.9 82.0 %copy-start.4 = (bf16[1024,256]{0,1:T(8,128)(2,1)}, bf16[1024,256]{0,1:T(8,128)(2,1)S(1)}, u32[]{:S(2)}) copy-start(bf16[1024,256]{0,1:T(8,128)(2,1)S(1)} %get-tuple-element.1955) | copy-start | bytes 1572868
  192.9 82.0 %copy-start.42 = (f32[2,8,128]{2,1,0:T(8,128)}, f32[2,8,128]{2,1,0:T(8,128)S(1)}, u32[]{:S(2)}) copy-start(f32[2,8,128]{2,1,0:T(8,128)S(1)} %get-tuple-element.1999) | copy-start | bytes 24580
  192.9 82.0 %copy-start.51 = (s32[1024]{0:T(1024)}, s32[1024]{0:T(1024)S(1)}, u32[]{:S(2)}) copy-start(s32[1024]{0:T(1024)S(1)} %get-tuple-element.2009) | copy-start | bytes 12292
  192.9 82.0 %copy-start.53 = (s32[1024]{0:T(1024)}, s32[1024]{0:T(1024)S(1)}, u32[]{:S(2)}) copy-start(s32[1024]{0:T(1024)S(1)} %get-tuple-element.2012) | copy-start | bytes 12292
  192.9 82.0 %copy-start.57 = (s32[128]{0:T(128)}, s32[128]{0:T(128)S(1)}, u32[]{:S(2)}) copy-start(s32[128]{0:T(128)S(1)} %get-tuple-element.2015) | copy-start | bytes 1540
  192.9 82.0 %copy-start.58 = (s32[128]{0:T(128)}, s32[128]{0:T(128)S(1)}, u32[]{:S(2)}) copy-start(s32[128]{0:T(128)S(1)} %get-tuple-element.2018) | copy-start | bytes 1540
  192.9 82.0 %copy-start.62 = (f32[2,8,128]{2,1,0:T(8,128)}, f32[2,8,128]{2,1,0:T(8,128)S(1)}, u32[]{:S(2)}) copy-start(f32[2,8,128]{2,1,0:T(8,128)S(1)} %get-tuple-element.2020) | copy-start | bytes 24580
  193.0 81.9 %copy-start.19 = (bf16[128,2,8,128]{0,3,2,1:T(8,128)(2,1)}, bf16[128,2,8,128]{0,3,2,1:T(8,128)(2,1)S(1)}, u32[]{:S(2)}) copy-start(bf16[128,2,8,128]{0,3,2,1:T(8,128)(2,1)S(1)} %convert_element_type.111) | copy-start | bytes 1572868
  275.0 22.3 copy-start.64
  297.5 265.9 %copy-start.18 = (bf16[128,2048]{1,0:T(8,128)(2,1)}, bf16[128,2048]{1,0:T(8,128)(2,1)S(1)}, u32[]{:S(2)}) copy-start(bf16[128,2048]{1,0:T(8,128)(2,1)S(1)} %multiply_convert_fusion) | copy-start | bytes 1572868
  303.2 204.1 %slice-start.8 = ((s8[4718592]{0:T(1024)(128)(4,1)}), s8[524288]{0:T(1024)(128)(4,1)S(1)}, s32[]{:S(2)}) async-start(s8[4718592]{0:T(1024)(128)(4,1)} %bitcast.437), calls=%async_computation.34 | async-start | bytes 1048576
  312.1 195.1 %slice-start.9 = ((s8[4718592]{0:T(1024)(128)(4,1)}), s8[4194304]{0:T(1024)(128)(4,1)S(1)}, s32[]{:S(2)}) async-start(s8[4718592]{0:T(1024)(128)(4,1)} %bitcast.437), calls=%async_computation.35 | async-start | bytes 8388608
  553.0 311.1 %all-to-all-start.1 = ((bf16[16,3,85,2048]{3,2,1,0:T(8,128)(2,1)}), bf16[16,3,85,2048]{3,2,1,0:T(8,128)(2,1)}, u32[]{:S(2)}, u32[]{:S(2)}) async-start(bf16[16,3,85,2048]{3,2,1,0:T(8,128)(2,1)} %bitcast.417), calls=%async_computation.1 | async-start | bytes 34603008 | tf_op jit(solution)/shard_map/all_to_all | solution.py:241
  1210.6 11.9 copy-start.29
  1210.6 11.9 copy-start.30
  1254.2 613.1 %all-to-all-start.3 = ((f32[16,3,85,2048]{3,2,1,0:T(8,128)}), f32[16,3,85,2048]{3,2,1,0:T(8,128)}, u32[]{:S(2)}, u32[]{:S(2)}) async-start(f32[16,3,85,2048]{3,2,1,0:T(8,128)} %bitcast.416), calls=%async_computation.3 | async-start | bytes 69206016 | tf_op jit(solution)/shard_map/all_to_all | solution.py:286
  1260.2 923.6 %reduce-scatter.8.cloned.1.call-start = ((), (), s32[]{:S(2)}) async-start(), calls=%async_computation.16 | async-start | bytes 1179648 | tf_op jit(solution)/shard_map/reduce_scatter | solution.py:359
  1260.3 669.1 %copy-start.66 = (bf16[128,24]{0,1:T(8,128)(2,1)}, bf16[128,24]{0,1:T(8,128)(2,1)S(1)}, u32[]{:S(2)}) copy-start(bf16[128,24]{0,1:T(8,128)(2,1)S(1)} %select_reduce_fusion.1) | copy-start | bytes 18436
  1919.1 10.3 copy-start.14
  1919.1 10.3 copy-start.41
  1919.1 10.3 copy-start.65
  1919.1 10.4 copy-start.76
  1919.1 11.4 copy-start.26
  1951.2 234.8 %copy-start.28 = (f32[128,2,128]{2,1,0:T(2,128)S(1)}, f32[128,2,128]{2,1,0:T(2,128)}, u32[]{:S(2)}) copy-start(f32[128,2,128]{2,1,0:T(2,128)} %copy-done.27) | copy-start | bytes 393220
  1982.7 204.8 %copy-start.37 = (f32[128,2]{1,0:T(8,128)S(1)}, f32[128,2]{1,0:T(8,128)}, u32[]{:S(2)}) copy-start(f32[128,2]{1,0:T(8,128)} %copy-done.36) | copy-start | bytes 3076
  1982.7 205.2 %copy-start.50 = (f32[128,256]{1,0:T(8,128)S(1)}, f32[128,256]{1,0:T(8,128)}, u32[]{:S(2)}) copy-start(f32[128,256]{1,0:T(8,128)} %copy-done.49) | copy-start | bytes 393220
  1982.7 205.2 %copy-start.7 = (bf16[128,2048]{1,0:T(8,128)(2,1)S(1)}, bf16[128,2048]{1,0:T(8,128)(2,1)}, u32[]{:S(2)}) copy-start(bf16[128,2048]{1,0:T(8,128)(2,1)} %param.27) | copy-start | bytes 1572868
  1982.7 205.2 %copy-start.45 = (f32[2048]{0:T(1024)S(1)}, f32[2048]{0:T(1024)}, u32[]{:S(2)}) copy-start(f32[2048]{0:T(1024)} %param.31) | copy-start | bytes 24580
  1982.7 205.2 %copy-start.70 = (f32[128]{0:T(128)S(1)}, f32[128]{0:T(128)}, u32[]{:S(2)}) copy-start(f32[128]{0:T(128)} %copy-done.69) | copy-start | bytes 1540
  1982.7 267.6 %reduce-scatter.10.cloned.1.call-start = ((), (), s32[]{:S(2)}) async-start(), calls=%async_computation.17 | async-start | bytes 1179648 | tf_op jit(solution)/shard_map/reduce_scatter | solution.py:360
  1983.5 337.8 %reduce-scatter.20.cloned.1.call-start = ((), (), s32[]{:S(2)}) async-start(), calls=%async_computation.23 | async-start | bytes 294912 | tf_op jit(solution)/shard_map/reduce_scatter | solution.py:416
  1986.1 335.2 %reduce-scatter.14.cloned.1.call-start = ((), (), s32[]{:S(2)}) async-start(), calls=%async_computation.20 | async-start | bytes 3145728 | tf_op jit(solution)/shard_map/reduce_scatter | solution.py:413
  2187.9 65.4 %copy-start.74 = (f32[128]{0:T(128)S(1)}, f32[128]{0:T(128)}, u32[]{:S(2)}) copy-start(f32[128]{0:T(128)} %param.36) | copy-start | bytes 1540
  2187.9 65.4 %copy-start.8 = (f32[128,2,8,128]{0,3,2,1:T(8,128)S(1)}, f32[128,2,8,128]{0,3,2,1:T(8,128)}, u32[]{:S(2)}) copy-start(f32[128,2,8,128]{0,3,2,1:T(8,128)} %get-tuple-element.803) | copy-start | bytes 3145732
  2189.8 142.1 %reduce-scatter.16.cloned.1.call-start = ((), (), s32[]{:S(2)}) async-start(), calls=%async_computation.21 | async-start | bytes 3145728 | tf_op jit(solution)/shard_map/reduce_scatter | solution.py:414
  2253.1 270.4 %reduce-scatter.12.cloned.1.call-start = ((), (), s32[]{:S(2)}) async-start(), calls=%async_computation.19 | async-start | bytes 25165824 | tf_op jit(solution)/shard_map/reduce_scatter | solution.py:412
  2270.4 444.4 %reduce-scatter.18.cloned.1.call-start = ((), (), s32[]{:S(2)}) async-start(), calls=%async_computation.22 | async-start | bytes 25165824 | tf_op jit(solution)/shard_map/reduce_scatter | solution.py:415
  2280.3 457.2 %all-reduce.12.cloned.1.call-start = ((), (), s32[]{:S(2)}) async-start(), calls=%async_computation.18 | async-start | bytes 2097152 | tf_op jit(solution)/shard_map/psum | solution.py:383
  2299.7 1070.2 %all-reduce.16.cloned.1.call-start = ((), (), s32[]{:S(2)}) async-start(), calls=%async_computation.25 | async-start | bytes 56623104 | tf_op jit(solution)/shard_map/psum | solution.py:399
  2299.8 10.2 copy-start.80
  2321.2 1630.4 %all-reduce.14.cloned.1.call-start = ((), (), s32[]{:S(2)}) async-start(), calls=%async_computation.24 | async-start | bytes 37945344 | tf_op jit(solution)/shard_map/psum | solution.py:428
  2714.8 24.3 copy-start.71
  3951.6 10.4 slice-start.6
  3951.6 9.4 copy-start.38
  3951.6 10.4 slice-start.7
  3962.0 14.3 slice-start.3
  3962.0 14.3 slice-start.4
  3966.9 9.4 slice-start.5
  3966.9 13.1 slice-start
  3966.9 13.1 slice-start.1
  (55 other events, 198.7 us)
Sparse Core Ops, SparseCore 0:
  9.6 24.0 all-gather.6
  35.2 21.2 all-gather.4
  58.1 103.9 all-gather.8
  163.6 103.9 all-gather.10
  275.1 19.7 all-reduce.9
  1982.8 200.9 reduce-scatter.7
  2187.3 62.9 reduce-scatter.9
  2252.6 9.9 reduce-scatter.19
  2265.5 31.8 reduce-scatter.13
  2300.0 31.8 reduce-scatter.15
  2334.3 189.1 reduce-scatter.11
  2525.6 189.1 reduce-scatter.17
  2717.8 19.5 all-reduce.11
  2740.6 629.1 all-reduce.15
  3374.8 576.7 all-reduce.13
where the time goes:
time: 4000 us; the launch traced here: 3990 us
  waiting for transfers between devices  2910 us (73%)
  blocking collectives  570 us (14%)
  local copies, waits for them, and re-layouts  190 us (5%)
  matrix products  184 us (5%)
  other arithmetic  107 us (3%)
    all_to_all x1, waiting for transfers between devices, body(): lax.all_to_all(spread_grad, ('ep', 'tp'), split_axis=0, concat_axis=0, ti...  607 us
    psum x1, waiting for transfers between devices, body(): lax.psum((gate_grad, up_grad, down_grad, attn_gain_part, ffn_gain_part, q...  582 us
    psum x1, waiting for transfers between devices, body(): lax.psum((query_share, key_share, value_share, out_share, router_share, a...  582 us
    all_to_all x1, waiting for transfers between devices, body(): lax.all_to_all(spread_out, ('ep', 'tp'), split_axis=0, concat_axis=0, til...  300 us
    all_to_all x1, blocking collectives, body(): lax.all_to_all(grad_slots, 'ep', split_axis=0, concat_axis=0, tiled=True)  263 us
    reduce_scatter x1, waiting for transfers between devices, body(): lax.psum_scatter(key_acc, 'ep', scatter_dimension=0, tiled=True)  198 us
    all_to_all x1, blocking collectives, body(): lax.all_to_all(outgoing, 'ep', split_axis=0, concat_axis=0, tiled=True)  195 us
    reduce_scatter x1, waiting for transfers between devices, body(): lax.psum_scatter(query_full, 'fsdp', scatter_dimension=0, tiled=True)  192 us
  transfers between devices with their start and end apart: 17, of which 15 were waited for; matrix products, arithmetic and copies ran while one was open for 3% of the time, Pallas kernels for 0%

commit v1 on v0

v1 whole, which is shorter than its diff:
```python
import math

import jax
import jax.numpy as jnp
import numpy as np
from jax import lax
from jax.sharding import PartitionSpec as P

PIECE = 256


EPSILON = 1e-06
LOG_THETA = math.log(1000000.0)
MASKED_SCORE = -1e30
LANES = 128
BF16 = jnp.bfloat16
F32 = jnp.float32


def inverse_norm(values):
    return lax.rsqrt(jnp.mean(values * values, axis=-1, keepdims=True) + EPSILON)


def rotate(vectors, cosine, sine):
    half_dim = vectors.shape[-1] // 2
    leading = vectors[..., :half_dim]
    trailing = vectors[..., half_dim:]
    return jnp.concatenate(
        [leading * cosine - trailing * sine, trailing * cosine + leading * sine], axis=-1
    )


def norm_backward(grad_rot, unit, inverse, gain, cosine, sine):
    grad_normed = rotate(grad_rot, cosine, -sine)
    gain_part = jnp.sum(grad_normed * unit, axis=(0, 1))
    unit_grad = grad_normed * gain
    raw_grad = inverse * (unit_grad - unit * jnp.mean(unit_grad * unit, axis=-1, keepdims=True))
    return (raw_grad, gain_part)


def dot(left, right):
    return jnp.dot(left, right, preferred_element_type=F32)


def contract_rows(left, right):
    return lax.dot_general(left, right, (((0,), (0,)), ((), ())), preferred_element_type=F32)


def contract_cols(left, right):
    return lax.dot_general(left, right, (((1,), (1,)), ((), ())), preferred_element_type=F32)


class Ring:
    def __init__(self):
        self.owners = lax.axis_size("ep")
        self.groups = lax.axis_size("fsdp")
        self.index = lax.axis_index("ep")
        self.group = lax.axis_index("fsdp")
        self.half = lax.axis_index("tp")
        n = self.owners
        if n == 8:
            order = [0, 2, 4, 6, 7, 5, 3, 1] if self.groups == 2 else [0, 1, 2, 3, 7, 6, 5, 4]
        else:
            order = list(range(n))
        self.forward = [(order[i], order[(i + 1) % n]) for i in range(n)]
        self.backward = [(dst, src) for src, dst in self.forward]
        self.ahead = n // 2
        self.behind = (n - 1) // 2
        offsets = [0]
        for step in range(1, self.ahead + 1):
            offsets.append(-step)
            if step <= self.behind:
                offsets.append(step)
        self.slot = {offset: place for place, offset in enumerate(offsets)}
        self.slot[self.ahead] = self.slot[-self.ahead] if n % 2 == 0 else self.slot[self.ahead]
        table = np.zeros((n, n), np.int32)
        for position, owner in enumerate(order):
            for place, offset in enumerate(offsets):
                table[owner, place] = order[(position + offset) % n]
        self.owners_by_slot = jnp.asarray(table)[self.index]

    def send(self, values, pairs, axis="ep"):
        return lax.ppermute(values, axis, pairs)

    def swap_halves(self, values):
        return self.send(values, [(0, 1), (1, 0)], "tp")

    def swap_groups(self, values):
        return self.send(values, [(0, 1), (1, 0)], "fsdp")

    def blocks(self, own):
        ahead, behind = own, own
        found = [own]
        for step in range(1, self.ahead + 1):
            ahead = self.send(ahead, self.forward)
            found.append(ahead)
            if step <= self.behind:
                behind = self.send(behind, self.backward)
                found.append(behind)
        return found

    def gather(self, own):
        mine = jnp.concatenate(self.blocks(own), axis=0)
        return mine, jnp.concatenate([mine, self.swap_halves(mine)], axis=0)

    def scatter(self, partial):
        rows, width = partial.shape
        mine = partial[: rows // 2].astype(F32) + self.swap_halves(partial[rows // 2 :]).astype(F32)
        mine = mine.astype(BF16).reshape(self.owners, rows // 2 // self.owners, width)

        def block(offset):
            return mine[self.slot[offset]].astype(F32)

        total = block(0)
        ahead = block(self.ahead)
        for offset in range(self.ahead - 1, -1, -1):
            ahead = self.send(ahead.astype(BF16), self.forward).astype(F32)
            if offset:
                ahead = ahead + block(offset)
        if self.behind:
            behind = block(-self.behind)
            for offset in range(self.behind - 1, -1, -1):
                behind = self.send(behind.astype(BF16), self.backward).astype(F32)
                if offset:
                    behind = behind + block(-offset)
            total = total + behind
        return total + ahead

    def own_rows(self, values):
        rows = values.shape[0] // 2
        return lax.dynamic_slice_in_dim(values, self.half * rows, rows)

    def join_halves(self, own):
        other = self.swap_halves(own)
        first = self.half == 0
        return jnp.concatenate([jnp.where(first, own, other), jnp.where(first, other, own)], axis=0)

    def whole_rows(self, own):
        if self.groups == 2:
            other = self.swap_groups(own)
            first = self.group == 0
            return jnp.concatenate(
                [jnp.where(first, own, other), jnp.where(first, other, own)], axis=0
            )
        return lax.all_gather(own, "fsdp", axis=0, tiled=True)

    def share_rows(self, left, right, kind):
        share = left.shape[1] // self.groups
        if self.groups == 2:
            theirs = lax.dynamic_slice_in_dim(left, (1 - self.group) * share, share, 1)
            ours = lax.dynamic_slice_in_dim(left, self.group * share, share, 1)
            arrived = self.swap_groups(contract_rows(theirs, right).astype(kind))
            return contract_rows(ours, right) + arrived.astype(F32)
        return lax.psum_scatter(
            contract_rows(left, right), "fsdp", scatter_dimension=0, tiled=True
        )

    def other_group(self, mine):
        theirs = self.swap_groups(mine)
        return jnp.concatenate([theirs, self.swap_halves(theirs)], axis=0)

    def all_groups(self, mine):
        theirs = lax.all_gather(mine, "fsdp", axis=0)
        return jnp.concatenate([theirs, self.swap_halves(theirs)], axis=1)

    def sum_all(self, values):
        for axis in ("ep", "fsdp", "tp"):
            step = 1
            while step < lax.axis_size(axis):
                pairs = [(i, i ^ step) for i in range(lax.axis_size(axis))]
                values = values + self.send(values, pairs, axis)
                step *= 2
        return values


def pad_lanes(values):
    return jnp.pad(values, ((0, 0), (0, LANES - values.shape[1])))


def expert_terms(rows, grads, weights, gate_up, down):
    tokens_here, experts_here = weights.shape
    hidden = down.shape[0]
    each = hidden // experts_here
    both = dot(rows, gate_up)
    gate_val, up_val = both[:, :hidden], both[:, hidden:]
    back = contract_cols(grads, down)
    spread = jnp.concatenate(
        [jnp.broadcast_to(weights[:, i : i + 1], (tokens_here, each)) for i in range(experts_here)],
        axis=1,
    )
    sigmoid_val = jax.nn.sigmoid(gate_val)
    silu_val = gate_val * sigmoid_val
    act = silu_val * up_val
    act_grad = spread * back
    weighted = (spread * act).astype(BF16)
    gate_low = (act_grad * up_val * sigmoid_val * (1.0 + gate_val * (1.0 - sigmoid_val))).astype(BF16)
    up_low = (act_grad * silu_val).astype(BF16)
    products = act * back
    row_grads = [
        jnp.sum(products[:, i * each : (i + 1) * each], axis=1, keepdims=True)
        for i in range(experts_here)
    ]
    return weighted, jnp.concatenate([gate_low, up_low], axis=1), row_grads


def body(
    tokens,
    routes,
    places,
    piece_starts,
    attn_gain,
    query_proj,
    key_matrix,
    value_matrix,
    out_proj,
    query_gain,
    key_gain,
    ffn_gain,
    router,
    gate_proj,
    up_proj,
    down_proj,
    out_grad,
):
    ring = Ring()
    local_rows, width = tokens.shape
    head_dim = query_gain.shape[0]
    owners, groups = ring.owners, ring.groups
    heads_tp = query_proj.shape[1] // head_dim
    kv_tp = key_matrix.shape[1] // head_dim
    heads_here = heads_tp // owners
    heads_each_key = heads_tp // kv_tp
    sharers = heads_each_key // heads_here
    experts_here, _, each = gate_proj.shape
    expert_count = experts_here * owners
    picks = routes.shape[1]
    seq_len = local_rows * owners
    half_rows = local_rows // 2
    scale = head_dim ** (-0.5)
    e, f, t = ring.index, ring.group, ring.half
    key_head = (e * heads_here) // heads_each_key
    shared_index = e % sharers

    q_cols = heads_here * head_dim
    attn_weights = ring.whole_rows(
        jnp.concatenate(
            [
                lax.dynamic_slice_in_dim(query_proj, e * q_cols, q_cols, 1),
                lax.dynamic_slice_in_dim(key_matrix, key_head * head_dim, head_dim, 1),
                lax.dynamic_slice_in_dim(value_matrix, key_head * head_dim, head_dim, 1),
            ],
            axis=1,
        )
    )
    out_weights = ring.whole_rows(lax.dynamic_slice_in_dim(out_proj, e * q_cols, q_cols, 1))
    whole_router = ring.whole_rows(router)
    gate_up = jnp.concatenate(
        [gate_proj[i] for i in range(experts_here)] + [up_proj[i] for i in range(experts_here)],
        axis=1,
    )
    down = down_proj.reshape(experts_here * each, width)

    group_places = lax.dynamic_slice_in_dim(places, f * seq_len, seq_len)
    by_slot = jnp.take(group_places.reshape(owners, 2, half_rows), ring.owners_by_slot, axis=0)
    order_places = jnp.concatenate(
        [
            lax.dynamic_index_in_dim(by_slot, t, 1, keepdims=False).reshape(-1),
            lax.dynamic_index_in_dim(by_slot, 1 - t, 1, keepdims=False).reshape(-1),
        ]
    )
    position = order_places % seq_len
    begins = lax.dynamic_slice_in_dim(piece_starts, f, 1)
    inside = (begins <= position[:, None]) & (position[:, None] < begins + PIECE)
    numbers = jnp.arange(1, piece_starts.shape[1] + 1, dtype=jnp.int32)
    pieces = jnp.sum(jnp.where(inside, numbers[None, :], 0), axis=1)
    half_dim = head_dim // 2
    freqs = jnp.exp(jnp.arange(half_dim, dtype=F32) * (-2.0 * LOG_THETA / head_dim))
    angles = position.astype(F32)[:, None] * freqs[None, :]
    cosine, sine = jnp.cos(angles)[:, None, :], jnp.sin(angles)[:, None, :]

    stream = ring.own_rows(tokens).astype(F32)
    first_inverse = inverse_norm(stream)
    normed = stream * first_inverse
    _, attn_in = ring.gather((normed * attn_gain).astype(BF16))
    raw = dot(attn_in, attn_weights)
    q_raw = raw[:, :q_cols].reshape(seq_len, heads_here, head_dim)
    k_raw = raw[:, q_cols : q_cols + head_dim].reshape(seq_len, 1, head_dim)
    value_low = raw[:, q_cols + head_dim :].astype(BF16)
    q_inverse = inverse_norm(q_raw)
    q_unit = q_raw * q_inverse
    k_inverse = inverse_norm(k_raw)
    k_unit = k_raw * k_inverse
    query_low = rotate(q_unit * query_gain, cosine, sine).astype(BF16)
    key_low = rotate(k_unit * key_gain, cosine, sine).astype(BF16).reshape(seq_len, head_dim)
    allowed = (position[None, :] <= position[:, None]) | (
        (pieces[:, None] == pieces[None, :]) & (pieces[:, None] > 0)
    )
    scores = jnp.einsum("thd,kd->htk", query_low, key_low, preferred_element_type=F32) * scale
    scores = jnp.where(allowed[None], scores, MASKED_SCORE)
    weights = jnp.exp(scores - jnp.max(scores, axis=-1, keepdims=True))
    probs = weights / jnp.sum(weights, axis=-1, keepdims=True)
    probs_low = probs.astype(BF16)
    attn_low = (
        jnp.einsum("htk,kd->thd", probs_low, value_low, preferred_element_type=F32)
        .astype(BF16)
        .reshape(seq_len, q_cols)
    )
    residual = stream + ring.scatter(contract_cols(attn_low, out_weights).astype(BF16))

    routes_low = pad_lanes(ring.own_rows(routes).astype(BF16))
    grads_own = ring.own_rows(out_grad)
    grads_mine, grads_all = ring.gather(jnp.concatenate([grads_own, routes_low], axis=1))

    second_inverse = inverse_norm(residual)
    mid_normed = residual * second_inverse
    ffn_own = (mid_normed * ffn_gain).astype(BF16)
    ffn_mine, ffn_in = ring.gather(ffn_own)

    def gates_of(rows, routed):
        logits = dot(rows, whole_router)
        names = routed[:, width : width + picks].astype(jnp.int32)
        chosen = jnp.any(
            names[:, :, None] == jnp.arange(expert_count, dtype=jnp.int32)[None, None, :], axis=1
        )
        logits = jnp.where(chosen, logits, MASKED_SCORE)
        powers = jnp.where(chosen, jnp.exp(logits - jnp.max(logits, axis=1, keepdims=True)), 0.0)
        gates = powers / jnp.sum(powers, axis=1, keepdims=True)
        return gates, lax.dynamic_slice_in_dim(gates, e * experts_here, experts_here, 1)

    gates, gates_here = gates_of(ffn_in, grads_all)
    weighted, hidden_grads, row_grads = expert_terms(
        ffn_in, grads_all[:, :width], gates_here, gate_up, down
    )
    input_part = contract_cols(hidden_grads, gate_up).astype(BF16)
    column = lax.broadcasted_iota(jnp.int32, (1, LANES), 1)
    side = jnp.zeros((seq_len, LANES), F32)
    for i in range(experts_here):
        high = row_grads[i].astype(BF16).astype(F32)
        place = t * expert_count + e * experts_here + i
        side = side + jnp.where(column == place, high, 0.0)
        side = side + jnp.where(column == place + 2 * expert_count, row_grads[i] - high, 0.0)
    back_sum = ring.scatter(jnp.concatenate([input_part, side.astype(BF16)], axis=1))
    layer_val = residual + ring.scatter(dot(weighted, down).astype(BF16))
    layer_out = ring.join_halves(layer_val.astype(BF16))

    gate_grad_rows = sum(
        back_sum[:, width + i * expert_count : width + (i + 1) * expert_count] for i in range(4)
    )
    own_gates = gates[:half_rows]
    picked_grad = own_gates * (
        gate_grad_rows - jnp.sum(own_gates * gate_grad_rows, axis=-1, keepdims=True)
    )
    logit_grad = picked_grad.astype(BF16)
    ffn_in_grad = back_sum[:, :width] + contract_cols(logit_grad, whole_router)
    ffn_gain_part = jnp.sum(ffn_in_grad * mid_normed, axis=0)
    second_normed_grad = ffn_in_grad * ffn_gain
    mid_grad = grads_own.astype(F32) + second_inverse * (
        second_normed_grad
        - mid_normed * jnp.mean(second_normed_grad * mid_normed, axis=-1, keepdims=True)
    )
    _, branch_all = ring.gather(
        jnp.concatenate([mid_grad.astype(BF16), pad_lanes(logit_grad)], axis=1)
    )
    branch_grad = branch_all[:, :width]

    value_grad_in = dot(branch_grad, out_weights).astype(BF16).reshape(seq_len, heads_here, head_dim)
    prob_grad = jnp.einsum("thd,kd->htk", value_grad_in, value_low, preferred_element_type=F32)
    delta = jnp.sum(probs * prob_grad, axis=-1, keepdims=True)
    score_grad = (probs * (prob_grad - delta)).astype(BF16)
    q_grad = jnp.einsum("htk,kd->thd", score_grad, key_low, preferred_element_type=F32) * scale
    k_grad = jnp.einsum("htk,thd->kd", score_grad, query_low, preferred_element_type=F32) * scale
    v_grad = jnp.einsum("htk,thd->kd", probs_low, value_grad_in, preferred_element_type=F32)
    q_raw_grad, query_gain_part = norm_backward(
        q_grad, q_unit, q_inverse, query_gain, cosine, sine
    )
    k_raw_grad, key_gain_part = norm_backward(
        k_grad[:, None, :], k_unit, k_inverse, key_gain, cosine, sine
    )
    q_low = q_raw_grad.reshape(seq_len, q_cols).astype(BF16)
    kv_low = jnp.concatenate([k_raw_grad.reshape(seq_len, head_dim), v_grad], axis=1).astype(BF16)
    raw_grads = jnp.concatenate([q_low, kv_low], axis=1)
    attn_in_grad = ring.scatter(contract_cols(raw_grads, attn_weights).astype(BF16))
    first_normed_grad = attn_in_grad * attn_gain
    tokens_grad = mid_grad + first_inverse * (
        first_normed_grad - normed * jnp.mean(first_normed_grad * normed, axis=-1, keepdims=True)
    )
    tokens_grad = ring.join_halves(tokens_grad)
    attn_gain_part = jnp.sum(attn_in_grad * normed, axis=0)
    gains = ring.sum_all(
        jnp.concatenate([attn_gain_part, ffn_gain_part, query_gain_part, key_gain_part])
    )

    def columns(share):
        found = ring.blocks(share.astype(BF16))
        cols = share.shape[1]
        whole = jnp.zeros((share.shape[0], cols * owners), F32)
        for place, part in enumerate(found):
            whole = lax.dynamic_update_slice_in_dim(
                whole, part.astype(F32), ring.owners_by_slot[place] * cols, 1
            )
        return whole

    out_grad_w = columns(ring.share_rows(branch_grad, attn_low, BF16))
    query_grad_w = columns(ring.share_rows(attn_in, q_low, BF16))
    kv_share = ring.share_rows(attn_in, kv_low, BF16)
    step = sharers // 2
    while step:
        cols = kv_share.shape[1] // 2
        bit = (shared_index // step) % 2
        pairs = [(i, i ^ step) for i in range(owners)]
        sent = lax.dynamic_slice_in_dim(kv_share, (1 - bit) * cols, cols, 1)
        kept = lax.dynamic_slice_in_dim(kv_share, bit * cols, cols, 1)
        kv_share = kept + ring.send(sent.astype(BF16), pairs).astype(F32)
        step //= 2
    kv_all = columns(kv_share).reshape(-1, kv_tp, 2, head_dim)
    key_grad_w = kv_all[:, :, 0].reshape(-1, kv_tp * head_dim)
    value_grad_w = kv_all[:, :, 1].reshape(-1, kv_tp * head_dim)
    router_grad = ring.share_rows(ffn_in, branch_all[:, width : width + expert_count], F32)

    def weight_terms(rows, routed):
        _, here = gates_of(rows, routed)
        weighted, hidden_grads, _ = expert_terms(rows, routed[:, :width], here, gate_up, down)
        return contract_rows(weighted, routed[:, :width]), contract_rows(rows, hidden_grads)

    if groups == 2:
        totals = weight_terms(ring.other_group(ffn_mine), ring.other_group(grads_mine))
        down_total = totals[0] + contract_rows(weighted, grads_all[:, :width])
        gate_up_total = totals[1] + contract_rows(ffn_in, hidden_grads)
    else:
        rows_by_group, routed_by_group = ring.all_groups(ffn_mine), ring.all_groups(grads_mine)

        def add_group(i, totals):
            more = weight_terms(rows_by_group[i], routed_by_group[i])
            return totals[0] + more[0], totals[1] + more[1]

        down_total, gate_up_total = lax.fori_loop(
            0, groups, add_group, (jnp.zeros(down.shape, F32), jnp.zeros(gate_up.shape, F32))
        )
    hidden = experts_here * each
    gate_total = jnp.stack([gate_up_total[:, i * each : (i + 1) * each] for i in range(experts_here)])
    up_total = jnp.stack(
        [gate_up_total[:, hidden + i * each : hidden + (i + 1) * each] for i in range(experts_here)]
    )
    return (
        layer_out,
        tokens_grad,
        gains[:width],
        query_grad_w,
        key_grad_w,
        value_grad_w,
        out_grad_w,
        gains[2 * width : 2 * width + head_dim],
        gains[2 * width + head_dim :],
        gains[width : 2 * width],
        router_grad,
        gate_total,
        up_total,
        down_total.reshape(experts_here, each, width),
    )


def solution(mesh):
    return jax.shard_map(
        body,
        mesh=mesh,
        in_specs=(
            P(("fsdp", "ep"), None),
            P(("fsdp", "ep"), None),
            P(),
            P(),
            P(),
            P("fsdp", "tp"),
            P("fsdp", "tp"),
            P("fsdp", "tp"),
            P("fsdp", "tp"),
            P(),
            P(),
            P(),
            P("fsdp", None),
            P("ep", None, "tp"),
            P("ep", None, "tp"),
            P("ep", "tp", None),
            P(("fsdp", "ep"), None),
        ),
        out_specs=(
            P(("fsdp", "ep"), None),
            P(("fsdp", "ep"), None),
            P(),
            P("fsdp", "tp"),
            P("fsdp", "tp"),
            P("fsdp", "tp"),
            P("fsdp", "tp"),
            P(),
            P(),
            P(),
            P("fsdp", None),
            P("ep", None, "tp"),
            P("ep", None, "tp"),
            P("ep", "tp", None),
        ),
        check_vma=False,
    )
```

time: 4000 us -> 898 us (0.22)
  waiting for transfers between devices: 2910 us -> 312 us
  blocking collectives: 570 us -> 0 us
  starting transfers between devices: 12.3 us -> 90.1 us
    psum x4 -> x0, waiting for transfers between devices: 1190 us -> none  [the longest x1 582 us: body(): lax.psum((gate_grad, up_grad, down_grad, attn_gain_part, ffn_gain_part, q...]
    all_to_all x2 -> x0, waiting for transfers between devices: 907 us -> none  [the longest x1 607 us: body(): lax.all_to_all(spread_grad, ('ep', 'tp'), split_axis=0, concat_axis=0, ti...]
    reduce_scatter x7 -> x0, waiting for transfers between devices: 652 us -> none  [the longest x1 198 us: body(): lax.psum_scatter(key_acc, 'ep', scatter_dimension=0, tiled=True)]
    all_to_all x2 -> x0, blocking collectives: 458 us -> none  [the longest x1 263 us: body(): lax.all_to_all(grad_slots, 'ep', split_axis=0, concat_axis=0, tiled=True)]
    ppermute x0 -> x105, waiting for transfers between devices: none -> 312 us  [send(): return lax.ppermute(values, axis, pairs)]
    all_gather x4 -> x0, waiting for transfers between devices: 161 us -> none  [the longest x1 74.6 us: body(): lax.all_gather(out_proj, 'fsdp', axis=0, tiled=True)]
    ppermute x0 -> x105, starting transfers between devices: none -> 90.1 us  [send(): return lax.ppermute(values, axis, pairs)]
    dot_general x33 -> x12, matrix products: 144 us -> 66.7 us  [the longest x7 52.7 us: dot(): return jnp.dot(left, right, preferred_element_type=F32)]
  transfers between devices with their start and end apart: 17 -> 105, of which waited for: 15 -> 47; matrix products, arithmetic and copies ran while one was open for 3% -> 47% of each run, Pallas kernels for 0% -> 0%
where the time goes in v1:
time: 898 us; the launch traced here: 888 us
  waiting for transfers between devices  312 us (35%)
  matrix products  195 us (22%)
  local copies, waits for them, and re-layouts  186 us (21%)
  other arithmetic  92.1 us (10%)
  starting transfers between devices  90.1 us (10%)
  between operations  13 us (1%)
    ppermute x105, waiting for transfers between devices, send(): return lax.ppermute(values, axis, pairs)  312 us
    ppermute x105, starting transfers between devices, send(): return lax.ppermute(values, axis, pairs)  90.1 us
    dot_general x12, matrix products, contract_rows(): lax.dot_general(left, right, (((0,), (0,)), ((), ())), preferred_element_...  69 us
    dot_general x7, matrix products, dot(): return jnp.dot(left, right, preferred_element_type=F32)  52.7 us
    dot_general x6, matrix products, contract_cols(): lax.dot_general(left, right, (((1,), (1,)), ((), ())), preferred_element_...  50.5 us
    concatenate x4, local copies, waits for them, and re-layouts, gather(): return (mine, jnp.concatenate([mine, self.swap_halves(mine)], axis=0))  37.3 us
    unnamed x204, local copies, waits for them, and re-layouts  33.9 us
    ppermute x22, local copies, waits for them, and re-layouts, send(): return lax.ppermute(values, axis, pairs)  29.3 us
  transfers between devices with their start and end apart: 105, of which 47 were waited for; matrix products, arithmetic and copies ran while one was open for 47% of the time, Pallas kernels for 0%

profile of v1, /device:TPU:0, one launch (start us, length us, event | category | flops | bytes accessed | tf_op | source)
XLA Modules:
  0.0 888.2 jit_solution(3987597904026650505)
XLA Ops:
  3.4 3.1 collective-permute-start
  8.6 9.7 %collective-permute-done = bf16[64,2048]{0,1:T(8,128)(2,1)S(1)} collective-permute-done((bf16[64,2048]{0,1:T(8,128)(2,1)S(1)}, bf16[64,2048]{0,1:T(8,128)(2,1)S(1)}, u32[]{:S(2)}, u32[]{:S(2)}) %collective-permute-start) | collective-permute-done | bytes 262176 | tf_op jit(solution)/shard_map/ppermute | solution.py:83
  25.3 6.2 collective-permute-done.2
  37.6 6.3 collective-permute-done.4
  48.5 7.1 collective-permute-done.6
  55.6 6.6 concatenate.150
  70.0 3.1 broadcast_select_fusion.1
  73.1 9.2 %concatenate.151 = bf16[1024,2048]{0,1:T(8,128)(2,1)} concatenate(bf16[64,2048]{0,1:T(8,128)(2,1)S(1)} %fusion.94, bf16[64,2048]{0,1:T(8,128)(2,1)S(1)} %collective-permute-done, bf16[64,2048]{0,1:T(8,128)(2,1)} %copy-done.38, bf16[64,2048]{0,1:T(8,128)(2,1)} %collective-permute-done.2, bf16[64,2048]{0,1:T(8,128)(2,1)} %collective-permute-done.3, ...), dimensions={0} | concatenate | bytes 8388608 | tf_op jit(solution)/shard_map/concatenate | solution.py:104
  82.3 5.2 fusion.62
  98.3 8.6 fusion.199
  106.9 4.2 fusion.63
  120.0 6.8 collective-permute-done.18
  138.4 9.2 %collective-permute-done.14 = bf16[64,2048]{0,1:T(8,128)(2,1)S(1)} collective-permute-done((bf16[64,2048]{0,1:T(8,128)(2,1)S(1)}, bf16[64,2048]{0,1:T(8,128)(2,1)S(1)}, u32[]{:S(2)}, u32[]{:S(2)}) %collective-permute-start.14) | collective-permute-done | bytes 262176 | tf_op jit(solution)/shard_map/ppermute | solution.py:83
  154.0 10.8 %collective-permute-done.15 = bf16[64,2048]{0,1:T(8,128)(2,1)S(1)} collective-permute-done((bf16[64,2048]{0,1:T(8,128)(2,1)S(1)}, bf16[64,2048]{0,1:T(8,128)(2,1)S(1)}, u32[]{:S(2)}, u32[]{:S(2)}) %collective-permute-start.15) | collective-permute-done | bytes 262176 | tf_op jit(solution)/shard_map/ppermute | solution.py:83
  183.9 7.0 concatenate.163
  197.8 5.6 collective-permute-done.17
  209.8 8.6 collective-permute-done.26
  221.3 16.0 %collective-permute-done.103 = bf16[512,2176]{0,1:T(8,128)(2,1)} collective-permute-done((bf16[512,2176]{0,1:T(8,128)(2,1)}, bf16[512,2176]{0,1:T(8,128)(2,1)}, u32[]{:S(2)}, u32[]{:S(2)}) %collective-permute-start.103) | collective-permute-done | bytes 2228256 | tf_op jit(solution)/shard_map/ppermute | solution.py:83
  240.7 11.3 %collective-permute-done.29 = bf16[64,2048]{0,1:T(8,128)(2,1)} collective-permute-done((bf16[64,2048]{0,1:T(8,128)(2,1)}, bf16[64,2048]{0,1:T(8,128)(2,1)}, u32[]{:S(2)}, u32[]{:S(2)}) %collective-permute-start.29) | collective-permute-done | bytes 262176 | tf_op jit(solution)/shard_map/ppermute | solution.py:83
  255.4 10.5 %collective-permute-done.31 = bf16[64,2048]{0,1:T(8,128)(2,1)} collective-permute-done((bf16[64,2048]{0,1:T(8,128)(2,1)}, bf16[64,2048]{0,1:T(8,128)(2,1)}, u32[]{:S(2)}, u32[]{:S(2)}) %collective-permute-start.31) | collective-permute-done | bytes 262176 | tf_op jit(solution)/shard_map/ppermute | solution.py:83
  266.6 6.5 concatenate.165
  284.7 9.4 %concatenate.164 = bf16[1024,2176]{0,1:T(8,128)(2,1)} concatenate(bf16[64,2176]{0,1:T(8,128)(2,1)S(1)} %fusion.113, bf16[64,2176]{0,1:T(8,128)(2,1)S(1)} %copy-done.29, bf16[64,2176]{0,1:T(8,128)(2,1)} %copy.130, bf16[64,2176]{0,1:T(8,128)(2,1)} %copy.131, bf16[64,2176]{0,1:T(8,128)(2,1)} %copy.132, bf16[64,2176]{0,1:T(8,128)(2,1)} %copy.133, bf16[64,2176]{0,1:T(8,128)(2,1)} %copy.134, ...), dimensions={0} | concatenate | bytes 8912896 | tf_op jit(solution)/shard_map/concatenate | solution.py:104
  302.6 9.2 %concatenate.166 = bf16[1024,2048]{0,1:T(8,128)(2,1)} concatenate(bf16[64,2048]{0,1:T(8,128)(2,1)S(1)} %multiply_convert_fusion.4, bf16[64,2048]{0,1:T(8,128)(2,1)S(1)} %copy-done.37, bf16[64,2048]{0,1:T(8,128)(2,1)} %collective-permute-done.27, bf16[64,2048]{0,1:T(8,128)(2,1)} %collective-permute-done.28, bf16[64,2048]{0,1:T(8,128)(2,1)} %collective-permute-done.29, ...), dimensions={0} | concatenate | bytes 8388608 | tf_op jit(solution)/shard_map/concatenate | solution.py:104
  315.3 14.1 %fusion.202 = f32[1024,2304]{1,0:T(8,128)} fusion(bf16[1024,2048]{0,1:T(8,128)(2,1)S(1)} %copy-done.2, bf16[2048,2304]{1,0:T(8,128)(2,1)} %bitcast_dynamic-update-slice_fusion), kind=kOutput, calls=%fused_computation.395 | convolution fusion | flops 9663676416 | bytes 23068672 | tf_op jit(solution)/shard_map/dot_general | solution.py:42
  331.2 15.9 %multiply_convert_fusion.3 = (bf16[1024,1152]{1,0:T(8,128)(2,1)}, bf16[1024,1152]{1,0:T(8,128)(2,1)}, f32[1024,1152]{1,0:T(8,128)}, bf16[1024,1152]{1,0:T(8,128)(2,1)}) fusion(f32[1024,2304]{1,0:T(8,128)} %fusion.202, f32[1024,384]{1,0:T(8,128)S(1)} %broadcast_in_dim.223, f32[1024,384]{1,0:T(8,128)S(1)} %broadcast_in_dim.221, ...), kind=kOutput, calls=%fused_computation.32 | convolution fusion | flops 4855431168 | bytes 34865152 | tf_op jit(solution)/shard_map/dot_general | solution.py:50
  350.2 8.4 convolution_convert_fusion.3
  359.1 13.9 %convolution_convert_fusion.2 = bf16[1024,2048]{0,1:T(8,128)(2,1)S(1)} fusion(bf16[2048,2304]{1,0:T(8,128)(2,1)} %bitcast_dynamic-update-slice_fusion, bf16[1024,1152]{1,0:T(8,128)(2,1)} %get-tuple-element.98, bf16[1024,1152]{1,0:T(8,128)(2,1)} %get-tuple-element.97), kind=kOutput, calls=%fused_computation.49 | convolution fusion | flops 9675210752 | bytes 18350080 | tf_op jit(solution)/shard_map/dot_general | solution.py:50
  376.3 7.6 fusion.21
  395.1 15.4 %fusion.203 = f32[1024,2304]{1,0:T(8,128)} fusion(bf16[1024,2048]{0,1:T(8,128)(2,1)} %copy-done.20, bf16[2048,2304]{1,0:T(8,128)(2,1)} %bitcast_dynamic-update-slice_fusion), kind=kOutput, calls=%fused_computation.396 | convolution fusion | flops 9663676416 | bytes 23068672 | tf_op jit(solution)/shard_map/dot_general | solution.py:42
  427.6 4.5 collective-permute-done.46
  444.8 17.6 %convolution_add_fusion.1 = f32[1152,2048]{1,0:T(8,128)} fusion(f32[1152,2048]{1,0:T(8,128)} %fusion.21, bf16[1024,2176]{0,1:T(8,128)(2,1)} %copy-done.46, f32[1024,384]{1,0:T(8,128)S(1)} %broadcast_in_dim.244, f32[1024,384]{1,0:T(8,128)} %broadcast_in_dim.242, f32[1024,384]{1,0:T(8,128)} %broadcast_in_dim.240, f32[1024,2304]{1,0:T(8,128)} %fusion.203), kind=kOutput, calls=%fused_computation.5 | convolution fusion | flops 4844814336 | bytes 37224448 | tf_op jit(solution)/shard_map/dot_general | solution.py:46
  469.7 13.8 %multiply_convert_fusion.1 = (bf16[1024,1152]{1,0:T(8,128)(2,1)}, bf16[1024,1152]{1,0:T(8,128)(2,1)}) fusion(f32[1024,2304]{1,0:T(8,128)} %fusion.203, bf16[1152,2048]{1,0:T(8,128)(2,1)} %bitcast.206, bf16[1024,2176]{0,1:T(8,128)(2,1)} %copy-done.46, f32[1024,384]{1,0:T(8,128)} %copy-done.45, f32[1024,384]{1,0:T(8,128)} %broadcast_in_dim.242, ...), kind=kOutput, calls=%fused_computation.28 | convolution fusion | flops 4850712576 | bytes 27787264 | tf_op jit(solution)/shard_map/dot_general | solution.py:50
  485.8 15.3 %fusion.10 = f32[2048,2304]{1,0:T(8,128)} fusion(bf16[1024,2048]{0,1:T(8,128)(2,1)S(1)} %copy-done.21, bf16[1024,1152]{1,0:T(8,128)(2,1)} %get-tuple-element.100, bf16[1024,1152]{1,0:T(8,128)(2,1)} %get-tuple-element.99), kind=kOutput, calls=%fused_computation.23 | convolution fusion | flops 9673113600 | bytes 27787264 | tf_op jit(solution)/shard_map/dot_general | solution.py:46
  503.2 19.3 %convolution_add_fusion = f32[2048,2304]{1,0:T(8,128)} fusion(f32[2048,2304]{1,0:T(8,128)} %fusion.10, bf16[1024,2048]{0,1:T(8,128)(2,1)} %concatenate.166, bf16[1024,1152]{1,0:T(8,128)(2,1)} %get-tuple-element.98, bf16[1024,1152]{1,0:T(8,128)(2,1)} %get-tuple-element.97), kind=kOutput, calls=%fused_computation.2 | convolution fusion | flops 9677832192 | bytes 46661632 | tf_op jit(solution)/shard_map/dot_general | solution.py:46
  524.5 13.6 %slice_bitcast_fusion.2 = (f32[1,2048,384]{2,1,0:T(8,128)}, f32[1,2048,384]{2,1,0:T(8,128)}, f32[1,2048,384]{2,1,0:T(8,128)}, f32[1,2048,384]{2,1,0:T(8,128)}, f...) fusion(f32[2048,2304]{1,0:T(8,128)} %convolution_add_fusion), kind=kLoop, calls=%fused_computation.59 | loop fusion | bytes 37748736 | tf_op jit(solution)/shard_map/stack | solution.py:441
  548.7 6.6 concatenate.174
  557.5 8.2 pad_maximum_fusion
  565.7 5.1 collective-permute-done.40
  574.3 4.3 pad_maximum_fusion.1
  578.7 7.2 collective-permute-done.37
  590.6 9.4 %concatenate.175 = bf16[1024,2176]{0,1:T(8,128)(2,1)} concatenate(bf16[64,2176]{0,1:T(8,128)(2,1)S(1)} %fusion.114, bf16[64,2176]{0,1:T(8,128)(2,1)} %copy.163, bf16[64,2176]{0,1:T(8,128)(2,1)} %copy.164, bf16[64,2176]{0,1:T(8,128)(2,1)} %copy.165, bf16[64,2176]{0,1:T(8,128)(2,1)} %copy.166, bf16[64,2176]{0,1:T(8,128)(2,1)} %copy.167, bf16[64,2176]{0,1:T(8,128)(2,1)} %copy.168, ...), dimensions={0} | concatenate | bytes 8912896 | tf_op jit(solution)/shard_map/concatenate | solution.py:104
  600.0 3.7 convolution_convert_fusion.4
  603.8 5.1 fusion.86
  627.5 4.0 convolution_convert_fusion
  638.5 9.3 %collective-permute-done.74 = bf16[1024,256]{1,0:T(8,128)(2,1)S(1)} collective-permute-done((bf16[1024,256]{1,0:T(8,128)(2,1)S(1)}, bf16[1024,256]{1,0:T(8,128)(2,1)S(1)}, u32[]{:S(2)}, u32[]{:S(2)}) %collective-permute-start.74) | collective-permute-done | bytes 524320 | tf_op jit(solution)/shard_map/ppermute | solution.py:83
  650.1 8.9 %collective-permute-done.82 = bf16[1024,256]{0,1:T(8,128)(2,1)S(1)} collective-permute-done((bf16[1024,256]{0,1:T(8,128)(2,1)S(1)}, bf16[1024,256]{0,1:T(8,128)(2,1)S(1)}, u32[]{:S(2)}, u32[]{:S(2)}) %collective-permute-start.82) | collective-permute-done | bytes 524320 | tf_op jit(solution)/shard_map/ppermute | solution.py:83
  660.3 8.0 collective-permute-done.92
  668.7 4.5 broadcast.417.clone.1
  679.1 9.1 %collective-permute-done.84 = bf16[1024,64]{0,1:T(8,128)(2,1)S(1)} collective-permute-done((bf16[1024,64]{0,1:T(8,128)(2,1)S(1)}, bf16[1024,64]{0,1:T(8,128)(2,1)S(1)}, u32[]{:S(2)}, u32[]{:S(2)}) %collective-permute-start.84) | collective-permute-done | bytes 131104 | tf_op jit(solution)/shard_map/ppermute | solution.py:83
  690.8 12.4 %collective-permute-done.76 = bf16[1024,256]{1,0:T(8,128)(2,1)S(1)} collective-permute-done((bf16[1024,256]{1,0:T(8,128)(2,1)S(1)}, bf16[1024,256]{1,0:T(8,128)(2,1)S(1)}, u32[]{:S(2)}, u32[]{:S(2)}) %collective-permute-start.76) | collective-permute-done | bytes 524320 | tf_op jit(solution)/shard_map/ppermute | solution.py:83
  703.4 10.7 %collective-permute-done.94 = bf16[1024,256]{1,0:T(8,128)(2,1)S(1)} collective-permute-done((bf16[1024,256]{1,0:T(8,128)(2,1)S(1)}, bf16[1024,256]{1,0:T(8,128)(2,1)S(1)}, u32[]{:S(2)}, u32[]{:S(2)}) %collective-permute-start.94) | collective-permute-done | bytes 524320 | tf_op jit(solution)/shard_map/ppermute | solution.py:83
  719.2 12.5 %collective-permute-done.87 = bf16[1024,64]{0,1:T(8,128)(2,1)S(1)} collective-permute-done((bf16[1024,64]{0,1:T(8,128)(2,1)S(1)}, bf16[1024,64]{0,1:T(8,128)(2,1)S(1)}, u32[]{:S(2)}, u32[]{:S(2)}) %collective-permute-start.87) | collective-permute-done | bytes 131104 | tf_op jit(solution)/shard_map/ppermute | solution.py:83
  732.0 4.7 collective-permute-done.88
  738.2 3.4 collective-permute-done.89
  742.1 4.5 collective-permute-done.90
  748.2 4.8 collective-permute-done.91
  766.5 6.9 collective-permute-done.78
  781.6 22.9 %collective-permute-done.64 = bf16[64,2048]{0,1:T(8,128)(2,1)S(1)} collective-permute-done((bf16[64,2048]{0,1:T(8,128)(2,1)S(1)}, bf16[64,2048]{0,1:T(8,128)(2,1)S(1)}, u32[]{:S(2)}, u32[]{:S(2)}) %collective-permute-start.64) | collective-permute-done | bytes 262176 | tf_op jit(solution)/shard_map/ppermute | solution.py:83
  807.8 8.2 collective-permute-done.61
  820.5 17.7 %collective-permute-done.62 = bf16[64,2048]{0,1:T(8,128)(2,1)S(1)} collective-permute-done((bf16[64,2048]{0,1:T(8,128)(2,1)S(1)}, bf16[64,2048]{0,1:T(8,128)(2,1)S(1)}, u32[]{:S(2)}, u32[]{:S(2)}) %collective-permute-start.62) | collective-permute-done | bytes 262176 | tf_op jit(solution)/shard_map/ppermute | solution.py:83
  842.6 6.0 collective-permute-done.67
  857.4 6.7 collective-permute-done.69
  869.0 3.6 collective-permute-done.71
  873.1 3.2 collective-permute-done.72
  (591 shorter events, 314.0 us)
Async XLA Ops:
  3.4 14.9 %collective-permute-start = (bf16[64,2048]{0,1:T(8,128)(2,1)S(1)}, bf16[64,2048]{0,1:T(8,128)(2,1)S(1)}, u32[]{:S(2)}, u32[]{:S(2)}) collective-permute-start(bf16[64,2048]{0,1:T(8,128)(2,1)S(1)} %fusion.94), channel_id=1, source_target_pairs={{0,4},{4,8},{8,12},{12,14},{14,10},{10,6},{6,2},{2,0},{1,5},{5,9},... | collective-permute-start | bytes 786440 | tf_op jit(solution)/shard_map/ppermute | solution.py:83
  6.4 18.6 %collective-permute-start.1 = (bf16[64,2048]{0,1:T(8,128)(2,1)S(1)}, bf16[64,2048]{0,1:T(8,128)(2,1)S(1)}, u32[]{:S(2)}, u32[]{:S(2)}) collective-permute-start(bf16[64,2048]{0,1:T(8,128)(2,1)S(1)} %fusion.94), channel_id=1, source_target_pairs={{4,0},{8,4},{12,8},{14,12},{10,14},{6,10},{2,6},{0,2},{5,1},{9,5},... | collective-permute-start | bytes 786440 | tf_op jit(solution)/shard_map/ppermute | solution.py:83
  21.2 48.8 %collective-permute-start.8 = (bf16[1024,512]{1,0:T(8,128)(2,1)}, bf16[1024,512]{1,0:T(8,128)(2,1)}, u32[]{:S(2)}, u32[]{:S(2)}) collective-permute-start(bf16[1024,512]{1,0:T(8,128)(2,1)} %pad_maximum_fusion.12), channel_id=1, source_target_pairs={{0,16},{16,0},{1,17},{17,1},{2,18},{18,2},{3,19},{19,3},{4,20},{20... | collective-permute-start | bytes 3145736 | tf_op jit(solution)/shard_map/ppermute | solution.py:83
  24.6 43.1 %collective-permute-start.9 = (bf16[1024,256]{1,0:T(8,128)(2,1)}, bf16[1024,256]{1,0:T(8,128)(2,1)}, u32[]{:S(2)}, u32[]{:S(2)}) collective-permute-start(bf16[1024,256]{1,0:T(8,128)(2,1)} %constant_dynamic-slice_fusion.5), channel_id=1, source_target_pairs={{0,16},{16,0},{1,17},{17,1},{2,18},{18,2},{3,19},{19,3},{4,20},{20... | collective-permute-start | bytes 1572872 | tf_op jit(solution)/shard_map/ppermute | solution.py:83
  118.9 15.1 %collective-permute-start.19 = (bf16[64,2176]{1,0:T(8,128)(2,1)}, bf16[64,2176]{1,0:T(8,128)(2,1)S(1)}, u32[]{:S(2)}, u32[]{:S(2)}) collective-permute-start(bf16[64,2176]{1,0:T(8,128)(2,1)} %copy.120), channel_id=1, source_target_pairs={{4,0},{8,4},{12,8},{14,12},{10,14},{6,10},{2,6},{0,2},{5,1},{9,5},... | collective-permute-start | bytes 835592 | tf_op jit(solution)/shard_map/ppermute | solution.py:83
  130.9 16.8 %collective-permute-start.14 = (bf16[64,2048]{0,1:T(8,128)(2,1)S(1)}, bf16[64,2048]{0,1:T(8,128)(2,1)S(1)}, u32[]{:S(2)}, u32[]{:S(2)}) collective-permute-start(bf16[64,2048]{0,1:T(8,128)(2,1)S(1)} %get-tuple-element.134), channel_id=1, source_target_pairs={{0,4},{4,8},{8,12},{12,14},{14,10},{10,6},{6,2},{2,0},{1,5},{5,9},... | collective-permute-start | bytes 786440 | tf_op jit(solution)/shard_map/ppermute | solution.py:83
  132.5 151.4 %collective-permute-start.34 = (bf16[1024,24]{0,1:T(8,128)(2,1)S(1)}, bf16[1024,24]{0,1:T(8,128)(2,1)}, u32[]{:S(2)}, u32[]{:S(2)}) collective-permute-start(bf16[1024,24]{0,1:T(8,128)(2,1)S(1)} %copy-done.65), channel_id=1, source_target_pairs={{0,16},{16,0},{1,17},{17,1},{2,18},{18,2},{3,19},{19,3},{4,20},{20... | collective-permute-start | bytes 147464 | tf_op jit(solution)/shard_map/ppermute | solution.py:83
  134.0 16.9 %collective-permute-start.21 = (bf16[64,2176]{1,0:T(8,128)(2,1)S(1)}, bf16[64,2176]{1,0:T(8,128)(2,1)}, u32[]{:S(2)}, u32[]{:S(2)}) collective-permute-start(bf16[64,2176]{1,0:T(8,128)(2,1)S(1)} %collective-permute-done.19), channel_id=1, source_target_pairs={{4,0},{8,4},{12,8},{14,12},{10,14},{6,10},{2,6},{0,2},{5,1},{9,5},... | collective-permute-start | bytes 835592 | tf_op jit(solution)/shard_map/ppermute | solution.py:83
  136.4 17.3 %collective-permute-start.22 = (bf16[64,2176]{1,0:T(8,128)(2,1)S(1)}, bf16[64,2176]{1,0:T(8,128)(2,1)}, u32[]{:S(2)}, u32[]{:S(2)}) collective-permute-start(bf16[64,2176]{1,0:T(8,128)(2,1)S(1)} %collective-permute-done.20), channel_id=1, source_target_pairs={{0,4},{4,8},{8,12},{12,14},{14,10},{10,6},{6,2},{2,0},{1,5},{5,9},... | collective-permute-start | bytes 835592 | tf_op jit(solution)/shard_map/ppermute | solution.py:83
  136.7 17.3 %collective-permute-start.11 = (bf16[64,2048]{0,1:T(8,128)(2,1)S(1)}, bf16[64,2048]{0,1:T(8,128)(2,1)S(1)}, u32[]{:S(2)}, u32[]{:S(2)}) collective-permute-start(bf16[64,2048]{0,1:T(8,128)(2,1)S(1)} %get-tuple-element.133), channel_id=1, source_target_pairs={{4,0},{8,4},{12,8},{14,12},{10,14},{6,10},{2,6},{0,2},{5,1},{9,5},... | collective-permute-start | bytes 786440 | tf_op jit(solution)/shard_map/ppermute | solution.py:83
  147.7 17.1 %collective-permute-start.15 = (bf16[64,2048]{0,1:T(8,128)(2,1)S(1)}, bf16[64,2048]{0,1:T(8,128)(2,1)S(1)}, u32[]{:S(2)}, u32[]{:S(2)}) collective-permute-start(bf16[64,2048]{0,1:T(8,128)(2,1)S(1)} %add_convert_fusion.22), channel_id=1, source_target_pairs={{0,4},{4,8},{8,12},{12,14},{14,10},{10,6},{6,2},{2,0},{1,5},{5,9},... | collective-permute-start | bytes 786440 | tf_op jit(solution)/shard_map/ppermute | solution.py:83
  150.9 29.0 %collective-permute-start.23 = (bf16[64,2176]{1,0:T(8,128)(2,1)}, bf16[64,2176]{1,0:T(8,128)(2,1)}, u32[]{:S(2)}, u32[]{:S(2)}) collective-permute-start(bf16[64,2176]{1,0:T(8,128)(2,1)} %collective-permute-done.21), channel_id=1, source_target_pairs={{4,0},{8,4},{12,8},{14,12},{10,14},{6,10},{2,6},{0,2},{5,1},{9,5},... | collective-permute-start | bytes 835592 | tf_op jit(solution)/shard_map/ppermute | solution.py:83
  153.7 28.2 %collective-permute-start.24 = (bf16[64,2176]{1,0:T(8,128)(2,1)}, bf16[64,2176]{1,0:T(8,128)(2,1)}, u32[]{:S(2)}, u32[]{:S(2)}) collective-permute-start(bf16[64,2176]{1,0:T(8,128)(2,1)} %collective-permute-done.22), channel_id=1, source_target_pairs={{0,4},{4,8},{8,12},{12,14},{14,10},{10,6},{6,2},{2,0},{1,5},{5,9},... | collective-permute-start | bytes 835592 | tf_op jit(solution)/shard_map/ppermute | solution.py:83
  166.0 25.2 %collective-permute-start.12 = (bf16[64,2048]{0,1:T(8,128)(2,1)}, bf16[64,2048]{0,1:T(8,128)(2,1)}, u32[]{:S(2)}, u32[]{:S(2)}) collective-permute-start(bf16[64,2048]{0,1:T(8,128)(2,1)} %get-tuple-element.131), channel_id=1, source_target_pairs={{4,0},{8,4},{12,8},{14,12},{10,14},{6,10},{2,6},{0,2},{5,1},{9,5},... | collective-permute-start | bytes 786440 | tf_op jit(solution)/shard_map/ppermute | solution.py:83
  166.7 24.5 %collective-permute-start.16 = (bf16[64,2048]{0,1:T(8,128)(2,1)}, bf16[64,2048]{0,1:T(8,128)(2,1)}, u32[]{:S(2)}, u32[]{:S(2)}) collective-permute-start(bf16[64,2048]{0,1:T(8,128)(2,1)} %get-tuple-element.132), channel_id=1, source_target_pairs={{0,4},{4,8},{8,12},{12,14},{14,10},{10,6},{6,2},{2,0},{1,5},{5,9},... | collective-permute-start | bytes 786440 | tf_op jit(solution)/shard_map/ppermute | solution.py:83
  190.9 46.5 %collective-permute-start.103 = (bf16[512,2176]{0,1:T(8,128)(2,1)}, bf16[512,2176]{0,1:T(8,128)(2,1)}, u32[]{:S(2)}, u32[]{:S(2)}) collective-permute-start(bf16[512,2176]{0,1:T(8,128)(2,1)} %concatenate.163), channel_id=1, source_target_pairs={{0,16},{16,0},{1,17},{17,1},{2,18},{18,2},{3,19},{19,3},{4,20},{20... | collective-permute-start | bytes 6684680 | tf_op jit(solution)/shard_map/ppermute | solution.py:83
  197.8 86.9 %collective-permute-start.25 = (bf16[512,2176]{0,1:T(8,128)(2,1)}, bf16[512,2176]{0,1:T(8,128)(2,1)}, u32[]{:S(2)}, u32[]{:S(2)}) collective-permute-start(bf16[512,2176]{0,1:T(8,128)(2,1)} %concatenate.163), channel_id=1, source_target_pairs={{0,1},{1,0},{2,3},{3,2},{4,5},{5,4},{6,7},{7,6},{8,9},{9,8},{10,11... | collective-permute-start | bytes 6684680 | tf_op jit(solution)/shard_map/ppermute | solution.py:83
  209.4 28.0 %collective-permute-start.27 = (bf16[64,2048]{0,1:T(8,128)(2,1)S(1)}, bf16[64,2048]{0,1:T(8,128)(2,1)}, u32[]{:S(2)}, u32[]{:S(2)}) collective-permute-start(bf16[64,2048]{0,1:T(8,128)(2,1)S(1)} %multiply_convert_fusion.4), channel_id=1, source_target_pairs={{4,0},{8,4},{12,8},{14,12},{10,14},{6,10},{2,6},{0,2},{5,1},{9,5},... | collective-permute-start | bytes 786440 | tf_op jit(solution)/shard_map/ppermute | solution.py:83
  218.5 19.9 %collective-permute-start.28 = (bf16[64,2048]{0,1:T(8,128)(2,1)S(1)}, bf16[64,2048]{0,1:T(8,128)(2,1)}, u32[]{:S(2)}, u32[]{:S(2)}) collective-permute-start(bf16[64,2048]{0,1:T(8,128)(2,1)S(1)} %collective-permute-done.26), channel_id=1, source_target_pairs={{0,4},{4,8},{8,12},{12,14},{14,10},{10,6},{6,2},{2,0},{1,5},{5,9},... | collective-permute-start | bytes 786440 | tf_op jit(solution)/shard_map/ppermute | solution.py:83
  237.3 59.6 %collective-permute-start.104 = (bf16[512,2176]{0,1:T(8,128)(2,1)}, bf16[512,2176]{0,1:T(8,128)(2,1)}, u32[]{:S(2)}, u32[]{:S(2)}) collective-permute-start(bf16[512,2176]{0,1:T(8,128)(2,1)} %collective-permute-done.103), channel_id=1, source_target_pairs={{0,1},{1,0},{2,3},{3,2},{4,5},{5,4},{6,7},{7,6},{8,9},{9,8},{10,11... | collective-permute-start | bytes 6684680 | tf_op jit(solution)/shard_map/ppermute | solution.py:83
  237.3 14.7 %collective-permute-start.29 = (bf16[64,2048]{0,1:T(8,128)(2,1)}, bf16[64,2048]{0,1:T(8,128)(2,1)}, u32[]{:S(2)}, u32[]{:S(2)}) collective-permute-start(bf16[64,2048]{0,1:T(8,128)(2,1)} %collective-permute-done.27), channel_id=1, source_target_pairs={{4,0},{8,4},{12,8},{14,12},{10,14},{6,10},{2,6},{0,2},{5,1},{9,5},... | collective-permute-start | bytes 786440 | tf_op jit(solution)/shard_map/ppermute | solution.py:83
  238.3 14.7 %collective-permute-start.30 = (bf16[64,2048]{0,1:T(8,128)(2,1)}, bf16[64,2048]{0,1:T(8,128)(2,1)}, u32[]{:S(2)}, u32[]{:S(2)}) collective-permute-start(bf16[64,2048]{0,1:T(8,128)(2,1)} %collective-permute-done.28), channel_id=1, source_target_pairs={{0,4},{4,8},{8,12},{12,14},{14,10},{10,6},{6,2},{2,0},{1,5},{5,9},... | collective-permute-start | bytes 786440 | tf_op jit(solution)/shard_map/ppermute | solution.py:83
  252.0 13.9 %collective-permute-start.31 = (bf16[64,2048]{0,1:T(8,128)(2,1)}, bf16[64,2048]{0,1:T(8,128)(2,1)}, u32[]{:S(2)}, u32[]{:S(2)}) collective-permute-start(bf16[64,2048]{0,1:T(8,128)(2,1)} %collective-permute-done.29), channel_id=1, source_target_pairs={{4,0},{8,4},{12,8},{14,12},{10,14},{6,10},{2,6},{0,2},{5,1},{9,5},... | collective-permute-start | bytes 786440 | tf_op jit(solution)/shard_map/ppermute | solution.py:83
  273.0 29.6 %collective-permute-start.33 = (bf16[512,2048]{0,1:T(8,128)(2,1)}, bf16[512,2048]{0,1:T(8,128)(2,1)}, u32[]{:S(2)}, u32[]{:S(2)}) collective-permute-start(bf16[512,2048]{0,1:T(8,128)(2,1)} %concatenate.165), channel_id=1, source_target_pairs={{0,1},{1,0},{2,3},{3,2},{4,5},{5,4},{6,7},{7,6},{8,9},{9,8},{10,11... | collective-permute-start | bytes 6291464 | tf_op jit(solution)/shard_map/ppermute | solution.py:83
  301.1 72.9 %collective-permute-start.101 = (bf16[512,2048]{0,1:T(8,128)(2,1)}, bf16[512,2048]{0,1:T(8,128)(2,1)}, u32[]{:S(2)}, u32[]{:S(2)}) collective-permute-start(bf16[512,2048]{0,1:T(8,128)(2,1)} %concatenate.165), channel_id=1, source_target_pairs={{0,16},{16,0},{1,17},{17,1},{2,18},{18,2},{3,19},{19,3},{4,20},{20... | collective-permute-start | bytes 6291464 | tf_op jit(solution)/shard_map/ppermute | solution.py:83
  358.9 25.0 %collective-permute-start.35 = (bf16[512,2048]{0,1:T(8,128)(2,1)S(1)}, bf16[512,2048]{0,1:T(8,128)(2,1)S(1)}, u32[]{:S(2)}, u32[]{:S(2)}) collective-permute-start(bf16[512,2048]{0,1:T(8,128)(2,1)S(1)} %slice.490), channel_id=1, source_target_pairs={{0,1},{1,0},{2,3},{3,2},{4,5},{5,4},{6,7},{7,6},{8,9},{9,8},{10,11... | collective-permute-start | bytes 6291464 | tf_op jit(solution)/shard_map/ppermute | solution.py:83
  373.7 17.3 %collective-permute-start.44 = (bf16[512,2176]{0,1:T(8,128)(2,1)S(1)}, bf16[512,2176]{0,1:T(8,128)(2,1)S(1)}, u32[]{:S(2)}, u32[]{:S(2)}) collective-permute-start(bf16[512,2176]{0,1:T(8,128)(2,1)S(1)} %pad_maximum_fusion.7), channel_id=1, source_target_pairs={{0,1},{1,0},{2,3},{3,2},{4,5},{5,4},{6,7},{7,6},{8,9},{9,8},{10,11... | collective-permute-start | bytes 6684680 | tf_op jit(solution)/shard_map/ppermute | solution.py:83
  374.1 14.5 %collective-permute-start.102 = (bf16[512,2048]{0,1:T(8,128)(2,1)}, bf16[512,2048]{0,1:T(8,128)(2,1)S(1)}, u32[]{:S(2)}, u32[]{:S(2)}) collective-permute-start(bf16[512,2048]{0,1:T(8,128)(2,1)} %collective-permute-done.101), channel_id=1, source_target_pairs={{0,1},{1,0},{2,3},{3,2},{4,5},{5,4},{6,7},{7,6},{8,9},{9,8},{10,11... | collective-permute-start | bytes 6291464 | tf_op jit(solution)/shard_map/ppermute | solution.py:83
  386.4 179.3 %collective-permute-start.36 = (bf16[64,2048]{0,1:T(8,128)(2,1)}, bf16[64,2048]{0,1:T(8,128)(2,1)}, u32[]{:S(2)}, u32[]{:S(2)}) collective-permute-start(bf16[64,2048]{0,1:T(8,128)(2,1)} %get-tuple-element.127), channel_id=1, source_target_pairs={{4,0},{8,4},{12,8},{14,12},{10,14},{6,10},{2,6},{0,2},{5,1},{9,5},... | collective-permute-start | bytes 786440 | tf_op jit(solution)/shard_map/ppermute | solution.py:83
  388.0 167.3 %collective-permute-start.39 = (bf16[64,2048]{0,1:T(8,128)(2,1)}, bf16[64,2048]{0,1:T(8,128)(2,1)}, u32[]{:S(2)}, u32[]{:S(2)}) collective-permute-start(bf16[64,2048]{0,1:T(8,128)(2,1)} %get-tuple-element.128), channel_id=1, source_target_pairs={{0,4},{4,8},{8,12},{12,14},{14,10},{10,6},{6,2},{2,0},{1,5},{5,9},... | collective-permute-start | bytes 786440 | tf_op jit(solution)/shard_map/ppermute | solution.py:83
  394.0 17.8 %collective-permute-start.48 = (bf16[64,2176]{1,0:T(8,128)(2,1)S(1)}, bf16[64,2176]{1,0:T(8,128)(2,1)S(1)}, u32[]{:S(2)}, u32[]{:S(2)}) collective-permute-start(bf16[64,2176]{1,0:T(8,128)(2,1)S(1)} %copy.144), channel_id=1, source_target_pairs={{0,4},{4,8},{8,12},{12,14},{14,10},{10,6},{6,2},{2,0},{1,5},{5,9},... | collective-permute-start | bytes 835592 | tf_op jit(solution)/shard_map/ppermute | solution.py:83
  438.4 24.0 %collective-permute-start.51 = (bf16[64,2176]{1,0:T(8,128)(2,1)}, bf16[64,2176]{1,0:T(8,128)(2,1)}, u32[]{:S(2)}, u32[]{:S(2)}) collective-permute-start(bf16[64,2176]{1,0:T(8,128)(2,1)} %copy.150), channel_id=1, source_target_pairs={{0,4},{4,8},{8,12},{12,14},{14,10},{10,6},{6,2},{2,0},{1,5},{5,9},... | collective-permute-start | bytes 835592 | tf_op jit(solution)/shard_map/ppermute | solution.py:83
  439.8 24.0 %collective-permute-start.47 = (bf16[64,2176]{1,0:T(8,128)(2,1)}, bf16[64,2176]{1,0:T(8,128)(2,1)}, u32[]{:S(2)}, u32[]{:S(2)}) collective-permute-start(bf16[64,2176]{1,0:T(8,128)(2,1)} %copy.142), channel_id=1, source_target_pairs={{4,0},{8,4},{12,8},{14,12},{10,14},{6,10},{2,6},{0,2},{5,1},{9,5},... | collective-permute-start | bytes 835592 | tf_op jit(solution)/shard_map/ppermute | solution.py:83
  469.3 16.0 %collective-permute-start.52 = (bf16[64,2176]{1,0:T(8,128)(2,1)S(1)}, bf16[64,2176]{1,0:T(8,128)(2,1)S(1)}, u32[]{:S(2)}, u32[]{:S(2)}) collective-permute-start(bf16[64,2176]{1,0:T(8,128)(2,1)S(1)} %copy.154), channel_id=1, source_target_pairs={{0,4},{4,8},{8,12},{12,14},{14,10},{10,6},{6,2},{2,0},{1,5},{5,9},... | collective-permute-start | bytes 835592 | tf_op jit(solution)/shard_map/ppermute | solution.py:83
  483.6 17.6 %collective-permute-start.53 = (bf16[64,2176]{1,0:T(8,128)(2,1)S(1)}, bf16[64,2176]{1,0:T(8,128)(2,1)S(1)}, u32[]{:S(2)}, u32[]{:S(2)}) collective-permute-start(bf16[64,2176]{1,0:T(8,128)(2,1)S(1)} %copy.154), channel_id=1, source_target_pairs={{4,0},{8,4},{12,8},{14,12},{10,14},{6,10},{2,6},{0,2},{5,1},{9,5},... | collective-permute-start | bytes 835592 | tf_op jit(solution)/shard_map/ppermute | solution.py:83
  485.2 17.5 %collective-permute-start.54 = (bf16[64,2176]{1,0:T(8,128)(2,1)S(1)}, bf16[64,2176]{1,0:T(8,128)(2,1)S(1)}, u32[]{:S(2)}, u32[]{:S(2)}) collective-permute-start(bf16[64,2176]{1,0:T(8,128)(2,1)S(1)} %collective-permute-done.52), channel_id=1, source_target_pairs={{0,4},{4,8},{8,12},{12,14},{14,10},{10,6},{6,2},{2,0},{1,5},{5,9},... | collective-permute-start | bytes 835592 | tf_op jit(solution)/shard_map/ppermute | solution.py:83
  501.1 21.3 %collective-permute-start.55 = (bf16[64,2176]{1,0:T(8,128)(2,1)S(1)}, bf16[64,2176]{1,0:T(8,128)(2,1)S(1)}, u32[]{:S(2)}, u32[]{:S(2)}) collective-permute-start(bf16[64,2176]{1,0:T(8,128)(2,1)S(1)} %collective-permute-done.53), channel_id=1, source_target_pairs={{4,0},{8,4},{12,8},{14,12},{10,14},{6,10},{2,6},{0,2},{5,1},{9,5},... | collective-permute-start | bytes 835592 | tf_op jit(solution)/shard_map/ppermute | solution.py:83
  502.7 21.3 %collective-permute-start.56 = (bf16[64,2176]{1,0:T(8,128)(2,1)S(1)}, bf16[64,2176]{1,0:T(8,128)(2,1)}, u32[]{:S(2)}, u32[]{:S(2)}) collective-permute-start(bf16[64,2176]{1,0:T(8,128)(2,1)S(1)} %collective-permute-done.54), channel_id=1, source_target_pairs={{0,4},{4,8},{8,12},{12,14},{14,10},{10,6},{6,2},{2,0},{1,5},{5,9},... | collective-permute-start | bytes 835592 | tf_op jit(solution)/shard_map/ppermute | solution.py:83
  522.5 22.0 %collective-permute-start.57 = (bf16[64,2176]{1,0:T(8,128)(2,1)S(1)}, bf16[64,2176]{1,0:T(8,128)(2,1)}, u32[]{:S(2)}, u32[]{:S(2)}) collective-permute-start(bf16[64,2176]{1,0:T(8,128)(2,1)S(1)} %collective-permute-done.55), channel_id=1, source_target_pairs={{4,0},{8,4},{12,8},{14,12},{10,14},{6,10},{2,6},{0,2},{5,1},{9,5},... | collective-permute-start | bytes 835592 | tf_op jit(solution)/shard_map/ppermute | solution.py:83
  524.1 22.6 %collective-permute-start.58 = (bf16[64,2176]{1,0:T(8,128)(2,1)}, bf16[64,2176]{1,0:T(8,128)(2,1)}, u32[]{:S(2)}, u32[]{:S(2)}) collective-permute-start(bf16[64,2176]{1,0:T(8,128)(2,1)} %collective-permute-done.56), channel_id=1, source_target_pairs={{0,4},{4,8},{8,12},{12,14},{14,10},{10,6},{6,2},{2,0},{1,5},{5,9},... | collective-permute-start | bytes 835592 | tf_op jit(solution)/shard_map/ppermute | solution.py:83
  555.3 35.3 %collective-permute-start.59 = (bf16[512,2176]{0,1:T(8,128)(2,1)}, bf16[512,2176]{0,1:T(8,128)(2,1)}, u32[]{:S(2)}, u32[]{:S(2)}) collective-permute-start(bf16[512,2176]{0,1:T(8,128)(2,1)} %concatenate.174), channel_id=1, source_target_pairs={{0,1},{1,0},{2,3},{3,2},{4,5},{5,4},{6,7},{7,6},{8,9},{9,8},{10,11... | collective-permute-start | bytes 6684680 | tf_op jit(solution)/shard_map/ppermute | solution.py:83
  556.5 14.4 %collective-permute-start.40 = (bf16[64,2048]{0,1:T(8,128)(2,1)S(1)}, bf16[64,2048]{0,1:T(8,128)(2,1)S(1)}, u32[]{:S(2)}, u32[]{:S(2)}) collective-permute-start(bf16[64,2048]{0,1:T(8,128)(2,1)S(1)} %add_convert_fusion.17), channel_id=1, source_target_pairs={{0,4},{4,8},{8,12},{12,14},{14,10},{10,6},{6,2},{2,0},{1,5},{5,9},... | collective-permute-start | bytes 786440 | tf_op jit(solution)/shard_map/ppermute | solution.py:83
  588.4 288.0 %collective-permute-start.42 = (bf16[64,2048]{0,1:T(8,128)(2,1)}, bf16[64,2048]{0,1:T(8,128)(2,1)}, u32[]{:S(2)}, u32[]{:S(2)}) collective-permute-start(bf16[64,2048]{0,1:T(8,128)(2,1)} %get-tuple-element.124), channel_id=1, source_target_pairs={{0,4},{4,8},{8,12},{12,14},{14,10},{10,6},{6,2},{2,0},{1,5},{5,9},... | collective-permute-start | bytes 786440 | tf_op jit(solution)/shard_map/ppermute | solution.py:83
  588.8 287.6 %collective-permute-start.38 = (bf16[64,2048]{0,1:T(8,128)(2,1)}, bf16[64,2048]{0,1:T(8,128)(2,1)}, u32[]{:S(2)}, u32[]{:S(2)}) collective-permute-start(bf16[64,2048]{0,1:T(8,128)(2,1)} %get-tuple-element.123), channel_id=1, source_target_pairs={{4,0},{8,4},{12,8},{14,12},{10,14},{6,10},{2,6},{0,2},{5,1},{9,5},... | collective-permute-start | bytes 786440 | tf_op jit(solution)/shard_map/ppermute | solution.py:83
  632.8 14.9 %collective-permute-start.74 = (bf16[1024,256]{1,0:T(8,128)(2,1)S(1)}, bf16[1024,256]{1,0:T(8,128)(2,1)S(1)}, u32[]{:S(2)}, u32[]{:S(2)}) collective-permute-start(bf16[1024,256]{1,0:T(8,128)(2,1)S(1)} %fusion.72), channel_id=1, source_target_pairs={{0,16},{16,0},{1,17},{17,1},{2,18},{18,2},{3,19},{19,3},{4,20},{20... | collective-permute-start | bytes 1572872 | tf_op jit(solution)/shard_map/ppermute | solution.py:83
  633.4 25.6 %collective-permute-start.82 = (bf16[1024,256]{0,1:T(8,128)(2,1)S(1)}, bf16[1024,256]{0,1:T(8,128)(2,1)S(1)}, u32[]{:S(2)}, u32[]{:S(2)}) collective-permute-start(bf16[1024,256]{0,1:T(8,128)(2,1)S(1)} %fusion.75), channel_id=1, source_target_pairs={{0,16},{16,0},{1,17},{17,1},{2,18},{18,2},{3,19},{19,3},{4,20},{20... | collective-permute-start | bytes 1572872 | tf_op jit(solution)/shard_map/ppermute | solution.py:83
  637.3 30.9 %collective-permute-start.92 = (bf16[1024,256]{1,0:T(8,128)(2,1)S(1)}, bf16[1024,256]{1,0:T(8,128)(2,1)S(1)}, u32[]{:S(2)}, u32[]{:S(2)}) collective-permute-start(bf16[1024,256]{1,0:T(8,128)(2,1)S(1)} %fusion.78), channel_id=1, source_target_pairs={{0,16},{16,0},{1,17},{17,1},{2,18},{18,2},{3,19},{19,3},{4,20},{20... | collective-permute-start | bytes 1572872 | tf_op jit(solution)/shard_map/ppermute | solution.py:83
  647.8 28.9 %collective-permute-start.100 = (f32[1024,24]{0,1:T(8,128)S(1)}, f32[1024,24]{0,1:T(8,128)S(1)}, u32[]{:S(2)}, u32[]{:S(2)}) collective-permute-start(f32[1024,24]{0,1:T(8,128)S(1)} %fusion.27), channel_id=1, source_target_pairs={{0,16},{16,0},{1,17},{17,1},{2,18},{18,2},{3,19},{19,3},{4,20},{20... | collective-permute-start | bytes 294920 | tf_op jit(solution)/shard_map/ppermute | solution.py:83
  659.0 29.5 %collective-permute-start.75 = (bf16[1024,256]{1,0:T(8,128)(2,1)S(1)}, bf16[1024,256]{1,0:T(8,128)(2,1)S(1)}, u32[]{:S(2)}, u32[]{:S(2)}) collective-permute-start(bf16[1024,256]{1,0:T(8,128)(2,1)S(1)} %get-tuple-element.190), channel_id=1, source_target_pairs={{0,4},{4,8},{8,12},{12,14},{14,10},{10,6},{6,2},{2,0},{1,5},{5,9},... | collective-permute-start | bytes 1572872 | tf_op jit(solution)/shard_map/ppermute | solution.py:83
  674.8 13.8 %collective-permute-start.93 = (bf16[1024,256]{1,0:T(8,128)(2,1)S(1)}, bf16[1024,256]{1,0:T(8,128)(2,1)}, u32[]{:S(2)}, u32[]{:S(2)}) collective-permute-start(bf16[1024,256]{1,0:T(8,128)(2,1)S(1)} %get-tuple-element.192), channel_id=1, source_target_pairs={{0,4},{4,8},{8,12},{12,14},{14,10},{10,6},{6,2},{2,0},{1,5},{5,9},... | collective-permute-start | bytes 1572872 | tf_op jit(solution)/shard_map/ppermute | solution.py:83
  688.2 86.8 %collective-permute-start.60 = (bf16[512,2048]{0,1:T(8,128)(2,1)}, bf16[512,2048]{0,1:T(8,128)(2,1)}, u32[]{:S(2)}, u32[]{:S(2)}) collective-permute-start(bf16[512,2048]{0,1:T(8,128)(2,1)} %slice.525), channel_id=1, source_target_pairs={{0,1},{1,0},{2,3},{3,2},{4,5},{5,4},{6,7},{7,6},{8,9},{9,8},{10,11... | collective-permute-start | bytes 6291464 | tf_op jit(solution)/shard_map/ppermute | solution.py:83
  688.5 14.8 %collective-permute-start.76 = (bf16[1024,256]{1,0:T(8,128)(2,1)S(1)}, bf16[1024,256]{1,0:T(8,128)(2,1)S(1)}, u32[]{:S(2)}, u32[]{:S(2)}) collective-permute-start(bf16[1024,256]{1,0:T(8,128)(2,1)S(1)} %get-tuple-element.190), channel_id=1, source_target_pairs={{4,0},{8,4},{12,8},{14,12},{10,14},{6,10},{2,6},{0,2},{5,1},{9,5},... | collective-permute-start | bytes 1572872 | tf_op jit(solution)/shard_map/ppermute | solution.py:83
  688.7 25.4 %collective-permute-start.94 = (bf16[1024,256]{1,0:T(8,128)(2,1)S(1)}, bf16[1024,256]{1,0:T(8,128)(2,1)S(1)}, u32[]{:S(2)}, u32[]{:S(2)}) collective-permute-start(bf16[1024,256]{1,0:T(8,128)(2,1)S(1)} %get-tuple-element.192), channel_id=1, source_target_pairs={{4,0},{8,4},{12,8},{14,12},{10,14},{6,10},{2,6},{0,2},{5,1},{9,5},... | collective-permute-start | bytes 1572872 | tf_op jit(solution)/shard_map/ppermute | solution.py:83
  715.4 45.7 %collective-permute-start.77 = (bf16[1024,256]{1,0:T(8,128)(2,1)S(1)}, bf16[1024,256]{1,0:T(8,128)(2,1)}, u32[]{:S(2)}, u32[]{:S(2)}) collective-permute-start(bf16[1024,256]{1,0:T(8,128)(2,1)S(1)} %collective-permute-done.75), channel_id=1, source_target_pairs={{0,4},{4,8},{8,12},{12,14},{14,10},{10,6},{6,2},{2,0},{1,5},{5,9},... | collective-permute-start | bytes 1572872 | tf_op jit(solution)/shard_map/ppermute | solution.py:83
  763.9 15.1 %collective-permute-start.96 = (bf16[1024,256]{1,0:T(8,128)(2,1)S(1)}, bf16[1024,256]{1,0:T(8,128)(2,1)S(1)}, u32[]{:S(2)}, u32[]{:S(2)}) collective-permute-start(bf16[1024,256]{1,0:T(8,128)(2,1)S(1)} %collective-permute-done.94), channel_id=1, source_target_pairs={{4,0},{8,4},{12,8},{14,12},{10,14},{6,10},{2,6},{0,2},{5,1},{9,5},... | collective-permute-start | bytes 1572872 | tf_op jit(solution)/shard_map/ppermute | solution.py:83
  773.4 31.9 %collective-permute-start.79 = (bf16[1024,256]{1,0:T(8,128)(2,1)}, bf16[1024,256]{1,0:T(8,128)(2,1)S(1)}, u32[]{:S(2)}, u32[]{:S(2)}) collective-permute-start(bf16[1024,256]{1,0:T(8,128)(2,1)} %collective-permute-done.77), channel_id=1, source_target_pairs={{0,4},{4,8},{8,12},{12,14},{14,10},{10,6},{6,2},{2,0},{1,5},{5,9},... | collective-permute-start | bytes 1572872 | tf_op jit(solution)/shard_map/ppermute | solution.py:83
  774.9 43.8 %collective-permute-start.97 = (bf16[1024,256]{1,0:T(8,128)(2,1)}, bf16[1024,256]{1,0:T(8,128)(2,1)S(1)}, u32[]{:S(2)}, u32[]{:S(2)}) collective-permute-start(bf16[1024,256]{1,0:T(8,128)(2,1)} %collective-permute-done.95), channel_id=1, source_target_pairs={{0,4},{4,8},{8,12},{12,14},{14,10},{10,6},{6,2},{2,0},{1,5},{5,9},... | collective-permute-start | bytes 1572872 | tf_op jit(solution)/shard_map/ppermute | solution.py:83
  779.1 25.4 %collective-permute-start.64 = (bf16[64,2048]{0,1:T(8,128)(2,1)S(1)}, bf16[64,2048]{0,1:T(8,128)(2,1)S(1)}, u32[]{:S(2)}, u32[]{:S(2)}) collective-permute-start(bf16[64,2048]{0,1:T(8,128)(2,1)S(1)} %get-tuple-element.120), channel_id=1, source_target_pairs={{0,4},{4,8},{8,12},{12,14},{14,10},{10,6},{6,2},{2,0},{1,5},{5,9},... | collective-permute-start | bytes 786440 | tf_op jit(solution)/shard_map/ppermute | solution.py:83
  816.0 24.7 %collective-permute-start.80 = (bf16[1024,256]{1,0:T(8,128)(2,1)S(1)}, bf16[1024,256]{1,0:T(8,128)(2,1)S(1)}, u32[]{:S(2)}, u32[]{:S(2)}) collective-permute-start(bf16[1024,256]{1,0:T(8,128)(2,1)S(1)} %collective-permute-done.78), channel_id=1, source_target_pairs={{4,0},{8,4},{12,8},{14,12},{10,14},{6,10},{2,6},{0,2},{5,1},{9,5},... | collective-permute-start | bytes 1572872 | tf_op jit(solution)/shard_map/ppermute | solution.py:83
  817.4 20.8 %collective-permute-start.62 = (bf16[64,2048]{0,1:T(8,128)(2,1)S(1)}, bf16[64,2048]{0,1:T(8,128)(2,1)S(1)}, u32[]{:S(2)}, u32[]{:S(2)}) collective-permute-start(bf16[64,2048]{0,1:T(8,128)(2,1)S(1)} %get-tuple-element.117), channel_id=1, source_target_pairs={{4,0},{8,4},{12,8},{14,12},{10,14},{6,10},{2,6},{0,2},{5,1},{9,5},... | collective-permute-start | bytes 786440 | tf_op jit(solution)/shard_map/ppermute | solution.py:83
  818.7 20.3 %collective-permute-start.66 = (bf16[64,2048]{0,1:T(8,128)(2,1)S(1)}, bf16[64,2048]{0,1:T(8,128)(2,1)S(1)}, u32[]{:S(2)}, u32[]{:S(2)}) collective-permute-start(bf16[64,2048]{0,1:T(8,128)(2,1)S(1)} %get-tuple-element.118), channel_id=1, source_target_pairs={{0,4},{4,8},{8,12},{12,14},{14,10},{10,6},{6,2},{2,0},{1,5},{5,9},... | collective-permute-start | bytes 786440 | tf_op jit(solution)/shard_map/ppermute | solution.py:83
  838.2 17.4 %collective-permute-start.98 = (bf16[1024,256]{1,0:T(8,128)(2,1)S(1)}, bf16[1024,256]{1,0:T(8,128)(2,1)S(1)}, u32[]{:S(2)}, u32[]{:S(2)}) collective-permute-start(bf16[1024,256]{1,0:T(8,128)(2,1)S(1)} %collective-permute-done.96), channel_id=1, source_target_pairs={{4,0},{8,4},{12,8},{14,12},{10,14},{6,10},{2,6},{0,2},{5,1},{9,5},... | collective-permute-start | bytes 1572872 | tf_op jit(solution)/shard_map/ppermute | solution.py:83
  848.6 15.5 %collective-permute-start.81 = (bf16[1024,256]{1,0:T(8,128)(2,1)S(1)}, bf16[1024,256]{1,0:T(8,128)(2,1)S(1)}, u32[]{:S(2)}, u32[]{:S(2)}) collective-permute-start(bf16[1024,256]{1,0:T(8,128)(2,1)S(1)} %collective-permute-done.79), channel_id=1, source_target_pairs={{0,4},{4,8},{8,12},{12,14},{14,10},{10,6},{6,2},{2,0},{1,5},{5,9},... | collective-permute-start | bytes 1572872 | tf_op jit(solution)/shard_map/ppermute | solution.py:83
  853.5 14.4 %collective-permute-start.99 = (bf16[1024,256]{1,0:T(8,128)(2,1)S(1)}, bf16[1024,256]{1,0:T(8,128)(2,1)S(1)}, u32[]{:S(2)}, u32[]{:S(2)}) collective-permute-start(bf16[1024,256]{1,0:T(8,128)(2,1)S(1)} %collective-permute-done.97), channel_id=1, source_target_pairs={{0,4},{4,8},{8,12},{12,14},{14,10},{10,6},{6,2},{2,0},{1,5},{5,9},... | collective-permute-start | bytes 1572872 | tf_op jit(solution)/shard_map/ppermute | solution.py:83
  (136 other events, 2430.3 us)

commit v2 on v1

v2 whole, which is shorter than its diff:
```python
import functools
import math

import jax
import jax.numpy as jnp
import numpy as np
from jax import lax
from jax.experimental import pallas as pl
from jax.experimental.pallas import tpu as pltpu
from jax.sharding import PartitionSpec as P

PIECE = 256


EPSILON = 1e-06
LOG_THETA = math.log(1000000.0)
MASKED_SCORE = -1e30
LANES = 128
BF16 = jnp.bfloat16
F32 = jnp.float32


def inverse_norm(values):
    return lax.rsqrt(jnp.mean(values * values, axis=-1, keepdims=True) + EPSILON)


def dot(left, right):
    return jnp.dot(left, right, preferred_element_type=F32)


def contract_rows(left, right):
    return lax.dot_general(left, right, (((0,), (0,)), ((), ())), preferred_element_type=F32)


def contract_cols(left, right):
    return lax.dot_general(left, right, (((1,), (1,)), ((), ())), preferred_element_type=F32)


class Ring:
    def __init__(self):
        self.owners = lax.axis_size("ep")
        self.groups = lax.axis_size("fsdp")
        self.index = lax.axis_index("ep")
        self.group = lax.axis_index("fsdp")
        self.half = lax.axis_index("tp")
        n = self.owners
        if n == 8:
            order = [0, 2, 4, 6, 7, 5, 3, 1] if self.groups == 2 else [0, 1, 2, 3, 7, 6, 5, 4]
        else:
            order = list(range(n))
        self.forward = [(order[i], order[(i + 1) % n]) for i in range(n)]
        self.backward = [(dst, src) for src, dst in self.forward]
        self.ahead = n // 2
        self.behind = (n - 1) // 2
        offsets = [0]
        for step in range(1, self.ahead + 1):
            offsets.append(-step)
            if step <= self.behind:
                offsets.append(step)
        self.slot = {offset: place for place, offset in enumerate(offsets)}
        self.slot[self.ahead] = self.slot[-self.ahead] if n % 2 == 0 else self.slot[self.ahead]
        table = np.zeros((n, n), np.int32)
        for position, owner in enumerate(order):
            for place, offset in enumerate(offsets):
                table[owner, place] = order[(position + offset) % n]
        self.owners_by_slot = jnp.asarray(table)[self.index]

    def send(self, values, pairs, axis="ep"):
        return lax.ppermute(values, axis, pairs)

    def swap_halves(self, values):
        return self.send(values, [(0, 1), (1, 0)], "tp")

    def swap_groups(self, values):
        return self.send(values, [(0, 1), (1, 0)], "fsdp")

    def walk(self, own, even=False):
        return Walk(self, own, even)

    def blocks(self, own, hook=None, even=False):
        walk = Walk(self, own, even)
        for step in range(self.ahead):
            done = None if hook is None else hook(step, walk)
            walk.step()
            walk.hold(done)
        return walk.found

    def gather(self, own, hook=None):
        found = self.blocks(own, hook)
        mine = jnp.concatenate(found, axis=0)
        return (mine, self.swap_halves(mine)), found

    def scatter(self, mine, other, hook=None):
        mine = mine.astype(F32) + self.swap_halves(other).astype(F32)
        mine = mine.astype(BF16).reshape(self.owners, -1, mine.shape[-1])

        def block(offset):
            return mine[self.slot[offset]].astype(F32)

        total = block(0)
        ahead = mine[self.slot[self.ahead]]
        behind = mine[self.slot[-self.behind]] if self.behind else None
        for step in range(self.ahead):
            done = None if hook is None else hook(step, ahead)
            offset = self.ahead - 1 - step
            ahead = self.send(ahead, self.forward)
            if done is not None:
                ahead = after(ahead, done)
            if offset:
                ahead = (ahead.astype(F32) + block(offset)).astype(BF16)
            offset = self.behind - 1 - step
            if offset >= 0:
                behind = self.send(behind, self.backward)
                if done is not None:
                    behind = after(behind, done)
                if offset:
                    behind = (behind.astype(F32) + block(-offset)).astype(BF16)
        if self.behind:
            total = total + behind.astype(F32)
        return total + ahead.astype(F32)

    def own_rows(self, values):
        rows = values.shape[0] // 2
        return lax.dynamic_slice_in_dim(values, self.half * rows, rows)

    def join_halves(self, own):
        other = self.swap_halves(own)
        first = self.half == 0
        return jnp.concatenate([jnp.where(first, own, other), jnp.where(first, other, own)], axis=0)

    def whole_rows(self, own):
        if self.groups == 2:
            other = self.swap_groups(own)
            first = self.group == 0
            return jnp.concatenate(
                [jnp.where(first, own, other), jnp.where(first, other, own)], axis=0
            )
        return lax.all_gather(own, "fsdp", axis=0, tiled=True)

    def send_share(self, lefts, rights, width, kind, cols=None, block=0):
        if self.groups != 2:
            return None, None
        theirs = transposed_product(lefts, rights, width // 2, 1 - self.group, kind, cols, block)
        return theirs, self.swap_groups(theirs)

    def add_share(self, arrived, lefts, rights, width, cols=None, block=0):
        if self.groups == 2:
            ours = transposed_product(lefts, rights, width // 2, self.group, F32, cols, block)
            return ours + arrived.astype(F32)
        cols = cols or rights[0].shape[1]
        whole = contract_rows(
            jnp.concatenate(lefts, axis=0)[:, :width],
            jnp.concatenate(rights, axis=0)[:, block * cols : (block + 1) * cols],
        )
        return lax.psum_scatter(whole, "fsdp", scatter_dimension=0, tiled=True)

    def all_groups(self, mine):
        theirs = lax.all_gather(mine, "fsdp", axis=0)
        return theirs, self.swap_halves(theirs)

    def sum_all(self, values):
        for axis in ("ep", "fsdp", "tp"):
            step = 1
            while step < lax.axis_size(axis):
                pairs = [(i, i ^ step) for i in range(lax.axis_size(axis))]
                values = values + self.send(values, pairs, axis)
                step *= 2
        return values


def after(values, signal):
    return lax.optimization_barrier((values, signal))[0]


class Walk:
    def __init__(self, ring, own, even):
        self.ring, self.ahead, self.behind, self.even = ring, own, own, even
        self.found, self.count = [own], 0

    def hold(self, done):
        if done is not None:
            self.ahead, self.behind, self.found[-1] = after(
                (self.ahead, self.behind, self.found[-1]), done
            )

    def step(self, signal=None):
        ring = self.ring
        self.count += 1
        if signal is not None:
            self.ahead, self.behind = after((self.ahead, self.behind), signal)
        if self.count > ring.behind and self.even and ring.behind:
            cut = self.ahead.shape[0] // 2
            self.found.append(
                (
                    ring.send(self.ahead[:cut], ring.forward),
                    ring.send(self.behind[cut:], ring.backward),
                )
            )
            return
        self.ahead = ring.send(self.ahead, ring.forward)
        self.found.append(self.ahead)
        if self.count <= ring.behind:
            self.behind = ring.send(self.behind, ring.backward)
            self.found.append(self.behind)


def pad_lanes(values):
    return jnp.pad(values, ((0, 0), (0, LANES - values.shape[1])))


VMEM = pltpu.VMEM
SMEM = pltpu.SMEM
ROW_BLOCK = 256


def call(kernel, micros, **kwargs):
    return pl.pallas_call(
        kernel,
        compiler_params=pltpu.CompilerParams(vmem_limit_bytes=56 * 1024 * 1024),
        cost_estimate=pl.CostEstimate(
            flops=int(micros * 1.15e9), bytes_accessed=0, transcendentals=0
        ),
        **kwargs,
    )


def whole_spec():
    return pl.BlockSpec(memory_space=VMEM)


def turned(values):
    return pltpu.roll(values, values.shape[-1] // 2, 1)


def row_blocks(mine, other, step=ROW_BLOCK):
    half = mine.shape[0]
    for place, ref in enumerate((mine, other)):
        for start in range(0, half, step):
            yield ref, start, place * half + start


def cut_kernel(e_ref, q_ref, k_ref, v_ref, o_ref, out_ref):
    cols, dim = q_ref.shape[1], k_ref.shape[1]
    out_ref[:, :cols] = q_ref[...]
    out_ref[:, cols : cols + dim] = k_ref[...]
    out_ref[:, cols + dim : cols + 2 * dim] = v_ref[...]
    out_ref[:, cols + 2 * dim :] = o_ref[...]


def cut_weights(device, key_head, query_proj, key_matrix, value_matrix, out_proj, cols, dim):
    rows = query_proj.shape[0]
    heads = pl.BlockSpec((rows, cols), lambda i, e: (0, e[0]))
    key = pl.BlockSpec((rows, dim), lambda i, e: (0, e[1]))
    return call(
        cut_kernel,
        3,
        grid_spec=pltpu.PrefetchScalarGridSpec(
            num_scalar_prefetch=1,
            grid=(1,),
            in_specs=[heads, key, key, heads],
            out_specs=pl.BlockSpec((rows, 2 * cols + 2 * dim), lambda i, e: (0, 0)),
        ),
        out_shape=jax.ShapeDtypeStruct((rows, 2 * cols + 2 * dim), BF16),
    )(jnp.stack([device, key_head]).astype(jnp.int32), query_proj, key_matrix, value_matrix, out_proj)


def spots(at_ref, w_refs):
    rows = w_refs[0].shape[0]
    return [(pl.ds(pl.multiple_of(at_ref[i] * rows, rows), rows), ref) for i, ref in enumerate(w_refs)]


def project_kernel(
    heads, parts, at_ref, xm_ref, xo_ref, cos_ref, sin_ref, qg_ref, kg_ref, *refs
):
    w_refs, (raw_ref, ql_ref, kl_ref, vl_ref) = refs[:parts], refs[parts:]
    dim = qg_ref.shape[1]
    cols = heads * dim
    for ref, start, row in row_blocks(xm_ref, xo_ref):
        rows = slice(row, row + ROW_BLOCK)
        raw = sum(
            dot(ref[start : start + ROW_BLOCK, spot], w_ref[:, : cols + 2 * dim])
            for spot, w_ref in spots(at_ref, w_refs)
        )
        raw_ref[rows, :] = raw[:, : cols + dim]
        cosine, sine = cos_ref[rows, :], sin_ref[rows, :]
        for head in range(heads + 1):
            part = raw[:, head * dim : (head + 1) * dim]
            gain = qg_ref[...] if head < heads else kg_ref[...]
            part = part * inverse_norm(part) * gain
            part = (part * cosine + turned(part) * sine).astype(BF16)
            if head < heads:
                ql_ref[rows, head * dim : (head + 1) * dim] = part
            else:
                kl_ref[rows, :] = part
        vl_ref[rows, :] = raw[:, cols + dim :].astype(BF16)


def smem_spec():
    return pl.BlockSpec(memory_space=SMEM)


def project(at, x, weights, heads, cosine, sine, q_gain, k_gain):
    rows, dim = 2 * x[0].shape[0], q_gain.shape[1]
    cols = heads * dim
    return call(
        functools.partial(project_kernel, heads, len(weights)),
        7,
        in_specs=[smem_spec()] + [whole_spec()] * (6 + len(weights)),
        out_specs=[whole_spec()] * 4,
        out_shape=[
            jax.ShapeDtypeStruct((rows, cols + dim), F32),
            jax.ShapeDtypeStruct((rows, cols), BF16),
            jax.ShapeDtypeStruct((rows, dim), BF16),
            jax.ShapeDtypeStruct((rows, dim), BF16),
        ],
    )(at, *x, cosine, sine, q_gain, k_gain, *weights)


def attend_kernel(heads, base, parts, at_ref, pos_ref, lim_ref, ql_ref, kl_ref, vl_ref, *refs):
    w_refs, (out_ref, lse_ref, part_ref) = refs[:parts], refs[parts:]
    dim = kl_ref.shape[1]
    cols = heads * dim
    scale = dim ** (-0.5)
    for row in range(0, out_ref.shape[0], ROW_BLOCK):
        rows, among = slice(row, row + ROW_BLOCK), slice(base + row, base + row + ROW_BLOCK)
        allowed = pos_ref[...] <= lim_ref[among, :]
        for head in range(heads):
            cut = slice(head * dim, (head + 1) * dim)
            scores = contract_cols(ql_ref[among, cut], kl_ref[...]) * scale
            scores = jnp.where(allowed, scores, MASKED_SCORE)
            top = jnp.max(scores, axis=1, keepdims=True)
            powers = jnp.exp(scores - top)
            total = jnp.sum(powers, axis=1, keepdims=True)
            lse_ref[head, rows, :] = top + jnp.log(total)
            probs = (powers * (1.0 / total)).astype(BF16)
            out_ref[rows, cut] = dot(probs, vl_ref[...]).astype(BF16)
        for spot, w_ref in spots(at_ref, w_refs):
            part_ref[rows, spot] = contract_cols(
                out_ref[rows, :], w_ref[:, cols + 2 * dim :]
            ).astype(BF16)


def attend(at, place, weights, position, limit, query, key, value):
    rows, dim = key.shape
    cols = query.shape[1]
    half, width = rows // 2, sum(w.shape[0] for w in weights)
    heads = cols // dim
    return call(
        functools.partial(attend_kernel, heads, place * half, len(weights)),
        6.5,
        in_specs=[smem_spec()] + [whole_spec()] * (5 + len(weights)),
        out_specs=[whole_spec()] * 3,
        out_shape=[
            jax.ShapeDtypeStruct((half, cols), BF16),
            jax.ShapeDtypeStruct((heads, half, 1), F32),
            jax.ShapeDtypeStruct((half, width), BF16),
        ],
    )(at, position, limit, query, key, value, *weights)


def attend_back_kernel(
    heads,
    parts,
    at_ref,
    bm_ref,
    bo_ref,
    cos_ref,
    sin_ref,
    qg_ref,
    kg_ref,
    pos_ref,
    lim_ref,
    raw_ref,
    ql_ref,
    kl_ref,
    vl_ref,
    lm_ref,
    lo_ref,
    *refs,
):
    w_refs, refs = refs[:parts], refs[parts:]
    layer_refs, (rm_ref, ro_ref, gains_ref, pm_ref, po_ref, dk_ref, dv_ref) = refs[:-7], refs[-7:]
    dim = qg_ref.shape[1]
    cols = heads * dim
    scale = dim ** (-0.5)
    q_part = jnp.zeros((1, dim), F32)
    k_part = jnp.zeros((1, dim), F32)

    def norm_back(grad, rows, raw, gain):
        inverse = inverse_norm(raw)
        unit = raw * inverse
        grad = grad * cos_ref[rows, :] - turned(grad) * sin_ref[rows, :]
        part = jnp.sum(grad * unit, axis=0, keepdims=True)
        grad = grad * gain
        return inverse * (grad - unit * jnp.mean(grad * unit, axis=1, keepdims=True)), part

    first = True
    for (ref, start, row), lse_ref, rg_ref in zip(
        row_blocks(bm_ref, bo_ref), (lm_ref, lm_ref, lo_ref, lo_ref), (rm_ref, rm_ref, ro_ref, ro_ref)
    ):
        rows, here = slice(row, row + ROW_BLOCK), slice(start, start + ROW_BLOCK)
        grads = sum(
            dot(ref[here, spot], w_ref[:, cols + 2 * dim :]) for spot, w_ref in spots(at_ref, w_refs)
        ).astype(BF16)
        allowed = pos_ref[...] <= lim_ref[rows, :]
        for head in range(heads):
            cut = slice(head * dim, (head + 1) * dim)
            query, value_grad = ql_ref[rows, cut], grads[:, cut]
            scores = contract_cols(query, kl_ref[...]) * scale
            probs = jnp.exp(jnp.where(allowed, scores - lse_ref[head, here, :], MASKED_SCORE))
            prob_grad = contract_cols(value_grad, vl_ref[...])
            weighed = probs * prob_grad
            delta = jnp.sum(weighed, axis=1, keepdims=True)
            score_grad = (weighed - probs * delta).astype(BF16)
            q_grad = dot(score_grad, kl_ref[...]) * scale
            k_more = contract_rows(query, score_grad)
            v_more = contract_rows(value_grad, probs.astype(BF16))
            if first:
                dk_ref[...] = k_more
                dv_ref[...] = v_more
                first = False
            else:
                dk_ref[...] += k_more
                dv_ref[...] += v_more
            q_raw_grad, part = norm_back(q_grad, rows, raw_ref[rows, cut], qg_ref[...])
            q_part = q_part + part
            rg_ref[here, cut] = q_raw_grad.astype(BF16)
    own = pm_ref.shape[1] // 2
    for out_ref, part_refs in (
        (pm_ref, layer_refs[: len(layer_refs) // 2]),
        (po_ref, layer_refs[len(layer_refs) // 2 :]),
    ):
        block = 0
        for part_ref in part_refs:
            for start in range(0, part_ref.shape[0], own):
                out_ref[block, own:, :] = part_ref[start : start + own, :]
                block += 1
    for (_, start, row), rg_ref, ref in zip(
        row_blocks(bm_ref, bo_ref),
        (rm_ref, rm_ref, ro_ref, ro_ref),
        (pm_ref, pm_ref, po_ref, po_ref),
    ):
        rows, here = slice(row, row + ROW_BLOCK), slice(start, start + ROW_BLOCK)
        k_grad = dk_ref[:, rows].T * scale
        k_raw_grad, part = norm_back(k_grad, rows, raw_ref[rows, cols : cols + dim], kg_ref[...])
        k_part = k_part + part
        rg_ref[here, cols : cols + dim] = k_raw_grad.astype(BF16)
        rg_ref[here, cols + dim :] = dv_ref[:, rows].T.astype(BF16)
        for spot, w_ref in spots(at_ref, w_refs):
            part = contract_cols(rg_ref[here, :], w_ref[:, : cols + 2 * dim]).astype(BF16)
            for i in range(ROW_BLOCK // own):
                ref[start // own + i, :own, spot] = part[i * own : (i + 1) * own, :]
    gains_ref[0:1, :] = q_part
    gains_ref[1:2, :] = k_part


def attend_back(
    at, branch, weights, layer, own, cosine, sine, q_gain, k_gain, position, limit, saved
):
    half = branch[0].shape[0]
    dim = q_gain.shape[1]
    width = sum(w.shape[0] for w in weights)
    cols = saved[1].shape[1]
    raw_half = jax.ShapeDtypeStruct((half, cols + 2 * dim), BF16)
    return call(
        functools.partial(attend_back_kernel, cols // dim, len(weights)),
        18.5,
        in_specs=[smem_spec()] + [whole_spec()] * (14 + len(weights) + len(layer)),
        out_specs=[whole_spec()] * 5,
        out_shape=[
            raw_half,
            raw_half,
            jax.ShapeDtypeStruct((2, dim), F32),
            jax.ShapeDtypeStruct((half // own, 2 * own, width), BF16),
            jax.ShapeDtypeStruct((half // own, 2 * own, width), BF16),
        ],
        scratch_shapes=[VMEM((dim, 2 * half), F32), VMEM((dim, 2 * half), F32)],
    )(at, *branch, cosine, sine, q_gain, k_gain, position, limit, *saved, *weights, *layer)


def routed_gates(x_ref, g_ref, router_ref, picks):
    lane = lax.broadcasted_iota(jnp.int32, (1, LANES), 1).astype(F32)
    logits = dot(x_ref[...], router_ref[...])
    names = g_ref[:, x_ref.shape[1] :].astype(F32)
    chosen = jnp.zeros(logits.shape, F32)
    for k in range(picks):
        chosen = jnp.where(names[:, k : k + 1] == lane, 1.0, chosen)
    logits = jnp.where(chosen > 0.0, logits, MASKED_SCORE)
    powers = chosen * jnp.exp(logits - jnp.max(logits, axis=1, keepdims=True))
    return powers / jnp.sum(powers, axis=1, keepdims=True)


def expert_values(x, g, gates, name, gate_up, down):
    each = down.shape[0]
    lane = lax.broadcasted_iota(jnp.int32, (1, LANES), 1)
    both = dot(x, gate_up)
    gate_val, up_val = both[:, :each], both[:, each:]
    grad = contract_cols(g, down)
    gate = jnp.sum(jnp.where(lane == name, gates, 0.0), axis=1, keepdims=True)
    sigmoid_val = 0.5 * jnp.tanh(0.5 * gate_val) + 0.5
    silu_val = gate_val * sigmoid_val
    act = silu_val * up_val
    act_grad = gate * grad
    gate_low = (act_grad * up_val * (sigmoid_val + silu_val * (1.0 - sigmoid_val))).astype(BF16)
    up_low = (act_grad * silu_val).astype(BF16)
    return (gate * act).astype(BF16), gate_low, up_low, act * grad


def experts_kernel(
    picks,
    expert_count,
    first_ref,
    xm_ref,
    xo_ref,
    gm_ref,
    go_ref,
    wg_ref,
    wu_ref,
    wd_ref,
    router_ref,
    weighted_ref,
    hidden_ref,
    gates_ref,
    pm_ref,
    po_ref,
    both_ref,
    side_ref,
):
    expert = pl.program_id(0)
    wide, width = xm_ref.shape
    each = wg_ref.shape[2]
    lane = lax.broadcasted_iota(jnp.int32, (1, LANES), 1)
    halves = ((xm_ref, gm_ref, pm_ref, 0), (xo_ref, go_ref, po_ref, wide))

    @pl.when(expert == 0)
    def _():
        for x_ref, g_ref, _, row in halves:
            gates_ref[row : row + wide, :] = routed_gates(x_ref, g_ref, router_ref, picks)

    name = first_ref[0] + expert
    place = first_ref[1] + name
    at = pl.multiple_of(expert * 2 * each, 2 * each)
    both_ref[:, pl.ds(at, each)] = wg_ref[0]
    both_ref[:, pl.ds(at + each, each)] = wu_ref[0]
    for x_ref, g_ref, _, row in halves:
        rows = slice(row, row + wide)
        weighted, gate_low, up_low, products = expert_values(
            x_ref[...],
            g_ref[:, :width],
            gates_ref[rows, :],
            name,
            both_ref[:, pl.ds(at, 2 * each)],
            wd_ref[0],
        )
        weighted_ref[rows, :] = weighted
        hidden_ref[rows, pl.ds(at, each)] = gate_low
        hidden_ref[rows, pl.ds(at + each, each)] = up_low
        row_grad = jnp.sum(products, axis=1, keepdims=True)
        high = row_grad.astype(BF16).astype(F32)
        side = jnp.where(lane == place, high, 0.0)
        side = side + jnp.where(lane == place + 2 * expert_count, row_grad - high, 0.0)
        side_ref[rows, :] = jnp.where(expert == 0, side, side_ref[rows, :] + side)

    @pl.when(expert == pl.num_programs(0) - 1)
    def _():
        for _, _, ref, row in halves:
            rows = slice(row, row + wide)
            ref[:, :width] = contract_cols(hidden_ref[rows, :], both_ref[...]).astype(BF16)
            ref[:, width:] = side_ref[rows, :].astype(BF16)


def experts(first, x, g, gate_proj, up_proj, down_proj, router, picks, expert_count):
    half, width = x[0].shape
    rows = 2 * half
    count, _, each = gate_proj.shape
    resident = lambda shape: pl.BlockSpec(
        shape, lambda i, first: (0,) * len(shape), pipeline_mode=pl.Buffered(1)
    )
    payload = (half, width + LANES)
    return call(
        functools.partial(experts_kernel, picks, expert_count),
        41,
        grid_spec=pltpu.PrefetchScalarGridSpec(
            num_scalar_prefetch=1,
            grid=(count,),
            in_specs=[resident((half, width))] * 2
            + [resident(payload)] * 2
            + [pl.BlockSpec((1, width, each), lambda i, first: (i, 0, 0))] * 2
            + [
                pl.BlockSpec((1, each, width), lambda i, first: (i, 0, 0)),
                resident((width, LANES)),
            ],
            out_specs=[
                pl.BlockSpec((rows, each), lambda i, first: (0, i)),
                resident((rows, 2 * count * each)),
                resident((rows, LANES)),
                resident(payload),
                resident(payload),
            ],
            scratch_shapes=[VMEM((width, 2 * count * each), BF16), VMEM((rows, LANES), F32)],
        ),
        out_shape=[
            jax.ShapeDtypeStruct((rows, count * each), BF16),
            jax.ShapeDtypeStruct((rows, 2 * count * each), BF16),
            jax.ShapeDtypeStruct((rows, LANES), F32),
            jax.ShapeDtypeStruct(payload, BF16),
            jax.ShapeDtypeStruct(payload, BF16),
        ],
    )(first, x[0], x[1], g[0], g[1], gate_proj, up_proj, down_proj, router)


def transposed_product_kernel(side_ref, am_ref, ao_ref, bm_ref, bo_ref, out_ref):
    total = contract_rows(am_ref[...], bm_ref[...]) + contract_rows(ao_ref[...], bo_ref[...])
    out_ref[...] = total.astype(out_ref.dtype)


def transposed_product(lefts, rights, share, side, kind, cols=None, block=0):
    half = rights[0].shape[0]
    cols = cols or rights[0].shape[1]
    left = pl.BlockSpec((half, share), lambda i, side: (0, side[0]))
    return call(
        transposed_product_kernel,
        4,
        grid_spec=pltpu.PrefetchScalarGridSpec(
            num_scalar_prefetch=1,
            grid=(1,),
            in_specs=[left, left] + [pl.BlockSpec((half, cols), lambda i, side: (0, block))] * 2,
            out_specs=pl.BlockSpec((share, cols), lambda i, side: (0, 0)),
        ),
        out_shape=jax.ShapeDtypeStruct((share, cols), kind),
    )(side.reshape(1).astype(jnp.int32), *lefts, *rights)


def layer_kernel(w_ref, d_ref, out_ref):
    out_ref[...] = dot(w_ref[...], d_ref[...]).astype(BF16)


def layer_part(part, parts, weighted, down):
    rows, hidden = weighted.shape
    width = down.shape[1]
    return call(
        layer_kernel,
        4,
        grid=(1,),
        in_specs=[
            pl.BlockSpec((rows // parts, hidden), lambda i: (part, 0)),
            pl.BlockSpec((hidden, width), lambda i: (0, 0)),
        ],
        out_specs=pl.BlockSpec((rows // parts, width), lambda i: (0, 0)),
        out_shape=jax.ShapeDtypeStruct((rows // parts, width), BF16),
    )(weighted, down)


def other_experts_kernel(
    picks, first_ref, x_ref, g_ref, wg_ref, wu_ref, wd_ref, router_ref, w_ref, h_ref, gates_ref
):
    expert = pl.program_id(0)
    width = x_ref.shape[1]
    each = wg_ref.shape[2]

    @pl.when(expert == 0)
    def _():
        gates_ref[...] = routed_gates(x_ref, g_ref, router_ref, picks)

    w_ref[...], h_ref[:, :each], h_ref[:, each:], _ = expert_values(
        x_ref[...],
        g_ref[:, :width],
        gates_ref[...],
        first_ref[0] + expert,
        jnp.concatenate([wg_ref[0], wu_ref[0]], axis=1),
        wd_ref[0],
    )


def other_experts(first, x, g, gate_proj, up_proj, down_proj, router, picks):
    rows, width = x.shape
    count, _, each = gate_proj.shape
    resident = lambda shape: pl.BlockSpec(
        shape, lambda i, first: (0,) * len(shape), pipeline_mode=pl.Buffered(1)
    )
    return call(
        functools.partial(other_experts_kernel, picks),
        14,
        grid_spec=pltpu.PrefetchScalarGridSpec(
            num_scalar_prefetch=1,
            grid=(count,),
            in_specs=[resident(x.shape), resident(g.shape)]
            + [pl.BlockSpec((1, width, each), lambda i, first: (i, 0, 0))] * 2
            + [
                pl.BlockSpec((1, each, width), lambda i, first: (i, 0, 0)),
                resident(router.shape),
            ],
            out_specs=[
                pl.BlockSpec((rows, each), lambda i, first: (0, i)),
                pl.BlockSpec((rows, 2 * each), lambda i, first: (0, i)),
            ],
            scratch_shapes=[VMEM((rows, LANES), F32)],
        ),
        out_shape=[
            jax.ShapeDtypeStruct((rows, count * each), BF16),
            jax.ShapeDtypeStruct((rows, 2 * count * each), BF16),
        ],
    )(first, x, g, gate_proj, up_proj, down_proj, router)


def in_halves(values, block, index):
    if isinstance(values, (tuple, list)):
        places = (0, 0)
    else:
        values, places = (values, values), (0, 1)
    specs = [
        pl.BlockSpec(block, lambda i, place=place: (place, index), pipeline_mode=pl.Buffered(1))
        for place in places
    ]
    return list(values), specs


def sign(token_ref):
    token_ref[...] = jnp.zeros(token_ref.shape, token_ref.dtype)


TOKEN = (8, LANES)


def gate_up_grad_kernel(x0, x1, x2, x3, d0, d1, d2, d3, *refs):
    gate_ref, up_ref, token_ref = refs[-3:]
    each = gate_ref.shape[2]
    total = (contract_rows(x0[...], d0[...]) + contract_rows(x1[...], d1[...])) + (
        contract_rows(x2[...], d2[...]) + contract_rows(x3[...], d3[...])
    )
    gate_ref[0] = total[:, :each]
    up_ref[0] = total[:, each:]
    sign(token_ref)


def gate_up_grad(expert, count, totals, own, other, own_hidden, other_hidden):
    half, width = own[0].shape
    each = own_hidden.shape[1] // 2 // count
    wide = 2 * ROW_BLOCK
    left = pl.BlockSpec((half, wide), lambda i: (0, i))
    part = pl.BlockSpec((1, wide, each), lambda i: (expert, i, 0))
    rights, specs = in_halves(own_hidden, (half, 2 * each), expert)
    more, more_specs = in_halves(other_hidden, (half, 2 * each), expert)
    return call(
        gate_up_grad_kernel,
        11.7,
        grid=(width // wide,),
        in_specs=[left] * 4
        + specs
        + more_specs
        + [pl.BlockSpec(memory_space=pl.ANY)] * len(totals),
        out_specs=[part] * 2 + [pl.BlockSpec(TOKEN, lambda i: (0, 0))],
        out_shape=[jax.ShapeDtypeStruct((count, width, each), F32)] * 2
        + [jax.ShapeDtypeStruct(TOKEN, F32)],
        input_output_aliases={8: 0, 9: 1} if totals else {},
    )(*own, *other, *rights, *more, *totals)


def down_grad_kernel(count, w0, w1, w2, w3, g0, g1, g2, g3, *refs):
    out_ref, token_ref = refs[-2:]
    each = out_ref.shape[1]
    total = (contract_rows(w0[...], g0[...]) + contract_rows(w1[...], g1[...])) + (
        contract_rows(w2[...], g2[...]) + contract_rows(w3[...], g3[...])
    )
    for i in range(count):
        out_ref[i] = total[i * each : (i + 1) * each, :]
    sign(token_ref)


def down_grad(part, parts, count, totals, own_weighted, other_weighted, own, other):
    half, width = own[0].shape[0], own[0].shape[1] - LANES
    hidden = own_weighted.shape[1]
    each = hidden // count
    wide = 2 * ROW_BLOCK
    steps = width // wide // parts
    right = pl.BlockSpec((half, wide), lambda i: (0, part * steps + i))
    place = pl.BlockSpec((count, each, wide), lambda i: (0, 0, part * steps + i))
    lefts, specs = in_halves(own_weighted, (half, hidden), 0)
    more, more_specs = in_halves(other_weighted, (half, hidden), 0)
    return call(
        functools.partial(down_grad_kernel, count),
        9.7,
        grid=(steps,),
        in_specs=specs
        + more_specs
        + [right] * 4
        + [pl.BlockSpec(memory_space=pl.ANY)] * len(totals),
        out_specs=[place, pl.BlockSpec(TOKEN, lambda i: (0, 0))],
        out_shape=[
            jax.ShapeDtypeStruct((count, each, width), F32),
            jax.ShapeDtypeStruct(TOKEN, F32),
        ],
        input_output_aliases={8: 0} if totals else {},
    )(*lefts, *more, *own, *other, *totals)


def join_kernel(*refs):
    out_ref = refs[-1]
    own = refs[0].shape[0]
    for i, ref in enumerate(refs[:-1]):
        out_ref[i * own : (i + 1) * own, :] = ref[...]


def join_rows(blocks):
    own, width = blocks[0].shape
    return call(
        join_kernel,
        2,
        in_specs=[whole_spec()] * len(blocks),
        out_specs=whole_spec(),
        out_shape=jax.ShapeDtypeStruct((own * len(blocks), width), blocks[0].dtype),
    )(*blocks)


def place_wide_kernel(owners_ref, *refs):
    blocks, out_ref = refs[:-1], refs[-1]
    cols = blocks[0].shape[1]
    start = 0
    slot = 0
    for ref in blocks:
        rows = ref.shape[0]
        at = pl.multiple_of(owners_ref[slot] * cols, cols)
        out_ref[start : start + rows, pl.ds(at, cols)] = ref[...].astype(F32)
        start += rows
        if start == out_ref.shape[0]:
            start, slot = 0, slot + 1


def place_wide(owners_by_slot, blocks, width):
    share = blocks[0].shape[0]
    return call(
        place_wide_kernel,
        6,
        in_specs=[smem_spec()] + [whole_spec()] * len(blocks),
        out_specs=whole_spec(),
        out_shape=jax.ShapeDtypeStruct((share, width), F32),
    )(owners_by_slot, *blocks)


def place_kernel(sharers, owners_ref, *refs):
    blocks, (q_ref, k_ref, v_ref) = refs[:-3], refs[-3:]
    share = q_ref.shape[0]
    cols = blocks[0].shape[1]
    dim = cols // 2
    rows = blocks[0].shape[0] - share
    for i, ref in enumerate(blocks):
        owner = owners_ref[i]
        at = pl.multiple_of(owner * cols, cols)
        q_ref[:, pl.ds(at, cols)] = ref[:share, :].astype(F32)
        down = pl.multiple_of(owner % sharers * rows, rows)
        right = pl.multiple_of(owner // sharers * dim, dim)
        k_ref[pl.ds(down, rows), pl.ds(right, dim)] = ref[share:, :dim].astype(F32)
        v_ref[pl.ds(down, rows), pl.ds(right, dim)] = ref[share:, dim:].astype(F32)


def place_blocks(owners_by_slot, blocks, shapes, sharers):
    return call(
        functools.partial(place_kernel, sharers),
        7,
        in_specs=[pl.BlockSpec(memory_space=SMEM)] + [whole_spec()] * len(blocks),
        out_specs=[whole_spec()] * 3,
        out_shape=[jax.ShapeDtypeStruct(shape, F32) for shape in shapes],
    )(owners_by_slot, *blocks)


def place_last_kernel(share, owner_ref, top_in, low_in, q_any, k_any, v_any, q_ref, k_ref, v_ref):
    dim = k_ref.shape[1]
    cut = top_in.shape[0]
    q_ref[:cut, :] = top_in[...].astype(F32)
    q_ref[cut:, :] = low_in[: share - cut, :].astype(F32)
    k_ref[...] = low_in[share - cut :, :dim].astype(F32)
    v_ref[...] = low_in[share - cut :, dim:].astype(F32)


def place_last(owner, halves, totals, sharers):
    share = totals[0].shape[0]
    top, low = halves
    cols = top.shape[1]
    rows = top.shape[0] + low.shape[0] - share
    spots = pl.BlockSpec((rows, cols // 2), lambda i, o: (o[0] % sharers, o[0] // sharers))
    return call(
        functools.partial(place_last_kernel, share),
        3,
        grid_spec=pltpu.PrefetchScalarGridSpec(
            num_scalar_prefetch=1,
            grid=(1,),
            in_specs=[
                pl.BlockSpec(top.shape, lambda i, o: (0, 0)),
                pl.BlockSpec(low.shape, lambda i, o: (0, 0)),
            ]
            + [pl.BlockSpec(memory_space=pl.ANY)] * 3,
            out_specs=[pl.BlockSpec((share, cols), lambda i, o: (0, o[0])), spots, spots],
        ),
        out_shape=[jax.ShapeDtypeStruct(total.shape, F32) for total in totals],
        input_output_aliases={3: 0, 4: 1, 5: 2},
    )(owner.reshape(1), top, low, *totals)


def body(
    tokens,
    routes,
    places,
    piece_starts,
    attn_gain,
    query_proj,
    key_matrix,
    value_matrix,
    out_proj,
    query_gain,
    key_gain,
    ffn_gain,
    router,
    gate_proj,
    up_proj,
    down_proj,
    out_grad,
):
    ring = Ring()
    local_rows, width = tokens.shape
    head_dim = query_gain.shape[0]
    owners, groups = ring.owners, ring.groups
    heads_tp = query_proj.shape[1] // head_dim
    kv_tp = key_matrix.shape[1] // head_dim
    heads_here = heads_tp // owners
    heads_each_key = heads_tp // kv_tp
    sharers = heads_each_key // heads_here
    experts_here, _, each = gate_proj.shape
    expert_count = experts_here * owners
    picks = routes.shape[1]
    seq_len = local_rows * owners
    half_rows = local_rows // 2
    scale = head_dim ** (-0.5)
    e, f, t = ring.index, ring.group, ring.half
    key_head = (e * heads_here) // heads_each_key
    shared_index = e % sharers

    pair = groups == 2
    q_cols = heads_here * head_dim
    down = down_proj.reshape(experts_here * each, width)
    first = jnp.stack([e * experts_here, t * expert_count]).astype(jnp.int32)

    def attention_tables(places, piece_starts):
        group_places = lax.dynamic_slice_in_dim(places, f * seq_len, seq_len)
        by_slot = jnp.take(group_places.reshape(owners, 2, half_rows), ring.owners_by_slot, axis=0)
        order_places = jnp.concatenate(
            [
                lax.dynamic_index_in_dim(by_slot, t, 1, keepdims=False).reshape(-1),
                lax.dynamic_index_in_dim(by_slot, 1 - t, 1, keepdims=False).reshape(-1),
            ]
        )
        position = order_places % seq_len
        begins = lax.dynamic_slice_in_dim(piece_starts, f, 1)
        inside = (begins <= position[:, None]) & (position[:, None] < begins + PIECE)
        limit = jnp.maximum(
            position, jnp.max(jnp.where(inside, begins + (PIECE - 1), 0), axis=1)
        )
        half_dim = head_dim // 2
        freqs = jnp.exp(jnp.arange(half_dim, dtype=F32) * (-2.0 * LOG_THETA / head_dim))
        angles = position.astype(F32)[:, None] * freqs[None, :]
        cosine, sine = jnp.cos(angles), jnp.sin(angles)
        return (
            jnp.concatenate([cosine, cosine], axis=1),
            jnp.concatenate([-sine, sine], axis=1),
            query_gain[None, :],
            key_gain[None, :],
            position[None, :],
            limit[:, None],
        )

    grads_own = ring.own_rows(out_grad)
    payload = jnp.concatenate([grads_own, pad_lanes(ring.own_rows(routes).astype(BF16))], axis=1)
    stream = ring.own_rows(tokens).astype(F32)
    first_inverse = inverse_norm(stream)
    normed = stream * first_inverse
    made = {}

    def first_hook(step, walk):
        done = []
        if step == 0:
            made["cut"] = cut_weights(
                e, key_head, query_proj, key_matrix, value_matrix, out_proj, q_cols, head_dim
            )
            made["chunks"] = []
            if not pair:
                made["weights"] = (lax.all_gather(made["cut"], "fsdp", axis=0, tiled=True),)
        if pair:
            rows = made["cut"].shape[0] // ring.ahead
            chunk = made["cut"][step * rows : (step + 1) * rows]
            if step:
                chunk = after(chunk, walk.ahead)
            made["chunks"].append(ring.swap_groups(chunk))
            done.append(made["chunks"][-1])
        grads_walk.step(walk.ahead if step else None)
        done.append(grads_walk.ahead)
        if step == 1:
            made["tables"] = attention_tables(*after((places, piece_starts), walk.ahead))
            done += made["tables"][:4]
        if step == 2:
            done += made["tables"][4:]
        return tuple(done)

    grads_walk = ring.walk(payload)
    attn_in, _ = ring.gather((normed * attn_gain).astype(BF16), first_hook)
    if pair:
        made["weights"] = (made["cut"], jnp.concatenate(made["chunks"], axis=0))
    tables, weights = made["tables"], made["weights"]
    at = jnp.stack([f, 1 - f] if pair else [jnp.zeros_like(f)]).astype(jnp.int32)
    raw, query_low, key_low, value_low = project(at, attn_in, weights, heads_here, *tables[:4])
    low = (query_low, key_low, value_low)
    attn_other, lse_other, part_other = attend(at, 1, weights, *tables[4:], *low)
    attn_mine, lse_mine, part_mine = attend(at, 0, weights, *tables[4:], *low)
    grads_found = grads_walk.found
    grads_mine = jnp.concatenate(grads_found, axis=0)
    grads = (grads_mine, ring.swap_halves(grads_mine))
    their_rows = []

    def across(signal):
        if not pair:
            return []
        rows = ffn_in[0].shape[0] // ring.ahead
        start = len(their_rows) * rows
        their_rows.append(ring.swap_groups(after(ffn_in[0], signal)[start : start + rows]))
        return their_rows[-1:]

    def branch_hook(step, signal):
        if step != 1:
            return None
        made["router"] = ring.whole_rows(after(router, signal))
        made["lanes"] = pad_lanes(made["router"])
        return made["lanes"]

    residual = stream + ring.scatter(part_mine, part_other, branch_hook)
    whole_router, router_lanes = made["router"], made["lanes"]

    second_inverse = inverse_norm(residual)
    mid_normed = residual * second_inverse
    ffn_in, _ = ring.gather((mid_normed * ffn_gain).astype(BF16))
    if pair:
        their_grads = ring.swap_groups(grads_mine)
    weighted, hidden, gates, back_mine, back_other = experts(
        first, ffn_in, grads, gate_proj, up_proj, down_proj, router_lanes, picks, expert_count
    )

    if pair:
        made["grads"], back_mine = after((their_grads, back_mine), their_grads)
    back_sum = ring.scatter(back_mine, back_other)

    gate_grad_rows = sum(
        back_sum[:, width + i * expert_count : width + (i + 1) * expert_count] for i in range(4)
    )
    own_gates = gates[:half_rows, :expert_count]
    picked_grad = own_gates * (
        gate_grad_rows - jnp.sum(own_gates * gate_grad_rows, axis=-1, keepdims=True)
    )
    logit_grad = picked_grad.astype(BF16)
    ffn_in_grad = back_sum[:, :width] + contract_cols(logit_grad, whole_router)
    ffn_gain_part = jnp.sum(ffn_in_grad * mid_normed, axis=0)
    second_normed_grad = ffn_in_grad * ffn_gain
    mid_grad = grads_own.astype(F32) + second_inverse * (
        second_normed_grad
        - mid_normed * jnp.mean(second_normed_grad * mid_normed, axis=-1, keepdims=True)
    )
    layer_parts = []

    def layer_hook(step, walk):
        layer_parts.append(layer_part(step, ring.ahead, after(weighted, walk.ahead), down))
        return tuple([layer_parts[-1]] + across(walk.ahead))

    branch, _ = ring.gather(
        jnp.concatenate([mid_grad.astype(BF16), pad_lanes(logit_grad)], axis=1), layer_hook
    )
    middle = len(layer_parts) // 2

    attn_halves = (attn_mine, attn_other)
    out_theirs, out_arrived = ring.send_share(branch, attn_halves, width, BF16)
    raw_mine, raw_other, head_gains, both_mine, both_other = attend_back(
        at,
        branch if out_theirs is None else after(branch, out_theirs),
        weights,
        layer_parts,
        half_rows,
        *tables,
        (raw, query_low, key_low, value_low, lse_mine, lse_other),
    )
    raw_halves = (raw_mine, raw_other)
    qkv_theirs, qkv_arrived = ring.send_share(attn_in, raw_halves, width, BF16)


    made["other"] = []

    def other_piece(half, signal):
        x, g = after([part[half] for part in made["theirs"]], signal)
        made["other"].append(
            other_experts(first, x, g, gate_proj, up_proj, down_proj, router_lanes, picks)
        )
        return made["other"][-1]

    totals = {"gate_up": [], "down": []}

    def last_piece(n, signal):
        x, g = made["theirs"]
        if n < experts_here:
            *totals["gate_up"], token = gate_up_grad(
                n,
                experts_here,
                totals["gate_up"],
                after(ffn_in, signal),
                x,
                hidden,
                [part[1] for part in made["other"]],
            )
        else:
            *totals["down"], token = down_grad(
                n - experts_here,
                2,
                experts_here,
                totals["down"],
                after(weighted, signal),
                [part[0] for part in made["other"]],
                grads,
                g,
            )
        return [token]

    def in_hook(step, signal):
        done = []
        if step == 0:
            share = ring.add_share(out_arrived, after(branch, signal), attn_halves, width)
            made["out_walk"] = ring.walk(share.astype(BF16), True)
            if pair:
                theirs = [join_rows(after(their_rows, signal)), after(made["grads"], signal)]
                made["theirs"] = [(part, ring.swap_halves(part)) for part in theirs]
                done += made["theirs"]
        else:
            made["out_walk"].step(signal)
        done.append(made["out_walk"].found[-1])
        if step == 1:
            made["qkv"] = ring.add_share(qkv_arrived, after(attn_in, signal), raw_halves, width)
            done.append(made["qkv"])
        if step in (1, 2) and pair:
            done += other_piece(step - 1, signal)
        if step == 3 and pair:
            done += last_piece(0, signal)
        return tuple(done)

    if qkv_theirs is not None:
        both_mine = after(both_mine, qkv_theirs)
    both_sum = ring.scatter(both_mine, both_other, in_hook)
    attn_in_grad = both_sum[:half_rows]
    layer_out = ring.join_halves((residual + both_sum[half_rows:]).astype(BF16))
    qkv_share = made["qkv"]
    first_normed_grad = attn_in_grad * attn_gain
    tokens_grad = mid_grad + first_inverse * (
        first_normed_grad - normed * jnp.mean(first_normed_grad * normed, axis=-1, keepdims=True)
    )
    tokens_grad = ring.join_halves(tokens_grad)
    attn_gain_part = jnp.sum(attn_in_grad * normed, axis=0)
    gains = ring.sum_all(
        jnp.concatenate([attn_gain_part, ffn_gain_part, head_gains[0], head_gains[1]])
    )

    kv_share = qkv_share[:, q_cols:]
    step = sharers // 2
    while step:
        rows = kv_share.shape[0] // 2
        bit = (shared_index // step) % 2
        pairs = [(i, i ^ step) for i in range(owners)]
        sent = lax.dynamic_slice_in_dim(kv_share, (1 - bit) * rows, rows)
        kept = lax.dynamic_slice_in_dim(kv_share, bit * rows, rows)
        kv_share = kept + ring.send(sent.astype(BF16), pairs).astype(F32)
        step //= 2
    own_share = jnp.concatenate([qkv_share[:, :q_cols], kv_share], axis=0).astype(BF16)

    last = ring.ahead - 1
    lanes_at = width // LANES

    share_rows = qkv_share.shape[0]
    shapes = [(share_rows, heads_tp * head_dim)] + [(share_rows, kv_tp * head_dim)] * 2

    def weight_hook(step, walk):
        signal = walk.ahead
        done = []
        if step == 0:
            made["out_walk"].step(signal)
            done += made["out_walk"].found[-1]
        if pair:
            done += last_piece(step + 1, signal)
        if step == 1:
            _, arrived = ring.send_share(after(ffn_in, signal), branch, width, F32, LANES, lanes_at)
            made["router_arrived"] = arrived
            done += [] if arrived is None else [arrived]
        if step == 2:
            made["router_grad"] = ring.add_share(
                made["router_arrived"], after(ffn_in, signal), branch, width, LANES, lanes_at
            )
            done.append(made["router_grad"])
        if step == last:
            found = made["out_walk"].found
            made["out_grad"] = place_wide(
                ring.owners_by_slot,
                [after(found[0], signal)] + found[1:-1] + list(found[-1]),
                heads_tp * head_dim,
            )
            done.append(made["out_grad"])
        if step == last:
            found = walk.found
            made["placed"] = place_blocks(
                ring.owners_by_slot, [after(found[0], signal)] + found[1:], shapes, sharers
            )
            done += made["placed"]
        return tuple(done)

    found = ring.blocks(own_share, weight_hook, True)
    out_grad_w = made["out_grad"]
    query_grad_w, key_grad_w, value_grad_w = place_last(
        ring.owners_by_slot[owners - 1], found[-1], made["placed"], sharers
    )
    router_grad = made["router_grad"][:, :expert_count]

    if pair:
        gate_total, up_total = totals["gate_up"]
        (down_total,) = totals["down"]
    else:
        all_rows, all_grads = ring.all_groups(ffn_in[0]), ring.all_groups(grads[0])

        def add_group(n, sums):
            gate_up, low = 0.0, 0.0
            for x, g in zip(all_rows, all_grads, strict=True):
                w, h = other_experts(
                    first, x[n], g[n], gate_proj, up_proj, down_proj, router_lanes, picks
                )
                gate_up = gate_up + contract_rows(x[n], h)
                low = low + contract_rows(w, g[n])[:, :width]
            gate_up = gate_up.reshape(width, experts_here, 2, each)
            return (
                sums[0] + jnp.swapaxes(gate_up[:, :, 0], 0, 1),
                sums[1] + jnp.swapaxes(gate_up[:, :, 1], 0, 1),
                sums[2] + low.reshape(experts_here, each, width),
            )

        gate_total, up_total, down_total = lax.fori_loop(
            0,
            groups,
            add_group,
            tuple(jnp.zeros(w.shape, F32) for w in (gate_proj, up_proj, down_proj)),
        )
    return (
        layer_out,
        tokens_grad,
        gains[:width],
        query_grad_w,
        key_grad_w,
        value_grad_w,
        out_grad_w,
        gains[2 * width : 2 * width + head_dim],
        gains[2 * width + head_dim :],
        gains[width : 2 * width],
        router_grad,
        gate_total,
        up_total,
        down_total,
    )


def solution(mesh):
    return jax.shard_map(
        body,
        mesh=mesh,
        in_specs=(
            P(("fsdp", "ep"), None),
            P(("fsdp", "ep"), None),
            P(),
            P(),
            P(),
            P("fsdp", "tp"),
            P("fsdp", "tp"),
            P("fsdp", "tp"),
            P("fsdp", "tp"),
            P(),
            P(),
            P(),
            P("fsdp", None),
            P("ep", None, "tp"),
            P("ep", None, "tp"),
            P("ep", "tp", None),
            P(("fsdp", "ep"), None),
        ),
        out_specs=(
            P(("fsdp", "ep"), None),
            P(("fsdp", "ep"), None),
            P(),
            P("fsdp", "tp"),
            P("fsdp", "tp"),
            P("fsdp", "tp"),
            P("fsdp", "tp"),
            P(),
            P(),
            P(),
            P("fsdp", None),
            P("ep", None, "tp"),
            P("ep", None, "tp"),
            P("ep", "tp", None),
        ),
        check_vma=False,
    )
```

time: 898 us -> 601 us (0.67)
  Pallas kernels: 0 us -> 234 us
  matrix products: 195 us -> 0.37 us
  local copies, waits for them, and re-layouts: 186 us -> 38.2 us
  waiting for transfers between devices: 312 us -> 184 us
  other arithmetic: 92.1 us -> 40.4 us
  between operations: 13 us -> 1.86 us
    pallas_call x0 -> x27, Pallas kernels: none -> 234 us  [the longest x1 41.3 us: experts(): call(functools.partial(experts_kernel, picks, expert_count), 41, grid_spe...]
    dot_general x24 -> x0, matrix products: 136 us -> none  [the longest x12 69 us: contract_rows(): lax.dot_general(left, right, (((0,), (0,)), ((), ())), preferred_element_...]
    ppermute x105 -> x96, waiting for transfers between devices: 312 us -> 184 us  [send(): return lax.ppermute(values, axis, pairs)]
    concatenate x17 -> x16, local copies, waits for them, and re-layouts: 71.3 us -> 2.52 us  [the longest x3 0.77 us: gather(): mine = jnp.concatenate(found, axis=0)]
    dot_general x6 -> x1, matrix products: 50.5 us -> 0.37 us  [contract_cols(): lax.dot_general(left, right, (((1,), (1,)), ((), ())), preferred_element_...]
    ppermute x22 -> x0, local copies, waits for them, and re-layouts: 29.3 us -> none  [send(): return lax.ppermute(values, axis, pairs)]
    another operation x3 -> x0, local copies, waits for them, and re-layouts: 19.1 us -> none  [the longest x1 13.6 us: body(): jnp.stack([gate_up_total[:, hidden + i * each:hidden + (i + 1) * each] fo...]
    dynamic_update_slice x22 -> x0, other arithmetic: 16.3 us -> none  [columns(): lax.dynamic_update_slice_in_dim(whole, part.astype(F32), ring.owners_by_s...]
  transfers between devices with their start and end apart: 105 -> 96, of which waited for: 47 -> 45; matrix products, arithmetic and copies ran while one was open for 47% -> 9% of each run, Pallas kernels for 0% -> 32%
where the time goes in v2:
time: 601 us; the launch traced here: 595 us
  Pallas kernels  234 us (39%)
  waiting for transfers between devices  184 us (31%)
  starting transfers between devices  96.5 us (16%)
  other arithmetic  40.4 us (7%)
  local copies, waits for them, and re-layouts  38.2 us (6%)
    ppermute x96, waiting for transfers between devices, send(): return lax.ppermute(values, axis, pairs)  184 us
    ppermute x96, starting transfers between devices, send(): return lax.ppermute(values, axis, pairs)  96.5 us
    pallas_call x1, Pallas kernels, experts(): call(functools.partial(experts_kernel, picks, expert_count), 41, grid_spe...  41.3 us
    pallas_call x3, Pallas kernels, gate_up_grad(): call(gate_up_grad_kernel, 11.7, grid=(width // wide,), in_specs=[left] *...  34.8 us
    pallas_call x2, Pallas kernels, other_experts(): call(functools.partial(other_experts_kernel, picks), 14, grid_spec=pltpu....  31 us
    unnamed x130, local copies, waits for them, and re-layouts  24.1 us
    pallas_call x6, Pallas kernels, transposed_product(): call(transposed_product_kernel, 4, grid_spec=pltpu.PrefetchScalarGridSpec...  21.8 us
    pallas_call x1, Pallas kernels, attend_back(): call(functools.partial(attend_back_kernel, cols // dim, len(weights)), 18...  21.4 us
  transfers between devices with their start and end apart: 96, of which 45 were waited for; matrix products, arithmetic and copies ran while one was open for 9% of the time, Pallas kernels for 32%

profile of v2, /device:TPU:0, one launch (start us, length us, event | category | flops | bytes accessed | tf_op | source)
XLA Modules:
  0.0 594.6 jit_solution(15048977567745435234)
XLA Ops:
  3.6 3.0 collective-permute-start
  11.2 3.3 shard_map.281.refs_0_
  21.1 4.9 collective-permute-done.2
  52.3 4.3 collective-permute-done.10
  63.0 3.0 collective-permute-done.17
  67.8 3.8 collective-permute-done.18.xo_ref.ao_ref
  71.5 7.4 %shard_map.282 = (f32[1024,384]{1,0:T(8,128)}, bf16[1024,256]{1,0:T(8,128)(2,1)}, bf16[1024,128]{1,0:T(8,128)(2,1)}, bf16[1024,128]{1,0:T(8,128)(2,1)}) custom-call(s32[2]{0:T(128)} %pad_add_fusion.at_ref, bf16[512,2048]{1,0:T(8,128)(2,1)} %constant_dynamic-update-slice_fusion.5.xm_ref.am_ref, bf16[512,2048]{1,0:T(8,128)(2,1)} %collective-permute-done.18.xo_ref.ao_ref, ...), custom_call_target="tpu_custom_call" | custom-call | flops 8049999872 | tf_op jit(solution)/shard_map/pallas_call | solution.py:305
  78.9 7.1 %shard_map.284 = (bf16[512,256]{1,0:T(8,128)(2,1)}, f32[2,512,1]{2,1,0:T(8,128)}, bf16[512,2048]{1,0:T(8,128)(2,1)}) custom-call(s32[2]{0:T(128)} %pad_add_fusion.at_ref, s32[1,1024]{1,0:T(1,128)} %and_select_fusion.1.pos_ref, s32[1024,1]{1,0:T(8,128)} %fusion.20.lim_ref, bf16[1024,256]{1,0:T(8,128)(2,1)} %get-tuple-element.166.ql_ref, ...), custom_call_target="tpu_custom_call" | custom-call | flops 7474999808 | tf_op jit(solution)/shard_map/pallas_call | solution.py:348
  88.6 7.1 %shard_map.283 = (bf16[512,256]{1,0:T(8,128)(2,1)}, f32[2,512,1]{2,1,0:T(8,128)}, bf16[512,2048]{1,0:T(8,128)(2,1)}) custom-call(s32[2]{0:T(128)} %pad_add_fusion.at_ref, s32[1,1024]{1,0:T(1,128)} %and_select_fusion.1.pos_ref, s32[1024,1]{1,0:T(8,128)} %fusion.20.lim_ref, bf16[1024,256]{1,0:T(8,128)(2,1)} %get-tuple-element.166.ql_ref, ...), custom_call_target="tpu_custom_call" | custom-call | flops 7474999808 | tf_op jit(solution)/shard_map/pallas_call | solution.py:348
  97.1 3.0 add_convert_fusion.2
  103.5 5.9 collective-permute-done.22
  116.3 4.7 collective-permute-done.25
  125.0 3.7 collective-permute-done.21
  133.0 3.6 collective-permute-done.24
  141.5 4.0 collective-permute-done.29
  147.8 5.7 collective-permute-done.31
  155.6 6.7 %collective-permute-done.33 = bf16[64,2048]{1,0:T(8,128)(2,1)S(1)} collective-permute-done((bf16[64,2048]{1,0:T(8,128)(2,1)S(1)}, bf16[64,2048]{1,0:T(8,128)(2,1)S(1)}, u32[]{:S(2)}, u32[]{:S(2)}) %collective-permute-start.33) | collective-permute-done | bytes 262176 | tf_op jit(solution)/shard_map/ppermute | solution.py:69
  164.3 4.4 collective-permute-done.35
  170.1 3.0 collective-permute-done.36.xo_ref.ao_ref.x1
  173.0 41.3 %shard_map.285 = (bf16[1024,1152]{1,0:T(8,128)(2,1)}, bf16[1024,2304]{1,0:T(8,128)(2,1)}, f32[1024,128]{1,0:T(8,128)}, bf16[512,2176]{1,0:T(8,128)(2,1)}, bf16[512,2176]{1,0:T(8,128)(2,1)}) custom-call(s32[2]{0:T(128)} %pad_add_fusion.2.first_ref, bf16[512,2048]{1,0:T(8,128)(2,1)} %copy-done.8, bf16[512,2048]{1,0:T(8,128)(2,1)} %collective-permute-done.36.xo_ref.ao_ref.x1, ...), custom_call_target="tpu_custom_call" | custom-call | flops 47149998080 | tf_op jit(solution)/shard_map/pallas_call | solution.py:580
  214.5 6.1 %collective-permute-done.28.g_ref.g2 = bf16[512,2176]{1,0:T(8,128)(2,1)} collective-permute-done((bf16[512,2176]{1,0:T(8,128)(2,1)}, bf16[512,2176]{1,0:T(8,128)(2,1)}, u32[]{:S(2)}, u32[]{:S(2)}) %collective-permute-start.28) | collective-permute-done | bytes 2228256 | tf_op jit(solution)/shard_map/ppermute | solution.py:69
  224.9 6.1 %collective-permute-done.42 = bf16[64,2176]{1,0:T(8,128)(2,1)S(1)} collective-permute-done((bf16[64,2176]{1,0:T(8,128)(2,1)S(1)}, bf16[64,2176]{1,0:T(8,128)(2,1)S(1)}, u32[]{:S(2)}, u32[]{:S(2)}) %collective-permute-start.42) | collective-permute-done | bytes 278560 | tf_op jit(solution)/shard_map/ppermute | solution.py:69
  233.1 5.3 collective-permute-done.43
  240.6 4.5 collective-permute-done.40
  247.9 4.5 collective-permute-done.41
  259.5 5.0 shard_map.286.refs_2_
  264.6 6.5 %collective-permute-done.48.refs_0_ = bf16[128,2048]{1,0:T(8,128)(2,1)S(1)} collective-permute-done((bf16[128,2048]{1,0:T(8,128)(2,1)S(1)}, bf16[128,2048]{1,0:T(8,128)(2,1)S(1)}, u32[]{:S(2)}, u32[]{:S(2)}) %collective-permute-start.48) | collective-permute-done | bytes 524320 | tf_op jit(solution)/shard_map/ppermute | solution.py:69
  271.3 2.5 collective-permute-start.51
  273.8 5.0 shard_map.287.refs_3_
  280.3 6.7 %collective-permute-done.50 = bf16[64,2176]{1,0:T(8,128)(2,1)S(1)} collective-permute-done((bf16[64,2176]{1,0:T(8,128)(2,1)S(1)}, bf16[64,2176]{1,0:T(8,128)(2,1)S(1)}, u32[]{:S(2)}, u32[]{:S(2)}) %collective-permute-start.50) | collective-permute-done | bytes 278560 | tf_op jit(solution)/shard_map/ppermute | solution.py:69
  288.7 5.0 shard_map.288.refs_4_
  296.4 5.1 collective-permute-done.53
  301.8 2.5 collective-permute-start.55
  306.1 5.0 shard_map.289.refs_5_
  311.1 2.4 collective-permute-done.56.refs_3_
  313.7 4.3 collective-permute-done.57.ao_ref.bo_ref
  319.3 3.3 shard_map.290
  322.6 21.4 %shard_map.291 = (bf16[512,512]{1,0:T(8,128)(2,1)}, bf16[512,512]{1,0:T(8,128)(2,1)}, f32[2,128]{1,0:T(2,128)}, bf16[8,128,2048]{2,1,0:T(8,128)(2,1)}, bf16[8,128,2048]{2,1,0:T(8,128)(2,1)}) custom-call(s32[2]{0:T(128)} %pad_add_fusion.at_ref, bf16[512,2176]{1,0:T(8,128)(2,1)} %copy-done.30, bf16[512,2176]{1,0:T(8,128)(2,1)} %copy-done.36, ...), custom_call_target="tpu_custom_call" | custom-call | flops 21275000832 | tf_op jit(solution)/shard_map/pallas_call | solution.py:465
  344.1 4.2 shard_map.292
  348.4 3.1 collective-permute-done.58
  351.5 4.1 add_convert_fusion
  358.7 3.0 shard_map.293.x_ref.x2
  366.2 3.6 shard_map.294
  369.8 7.0 %collective-permute-done.62 = bf16[1024,256]{1,0:T(8,128)(2,1)S(1)} collective-permute-done((bf16[1024,256]{1,0:T(8,128)(2,1)S(1)}, bf16[1024,256]{1,0:T(8,128)(2,1)S(1)}, u32[]{:S(2)}, u32[]{:S(2)}) %collective-permute-start.62) | collective-permute-done | bytes 524320 | tf_op jit(solution)/shard_map/ppermute | solution.py:69
  381.2 4.4 shard_map.295
  385.6 12.9 %collective-permute-done.66 = bf16[1024,512]{1,0:T(8,128)(2,1)} collective-permute-done((bf16[1024,512]{1,0:T(8,128)(2,1)}, bf16[1024,512]{1,0:T(8,128)(2,1)}, u32[]{:S(2)}, u32[]{:S(2)}) %collective-permute-start.66) | collective-permute-done | bytes 1048608 | tf_op jit(solution)/shard_map/ppermute | solution.py:69
  404.9 15.5 %shard_map.296 = (bf16[512,1152]{1,0:T(8,128)(2,1)}, bf16[512,2304]{1,0:T(8,128)(2,1)}) custom-call(s32[2]{0:T(128)} %pad_add_fusion.2.first_ref, bf16[512,2048]{1,0:T(8,128)(2,1)} %shard_map.293.x_ref.x2, bf16[512,2176]{1,0:T(8,128)(2,1)} %collective-permute-done.28.g_ref.g2, bf16[3,2048,384]{2,1,0:T(8,128)(2,1)} %wg_ref.5, bf16[3,2048,384]{2,1,0:T(8,128)(2,1)} %wu_ref.5, ...), custom_call_target="tpu_custom_call" | custom-call | flops 16099999744 | tf_op jit(solution)/shard_map/pallas_call | solution.py:681
  422.3 2.6 fusion.4
  429.1 15.5 %shard_map.297 = (bf16[512,1152]{1,0:T(8,128)(2,1)}, bf16[512,2304]{1,0:T(8,128)(2,1)}) custom-call(s32[2]{0:T(128)} %pad_add_fusion.2.first_ref, bf16[512,2048]{1,0:T(8,128)(2,1)} %collective-permute-done.60.x_ref.x3, bf16[512,2176]{1,0:T(8,128)(2,1)} %collective-permute-done.61.g_ref.g3, bf16[3,2048,384]{2,1,0:T(8,128)(2,1)} %wg_ref.5, ...), custom_call_target="tpu_custom_call" | custom-call | flops 16099999744 | tf_op jit(solution)/shard_map/pallas_call | solution.py:681
  444.6 5.6 collective-permute-done.63
  455.6 20.8 %collective-permute-done.83 = bf16[256,256]{1,0:T(8,128)(2,1)S(1)} collective-permute-done((bf16[256,256]{1,0:T(8,128)(2,1)S(1)}, bf16[256,256]{1,0:T(8,128)(2,1)S(1)}, u32[]{:S(2)}, u32[]{:S(2)}) %collective-permute-start.83) | collective-permute-done | bytes 131104 | tf_op jit(solution)/shard_map/ppermute | solution.py:69
  477.8 2.5 collective-permute-start.77
  482.7 11.6 %shard_map.303 = (f32[3,2048,384]{2,1,0:T(8,128)}, f32[3,2048,384]{2,1,0:T(8,128)}, f32[8,128]{1,0:T(8,128)}) custom-call(bf16[512,2048]{1,0:T(8,128)(2,1)} %copy-done.8, bf16[512,2048]{1,0:T(8,128)(2,1)} %collective-permute-done.36.xo_ref.ao_ref.x1, bf16[512,2048]{1,0:T(8,128)(2,1)} %shard_map.293.x_ref.x2, ...), custom_call_target="tpu_custom_call" | custom-call | flops 13454999552 | tf_op jit(solution)/shard_map/pallas_call | solution.py:744
  494.3 8.3 %collective-permute-done.78 = f32[4352]{0:T(1024)S(1)} collective-permute-done((f32[4352]{0:T(1024)S(1)}, f32[4352]{0:T(1024)S(1)}, u32[]{:S(2)}, u32[]{:S(2)}) %collective-permute-start.78) | collective-permute-done | bytes 17440 | tf_op jit(solution)/shard_map/ppermute | solution.py:69
  504.2 11.6 %shard_map.304 = (f32[3,2048,384]{2,1,0:T(8,128)}, f32[3,2048,384]{2,1,0:T(8,128)}, f32[8,128]{1,0:T(8,128)}) custom-call(bf16[512,2048]{1,0:T(8,128)(2,1)} %copy-done.8, bf16[512,2048]{1,0:T(8,128)(2,1)} %collective-permute-done.36.xo_ref.ao_ref.x1, bf16[512,2048]{1,0:T(8,128)(2,1)} %shard_map.293.x_ref.x2, ...), custom_call_target="tpu_custom_call", output_to_operand_aliasing={{0}: (8, {}), {1}: (9, {})} | custom-call | flops 13454999552 | tf_op jit(solution)/shard_map/pallas_call | solution.py:744
  515.9 2.5 collective-permute-start.87
  527.4 3.2 shard_map.298
  532.9 11.6 %shard_map.305 = (f32[3,2048,384]{2,1,0:T(8,128)}, f32[3,2048,384]{2,1,0:T(8,128)}, f32[8,128]{1,0:T(8,128)}) custom-call(bf16[512,2048]{1,0:T(8,128)(2,1)} %copy-done.8, bf16[512,2048]{1,0:T(8,128)(2,1)} %collective-permute-done.36.xo_ref.ao_ref.x1, bf16[512,2048]{1,0:T(8,128)(2,1)} %shard_map.293.x_ref.x2, ...), custom_call_target="tpu_custom_call", output_to_operand_aliasing={{0}: (8, {}), {1}: (9, {})} | custom-call | flops 13454999552 | tf_op jit(solution)/shard_map/pallas_call | solution.py:744
  550.8 3.2 shard_map.299
  555.9 9.7 %shard_map.306 = (f32[3,384,2048]{2,1,0:T(8,128)}, f32[8,128]{1,0:T(8,128)}) custom-call(bf16[1024,1152]{1,0:T(8,128)(2,1)} %get-tuple-element.277.w_ref.w0.w1, bf16[1024,1152]{1,0:T(8,128)(2,1)} %get-tuple-element.277.w_ref.w0.w1, bf16[512,1152]{1,0:T(8,128)(2,1)} %get-tuple-element.223.w2, bf16[512,1152]{1,0:T(8,128)(2,1)} %get-tuple-element.231.w3, ...), custom_call_target="tpu_custom_call" | custom-call | flops 11155000320 | tf_op jit(solution)/shard_map/pallas_call | solution.py:780
  567.9 9.7 %shard_map.307 = (f32[3,384,2048]{2,1,0:T(8,128)}, f32[8,128]{1,0:T(8,128)}) custom-call(bf16[1024,1152]{1,0:T(8,128)(2,1)} %get-tuple-element.277.w_ref.w0.w1, bf16[1024,1152]{1,0:T(8,128)(2,1)} %get-tuple-element.277.w_ref.w0.w1, bf16[512,1152]{1,0:T(8,128)(2,1)} %get-tuple-element.223.w2, ...), custom_call_target="tpu_custom_call", output_to_operand_aliasing={{0}: (8, {})} | custom-call | flops 11155000320 | tf_op jit(solution)/shard_map/pallas_call | solution.py:780
  577.7 6.9 %shard_map.301 = (f32[1024,2048]{1,0:T(8,128)}, f32[1024,256]{1,0:T(8,128)}, f32[1024,256]{1,0:T(8,128)}) custom-call(s32[8]{0:T(128)} %get-tuple-element.395.owners_ref, bf16[1280,256]{1,0:T(8,128)(2,1)} %copy-done.14, bf16[1280,256]{1,0:T(8,128)(2,1)} %copy-done.37, bf16[1280,256]{1,0:T(8,128)(2,1)} %copy-done.38, bf16[1280,256]{1,0:T(8,128)(2,1)} %copy-done.39, ...), custom_call_target="tpu_custom_call" | custom-call | flops 8049999872 | tf_op jit(solution)/shard_map/pallas_call | solution.py:857
  584.6 6.1 %shard_map.300 = f32[1024,2048]{1,0:T(8,128)} custom-call(s32[8]{0:T(128)} %get-tuple-element.395.owners_ref, bf16[1024,256]{1,0:T(8,128)(2,1)} %add_convert_fusion.3.refs_0_, bf16[1024,256]{1,0:T(8,128)(2,1)} %collective-permute-done.68.refs_1_, bf16[1024,256]{1,0:T(8,128)(2,1)} %collective-permute-done.65.refs_2_, ...), custom_call_target="tpu_custom_call" | custom-call | flops 6899999744 | tf_op jit(solution)/shard_map/pallas_call | solution.py:831
  591.6 2.9 shard_map.302
  (398 shorter events, 169.6 us)
Async XLA Ops:
  3.6 15.8 %collective-permute-start = (bf16[64,2048]{1,0:T(8,128)(2,1)S(1)}, bf16[64,2048]{1,0:T(8,128)(2,1)}, u32[]{:S(2)}, u32[]{:S(2)}) collective-permute-start(bf16[64,2048]{1,0:T(8,128)(2,1)S(1)} %get-tuple-element.347), channel_id=1, source_target_pairs={{0,4},{4,8},{8,12},{12,14},{14,10},{10,6},{6,2},{2,0},{1,5},{5,9},... | collective-permute-start | bytes 786440 | tf_op jit(solution)/shard_map/ppermute | solution.py:69
  6.6 14.5 %collective-permute-start.1 = (bf16[64,2048]{1,0:T(8,128)(2,1)S(1)}, bf16[64,2048]{1,0:T(8,128)(2,1)}, u32[]{:S(2)}, u32[]{:S(2)}) collective-permute-start(bf16[64,2048]{1,0:T(8,128)(2,1)S(1)} %get-tuple-element.347), channel_id=1, source_target_pairs={{4,0},{8,4},{12,8},{14,12},{10,14},{6,10},{2,6},{0,2},{5,1},{9,5},... | collective-permute-start | bytes 786440 | tf_op jit(solution)/shard_map/ppermute | solution.py:69
  8.6 12.6 %collective-permute-start.3 = (bf16[64,2176]{1,0:T(8,128)(2,1)S(1)}, bf16[64,2176]{1,0:T(8,128)(2,1)S(1)}, u32[]{:S(2)}, u32[]{:S(2)}) collective-permute-start(bf16[64,2176]{1,0:T(8,128)(2,1)S(1)} %get-tuple-element.383), channel_id=1, source_target_pairs={{0,4},{4,8},{8,12},{12,14},{14,10},{10,6},{6,2},{2,0},{1,5},{5,9},... | collective-permute-start | bytes 835592 | tf_op jit(solution)/shard_map/ppermute | solution.py:69
  10.6 19.5 %collective-permute-start.7 = (bf16[64,2176]{1,0:T(8,128)(2,1)S(1)}, bf16[64,2176]{1,0:T(8,128)(2,1)}, u32[]{:S(2)}, u32[]{:S(2)}) collective-permute-start(bf16[64,2176]{1,0:T(8,128)(2,1)S(1)} %get-tuple-element.383), channel_id=1, source_target_pairs={{4,0},{8,4},{12,8},{14,12},{10,14},{6,10},{2,6},{0,2},{5,1},{9,5},... | collective-permute-start | bytes 835592 | tf_op jit(solution)/shard_map/ppermute | solution.py:69
  16.0 10.1 %collective-permute-start.2 = (bf16[256,768]{1,0:T(8,128)(2,1)S(1)}, bf16[256,768]{1,0:T(8,128)(2,1)S(1)}, u32[]{:S(2)}, u32[]{:S(2)}) collective-permute-start(bf16[256,768]{1,0:T(8,128)(2,1)S(1)} %get-tuple-element.375), channel_id=1, source_target_pairs={{0,16},{16,0},{1,17},{17,1},{2,18},{18,2},{3,19},{19,3},{4,20},{20... | collective-permute-start | bytes 1179656 | tf_op jit(solution)/shard_map/ppermute | solution.py:69
  26.0 15.7 %collective-permute-start.4 = (bf16[64,2048]{1,0:T(8,128)(2,1)}, bf16[64,2048]{1,0:T(8,128)(2,1)}, u32[]{:S(2)}, u32[]{:S(2)}) collective-permute-start(bf16[64,2048]{1,0:T(8,128)(2,1)} %collective-permute-done), channel_id=1, source_target_pairs={{0,4},{4,8},{8,12},{12,14},{14,10},{10,6},{6,2},{2,0},{1,5},{5,9},... | collective-permute-start | bytes 786440 | tf_op jit(solution)/shard_map/ppermute | solution.py:69
  30.0 13.3 %collective-permute-start.8 = (bf16[64,2176]{1,0:T(8,128)(2,1)S(1)}, bf16[64,2176]{1,0:T(8,128)(2,1)}, u32[]{:S(2)}, u32[]{:S(2)}) collective-permute-start(bf16[64,2176]{1,0:T(8,128)(2,1)S(1)} %collective-permute-done.3), channel_id=1, source_target_pairs={{0,4},{4,8},{8,12},{12,14},{14,10},{10,6},{6,2},{2,0},{1,5},{5,9},... | collective-permute-start | bytes 835592 | tf_op jit(solution)/shard_map/ppermute | solution.py:69
  31.6 13.3 %collective-permute-start.12 = (bf16[64,2176]{1,0:T(8,128)(2,1)}, bf16[64,2176]{1,0:T(8,128)(2,1)}, u32[]{:S(2)}, u32[]{:S(2)}) collective-permute-start(bf16[64,2176]{1,0:T(8,128)(2,1)} %collective-permute-done.7), channel_id=1, source_target_pairs={{4,0},{8,4},{12,8},{14,12},{10,14},{6,10},{2,6},{0,2},{5,1},{9,5},... | collective-permute-start | bytes 835592 | tf_op jit(solution)/shard_map/ppermute | solution.py:69
  32.1 11.3 %collective-permute-start.6 = (bf16[256,768]{1,0:T(8,128)(2,1)S(1)}, bf16[256,768]{1,0:T(8,128)(2,1)S(1)}, u32[]{:S(2)}, u32[]{:S(2)}) collective-permute-start(bf16[256,768]{1,0:T(8,128)(2,1)S(1)} %get-tuple-element.152), channel_id=1, source_target_pairs={{0,16},{16,0},{1,17},{17,1},{2,18},{18,2},{3,19},{19,3},{4,20},{20... | collective-permute-start | bytes 1179656 | tf_op jit(solution)/shard_map/ppermute | solution.py:69
  33.7 9.7 %collective-permute-start.5 = (bf16[64,2048]{1,0:T(8,128)(2,1)}, bf16[64,2048]{1,0:T(8,128)(2,1)}, u32[]{:S(2)}, u32[]{:S(2)}) collective-permute-start(bf16[64,2048]{1,0:T(8,128)(2,1)} %collective-permute-done.1), channel_id=1, source_target_pairs={{4,0},{8,4},{12,8},{14,12},{10,14},{6,10},{2,6},{0,2},{5,1},{9,5},... | collective-permute-start | bytes 786440 | tf_op jit(solution)/shard_map/ppermute | solution.py:69
  43.3 13.2 %collective-permute-start.9 = (bf16[64,2048]{1,0:T(8,128)(2,1)}, bf16[64,2048]{1,0:T(8,128)(2,1)S(1)}, u32[]{:S(2)}, u32[]{:S(2)}) collective-permute-start(bf16[64,2048]{1,0:T(8,128)(2,1)} %collective-permute-done.4), channel_id=1, source_target_pairs={{0,4},{4,8},{8,12},{12,14},{14,10},{10,6},{6,2},{2,0},{1,5},{5,9},... | collective-permute-start | bytes 786440 | tf_op jit(solution)/shard_map/ppermute | solution.py:69
  44.9 11.6 %collective-permute-start.13 = (bf16[64,2176]{1,0:T(8,128)(2,1)}, bf16[64,2176]{1,0:T(8,128)(2,1)S(1)}, u32[]{:S(2)}, u32[]{:S(2)}) collective-permute-start(bf16[64,2176]{1,0:T(8,128)(2,1)} %collective-permute-done.8), channel_id=1, source_target_pairs={{0,4},{4,8},{8,12},{12,14},{14,10},{10,6},{6,2},{2,0},{1,5},{5,9},... | collective-permute-start | bytes 835592 | tf_op jit(solution)/shard_map/ppermute | solution.py:69
  46.4 10.7 %collective-permute-start.16 = (bf16[64,2176]{1,0:T(8,128)(2,1)}, bf16[64,2176]{1,0:T(8,128)(2,1)S(1)}, u32[]{:S(2)}, u32[]{:S(2)}) collective-permute-start(bf16[64,2176]{1,0:T(8,128)(2,1)} %collective-permute-done.12), channel_id=1, source_target_pairs={{4,0},{8,4},{12,8},{14,12},{10,14},{6,10},{2,6},{0,2},{5,1},{9,5},... | collective-permute-start | bytes 835592 | tf_op jit(solution)/shard_map/ppermute | solution.py:69
  47.0 9.6 %collective-permute-start.11 = (bf16[256,768]{1,0:T(8,128)(2,1)S(1)}, bf16[256,768]{1,0:T(8,128)(2,1)S(1)}, u32[]{:S(2)}, u32[]{:S(2)}) collective-permute-start(bf16[256,768]{1,0:T(8,128)(2,1)S(1)} %get-tuple-element.157), channel_id=1, source_target_pairs={{0,16},{16,0},{1,17},{17,1},{2,18},{18,2},{3,19},{19,3},{4,20},{20... | collective-permute-start | bytes 1179656 | tf_op jit(solution)/shard_map/ppermute | solution.py:69
  57.1 8.9 %collective-permute-start.17 = (bf16[64,2176]{1,0:T(8,128)(2,1)S(1)}, bf16[64,2176]{1,0:T(8,128)(2,1)S(1)}, u32[]{:S(2)}, u32[]{:S(2)}) collective-permute-start(bf16[64,2176]{1,0:T(8,128)(2,1)S(1)} %collective-permute-done.13), channel_id=1, source_target_pairs={{0,4},{4,8},{8,12},{12,14},{14,10},{10,6},{6,2},{2,0},{1,5},{5,9},... | collective-permute-start | bytes 835592 | tf_op jit(solution)/shard_map/ppermute | solution.py:69
  86.0 9.7 %collective-permute-start.19 = (bf16[512,2048]{1,0:T(8,128)(2,1)}, bf16[512,2048]{1,0:T(8,128)(2,1)S(1)}, u32[]{:S(2)}, u32[]{:S(2)}) collective-permute-start(bf16[512,2048]{1,0:T(8,128)(2,1)} %get-tuple-element.170), channel_id=1, source_target_pairs={{0,1},{1,0},{2,3},{3,2},{4,5},{5,4},{6,7},{7,6},{8,9},{9,8},{10,11... | collective-permute-start | bytes 6291464 | tf_op jit(solution)/shard_map/ppermute | solution.py:69
  100.8 8.6 %collective-permute-start.22 = (bf16[64,2048]{1,0:T(8,128)(2,1)S(1)}, bf16[64,2048]{1,0:T(8,128)(2,1)S(1)}, u32[]{:S(2)}, u32[]{:S(2)}) collective-permute-start(bf16[64,2048]{1,0:T(8,128)(2,1)S(1)} %get-tuple-element.369), channel_id=1, source_target_pairs={{0,4},{4,8},{8,12},{12,14},{14,10},{10,6},{6,2},{2,0},{1,5},{5,9},... | collective-permute-start | bytes 786440 | tf_op jit(solution)/shard_map/ppermute | solution.py:69
  141.5 28.5 %collective-permute-start.37 = (bf16[512,2176]{1,0:T(8,128)(2,1)}, bf16[512,2176]{1,0:T(8,128)(2,1)}, u32[]{:S(2)}, u32[]{:S(2)}) collective-permute-start(bf16[512,2176]{1,0:T(8,128)(2,1)} %constant_dynamic-update-slice_fusion.17.gm_ref.g0), channel_id=1, source_target_pairs={{0,1},{1,0},{2,3},{3,2},{4,5},{5,4},{6,7},{7,6},{8,9},{9,8},{10,11... | collective-permute-start | bytes 6684680 | tf_op jit(solution)/shard_map/ppermute | solution.py:69
  153.4 8.8 %collective-permute-start.33 = (bf16[64,2048]{1,0:T(8,128)(2,1)S(1)}, bf16[64,2048]{1,0:T(8,128)(2,1)S(1)}, u32[]{:S(2)}, u32[]{:S(2)}) collective-permute-start(bf16[64,2048]{1,0:T(8,128)(2,1)S(1)} %collective-permute-done.31), channel_id=1, source_target_pairs={{0,4},{4,8},{8,12},{12,14},{14,10},{10,6},{6,2},{2,0},{1,5},{5,9},... | collective-permute-start | bytes 786440 | tf_op jit(solution)/shard_map/ppermute | solution.py:69
  155.3 9.0 %collective-permute-start.34 = (bf16[64,2048]{1,0:T(8,128)(2,1)S(1)}, bf16[64,2048]{1,0:T(8,128)(2,1)S(1)}, u32[]{:S(2)}, u32[]{:S(2)}) collective-permute-start(bf16[64,2048]{1,0:T(8,128)(2,1)S(1)} %collective-permute-done.32), channel_id=1, source_target_pairs={{4,0},{8,4},{12,8},{14,12},{10,14},{6,10},{2,6},{0,2},{5,1},{9,5},... | collective-permute-start | bytes 786440 | tf_op jit(solution)/shard_map/ppermute | solution.py:69
  169.6 51.0 %collective-permute-start.28 = (bf16[512,2176]{1,0:T(8,128)(2,1)}, bf16[512,2176]{1,0:T(8,128)(2,1)}, u32[]{:S(2)}, u32[]{:S(2)}) collective-permute-start(bf16[512,2176]{1,0:T(8,128)(2,1)} %constant_dynamic-update-slice_fusion.17.gm_ref.g0), channel_id=1, source_target_pairs={{0,16},{16,0},{1,17},{17,1},{2,18},{18,2},{3,19},{19,3},{4,20},{20... | collective-permute-start | bytes 6684680 | tf_op jit(solution)/shard_map/ppermute | solution.py:69
  222.9 8.2 %collective-permute-start.42 = (bf16[64,2176]{1,0:T(8,128)(2,1)S(1)}, bf16[64,2176]{1,0:T(8,128)(2,1)S(1)}, u32[]{:S(2)}, u32[]{:S(2)}) collective-permute-start(bf16[64,2176]{1,0:T(8,128)(2,1)S(1)} %get-tuple-element.363), channel_id=1, source_target_pairs={{0,4},{4,8},{8,12},{12,14},{14,10},{10,6},{6,2},{2,0},{1,5},{5,9},... | collective-permute-start | bytes 835592 | tf_op jit(solution)/shard_map/ppermute | solution.py:69
  224.9 8.2 %collective-permute-start.39 = (bf16[64,2176]{1,0:T(8,128)(2,1)S(1)}, bf16[64,2176]{1,0:T(8,128)(2,1)S(1)}, u32[]{:S(2)}, u32[]{:S(2)}) collective-permute-start(bf16[64,2176]{1,0:T(8,128)(2,1)S(1)} %get-tuple-element.362), channel_id=1, source_target_pairs={{4,0},{8,4},{12,8},{14,12},{10,14},{6,10},{2,6},{0,2},{5,1},{9,5},... | collective-permute-start | bytes 835592 | tf_op jit(solution)/shard_map/ppermute | solution.py:69
  258.9 12.2 %collective-permute-start.48 = (bf16[128,2048]{1,0:T(8,128)(2,1)S(1)}, bf16[128,2048]{1,0:T(8,128)(2,1)S(1)}, u32[]{:S(2)}, u32[]{:S(2)}) collective-permute-start(bf16[128,2048]{1,0:T(8,128)(2,1)S(1)} %slice.208), channel_id=1, source_target_pairs={{0,16},{16,0},{1,17},{17,1},{2,18},{18,2},{3,19},{19,3},{4,20},{20... | collective-permute-start | bytes 1572872 | tf_op jit(solution)/shard_map/ppermute | solution.py:69
  271.1 9.2 %collective-permute-start.49 = (bf16[64,2176]{1,0:T(8,128)(2,1)S(1)}, bf16[64,2176]{1,0:T(8,128)(2,1)S(1)}, u32[]{:S(2)}, u32[]{:S(2)}) collective-permute-start(bf16[64,2176]{1,0:T(8,128)(2,1)S(1)} %collective-permute-done.46), channel_id=1, source_target_pairs={{0,4},{4,8},{8,12},{12,14},{14,10},{10,6},{6,2},{2,0},{1,5},{5,9},... | collective-permute-start | bytes 835592 | tf_op jit(solution)/shard_map/ppermute | solution.py:69
  271.3 15.8 %collective-permute-start.51 = (bf16[128,2048]{1,0:T(8,128)(2,1)S(1)}, bf16[128,2048]{1,0:T(8,128)(2,1)}, u32[]{:S(2)}, u32[]{:S(2)}) collective-permute-start(bf16[128,2048]{1,0:T(8,128)(2,1)S(1)} %slice.209), channel_id=1, source_target_pairs={{0,16},{16,0},{1,17},{17,1},{2,18},{18,2},{3,19},{19,3},{4,20},{20... | collective-permute-start | bytes 1572872 | tf_op jit(solution)/shard_map/ppermute | solution.py:69
  278.8 8.2 %collective-permute-start.50 = (bf16[64,2176]{1,0:T(8,128)(2,1)S(1)}, bf16[64,2176]{1,0:T(8,128)(2,1)S(1)}, u32[]{:S(2)}, u32[]{:S(2)}) collective-permute-start(bf16[64,2176]{1,0:T(8,128)(2,1)S(1)} %collective-permute-done.47), channel_id=1, source_target_pairs={{4,0},{8,4},{12,8},{14,12},{10,14},{6,10},{2,6},{0,2},{5,1},{9,5},... | collective-permute-start | bytes 835592 | tf_op jit(solution)/shard_map/ppermute | solution.py:69
  287.1 9.4 %collective-permute-start.52 = (bf16[64,2176]{1,0:T(8,128)(2,1)S(1)}, bf16[64,2176]{1,0:T(8,128)(2,1)S(1)}, u32[]{:S(2)}, u32[]{:S(2)}) collective-permute-start(bf16[64,2176]{1,0:T(8,128)(2,1)S(1)} %collective-permute-done.49), channel_id=1, source_target_pairs={{0,4},{4,8},{8,12},{12,14},{14,10},{10,6},{6,2},{2,0},{1,5},{5,9},... | collective-permute-start | bytes 835592 | tf_op jit(solution)/shard_map/ppermute | solution.py:69
  287.1 14.7 %collective-permute-start.54 = (bf16[128,2048]{1,0:T(8,128)(2,1)S(1)}, bf16[128,2048]{1,0:T(8,128)(2,1)S(1)}, u32[]{:S(2)}, u32[]{:S(2)}) collective-permute-start(bf16[128,2048]{1,0:T(8,128)(2,1)S(1)} %slice.210), channel_id=1, source_target_pairs={{0,16},{16,0},{1,17},{17,1},{2,18},{18,2},{3,19},{19,3},{4,20},{20... | collective-permute-start | bytes 1572872 | tf_op jit(solution)/shard_map/ppermute | solution.py:69
  301.8 9.4 %collective-permute-start.55 = (bf16[64,2176]{1,0:T(8,128)(2,1)S(1)}, bf16[64,2176]{1,0:T(8,128)(2,1)S(1)}, u32[]{:S(2)}, u32[]{:S(2)}) collective-permute-start(bf16[64,2176]{1,0:T(8,128)(2,1)S(1)} %collective-permute-done.52), channel_id=1, source_target_pairs={{0,4},{4,8},{8,12},{12,14},{14,10},{10,6},{6,2},{2,0},{1,5},{5,9},... | collective-permute-start | bytes 835592 | tf_op jit(solution)/shard_map/ppermute | solution.py:69
  304.3 9.2 %collective-permute-start.56 = (bf16[128,2048]{1,0:T(8,128)(2,1)S(1)}, bf16[128,2048]{1,0:T(8,128)(2,1)S(1)}, u32[]{:S(2)}, u32[]{:S(2)}) collective-permute-start(bf16[128,2048]{1,0:T(8,128)(2,1)S(1)} %slice.211), channel_id=1, source_target_pairs={{0,16},{16,0},{1,17},{17,1},{2,18},{18,2},{3,19},{19,3},{4,20},{20... | collective-permute-start | bytes 1572872 | tf_op jit(solution)/shard_map/ppermute | solution.py:69
  358.5 20.8 %collective-permute-start.61 = (bf16[512,2176]{1,0:T(8,128)(2,1)}, bf16[512,2176]{1,0:T(8,128)(2,1)}, u32[]{:S(2)}, u32[]{:S(2)}) collective-permute-start(bf16[512,2176]{1,0:T(8,128)(2,1)} %collective-permute-done.28.g_ref.g2), channel_id=1, source_target_pairs={{0,1},{1,0},{2,3},{3,2},{4,5},{5,4},{6,7},{7,6},{8,9},{9,8},{10,11... | collective-permute-start | bytes 6684680 | tf_op jit(solution)/shard_map/ppermute | solution.py:69
  361.6 17.7 %collective-permute-start.60 = (bf16[512,2048]{1,0:T(8,128)(2,1)}, bf16[512,2048]{1,0:T(8,128)(2,1)}, u32[]{:S(2)}, u32[]{:S(2)}) collective-permute-start(bf16[512,2048]{1,0:T(8,128)(2,1)} %shard_map.293.x_ref.x2), channel_id=1, source_target_pairs={{0,1},{1,0},{2,3},{3,2},{4,5},{5,4},{6,7},{7,6},{8,9},{9,8},{10,11... | collective-permute-start | bytes 6291464 | tf_op jit(solution)/shard_map/ppermute | solution.py:69
  362.0 14.8 %collective-permute-start.62 = (bf16[1024,256]{1,0:T(8,128)(2,1)S(1)}, bf16[1024,256]{1,0:T(8,128)(2,1)S(1)}, u32[]{:S(2)}, u32[]{:S(2)}) collective-permute-start(bf16[1024,256]{1,0:T(8,128)(2,1)S(1)} %copy-done.41), channel_id=1, source_target_pairs={{0,16},{16,0},{1,17},{17,1},{2,18},{18,2},{3,19},{19,3},{4,20},{20... | collective-permute-start | bytes 1572872 | tf_op jit(solution)/shard_map/ppermute | solution.py:69
  365.6 32.9 %collective-permute-start.66 = (bf16[1024,512]{1,0:T(8,128)(2,1)}, bf16[1024,512]{1,0:T(8,128)(2,1)}, u32[]{:S(2)}, u32[]{:S(2)}) collective-permute-start(bf16[1024,512]{1,0:T(8,128)(2,1)} %shard_map.292), channel_id=1, source_target_pairs={{0,16},{16,0},{1,17},{17,1},{2,18},{18,2},{3,19},{19,3},{4,20},{20... | collective-permute-start | bytes 3145736 | tf_op jit(solution)/shard_map/ppermute | solution.py:69
  365.9 13.4 %collective-permute-start.64 = (bf16[128,2048]{1,0:T(8,128)(2,1)S(1)}, bf16[128,2048]{1,0:T(8,128)(2,1)S(1)}, u32[]{:S(2)}, u32[]{:S(2)}) collective-permute-start(bf16[128,2048]{1,0:T(8,128)(2,1)S(1)} %get-tuple-element.357), channel_id=1, source_target_pairs={{0,4},{4,8},{8,12},{12,14},{14,10},{10,6},{6,2},{2,0},{1,5},{5,9},... | collective-permute-start | bytes 1572872 | tf_op jit(solution)/shard_map/ppermute | solution.py:69
  376.7 27.5 %collective-permute-start.59 = (bf16[128,2048]{1,0:T(8,128)(2,1)}, bf16[128,2048]{1,0:T(8,128)(2,1)}, u32[]{:S(2)}, u32[]{:S(2)}) collective-permute-start(bf16[128,2048]{1,0:T(8,128)(2,1)} %get-tuple-element.356), channel_id=1, source_target_pairs={{4,0},{8,4},{12,8},{14,12},{10,14},{6,10},{2,6},{0,2},{5,1},{9,5},... | collective-permute-start | bytes 1572872 | tf_op jit(solution)/shard_map/ppermute | solution.py:69
  379.5 42.8 %collective-permute-start.69 = (bf16[128,2048]{1,0:T(8,128)(2,1)S(1)}, bf16[128,2048]{1,0:T(8,128)(2,1)}, u32[]{:S(2)}, u32[]{:S(2)}) collective-permute-start(bf16[128,2048]{1,0:T(8,128)(2,1)S(1)} %fusion.3), channel_id=1, source_target_pairs={{0,4},{4,8},{8,12},{12,14},{14,10},{10,6},{6,2},{2,0},{1,5},{5,9},... | collective-permute-start | bytes 1572872 | tf_op jit(solution)/shard_map/ppermute | solution.py:69
  402.6 17.8 %collective-permute-start.82 = (bf16[512,256]{1,0:T(8,128)(2,1)}, bf16[512,256]{1,0:T(8,128)(2,1)S(1)}, u32[]{:S(2)}, u32[]{:S(2)}) collective-permute-start(bf16[512,256]{1,0:T(8,128)(2,1)} %dynamic-slice_convert_fusion), channel_id=1, source_target_pairs={{0,4},{2,6},{4,0},{6,2},{8,12},{10,14},{12,8},{14,10},{1,5},{3,7},... | collective-permute-start | bytes 786440 | tf_op jit(solution)/shard_map/ppermute | solution.py:69
  402.9 19.4 %collective-permute-start.65 = (bf16[1024,256]{1,0:T(8,128)(2,1)}, bf16[1024,256]{1,0:T(8,128)(2,1)}, u32[]{:S(2)}, u32[]{:S(2)}) collective-permute-start(bf16[1024,256]{1,0:T(8,128)(2,1)} %add_convert_fusion.3.refs_0_), channel_id=1, source_target_pairs={{4,0},{8,4},{12,8},{14,12},{10,14},{6,10},{2,6},{0,2},{5,1},{9,5},... | collective-permute-start | bytes 1572872 | tf_op jit(solution)/shard_map/ppermute | solution.py:69
  404.2 22.4 %collective-permute-start.68 = (bf16[1024,256]{1,0:T(8,128)(2,1)}, bf16[1024,256]{1,0:T(8,128)(2,1)}, u32[]{:S(2)}, u32[]{:S(2)}) collective-permute-start(bf16[1024,256]{1,0:T(8,128)(2,1)} %add_convert_fusion.3.refs_0_), channel_id=1, source_target_pairs={{0,4},{4,8},{8,12},{12,14},{14,10},{10,6},{6,2},{2,0},{1,5},{5,9},... | collective-permute-start | bytes 1572872 | tf_op jit(solution)/shard_map/ppermute | solution.py:69
  424.9 19.7 %collective-permute-start.71 = (bf16[128,2048]{1,0:T(8,128)(2,1)}, bf16[128,2048]{1,0:T(8,128)(2,1)S(1)}, u32[]{:S(2)}, u32[]{:S(2)}) collective-permute-start(bf16[128,2048]{1,0:T(8,128)(2,1)} %get-tuple-element.355), channel_id=1, source_target_pairs={{0,4},{4,8},{8,12},{12,14},{14,10},{10,6},{6,2},{2,0},{1,5},{5,9},... | collective-permute-start | bytes 1572872 | tf_op jit(solution)/shard_map/ppermute | solution.py:69
  426.6 18.0 %collective-permute-start.70 = (bf16[1024,256]{1,0:T(8,128)(2,1)}, bf16[1024,256]{1,0:T(8,128)(2,1)}, u32[]{:S(2)}, u32[]{:S(2)}) collective-permute-start(bf16[1024,256]{1,0:T(8,128)(2,1)} %collective-permute-done.65.refs_2_), channel_id=1, source_target_pairs={{4,0},{8,4},{12,8},{14,12},{10,14},{6,10},{2,6},{0,2},{5,1},{9,5},... | collective-permute-start | bytes 1572872 | tf_op jit(solution)/shard_map/ppermute | solution.py:69
  426.9 23.3 %collective-permute-start.63 = (bf16[128,2048]{1,0:T(8,128)(2,1)}, bf16[128,2048]{1,0:T(8,128)(2,1)}, u32[]{:S(2)}, u32[]{:S(2)}) collective-permute-start(bf16[128,2048]{1,0:T(8,128)(2,1)} %get-tuple-element.354), channel_id=1, source_target_pairs={{4,0},{8,4},{12,8},{14,12},{10,14},{6,10},{2,6},{0,2},{5,1},{9,5},... | collective-permute-start | bytes 1572872 | tf_op jit(solution)/shard_map/ppermute | solution.py:69
  428.3 23.8 %collective-permute-start.73 = (bf16[1024,256]{1,0:T(8,128)(2,1)}, bf16[1024,256]{1,0:T(8,128)(2,1)}, u32[]{:S(2)}, u32[]{:S(2)}) collective-permute-start(bf16[1024,256]{1,0:T(8,128)(2,1)} %collective-permute-done.68.refs_1_), channel_id=1, source_target_pairs={{0,4},{4,8},{8,12},{12,14},{14,10},{10,6},{6,2},{2,0},{1,5},{5,9},... | collective-permute-start | bytes 1572872 | tf_op jit(solution)/shard_map/ppermute | solution.py:69
  451.6 25.6 %collective-permute-start.72 = (bf16[128,2048]{1,0:T(8,128)(2,1)S(1)}, bf16[128,2048]{1,0:T(8,128)(2,1)S(1)}, u32[]{:S(2)}, u32[]{:S(2)}) collective-permute-start(bf16[128,2048]{1,0:T(8,128)(2,1)S(1)} %get-tuple-element.353), channel_id=1, source_target_pairs={{0,4},{4,8},{8,12},{12,14},{14,10},{10,6},{6,2},{2,0},{1,5},{5,9},... | collective-permute-start | bytes 1572872 | tf_op jit(solution)/shard_map/ppermute | solution.py:69
  452.1 24.3 %collective-permute-start.74 = (bf16[1024,256]{1,0:T(8,128)(2,1)}, bf16[1024,256]{1,0:T(8,128)(2,1)S(1)}, u32[]{:S(2)}, u32[]{:S(2)}) collective-permute-start(bf16[1024,256]{1,0:T(8,128)(2,1)} %collective-permute-done.70.refs_4_), channel_id=1, source_target_pairs={{4,0},{8,4},{12,8},{14,12},{10,14},{6,10},{2,6},{0,2},{5,1},{9,5},... | collective-permute-start | bytes 1572872 | tf_op jit(solution)/shard_map/ppermute | solution.py:69
  453.7 22.7 %collective-permute-start.67 = (bf16[128,2048]{1,0:T(8,128)(2,1)S(1)}, bf16[128,2048]{1,0:T(8,128)(2,1)S(1)}, u32[]{:S(2)}, u32[]{:S(2)}) collective-permute-start(bf16[128,2048]{1,0:T(8,128)(2,1)S(1)} %get-tuple-element.352), channel_id=1, source_target_pairs={{4,0},{8,4},{12,8},{14,12},{10,14},{6,10},{2,6},{0,2},{5,1},{9,5},... | collective-permute-start | bytes 1572872 | tf_op jit(solution)/shard_map/ppermute | solution.py:69
  454.1 22.3 %collective-permute-start.83 = (bf16[256,256]{1,0:T(8,128)(2,1)S(1)}, bf16[256,256]{1,0:T(8,128)(2,1)S(1)}, u32[]{:S(2)}, u32[]{:S(2)}) collective-permute-start(bf16[256,256]{1,0:T(8,128)(2,1)S(1)} %dynamic-slice_convert_fusion.1), channel_id=1, source_target_pairs={{0,2},{2,0},{4,6},{6,4},{8,10},{10,8},{12,14},{14,12},{1,3},{3,1},... | collective-permute-start | bytes 393224 | tf_op jit(solution)/shard_map/ppermute | solution.py:69
  480.4 44.6 %collective-permute-start.84 = (bf16[1280,256]{1,0:T(8,128)(2,1)S(1)}, bf16[1280,256]{1,0:T(8,128)(2,1)S(1)}, u32[]{:S(2)}, u32[]{:S(2)}) collective-permute-start(bf16[1280,256]{1,0:T(8,128)(2,1)S(1)} %pad_maximum_fusion.1.refs_0_), channel_id=1, source_target_pairs={{0,4},{4,8},{8,12},{12,14},{14,10},{10,6},{6,2},{2,0},{1,5},{5,9},... | collective-permute-start | bytes 1966088 | tf_op jit(solution)/shard_map/ppermute | solution.py:69
  480.4 44.9 %collective-permute-start.85 = (bf16[1280,256]{1,0:T(8,128)(2,1)S(1)}, bf16[1280,256]{1,0:T(8,128)(2,1)S(1)}, u32[]{:S(2)}, u32[]{:S(2)}) collective-permute-start(bf16[1280,256]{1,0:T(8,128)(2,1)S(1)} %pad_maximum_fusion.1.refs_0_), channel_id=1, source_target_pairs={{4,0},{8,4},{12,8},{14,12},{10,14},{6,10},{2,6},{0,2},{5,1},{9,5},... | collective-permute-start | bytes 1966088 | tf_op jit(solution)/shard_map/ppermute | solution.py:69
  482.5 33.4 %collective-permute-start.86 = (bf16[1024,256]{1,0:T(8,128)(2,1)}, bf16[1024,256]{1,0:T(8,128)(2,1)S(1)}, u32[]{:S(2)}, u32[]{:S(2)}) collective-permute-start(bf16[1024,256]{1,0:T(8,128)(2,1)} %collective-permute-done.73.refs_3_), channel_id=1, source_target_pairs={{0,4},{4,8},{8,12},{12,14},{14,10},{10,6},{6,2},{2,0},{1,5},{5,9},... | collective-permute-start | bytes 1572872 | tf_op jit(solution)/shard_map/ppermute | solution.py:69
  482.5 20.1 %collective-permute-start.78 = (f32[4352]{0:T(1024)S(1)}, f32[4352]{0:T(1024)S(1)}, u32[]{:S(2)}, u32[]{:S(2)}) collective-permute-start(f32[4352]{0:T(1024)S(1)} %fusion.32), channel_id=1, source_target_pairs={{0,4},{2,6},{4,0},{6,2},{8,12},{10,14},{12,8},{14,10},{1,5},{3,7},... | collective-permute-start | bytes 52232 | tf_op jit(solution)/shard_map/ppermute | solution.py:69
  502.6 15.9 %collective-permute-start.79 = (f32[4352]{0:T(1024)S(1)}, f32[4352]{0:T(1024)S(1)}, u32[]{:S(2)}, u32[]{:S(2)}) collective-permute-start(f32[4352]{0:T(1024)S(1)} %add.296), channel_id=1, source_target_pairs={{0,8},{2,10},{4,12},{6,14},{8,0},{10,2},{12,4},{14,6},{1,9},{3,11}... | collective-permute-start | bytes 52232 | tf_op jit(solution)/shard_map/ppermute | solution.py:69
  515.9 9.4 %collective-permute-start.87 = (bf16[512,256]{1,0:T(8,128)(2,1)S(1)}, bf16[512,256]{1,0:T(8,128)(2,1)S(1)}, u32[]{:S(2)}, u32[]{:S(2)}) collective-permute-start(bf16[512,256]{1,0:T(8,128)(2,1)S(1)} %slice.229), channel_id=1, source_target_pairs={{0,4},{4,8},{8,12},{12,14},{14,10},{10,6},{6,2},{2,0},{1,5},{5,9},... | collective-permute-start | bytes 786440 | tf_op jit(solution)/shard_map/ppermute | solution.py:69
  523.7 21.7 %collective-permute-start.76 = (f32[64,2048]{1,0:T(8,128)S(1)}, f32[64,2048]{1,0:T(8,128)S(1)}, u32[]{:S(2)}, u32[]{:S(2)}) collective-permute-start(f32[64,2048]{1,0:T(8,128)S(1)} %get-tuple-element.370), channel_id=1, source_target_pairs={{0,1},{1,0},{2,3},{3,2},{4,5},{5,4},{6,7},{7,6},{8,9},{9,8},{10,11... | collective-permute-start | bytes 1572872 | tf_op jit(solution)/shard_map/ppermute | solution.py:69
  525.0 19.5 %collective-permute-start.75 = (bf16[64,2048]{1,0:T(8,128)(2,1)S(1)}, bf16[64,2048]{1,0:T(8,128)(2,1)S(1)}, u32[]{:S(2)}, u32[]{:S(2)}) collective-permute-start(bf16[64,2048]{1,0:T(8,128)(2,1)S(1)} %get-tuple-element.371), channel_id=1, source_target_pairs={{0,1},{1,0},{2,3},{3,2},{4,5},{5,4},{6,7},{7,6},{8,9},{9,8},{10,11... | collective-permute-start | bytes 786440 | tf_op jit(solution)/shard_map/ppermute | solution.py:69
  525.4 21.1 %collective-permute-start.89 = (bf16[1280,256]{1,0:T(8,128)(2,1)S(1)}, bf16[1280,256]{1,0:T(8,128)(2,1)S(1)}, u32[]{:S(2)}, u32[]{:S(2)}) collective-permute-start(bf16[1280,256]{1,0:T(8,128)(2,1)S(1)} %collective-permute-done.84.refs_1_), channel_id=1, source_target_pairs={{0,4},{4,8},{8,12},{12,14},{14,10},{10,6},{6,2},{2,0},{1,5},{5,9},... | collective-permute-start | bytes 1966088 | tf_op jit(solution)/shard_map/ppermute | solution.py:69
  530.6 15.9 %collective-permute-start.91 = (f32[1024,128]{1,0:T(8,128)}, f32[1024,128]{1,0:T(8,128)S(1)}, u32[]{:S(2)}, u32[]{:S(2)}) collective-permute-start(f32[1024,128]{1,0:T(8,128)} %shard_map.298), channel_id=1, source_target_pairs={{0,16},{16,0},{1,17},{17,1},{2,18},{18,2},{3,19},{19,3},{4,20},{20... | collective-permute-start | bytes 1572872 | tf_op jit(solution)/shard_map/ppermute | solution.py:69
  532.4 16.4 %collective-permute-start.90 = (bf16[1280,256]{1,0:T(8,128)(2,1)S(1)}, bf16[1280,256]{1,0:T(8,128)(2,1)S(1)}, u32[]{:S(2)}, u32[]{:S(2)}) collective-permute-start(bf16[1280,256]{1,0:T(8,128)(2,1)S(1)} %collective-permute-done.85.refs_2_), channel_id=1, source_target_pairs={{4,0},{8,4},{12,8},{14,12},{10,14},{6,10},{2,6},{0,2},{5,1},{9,5},... | collective-permute-start | bytes 1966088 | tf_op jit(solution)/shard_map/ppermute | solution.py:69
  548.8 16.9 %collective-permute-start.92 = (bf16[1280,256]{1,0:T(8,128)(2,1)S(1)}, bf16[1280,256]{1,0:T(8,128)(2,1)S(1)}, u32[]{:S(2)}, u32[]{:S(2)}) collective-permute-start(bf16[1280,256]{1,0:T(8,128)(2,1)S(1)} %collective-permute-done.89.refs_3_), channel_id=1, source_target_pairs={{0,4},{4,8},{8,12},{12,14},{14,10},{10,6},{6,2},{2,0},{1,5},{5,9},... | collective-permute-start | bytes 1966088 | tf_op jit(solution)/shard_map/ppermute | solution.py:69
  549.5 16.2 %collective-permute-start.93 = (bf16[1280,256]{1,0:T(8,128)(2,1)S(1)}, bf16[1280,256]{1,0:T(8,128)(2,1)S(1)}, u32[]{:S(2)}, u32[]{:S(2)}) collective-permute-start(bf16[1280,256]{1,0:T(8,128)(2,1)S(1)} %collective-permute-done.90.refs_4_), channel_id=1, source_target_pairs={{4,0},{8,4},{12,8},{14,12},{10,14},{6,10},{2,6},{0,2},{5,1},{9,5},... | collective-permute-start | bytes 1966088 | tf_op jit(solution)/shard_map/ppermute | solution.py:69
  565.7 25.0 %collective-permute-start.94 = (bf16[640,256]{1,0:T(8,128)(2,1)S(1)}, bf16[640,256]{1,0:T(8,128)(2,1)S(1)}, u32[]{:S(2)}, u32[]{:S(2)}) collective-permute-start(bf16[640,256]{1,0:T(8,128)(2,1)S(1)} %slice.231), channel_id=1, source_target_pairs={{0,4},{4,8},{8,12},{12,14},{14,10},{10,6},{6,2},{2,0},{1,5},{5,9},... | collective-permute-start | bytes 983048 | tf_op jit(solution)/shard_map/ppermute | solution.py:69
  566.5 24.2 %collective-permute-start.95 = (bf16[640,256]{1,0:T(8,128)(2,1)S(1)}, bf16[640,256]{1,0:T(8,128)(2,1)S(1)}, u32[]{:S(2)}, u32[]{:S(2)}) collective-permute-start(bf16[640,256]{1,0:T(8,128)(2,1)S(1)} %slice.232), channel_id=1, source_target_pairs={{4,0},{8,4},{12,8},{14,12},{10,14},{6,10},{2,6},{0,2},{5,1},{9,5},... | collective-permute-start | bytes 983048 | tf_op jit(solution)/shard_map/ppermute | solution.py:69
  (81 other events, 652.9 us)

commit v3 on v2

--- a/solution.py
+++ b/solution.py
@@ -91,33 +91,11 @@
         return (mine, self.swap_halves(mine)), found
 
     def scatter(self, mine, other, hook=None):
-        mine = mine.astype(F32) + self.swap_halves(other).astype(F32)
-        mine = mine.astype(BF16).reshape(self.owners, -1, mine.shape[-1])
-
-        def block(offset):
-            return mine[self.slot[offset]].astype(F32)
-
-        total = block(0)
-        ahead = mine[self.slot[self.ahead]]
-        behind = mine[self.slot[-self.behind]] if self.behind else None
+        fold = Fold(self, mine, other)
         for step in range(self.ahead):
-            done = None if hook is None else hook(step, ahead)
-            offset = self.ahead - 1 - step
-            ahead = self.send(ahead, self.forward)
-            if done is not None:
-                ahead = after(ahead, done)
-            if offset:
-                ahead = (ahead.astype(F32) + block(offset)).astype(BF16)
-            offset = self.behind - 1 - step
-            if offset >= 0:
-                behind = self.send(behind, self.backward)
-                if done is not None:
-                    behind = after(behind, done)
-                if offset:
-                    behind = (behind.astype(F32) + block(-offset)).astype(BF16)
-        if self.behind:
-            total = total + behind.astype(F32)
-        return total + ahead.astype(F32)
+            done = None if hook is None else hook(step, fold.ahead)
+            fold.step(None, done)
+        return fold.result()
 
     def own_rows(self, values):
         rows = values.shape[0] // 2
@@ -202,6 +180,44 @@
         if self.count <= ring.behind:
             self.behind = ring.send(self.behind, ring.backward)
             self.found.append(self.behind)
+
+
+class Fold:
+    def __init__(self, ring, mine, other):
+        mine = mine.astype(F32) + ring.swap_halves(other).astype(F32)
+        self.ring = ring
+        self.mine = mine.astype(BF16).reshape(ring.owners, -1, mine.shape[-1])
+        self.ahead = self.mine[ring.slot[ring.ahead]]
+        self.behind = self.mine[ring.slot[-ring.behind]] if ring.behind else None
+        self.count = 0
+
+    def block(self, offset):
+        return self.mine[self.ring.slot[offset]].astype(F32)
+
+    def step(self, signal=None, done=None):
+        ring = self.ring
+        self.count += 1
+        if signal is not None:
+            self.ahead = after(self.ahead, signal)
+        offset = ring.ahead - self.count
+        self.ahead = ring.send(self.ahead, ring.forward)
+        if done is not None:
+            self.ahead = after(self.ahead, done)
+        if offset:
+            self.ahead = (self.ahead.astype(F32) + self.block(offset)).astype(BF16)
+        offset = ring.behind - self.count
+        if offset >= 0:
+            if signal is not None:
+                self.behind = after(self.behind, signal)
+            self.behind = ring.send(self.behind, ring.backward)
+            if done is not None:
+                self.behind = after(self.behind, done)
+            if offset:
+                self.behind = (self.behind.astype(F32) + self.block(-offset)).astype(BF16)
+
+    def result(self):
+        total = self.block(0) + self.ahead.astype(F32)
+        return total if self.behind is None else total + self.behind.astype(F32)
 
 
 def pad_lanes(values):
@@ -378,8 +394,7 @@
     lo_ref,
     *refs,
 ):
-    w_refs, refs = refs[:parts], refs[parts:]
-    layer_refs, (rm_ref, ro_ref, gains_ref, pm_ref, po_ref, dk_ref, dv_ref) = refs[:-7], refs[-7:]
+    w_refs, (rm_ref, ro_ref, gains_ref, pm_ref, po_ref, dk_ref, dv_ref) = refs[:parts], refs[parts:]
     dim = qg_ref.shape[1]
     cols = heads * dim
     scale = dim ** (-0.5)
@@ -425,16 +440,6 @@
             q_raw_grad, part = norm_back(q_grad, rows, raw_ref[rows, cut], qg_ref[...])
             q_part = q_part + part
             rg_ref[here, cut] = q_raw_grad.astype(BF16)
-    own = pm_ref.shape[1] // 2
-    for out_ref, part_refs in (
-        (pm_ref, layer_refs[: len(layer_refs) // 2]),
-        (po_ref, layer_refs[len(layer_refs) // 2 :]),
-    ):
-        block = 0
-        for part_ref in part_refs:
-            for start in range(0, part_ref.shape[0], own):
-                out_ref[block, own:, :] = part_ref[start : start + own, :]
-                block += 1
     for (_, start, row), rg_ref, ref in zip(
         row_blocks(bm_ref, bo_ref),
         (rm_ref, rm_ref, ro_ref, ro_ref),
@@ -448,15 +453,12 @@
         rg_ref[here, cols + dim :] = dv_ref[:, rows].T.astype(BF16)
         for spot, w_ref in spots(at_ref, w_refs):
             part = contract_cols(rg_ref[here, :], w_ref[:, : cols + 2 * dim]).astype(BF16)
-            for i in range(ROW_BLOCK // own):
-                ref[start // own + i, :own, spot] = part[i * own : (i + 1) * own, :]
+            ref[here, spot] = part
     gains_ref[0:1, :] = q_part
     gains_ref[1:2, :] = k_part
 
 
-def attend_back(
-    at, branch, weights, layer, own, cosine, sine, q_gain, k_gain, position, limit, saved
-):
+def attend_back(at, branch, weights, cosine, sine, q_gain, k_gain, position, limit, saved):
     half = branch[0].shape[0]
     dim = q_gain.shape[1]
     width = sum(w.shape[0] for w in weights)
@@ -465,17 +467,17 @@
     return call(
         functools.partial(attend_back_kernel, cols // dim, len(weights)),
         18.5,
-        in_specs=[smem_spec()] + [whole_spec()] * (14 + len(weights) + len(layer)),
+        in_specs=[smem_spec()] + [whole_spec()] * (14 + len(weights)),
         out_specs=[whole_spec()] * 5,
         out_shape=[
             raw_half,
             raw_half,
             jax.ShapeDtypeStruct((2, dim), F32),
-            jax.ShapeDtypeStruct((half // own, 2 * own, width), BF16),
-            jax.ShapeDtypeStruct((half // own, 2 * own, width), BF16),
+            jax.ShapeDtypeStruct((half, width), BF16),
+            jax.ShapeDtypeStruct((half, width), BF16),
         ],
         scratch_shapes=[VMEM((dim, 2 * half), F32), VMEM((dim, 2 * half), F32)],
-    )(at, *branch, cosine, sine, q_gain, k_gain, position, limit, *saved, *weights, *layer)
+    )(at, *branch, cosine, sine, q_gain, k_gain, position, limit, *saved, *weights)
 
 
 def routed_gates(x_ref, g_ref, router_ref, picks):
@@ -680,7 +682,7 @@
     )
     return call(
         functools.partial(other_experts_kernel, picks),
-        14,
+        15,
         grid_spec=pltpu.PrefetchScalarGridSpec(
             num_scalar_prefetch=1,
             grid=(count,),
@@ -722,12 +724,15 @@
 TOKEN = (8, LANES)
 
 
+def product_sum(lefts, rights):
+    parts = [contract_rows(left[...], right[...]) for left, right in zip(lefts, rights)]
+    return parts[0] + parts[1]
+
+
 def gate_up_grad_kernel(x0, x1, x2, x3, d0, d1, d2, d3, *refs):
     gate_ref, up_ref, token_ref = refs[-3:]
     each = gate_ref.shape[2]
-    total = (contract_rows(x0[...], d0[...]) + contract_rows(x1[...], d1[...])) + (
-        contract_rows(x2[...], d2[...]) + contract_rows(x3[...], d3[...])
-    )
+    total = product_sum((x0, x1), (d0, d1)) + product_sum((x2, x3), (d2, d3))
     gate_ref[0] = total[:, :each]
     up_ref[0] = total[:, each:]
     sign(token_ref)
@@ -737,31 +742,28 @@
     half, width = own[0].shape
     each = own_hidden.shape[1] // 2 // count
     wide = 2 * ROW_BLOCK
-    left = pl.BlockSpec((half, wide), lambda i: (0, i))
     part = pl.BlockSpec((1, wide, each), lambda i: (expert, i, 0))
     rights, specs = in_halves(own_hidden, (half, 2 * each), expert)
-    more, more_specs = in_halves(other_hidden, (half, 2 * each), expert)
+    single = pl.Buffered(1)
     return call(
         gate_up_grad_kernel,
         11.7,
         grid=(width // wide,),
-        in_specs=[left] * 4
+        in_specs=[pl.BlockSpec((half, wide), lambda i: (0, i))] * 4
         + specs
-        + more_specs
+        + [pl.BlockSpec((half, 2 * each), lambda i: (0, expert), pipeline_mode=single)] * 2
         + [pl.BlockSpec(memory_space=pl.ANY)] * len(totals),
         out_specs=[part] * 2 + [pl.BlockSpec(TOKEN, lambda i: (0, 0))],
         out_shape=[jax.ShapeDtypeStruct((count, width, each), F32)] * 2
         + [jax.ShapeDtypeStruct(TOKEN, F32)],
         input_output_aliases={8: 0, 9: 1} if totals else {},
-    )(*own, *other, *rights, *more, *totals)
-
-
-def down_grad_kernel(count, w0, w1, w2, w3, g0, g1, g2, g3, *refs):
+    )(*own, *other, *rights, *other_hidden, *totals)
+
+
+def down_grad_kernel(count, w0, w1, g0, g1, g2, g3, w2, w3, *refs):
     out_ref, token_ref = refs[-2:]
     each = out_ref.shape[1]
-    total = (contract_rows(w0[...], g0[...]) + contract_rows(w1[...], g1[...])) + (
-        contract_rows(w2[...], g2[...]) + contract_rows(w3[...], g3[...])
-    )
+    total = product_sum((w0, w1), (g0, g1)) + product_sum((w2, w3), (g2, g3))
     for i in range(count):
         out_ref[i] = total[i * each : (i + 1) * each, :]
     sign(token_ref)
@@ -776,14 +778,14 @@
     right = pl.BlockSpec((half, wide), lambda i: (0, part * steps + i))
     place = pl.BlockSpec((count, each, wide), lambda i: (0, 0, part * steps + i))
     lefts, specs = in_halves(own_weighted, (half, hidden), 0)
-    more, more_specs = in_halves(other_weighted, (half, hidden), 0)
+    single = pl.Buffered(1)
     return call(
         functools.partial(down_grad_kernel, count),
         9.7,
         grid=(steps,),
         in_specs=specs
-        + more_specs
         + [right] * 4
+        + [pl.BlockSpec((half, hidden), lambda i: (0, 0), pipeline_mode=single)] * 2
         + [pl.BlockSpec(memory_space=pl.ANY)] * len(totals),
         out_specs=[place, pl.BlockSpec(TOKEN, lambda i: (0, 0))],
         out_shape=[
@@ -791,76 +793,86 @@
             jax.ShapeDtypeStruct(TOKEN, F32),
         ],
         input_output_aliases={8: 0} if totals else {},
-    )(*lefts, *more, *own, *other, *totals)
-
-
-def join_kernel(*refs):
-    out_ref = refs[-1]
-    own = refs[0].shape[0]
-    for i, ref in enumerate(refs[:-1]):
-        out_ref[i * own : (i + 1) * own, :] = ref[...]
-
-
-def join_rows(blocks):
-    own, width = blocks[0].shape
-    return call(
-        join_kernel,
-        2,
-        in_specs=[whole_spec()] * len(blocks),
-        out_specs=whole_spec(),
-        out_shape=jax.ShapeDtypeStruct((own * len(blocks), width), blocks[0].dtype),
-    )(*blocks)
+    )(*lefts, *own, *other, *other_weighted, *totals)
 
 
 def place_wide_kernel(owners_ref, *refs):
-    blocks, out_ref = refs[:-1], refs[-1]
+    blocks, (last_top, last_low), out_ref = refs[:-3], refs[-3:-1], refs[-1]
     cols = blocks[0].shape[1]
-    start = 0
-    slot = 0
-    for ref in blocks:
-        rows = ref.shape[0]
+
+    def put(slot, ref):
         at = pl.multiple_of(owners_ref[slot] * cols, cols)
-        out_ref[start : start + rows, pl.ds(at, cols)] = ref[...].astype(F32)
-        start += rows
-        if start == out_ref.shape[0]:
-            start, slot = 0, slot + 1
+        out_ref[:, pl.ds(at, cols)] = ref[...].astype(F32)
+
+    for slot, ref in enumerate(blocks):
+        put(slot, ref)
+    top = pl.program_id(0) < pl.num_programs(0) // 2
+
+    @pl.when(top)
+    def _():
+        put(len(blocks), last_top)
+
+    @pl.when(jnp.logical_not(top))
+    def _():
+        put(len(blocks), last_low)
 
 
 def place_wide(owners_by_slot, blocks, width):
-    share = blocks[0].shape[0]
+    share, cols = blocks[0].shape
+    steps = share // ROW_BLOCK
+    half = steps // 2
     return call(
         place_wide_kernel,
-        6,
-        in_specs=[smem_spec()] + [whole_spec()] * len(blocks),
-        out_specs=whole_spec(),
+        4,
+        grid=(steps,),
+        in_specs=[smem_spec()]
+        + [pl.BlockSpec((ROW_BLOCK, cols), lambda i: (i, 0))] * (len(blocks) - 2)
+        + [
+            pl.BlockSpec((ROW_BLOCK, cols), lambda i: (jnp.minimum(i, half - 1), 0)),
+            pl.BlockSpec((ROW_BLOCK, cols), lambda i: (jnp.maximum(i - half, 0), 0)),
+        ],
+        out_specs=pl.BlockSpec((ROW_BLOCK, width), lambda i: (i, 0)),
         out_shape=jax.ShapeDtypeStruct((share, width), F32),
     )(owners_by_slot, *blocks)
 
 
 def place_kernel(sharers, owners_ref, *refs):
-    blocks, (q_ref, k_ref, v_ref) = refs[:-3], refs[-3:]
-    share = q_ref.shape[0]
+    count = (len(refs) - 3) // 2
+    blocks, lows, (q_ref, k_ref, v_ref) = refs[:count], refs[count:-3], refs[-3:]
     cols = blocks[0].shape[1]
     dim = cols // 2
+    for i, ref in enumerate(blocks):
+        at = pl.multiple_of(owners_ref[i] * cols, cols)
+        q_ref[:, pl.ds(at, cols)] = ref[...].astype(F32)
+
+    @pl.when(pl.program_id(0) == 0)
+    def _():
+        for i, ref in enumerate(lows):
+            rows = ref.shape[0]
+            down = pl.multiple_of(owners_ref[i] % sharers * rows, rows)
+            right = pl.multiple_of(owners_ref[i] // sharers * dim, dim)
+            k_ref[pl.ds(down, rows), pl.ds(right, dim)] = ref[:, :dim].astype(F32)
+            v_ref[pl.ds(down, rows), pl.ds(right, dim)] = ref[:, dim:].astype(F32)
+
+
+def place_blocks(owners_by_slot, blocks, shapes, sharers):
+    share, width = shapes[0]
+    cols = blocks[0].shape[1]
     rows = blocks[0].shape[0] - share
-    for i, ref in enumerate(blocks):
-        owner = owners_ref[i]
-        at = pl.multiple_of(owner * cols, cols)
-        q_ref[:, pl.ds(at, cols)] = ref[:share, :].astype(F32)
-        down = pl.multiple_of(owner % sharers * rows, rows)
-        right = pl.multiple_of(owner // sharers * dim, dim)
-        k_ref[pl.ds(down, rows), pl.ds(right, dim)] = ref[share:, :dim].astype(F32)
-        v_ref[pl.ds(down, rows), pl.ds(right, dim)] = ref[share:, dim:].astype(F32)
-
-
-def place_blocks(owners_by_slot, blocks, shapes, sharers):
     return call(
         functools.partial(place_kernel, sharers),
-        7,
-        in_specs=[pl.BlockSpec(memory_space=SMEM)] + [whole_spec()] * len(blocks),
-        out_specs=[whole_spec()] * 3,
+        5,
+        grid=(share // ROW_BLOCK,),
+        in_specs=[smem_spec()]
+        + [pl.BlockSpec((ROW_BLOCK, cols), lambda i: (i, 0))] * len(blocks)
+        + [pl.BlockSpec((rows, cols), lambda i: (share // rows, 0))] * len(blocks),
+        out_specs=[
+            pl.BlockSpec((ROW_BLOCK, width), lambda i: (i, 0)),
+            pl.BlockSpec(shapes[1], lambda i: (0, 0)),
+            pl.BlockSpec(shapes[2], lambda i: (0, 0)),
+        ],
         out_shape=[jax.ShapeDtypeStruct(shape, F32) for shape in shapes],
-    )(owners_by_slot, *blocks)
+    )(owners_by_slot, *blocks, *blocks)
 
 
 def place_last_kernel(share, owner_ref, top_in, low_in, q_any, k_any, v_any, q_ref, k_ref, v_ref):
@@ -1043,7 +1055,15 @@
 
     if pair:
         made["grads"], back_mine = after((their_grads, back_mine), their_grads)
-    back_sum = ring.scatter(back_mine, back_other)
+    layer_parts = []
+
+    def back_hook(step, signal):
+        layer_parts.append(layer_part(step, ring.ahead, after(weighted, signal), down))
+        if step == 1 and pair:
+            made["routed"] = (made["grads"], ring.swap_halves(made["grads"]))
+        return tuple([layer_parts[-1]] + across(signal))
+
+    back_sum = ring.scatter(back_mine, back_other, back_hook)
 
     gate_grad_rows = sum(
         back_sum[:, width + i * expert_count : width + (i + 1) * expert_count] for i in range(4)
@@ -1060,52 +1080,59 @@
         second_normed_grad
         - mid_normed * jnp.mean(second_normed_grad * mid_normed, axis=-1, keepdims=True)
     )
-    layer_parts = []
-
-    def layer_hook(step, walk):
-        layer_parts.append(layer_part(step, ring.ahead, after(weighted, walk.ahead), down))
-        return tuple([layer_parts[-1]] + across(walk.ahead))
+    made["theirs"], made["other"] = [], []
+
+    def other_hook(step, walk):
+        done = []
+        if step == 0:
+            middle = len(layer_parts) // 2
+            halves = [
+                jnp.concatenate(part, axis=0) for part in (layer_parts[:middle], layer_parts[middle:])
+            ]
+            made["layer"] = Fold(ring, *after(halves, walk.ahead))
+            made["layer"].step()
+        else:
+            made["layer"].step(walk.ahead)
+        done.append(made["layer"].ahead)
+        if pair and step == 0:
+            rows = jnp.concatenate(after(their_rows, walk.ahead), axis=0)
+            made["theirs"] = [rows, ring.swap_halves(rows)]
+            done.append(rows)
+        if pair and step % 2:
+            x, g = after((made["theirs"][step // 2], made["routed"][step // 2]), walk.ahead)
+            made["other"].append(
+                other_experts(first, x, g, gate_proj, up_proj, down_proj, router_lanes, picks)
+            )
+            done += made["other"][-1]
+        return tuple(done)
 
     branch, _ = ring.gather(
-        jnp.concatenate([mid_grad.astype(BF16), pad_lanes(logit_grad)], axis=1), layer_hook
-    )
-    middle = len(layer_parts) // 2
+        jnp.concatenate([mid_grad.astype(BF16), pad_lanes(logit_grad)], axis=1), other_hook
+    )
+    layer_out = ring.join_halves((residual + made["layer"].result()).astype(BF16))
 
     attn_halves = (attn_mine, attn_other)
     out_theirs, out_arrived = ring.send_share(branch, attn_halves, width, BF16)
-    raw_mine, raw_other, head_gains, both_mine, both_other = attend_back(
+    raw_mine, raw_other, head_gains, in_mine, in_other = attend_back(
         at,
         branch if out_theirs is None else after(branch, out_theirs),
         weights,
-        layer_parts,
-        half_rows,
         *tables,
         (raw, query_low, key_low, value_low, lse_mine, lse_other),
     )
     raw_halves = (raw_mine, raw_other)
     qkv_theirs, qkv_arrived = ring.send_share(attn_in, raw_halves, width, BF16)
 
-
-    made["other"] = []
-
-    def other_piece(half, signal):
-        x, g = after([part[half] for part in made["theirs"]], signal)
-        made["other"].append(
-            other_experts(first, x, g, gate_proj, up_proj, down_proj, router_lanes, picks)
-        )
-        return made["other"][-1]
-
     totals = {"gate_up": [], "down": []}
 
     def last_piece(n, signal):
-        x, g = made["theirs"]
         if n < experts_here:
             *totals["gate_up"], token = gate_up_grad(
                 n,
                 experts_here,
                 totals["gate_up"],
                 after(ffn_in, signal),
-                x,
+                made["theirs"],
                 hidden,
                 [part[1] for part in made["other"]],
             )
@@ -1118,7 +1145,7 @@
                 after(weighted, signal),
                 [part[0] for part in made["other"]],
                 grads,
-                g,
+                made["routed"],
             )
         return [token]
 
@@ -1127,27 +1154,19 @@
         if step == 0:
             share = ring.add_share(out_arrived, after(branch, signal), attn_halves, width)
             made["out_walk"] = ring.walk(share.astype(BF16), True)
-            if pair:
-                theirs = [join_rows(after(their_rows, signal)), after(made["grads"], signal)]
-                made["theirs"] = [(part, ring.swap_halves(part)) for part in theirs]
-                done += made["theirs"]
         else:
             made["out_walk"].step(signal)
         done.append(made["out_walk"].found[-1])
         if step == 1:
             made["qkv"] = ring.add_share(qkv_arrived, after(attn_in, signal), raw_halves, width)
             done.append(made["qkv"])
-        if step in (1, 2) and pair:
-            done += other_piece(step - 1, signal)
-        if step == 3 and pair:
-            done += last_piece(0, signal)
+        if pair and step < 3:
+            done += last_piece(step, signal)
         return tuple(done)
 
     if qkv_theirs is not None:
-        both_mine = after(both_mine, qkv_theirs)
-    both_sum = ring.scatter(both_mine, both_other, in_hook)
-    attn_in_grad = both_sum[:half_rows]
-    layer_out = ring.join_halves((residual + both_sum[half_rows:]).astype(BF16))
+        in_mine = after(in_mine, qkv_theirs)
+    attn_in_grad = ring.scatter(in_mine, in_other, in_hook)
     qkv_share = made["qkv"]
     first_normed_grad = attn_in_grad * attn_gain
     tokens_grad = mid_grad + first_inverse * (
@@ -1183,8 +1202,8 @@
         if step == 0:
             made["out_walk"].step(signal)
             done += made["out_walk"].found[-1]
-        if pair:
-            done += last_piece(step + 1, signal)
+        if pair and step < 2:
+            done += last_piece(step + 3, signal)
         if step == 1:
             _, arrived = ring.send_share(after(ffn_in, signal), branch, width, F32, LANES, lanes_at)
             made["router_arrived"] = arrived
@@ -1194,7 +1213,7 @@
                 made["router_arrived"], after(ffn_in, signal), branch, width, LANES, lanes_at
             )
             done.append(made["router_grad"])
-        if step == last:
+        if step == 2:
             found = made["out_walk"].found
             made["out_grad"] = place_wide(
                 ring.owners_by_slot,

time: 601 us -> 578 us (0.962)
  waiting for transfers between devices: 184 us -> 151 us
  local copies, waits for them, and re-layouts: 38.2 us -> 44.8 us
    ppermute x96 -> x104, waiting for transfers between devices: 184 us -> 151 us  [send(): return lax.ppermute(values, axis, pairs)]
    ppermute x96 -> x104, starting transfers between devices: 96.5 us -> 101 us  [send(): return lax.ppermute(values, axis, pairs)]
    unnamed x130 -> x131, local copies, waits for them, and re-layouts: 24.1 us -> 28.3 us
    pallas_call x8 -> x7, Pallas kernels: 81.8 us -> 79.1 us  [the longest x3 34.8 us: gate_up_grad(): call(gate_up_grad_kernel, 11.7, grid=(width // wide,), in_specs=[pl.Block...]
    convert_element_type x12 -> x16, other arithmetic: 15.2 us -> 17.8 us  [the longest x4 8.55 us: __init__(): self.mine = mine.astype(BF16).reshape(ring.owners, -1, mine.shape[-1])]
  transfers between devices with their start and end apart: 96 -> 104, of which waited for: 45 -> 43; matrix products, arithmetic and copies ran while one was open for 9% -> 12% of each run, Pallas kernels for 32% -> 33%
where the time goes in v3:
time: 578 us; the launch traced here: 572 us
  Pallas kernels  228 us (39%)
  waiting for transfers between devices  151 us (26%)
  starting transfers between devices  101 us (17%)
  other arithmetic  45.3 us (8%)
  local copies, waits for them, and re-layouts  44.8 us (8%)
    ppermute x104, waiting for transfers between devices, send(): return lax.ppermute(values, axis, pairs)  151 us
    ppermute x104, starting transfers between devices, send(): return lax.ppermute(values, axis, pairs)  101 us
    pallas_call x1, Pallas kernels, experts(): call(functools.partial(experts_kernel, picks, expert_count), 41, grid_spe...  41.3 us
    pallas_call x3, Pallas kernels, gate_up_grad(): call(gate_up_grad_kernel, 11.7, grid=(width // wide,), in_specs=[pl.Block...  34.8 us
    pallas_call x2, Pallas kernels, other_experts(): call(functools.partial(other_experts_kernel, picks), 15, grid_spec=pltpu....  31.1 us
    unnamed x131, local copies, waits for them, and re-layouts  28.3 us
    pallas_call x6, Pallas kernels, transposed_product(): call(transposed_product_kernel, 4, grid_spec=pltpu.PrefetchScalarGridSpec...  21.7 us
    pallas_call x4, Pallas kernels, layer_part(): call(layer_kernel, 4, grid=(1,), in_specs=[pl.BlockSpec((rows // parts, h...  20.1 us
  transfers between devices with their start and end apart: 104, of which 43 were waited for; matrix products, arithmetic and copies ran while one was open for 12% of the time, Pallas kernels for 33%

profile of v3, /device:TPU:0, one launch (start us, length us, event | category | flops | bytes accessed | tf_op | source)
XLA Modules:
  0.0 571.6 jit_solution(1900794747760175977)
XLA Ops:
  3.2 2.9 collective-permute-start.7
  11.8 3.4 shard_map.281.refs_0_
  16.7 2.0 collective-permute-start.2
  21.9 4.9 collective-permute-done.2
  52.1 2.6 collective-permute-done.13
  61.9 3.0 collective-permute-done.17
  67.7 3.8 collective-permute-done.18.xo_ref.ao_ref
  71.5 7.3 %shard_map.282 = (f32[1024,384]{1,0:T(8,128)}, bf16[1024,256]{1,0:T(8,128)(2,1)}, bf16[1024,128]{1,0:T(8,128)(2,1)}, bf16[1024,128]{1,0:T(8,128)(2,1)}) custom-call(s32[2]{0:T(128)} %pad_add_fusion.at_ref, bf16[512,2048]{1,0:T(8,128)(2,1)} %constant_dynamic-update-slice_fusion.5.xm_ref.am_ref, bf16[512,2048]{1,0:T(8,128)(2,1)} %collective-permute-done.18.xo_ref.ao_ref, ...), custom_call_target="tpu_custom_call" | custom-call | flops 8049999872 | tf_op jit(solution)/shard_map/pallas_call | solution.py:321
  78.8 7.1 %shard_map.284 = (bf16[512,256]{1,0:T(8,128)(2,1)}, f32[2,512,1]{2,1,0:T(8,128)}, bf16[512,2048]{1,0:T(8,128)(2,1)}) custom-call(s32[2]{0:T(128)} %pad_add_fusion.at_ref, s32[1,1024]{1,0:T(1,128)} %and_select_fusion.1.pos_ref, s32[1024,1]{1,0:T(8,128)} %fusion.14.lim_ref, bf16[1024,256]{1,0:T(8,128)(2,1)} %get-tuple-element.184.ql_ref, ...), custom_call_target="tpu_custom_call" | custom-call | flops 7474999808 | tf_op jit(solution)/shard_map/pallas_call | solution.py:364
  88.5 7.1 %shard_map.283 = (bf16[512,256]{1,0:T(8,128)(2,1)}, f32[2,512,1]{2,1,0:T(8,128)}, bf16[512,2048]{1,0:T(8,128)(2,1)}) custom-call(s32[2]{0:T(128)} %pad_add_fusion.at_ref, s32[1,1024]{1,0:T(1,128)} %and_select_fusion.1.pos_ref, s32[1024,1]{1,0:T(8,128)} %fusion.14.lim_ref, bf16[1024,256]{1,0:T(8,128)(2,1)} %get-tuple-element.184.ql_ref, ...), custom_call_target="tpu_custom_call" | custom-call | flops 7474999808 | tf_op jit(solution)/shard_map/pallas_call | solution.py:364
  97.0 3.0 add_convert_fusion.3
  104.0 5.3 collective-permute-done.20
  115.9 6.1 %collective-permute-done.21 = bf16[64,2048]{1,0:T(8,128)(2,1)} collective-permute-done((bf16[64,2048]{1,0:T(8,128)(2,1)}, bf16[64,2048]{1,0:T(8,128)(2,1)}, u32[]{:S(2)}, u32[]{:S(2)}) %collective-permute-start.21) | collective-permute-done | bytes 262176 | tf_op jit(solution)/shard_map/ppermute | solution.py:69
  126.0 5.0 collective-permute-done.26
  133.9 3.6 collective-permute-done.24
  137.5 2.3 collective-permute-done.27
  143.2 3.7 collective-permute-done.29
  149.3 5.5 collective-permute-done.31
  157.2 7.5 %collective-permute-done.32 = bf16[64,2048]{1,0:T(8,128)(2,1)S(1)} collective-permute-done((bf16[64,2048]{1,0:T(8,128)(2,1)S(1)}, bf16[64,2048]{1,0:T(8,128)(2,1)S(1)}, u32[]{:S(2)}, u32[]{:S(2)}) %collective-permute-start.32) | collective-permute-done | bytes 262176 | tf_op jit(solution)/shard_map/ppermute | solution.py:69
  166.2 4.9 collective-permute-done.34
  172.6 2.9 collective-permute-done.35.xo_ref.x1.ao_ref
  175.5 41.3 %shard_map.285 = (bf16[1024,1152]{1,0:T(8,128)(2,1)}, bf16[1024,2304]{1,0:T(8,128)(2,1)}, f32[1024,128]{1,0:T(8,128)}, bf16[512,2176]{1,0:T(8,128)(2,1)}, bf16[512,2176]{1,0:T(8,128)(2,1)}) custom-call(s32[2]{0:T(128)} %pad_add_fusion.2.first_ref, bf16[512,2048]{1,0:T(8,128)(2,1)} %copy-done.6, bf16[512,2048]{1,0:T(8,128)(2,1)} %collective-permute-done.35.xo_ref.x1.ao_ref, ...), custom_call_target="tpu_custom_call" | custom-call | flops 47149998080 | tf_op jit(solution)/shard_map/pallas_call | solution.py:582
  217.0 6.0 %collective-permute-done.37.g_ref.g2 = bf16[512,2176]{1,0:T(8,128)(2,1)} collective-permute-done((bf16[512,2176]{1,0:T(8,128)(2,1)}, bf16[512,2176]{1,0:T(8,128)(2,1)}, u32[]{:S(2)}, u32[]{:S(2)}) %collective-permute-start.37) | collective-permute-done | bytes 2228256 | tf_op jit(solution)/shard_map/ppermute | solution.py:69
  223.0 2.3 add_convert_fusion
  228.1 5.0 shard_map.286
  234.0 4.9 collective-permute-done.40
  241.1 5.0 shard_map.287
  246.6 4.9 collective-permute-done.42
  256.3 5.0 shard_map.288
  262.8 2.5 collective-permute-done.44
  270.7 5.0 shard_map.289
  277.2 3.2 collective-permute-done.46
  296.9 4.3 collective-permute-done.51
  305.0 15.5 %shard_map.290 = (bf16[512,1152]{1,0:T(8,128)(2,1)}, bf16[512,2304]{1,0:T(8,128)(2,1)}) custom-call(s32[2]{0:T(128)} %pad_add_fusion.2.first_ref, bf16[512,2048]{1,0:T(8,128)(2,1)} %constant_dynamic-update-slice_fusion.33.x_ref.x2, bf16[512,2176]{1,0:T(8,128)(2,1)} %collective-permute-done.37.g_ref.g2, bf16[3,2048,384]{2,1,0:T(8,128)(2,1)} %wg_ref.5, ...), custom_call_target="tpu_custom_call" | custom-call | flops 17250000896 | tf_op jit(solution)/shard_map/pallas_call | solution.py:683
  322.2 9.0 %collective-permute-done.56 = bf16[64,2176]{1,0:T(8,128)(2,1)S(1)} collective-permute-done((bf16[64,2176]{1,0:T(8,128)(2,1)S(1)}, bf16[64,2176]{1,0:T(8,128)(2,1)S(1)}, u32[]{:S(2)}, u32[]{:S(2)}) %collective-permute-start.56) | collective-permute-done | bytes 278560 | tf_op jit(solution)/shard_map/ppermute | solution.py:69
  335.5 6.1 %collective-permute-done.57 = bf16[64,2048]{1,0:T(8,128)(2,1)S(1)} collective-permute-done((bf16[64,2048]{1,0:T(8,128)(2,1)S(1)}, bf16[64,2048]{1,0:T(8,128)(2,1)S(1)}, u32[]{:S(2)}, u32[]{:S(2)}) %collective-permute-start.57) | collective-permute-done | bytes 262176 | tf_op jit(solution)/shard_map/ppermute | solution.py:69
  345.1 15.6 %shard_map.291 = (bf16[512,1152]{1,0:T(8,128)(2,1)}, bf16[512,2304]{1,0:T(8,128)(2,1)}) custom-call(s32[2]{0:T(128)} %pad_add_fusion.2.first_ref, bf16[512,2048]{1,0:T(8,128)(2,1)} %collective-permute-done.66.x_ref.x3, bf16[512,2176]{1,0:T(8,128)(2,1)} %collective-permute-done.67.g_ref.g3, bf16[3,2048,384]{2,1,0:T(8,128)(2,1)} %wg_ref.5, ...), custom_call_target="tpu_custom_call" | custom-call | flops 17250000896 | tf_op jit(solution)/shard_map/pallas_call | solution.py:683
  360.9 4.3 collective-permute-done.68.ao_ref.bo_ref
  366.6 3.3 shard_map.292
  369.9 18.1 %shard_map.293 = (bf16[512,512]{1,0:T(8,128)(2,1)}, bf16[512,512]{1,0:T(8,128)(2,1)}, f32[2,128]{1,0:T(2,128)}, bf16[512,2048]{1,0:T(8,128)(2,1)}, bf16[512,2048]{1,0:T(8,128)(2,1)}) custom-call(s32[2]{0:T(128)} %pad_add_fusion.at_ref, bf16[512,2176]{1,0:T(8,128)(2,1)} %copy-done.35, bf16[512,2176]{1,0:T(8,128)(2,1)} %copy-done.41, ...), custom_call_target="tpu_custom_call" | custom-call | flops 21275000832 | tf_op jit(solution)/shard_map/pallas_call | solution.py:467
  391.0 4.2 shard_map.294
  396.7 2.5 add_convert_fusion.1
  402.0 11.6 %shard_map.296 = (f32[3,2048,384]{2,1,0:T(8,128)}, f32[3,2048,384]{2,1,0:T(8,128)}, f32[8,128]{1,0:T(8,128)}) custom-call(bf16[512,2048]{1,0:T(8,128)(2,1)} %copy-done.6, bf16[512,2048]{1,0:T(8,128)(2,1)} %collective-permute-done.35.xo_ref.x1.ao_ref, bf16[512,2048]{1,0:T(8,128)(2,1)} %constant_dynamic-update-slice_fusion.33.x_ref.x2, ...), custom_call_target="tpu_custom_call" | custom-call | flops 13454999552 | tf_op jit(solution)/shard_map/pallas_call | solution.py:748
  413.5 3.4 shard_map.295
  420.5 11.6 %shard_map.298 = (f32[3,2048,384]{2,1,0:T(8,128)}, f32[3,2048,384]{2,1,0:T(8,128)}, f32[8,128]{1,0:T(8,128)}) custom-call(bf16[512,2048]{1,0:T(8,128)(2,1)} %copy-done.6, bf16[512,2048]{1,0:T(8,128)(2,1)} %collective-permute-done.35.xo_ref.x1.ao_ref, ...), custom_call_target="tpu_custom_call", output_to_operand_aliasing={{0}: (8, {}), {1}: (9, {})} | custom-call | flops 13454999552 | tf_op jit(solution)/shard_map/pallas_call | solution.py:748
  432.1 4.5 shard_map.297
  438.3 2.2 convert_add_fusion
  446.3 5.2 collective-permute-done.76.refs_1_
  453.5 11.6 %shard_map.299 = (f32[3,2048,384]{2,1,0:T(8,128)}, f32[3,2048,384]{2,1,0:T(8,128)}, f32[8,128]{1,0:T(8,128)}) custom-call(bf16[512,2048]{1,0:T(8,128)(2,1)} %copy-done.6, bf16[512,2048]{1,0:T(8,128)(2,1)} %collective-permute-done.35.xo_ref.x1.ao_ref, ...), custom_call_target="tpu_custom_call", output_to_operand_aliasing={{0}: (8, {}), {1}: (9, {})} | custom-call | flops 13454999552 | tf_op jit(solution)/shard_map/pallas_call | solution.py:748
  471.7 2.8 collective-permute-done.90
  475.4 10.4 %collective-permute-done.83 = bf16[64,2048]{1,0:T(8,128)(2,1)S(1)} collective-permute-done((bf16[64,2048]{1,0:T(8,128)(2,1)S(1)}, bf16[64,2048]{1,0:T(8,128)(2,1)S(1)}, u32[]{:S(2)}, u32[]{:S(2)}) %collective-permute-start.83) | collective-permute-done | bytes 262176 | tf_op jit(solution)/shard_map/ppermute | solution.py:69
  486.3 4.0 collective-permute-done.85
  495.7 9.7 %shard_map.305 = (f32[3,384,2048]{2,1,0:T(8,128)}, f32[8,128]{1,0:T(8,128)}) custom-call(bf16[1024,1152]{1,0:T(8,128)(2,1)} %get-tuple-element.313.w_ref.w0.w1, bf16[1024,1152]{1,0:T(8,128)(2,1)} %get-tuple-element.313.w_ref.w0.w1, bf16[512,2176]{1,0:T(8,128)(2,1)} %constant_dynamic-update-slice_fusion.25.gm_ref.g0, ...), custom_call_target="tpu_custom_call" | custom-call | flops 11155000320 | tf_op jit(solution)/shard_map/pallas_call | solution.py:782
  507.1 3.3 collective-permute-done.88
  512.4 2.4 collective-permute-done.94.refs_5_
  518.1 3.2 collective-permute-done.96.refs_8_
  523.7 3.2 shard_map.300
  528.2 9.7 %shard_map.306 = (f32[3,384,2048]{2,1,0:T(8,128)}, f32[8,128]{1,0:T(8,128)}) custom-call(bf16[1024,1152]{1,0:T(8,128)(2,1)} %get-tuple-element.313.w_ref.w0.w1, bf16[1024,1152]{1,0:T(8,128)(2,1)} %get-tuple-element.313.w_ref.w0.w1, bf16[512,2176]{1,0:T(8,128)(2,1)} %constant_dynamic-update-slice_fusion.25.gm_ref.g0, ...), custom_call_target="tpu_custom_call", output_to_operand_aliasing={{0}: (8, {})} | custom-call | flops 11155000320 | tf_op jit(solution)/shard_map/pallas_call | solution.py:782
  540.9 3.3 collective-permute-start.100
  544.2 3.2 shard_map.301
  549.3 6.0 %shard_map.302 = f32[1024,2048]{1,0:T(8,128)} custom-call(s32[8]{0:T(128)} %get-tuple-element.437.owners_ref, bf16[1024,256]{1,0:T(8,128)(2,1)} %copy-done.15, bf16[1024,256]{1,0:T(8,128)(2,1)} %collective-permute-done.76.refs_1_, bf16[1024,256]{1,0:T(8,128)(2,1)} %collective-permute-done.73.refs_2_, bf16[1024,256]{1,0:T(8,128)(2,1)} %collective-permute-done.79.refs_3_, ...), custom_call_target="tpu_custom_call" | custom-call | flops 4600000000 | tf_op jit(solution)/shard_map/pallas_call | solution.py:824
  555.3 3.0 collective-permute-done.101.refs_6_.refs_13_
  560.5 7.2 %shard_map.303 = (f32[1024,2048]{1,0:T(8,128)}, f32[1024,256]{1,0:T(8,128)}, f32[1024,256]{1,0:T(8,128)}) custom-call(s32[8]{0:T(128)} %get-tuple-element.437.owners_ref, bf16[1280,256]{1,0:T(8,128)(2,1)} %pad_maximum_fusion.3.refs_0_.refs_7_, bf16[1280,256]{1,0:T(8,128)(2,1)} %collective-permute-done.92.refs_1_.refs_8_, ...), custom_call_target="tpu_custom_call" | custom-call | flops 5750000128 | tf_op jit(solution)/shard_map/pallas_call | solution.py:862
  568.5 2.8 shard_map.304
  (421 shorter events, 183.2 us)
Async XLA Ops:
  3.2 27.5 %collective-permute-start.7 = (bf16[64,2176]{1,0:T(8,128)(2,1)S(1)}, bf16[64,2176]{1,0:T(8,128)(2,1)S(1)}, u32[]{:S(2)}, u32[]{:S(2)}) collective-permute-start(bf16[64,2176]{1,0:T(8,128)(2,1)S(1)} %get-tuple-element.425), channel_id=1, source_target_pairs={{4,0},{8,4},{12,8},{14,12},{10,14},{6,10},{2,6},{0,2},{5,1},{9,5},... | collective-permute-start | bytes 835592 | tf_op jit(solution)/shard_map/ppermute | solution.py:69
  6.2 15.7 %collective-permute-start.3 = (bf16[64,2176]{1,0:T(8,128)(2,1)S(1)}, bf16[64,2176]{1,0:T(8,128)(2,1)}, u32[]{:S(2)}, u32[]{:S(2)}) collective-permute-start(bf16[64,2176]{1,0:T(8,128)(2,1)S(1)} %get-tuple-element.425), channel_id=1, source_target_pairs={{0,4},{4,8},{8,12},{12,14},{14,10},{10,6},{6,2},{2,0},{1,5},{5,9},... | collective-permute-start | bytes 835592 | tf_op jit(solution)/shard_map/ppermute | solution.py:69
  9.2 12.7 %collective-permute-start.1 = (bf16[64,2048]{1,0:T(8,128)(2,1)S(1)}, bf16[64,2048]{1,0:T(8,128)(2,1)}, u32[]{:S(2)}, u32[]{:S(2)}) collective-permute-start(bf16[64,2048]{1,0:T(8,128)(2,1)S(1)} %get-tuple-element.383), channel_id=1, source_target_pairs={{4,0},{8,4},{12,8},{14,12},{10,14},{6,10},{2,6},{0,2},{5,1},{9,5},... | collective-permute-start | bytes 786440 | tf_op jit(solution)/shard_map/ppermute | solution.py:69
  16.7 10.1 %collective-permute-start.2 = (bf16[256,768]{1,0:T(8,128)(2,1)S(1)}, bf16[256,768]{1,0:T(8,128)(2,1)S(1)}, u32[]{:S(2)}, u32[]{:S(2)}) collective-permute-start(bf16[256,768]{1,0:T(8,128)(2,1)S(1)} %get-tuple-element.415), channel_id=1, source_target_pairs={{0,16},{16,0},{1,17},{17,1},{2,18},{18,2},{3,19},{19,3},{4,20},{20... | collective-permute-start | bytes 1179656 | tf_op jit(solution)/shard_map/ppermute | solution.py:69
  29.0 13.5 %collective-permute-start.4 = (bf16[64,2048]{1,0:T(8,128)(2,1)}, bf16[64,2048]{1,0:T(8,128)(2,1)}, u32[]{:S(2)}, u32[]{:S(2)}) collective-permute-start(bf16[64,2048]{1,0:T(8,128)(2,1)} %collective-permute-done), channel_id=1, source_target_pairs={{0,4},{4,8},{8,12},{12,14},{14,10},{10,6},{6,2},{2,0},{1,5},{5,9},... | collective-permute-start | bytes 786440 | tf_op jit(solution)/shard_map/ppermute | solution.py:69
  31.6 10.9 %collective-permute-start.5 = (bf16[64,2048]{1,0:T(8,128)(2,1)}, bf16[64,2048]{1,0:T(8,128)(2,1)}, u32[]{:S(2)}, u32[]{:S(2)}) collective-permute-start(bf16[64,2048]{1,0:T(8,128)(2,1)} %collective-permute-done.1), channel_id=1, source_target_pairs={{4,0},{8,4},{12,8},{14,12},{10,14},{6,10},{2,6},{0,2},{5,1},{9,5},... | collective-permute-start | bytes 786440 | tf_op jit(solution)/shard_map/ppermute | solution.py:69
  31.9 10.5 %collective-permute-start.8 = (bf16[64,2176]{1,0:T(8,128)(2,1)}, bf16[64,2176]{1,0:T(8,128)(2,1)}, u32[]{:S(2)}, u32[]{:S(2)}) collective-permute-start(bf16[64,2176]{1,0:T(8,128)(2,1)} %collective-permute-done.3), channel_id=1, source_target_pairs={{0,4},{4,8},{8,12},{12,14},{14,10},{10,6},{6,2},{2,0},{1,5},{5,9},... | collective-permute-start | bytes 835592 | tf_op jit(solution)/shard_map/ppermute | solution.py:69
  33.7 10.4 %collective-permute-start.12 = (bf16[64,2176]{1,0:T(8,128)(2,1)S(1)}, bf16[64,2176]{1,0:T(8,128)(2,1)}, u32[]{:S(2)}, u32[]{:S(2)}) collective-permute-start(bf16[64,2176]{1,0:T(8,128)(2,1)S(1)} %collective-permute-done.7), channel_id=1, source_target_pairs={{4,0},{8,4},{12,8},{14,12},{10,14},{6,10},{2,6},{0,2},{5,1},{9,5},... | collective-permute-start | bytes 835592 | tf_op jit(solution)/shard_map/ppermute | solution.py:69
  42.5 9.7 %collective-permute-start.9 = (bf16[64,2048]{1,0:T(8,128)(2,1)}, bf16[64,2048]{1,0:T(8,128)(2,1)S(1)}, u32[]{:S(2)}, u32[]{:S(2)}) collective-permute-start(bf16[64,2048]{1,0:T(8,128)(2,1)} %collective-permute-done.4), channel_id=1, source_target_pairs={{0,4},{4,8},{8,12},{12,14},{14,10},{10,6},{6,2},{2,0},{1,5},{5,9},... | collective-permute-start | bytes 786440 | tf_op jit(solution)/shard_map/ppermute | solution.py:69
  44.6 10.2 %collective-permute-start.13 = (bf16[64,2176]{1,0:T(8,128)(2,1)}, bf16[64,2176]{1,0:T(8,128)(2,1)S(1)}, u32[]{:S(2)}, u32[]{:S(2)}) collective-permute-start(bf16[64,2176]{1,0:T(8,128)(2,1)} %collective-permute-done.8), channel_id=1, source_target_pairs={{0,4},{4,8},{8,12},{12,14},{14,10},{10,6},{6,2},{2,0},{1,5},{5,9},... | collective-permute-start | bytes 835592 | tf_op jit(solution)/shard_map/ppermute | solution.py:69
  46.1 10.6 %collective-permute-start.16 = (bf16[64,2176]{1,0:T(8,128)(2,1)}, bf16[64,2176]{1,0:T(8,128)(2,1)S(1)}, u32[]{:S(2)}, u32[]{:S(2)}) collective-permute-start(bf16[64,2176]{1,0:T(8,128)(2,1)} %collective-permute-done.12), channel_id=1, source_target_pairs={{4,0},{8,4},{12,8},{14,12},{10,14},{6,10},{2,6},{0,2},{5,1},{9,5},... | collective-permute-start | bytes 835592 | tf_op jit(solution)/shard_map/ppermute | solution.py:69
  85.9 9.7 %collective-permute-start.19 = (bf16[512,2048]{1,0:T(8,128)(2,1)}, bf16[512,2048]{1,0:T(8,128)(2,1)S(1)}, u32[]{:S(2)}, u32[]{:S(2)}) collective-permute-start(bf16[512,2048]{1,0:T(8,128)(2,1)} %get-tuple-element.188), channel_id=1, source_target_pairs={{0,1},{1,0},{2,3},{3,2},{4,5},{5,4},{6,7},{7,6},{8,9},{9,8},{10,11... | collective-permute-start | bytes 6291464 | tf_op jit(solution)/shard_map/ppermute | solution.py:69
  112.6 9.5 %collective-permute-start.25 = (bf16[64,2048]{1,0:T(8,128)(2,1)}, bf16[64,2048]{1,0:T(8,128)(2,1)}, u32[]{:S(2)}, u32[]{:S(2)}) collective-permute-start(bf16[64,2048]{1,0:T(8,128)(2,1)} %get-tuple-element.411), channel_id=1, source_target_pairs={{4,0},{8,4},{12,8},{14,12},{10,14},{6,10},{2,6},{0,2},{5,1},{9,5},... | collective-permute-start | bytes 786440 | tf_op jit(solution)/shard_map/ppermute | solution.py:69
  143.2 29.4 %collective-permute-start.36 = (bf16[512,2176]{1,0:T(8,128)(2,1)}, bf16[512,2176]{1,0:T(8,128)(2,1)}, u32[]{:S(2)}, u32[]{:S(2)}) collective-permute-start(bf16[512,2176]{1,0:T(8,128)(2,1)} %constant_dynamic-update-slice_fusion.25.gm_ref.g0), channel_id=1, source_target_pairs={{0,1},{1,0},{2,3},{3,2},{4,5},{5,4},{6,7},{7,6},{8,9},{9,8},{10,11... | collective-permute-start | bytes 6684680 | tf_op jit(solution)/shard_map/ppermute | solution.py:69
  154.7 11.5 %collective-permute-start.33 = (bf16[64,2048]{1,0:T(8,128)(2,1)S(1)}, bf16[64,2048]{1,0:T(8,128)(2,1)S(1)}, u32[]{:S(2)}, u32[]{:S(2)}) collective-permute-start(bf16[64,2048]{1,0:T(8,128)(2,1)S(1)} %collective-permute-done.31), channel_id=1, source_target_pairs={{4,0},{8,4},{12,8},{14,12},{10,14},{6,10},{2,6},{0,2},{5,1},{9,5},... | collective-permute-start | bytes 786440 | tf_op jit(solution)/shard_map/ppermute | solution.py:69
  155.6 9.1 %collective-permute-start.32 = (bf16[64,2048]{1,0:T(8,128)(2,1)S(1)}, bf16[64,2048]{1,0:T(8,128)(2,1)S(1)}, u32[]{:S(2)}, u32[]{:S(2)}) collective-permute-start(bf16[64,2048]{1,0:T(8,128)(2,1)S(1)} %collective-permute-done.30), channel_id=1, source_target_pairs={{0,4},{4,8},{8,12},{12,14},{14,10},{10,6},{6,2},{2,0},{1,5},{5,9},... | collective-permute-start | bytes 786440 | tf_op jit(solution)/shard_map/ppermute | solution.py:69
  172.0 51.0 %collective-permute-start.37 = (bf16[512,2176]{1,0:T(8,128)(2,1)}, bf16[512,2176]{1,0:T(8,128)(2,1)}, u32[]{:S(2)}, u32[]{:S(2)}) collective-permute-start(bf16[512,2176]{1,0:T(8,128)(2,1)} %constant_dynamic-update-slice_fusion.25.gm_ref.g0), channel_id=1, source_target_pairs={{0,16},{16,0},{1,17},{17,1},{2,18},{18,2},{3,19},{19,3},{4,20},{20... | collective-permute-start | bytes 6684680 | tf_op jit(solution)/shard_map/ppermute | solution.py:69
  225.4 13.5 %collective-permute-start.40 = (bf16[128,2048]{1,0:T(8,128)(2,1)S(1)}, bf16[128,2048]{1,0:T(8,128)(2,1)S(1)}, u32[]{:S(2)}, u32[]{:S(2)}) collective-permute-start(bf16[128,2048]{1,0:T(8,128)(2,1)S(1)} %slice.229), channel_id=1, source_target_pairs={{0,16},{16,0},{1,17},{17,1},{2,18},{18,2},{3,19},{19,3},{4,20},{20... | collective-permute-start | bytes 1572872 | tf_op jit(solution)/shard_map/ppermute | solution.py:69
  227.6 13.6 %collective-permute-start.47 = (bf16[64,2176]{1,0:T(8,128)(2,1)S(1)}, bf16[64,2176]{1,0:T(8,128)(2,1)S(1)}, u32[]{:S(2)}, u32[]{:S(2)}) collective-permute-start(bf16[64,2176]{1,0:T(8,128)(2,1)S(1)} %get-tuple-element.392), channel_id=1, source_target_pairs={{4,0},{8,4},{12,8},{14,12},{10,14},{6,10},{2,6},{0,2},{5,1},{9,5},... | collective-permute-start | bytes 835592 | tf_op jit(solution)/shard_map/ppermute | solution.py:69
  239.0 12.5 %collective-permute-start.42 = (bf16[128,2048]{1,0:T(8,128)(2,1)S(1)}, bf16[128,2048]{1,0:T(8,128)(2,1)S(1)}, u32[]{:S(2)}, u32[]{:S(2)}) collective-permute-start(bf16[128,2048]{1,0:T(8,128)(2,1)S(1)} %slice.231), channel_id=1, source_target_pairs={{0,16},{16,0},{1,17},{17,1},{2,18},{18,2},{3,19},{19,3},{4,20},{20... | collective-permute-start | bytes 1572872 | tf_op jit(solution)/shard_map/ppermute | solution.py:69
  253.4 11.9 %collective-permute-start.44 = (bf16[128,2048]{1,0:T(8,128)(2,1)}, bf16[128,2048]{1,0:T(8,128)(2,1)}, u32[]{:S(2)}, u32[]{:S(2)}) collective-permute-start(bf16[128,2048]{1,0:T(8,128)(2,1)} %slice.233), channel_id=1, source_target_pairs={{0,16},{16,0},{1,17},{17,1},{2,18},{18,2},{3,19},{19,3},{4,20},{20... | collective-permute-start | bytes 1572872 | tf_op jit(solution)/shard_map/ppermute | solution.py:69
  267.2 10.0 %collective-permute-start.45 = (bf16[64,2176]{1,0:T(8,128)(2,1)}, bf16[64,2176]{1,0:T(8,128)(2,1)}, u32[]{:S(2)}, u32[]{:S(2)}) collective-permute-start(bf16[64,2176]{1,0:T(8,128)(2,1)} %get-tuple-element.389), channel_id=1, source_target_pairs={{0,4},{4,8},{8,12},{12,14},{14,10},{10,6},{6,2},{2,0},{1,5},{5,9},... | collective-permute-start | bytes 835592 | tf_op jit(solution)/shard_map/ppermute | solution.py:69
  270.1 10.3 %collective-permute-start.46 = (bf16[128,2048]{1,0:T(8,128)(2,1)}, bf16[128,2048]{1,0:T(8,128)(2,1)S(1)}, u32[]{:S(2)}, u32[]{:S(2)}) collective-permute-start(bf16[128,2048]{1,0:T(8,128)(2,1)} %slice.236), channel_id=1, source_target_pairs={{0,16},{16,0},{1,17},{17,1},{2,18},{18,2},{3,19},{19,3},{4,20},{20... | collective-permute-start | bytes 1572872 | tf_op jit(solution)/shard_map/ppermute | solution.py:69
  284.7 58.7 %collective-permute-start.67 = (bf16[512,2176]{1,0:T(8,128)(2,1)}, bf16[512,2176]{1,0:T(8,128)(2,1)}, u32[]{:S(2)}, u32[]{:S(2)}) collective-permute-start(bf16[512,2176]{1,0:T(8,128)(2,1)} %collective-permute-done.37.g_ref.g2), channel_id=1, source_target_pairs={{0,1},{1,0},{2,3},{3,2},{4,5},{5,4},{6,7},{7,6},{8,9},{9,8},{10,11... | collective-permute-start | bytes 6684680 | tf_op jit(solution)/shard_map/ppermute | solution.py:69
  285.2 16.1 %collective-permute-start.53 = (bf16[64,2176]{1,0:T(8,128)(2,1)S(1)}, bf16[64,2176]{1,0:T(8,128)(2,1)S(1)}, u32[]{:S(2)}, u32[]{:S(2)}) collective-permute-start(bf16[64,2176]{1,0:T(8,128)(2,1)S(1)} %get-tuple-element.423), channel_id=1, source_target_pairs={{4,0},{8,4},{12,8},{14,12},{10,14},{6,10},{2,6},{0,2},{5,1},{9,5},... | collective-permute-start | bytes 835592 | tf_op jit(solution)/shard_map/ppermute | solution.py:69
  291.6 51.7 %collective-permute-start.66 = (bf16[512,2048]{1,0:T(8,128)(2,1)}, bf16[512,2048]{1,0:T(8,128)(2,1)}, u32[]{:S(2)}, u32[]{:S(2)}) collective-permute-start(bf16[512,2048]{1,0:T(8,128)(2,1)} %constant_dynamic-update-slice_fusion.33.x_ref.x2), channel_id=1, source_target_pairs={{0,1},{1,0},{2,3},{3,2},{4,5},{5,4},{6,7},{7,6},{8,9},{9,8},{10,11... | collective-permute-start | bytes 6291464 | tf_op jit(solution)/shard_map/ppermute | solution.py:69
  295.3 26.0 %collective-permute-start.61 = (bf16[64,2048]{1,0:T(8,128)(2,1)S(1)}, bf16[64,2048]{1,0:T(8,128)(2,1)S(1)}, u32[]{:S(2)}, u32[]{:S(2)}) collective-permute-start(bf16[64,2048]{1,0:T(8,128)(2,1)S(1)} %get-tuple-element.405), channel_id=1, source_target_pairs={{4,0},{8,4},{12,8},{14,12},{10,14},{6,10},{2,6},{0,2},{5,1},{9,5},... | collective-permute-start | bytes 786440 | tf_op jit(solution)/shard_map/ppermute | solution.py:69
  301.3 29.9 %collective-permute-start.55 = (bf16[64,2176]{1,0:T(8,128)(2,1)S(1)}, bf16[64,2176]{1,0:T(8,128)(2,1)S(1)}, u32[]{:S(2)}, u32[]{:S(2)}) collective-permute-start(bf16[64,2176]{1,0:T(8,128)(2,1)S(1)} %collective-permute-done.52), channel_id=1, source_target_pairs={{0,4},{4,8},{8,12},{12,14},{14,10},{10,6},{6,2},{2,0},{1,5},{5,9},... | collective-permute-start | bytes 835592 | tf_op jit(solution)/shard_map/ppermute | solution.py:69
  303.3 18.6 %collective-permute-start.54 = (bf16[64,2048]{1,0:T(8,128)(2,1)S(1)}, bf16[64,2048]{1,0:T(8,128)(2,1)S(1)}, u32[]{:S(2)}, u32[]{:S(2)}) collective-permute-start(bf16[64,2048]{1,0:T(8,128)(2,1)S(1)} %add_convert_fusion.20), channel_id=1, source_target_pairs={{0,4},{4,8},{8,12},{12,14},{14,10},{10,6},{6,2},{2,0},{1,5},{5,9},... | collective-permute-start | bytes 786440 | tf_op jit(solution)/shard_map/ppermute | solution.py:69
  321.3 10.0 %collective-permute-start.56 = (bf16[64,2176]{1,0:T(8,128)(2,1)S(1)}, bf16[64,2176]{1,0:T(8,128)(2,1)S(1)}, u32[]{:S(2)}, u32[]{:S(2)}) collective-permute-start(bf16[64,2176]{1,0:T(8,128)(2,1)S(1)} %collective-permute-done.53), channel_id=1, source_target_pairs={{4,0},{8,4},{12,8},{14,12},{10,14},{6,10},{2,6},{0,2},{5,1},{9,5},... | collective-permute-start | bytes 835592 | tf_op jit(solution)/shard_map/ppermute | solution.py:69
  322.1 13.2 %collective-permute-start.62 = (bf16[64,2048]{1,0:T(8,128)(2,1)S(1)}, bf16[64,2048]{1,0:T(8,128)(2,1)S(1)}, u32[]{:S(2)}, u32[]{:S(2)}) collective-permute-start(bf16[64,2048]{1,0:T(8,128)(2,1)S(1)} %get-tuple-element.231), channel_id=1, source_target_pairs={{4,0},{8,4},{12,8},{14,12},{10,14},{6,10},{2,6},{0,2},{5,1},{9,5},... | collective-permute-start | bytes 786440 | tf_op jit(solution)/shard_map/ppermute | solution.py:69
  331.3 11.2 %collective-permute-start.58 = (bf16[64,2176]{1,0:T(8,128)(2,1)S(1)}, bf16[64,2176]{1,0:T(8,128)(2,1)S(1)}, u32[]{:S(2)}, u32[]{:S(2)}) collective-permute-start(bf16[64,2176]{1,0:T(8,128)(2,1)S(1)} %collective-permute-done.55), channel_id=1, source_target_pairs={{0,4},{4,8},{8,12},{12,14},{14,10},{10,6},{6,2},{2,0},{1,5},{5,9},... | collective-permute-start | bytes 835592 | tf_op jit(solution)/shard_map/ppermute | solution.py:69
  332.0 9.6 %collective-permute-start.57 = (bf16[64,2048]{1,0:T(8,128)(2,1)S(1)}, bf16[64,2048]{1,0:T(8,128)(2,1)S(1)}, u32[]{:S(2)}, u32[]{:S(2)}) collective-permute-start(bf16[64,2048]{1,0:T(8,128)(2,1)S(1)} %get-tuple-element.227), channel_id=1, source_target_pairs={{0,4},{4,8},{8,12},{12,14},{14,10},{10,6},{6,2},{2,0},{1,5},{5,9},... | collective-permute-start | bytes 786440 | tf_op jit(solution)/shard_map/ppermute | solution.py:69
  342.5 18.3 %collective-permute-start.65 = (bf16[64,2176]{1,0:T(8,128)(2,1)S(1)}, bf16[64,2176]{1,0:T(8,128)(2,1)S(1)}, u32[]{:S(2)}, u32[]{:S(2)}) collective-permute-start(bf16[64,2176]{1,0:T(8,128)(2,1)S(1)} %collective-permute-done.58), channel_id=1, source_target_pairs={{0,4},{4,8},{8,12},{12,14},{14,10},{10,6},{6,2},{2,0},{1,5},{5,9},... | collective-permute-start | bytes 835592 | tf_op jit(solution)/shard_map/ppermute | solution.py:69
  343.3 17.4 %collective-permute-start.60 = (bf16[64,2048]{1,0:T(8,128)(2,1)S(1)}, bf16[64,2048]{1,0:T(8,128)(2,1)S(1)}, u32[]{:S(2)}, u32[]{:S(2)}) collective-permute-start(bf16[64,2048]{1,0:T(8,128)(2,1)S(1)} %get-tuple-element.230), channel_id=1, source_target_pairs={{0,4},{4,8},{8,12},{12,14},{14,10},{10,6},{6,2},{2,0},{1,5},{5,9},... | collective-permute-start | bytes 786440 | tf_op jit(solution)/shard_map/ppermute | solution.py:69
  390.0 120.4 %collective-permute-start.63 = (bf16[64,2048]{1,0:T(8,128)(2,1)}, bf16[64,2048]{1,0:T(8,128)(2,1)}, u32[]{:S(2)}, u32[]{:S(2)}) collective-permute-start(bf16[64,2048]{1,0:T(8,128)(2,1)} %get-tuple-element.232), channel_id=1, source_target_pairs={{4,0},{8,4},{12,8},{14,12},{10,14},{6,10},{2,6},{0,2},{5,1},{9,5},... | collective-permute-start | bytes 786440 | tf_op jit(solution)/shard_map/ppermute | solution.py:69
  390.4 26.5 %collective-permute-start.71 = (bf16[1024,256]{1,0:T(8,128)(2,1)}, bf16[1024,256]{1,0:T(8,128)(2,1)S(1)}, u32[]{:S(2)}, u32[]{:S(2)}) collective-permute-start(bf16[1024,256]{1,0:T(8,128)(2,1)} %shard_map.292), channel_id=1, source_target_pairs={{0,16},{16,0},{1,17},{17,1},{2,18},{18,2},{3,19},{19,3},{4,20},{20... | collective-permute-start | bytes 1572872 | tf_op jit(solution)/shard_map/ppermute | solution.py:69
  395.3 41.3 %collective-permute-start.74 = (bf16[1024,512]{1,0:T(8,128)(2,1)}, bf16[1024,512]{1,0:T(8,128)(2,1)}, u32[]{:S(2)}, u32[]{:S(2)}) collective-permute-start(bf16[1024,512]{1,0:T(8,128)(2,1)} %shard_map.294), channel_id=1, source_target_pairs={{0,16},{16,0},{1,17},{17,1},{2,18},{18,2},{3,19},{19,3},{4,20},{20... | collective-permute-start | bytes 3145736 | tf_op jit(solution)/shard_map/ppermute | solution.py:69
  399.9 18.4 %collective-permute-start.70 = (bf16[64,2048]{1,0:T(8,128)(2,1)S(1)}, bf16[64,2048]{1,0:T(8,128)(2,1)S(1)}, u32[]{:S(2)}, u32[]{:S(2)}) collective-permute-start(bf16[64,2048]{1,0:T(8,128)(2,1)S(1)} %get-tuple-element.398), channel_id=1, source_target_pairs={{0,4},{4,8},{8,12},{12,14},{14,10},{10,6},{6,2},{2,0},{1,5},{5,9},... | collective-permute-start | bytes 786440 | tf_op jit(solution)/shard_map/ppermute | solution.py:69
  401.7 40.6 %collective-permute-start.81 = (bf16[64,2048]{1,0:T(8,128)(2,1)}, bf16[64,2048]{1,0:T(8,128)(2,1)}, u32[]{:S(2)}, u32[]{:S(2)}) collective-permute-start(bf16[64,2048]{1,0:T(8,128)(2,1)} %get-tuple-element.399), channel_id=1, source_target_pairs={{4,0},{8,4},{12,8},{14,12},{10,14},{6,10},{2,6},{0,2},{5,1},{9,5},... | collective-permute-start | bytes 786440 | tf_op jit(solution)/shard_map/ppermute | solution.py:69
  418.4 23.9 %collective-permute-start.72 = (bf16[64,2048]{1,0:T(8,128)(2,1)S(1)}, bf16[64,2048]{1,0:T(8,128)(2,1)}, u32[]{:S(2)}, u32[]{:S(2)}) collective-permute-start(bf16[64,2048]{1,0:T(8,128)(2,1)S(1)} %add_convert_fusion.14), channel_id=1, source_target_pairs={{0,4},{4,8},{8,12},{12,14},{14,10},{10,6},{6,2},{2,0},{1,5},{5,9},... | collective-permute-start | bytes 786440 | tf_op jit(solution)/shard_map/ppermute | solution.py:69
  420.2 22.1 %collective-permute-start.73 = (bf16[1024,256]{1,0:T(8,128)(2,1)S(1)}, bf16[1024,256]{1,0:T(8,128)(2,1)}, u32[]{:S(2)}, u32[]{:S(2)}) collective-permute-start(bf16[1024,256]{1,0:T(8,128)(2,1)S(1)} %add_convert_fusion.4.refs_0_), channel_id=1, source_target_pairs={{4,0},{8,4},{12,8},{14,12},{10,14},{6,10},{2,6},{0,2},{5,1},{9,5},... | collective-permute-start | bytes 1572872 | tf_op jit(solution)/shard_map/ppermute | solution.py:69
  436.5 15.0 %collective-permute-start.76 = (bf16[1024,256]{1,0:T(8,128)(2,1)S(1)}, bf16[1024,256]{1,0:T(8,128)(2,1)}, u32[]{:S(2)}, u32[]{:S(2)}) collective-permute-start(bf16[1024,256]{1,0:T(8,128)(2,1)S(1)} %add_convert_fusion.4.refs_0_), channel_id=1, source_target_pairs={{0,4},{4,8},{8,12},{12,14},{14,10},{10,6},{6,2},{2,0},{1,5},{5,9},... | collective-permute-start | bytes 1572872 | tf_op jit(solution)/shard_map/ppermute | solution.py:69
  444.2 22.8 %collective-permute-start.75 = (bf16[64,2048]{1,0:T(8,128)(2,1)}, bf16[64,2048]{1,0:T(8,128)(2,1)}, u32[]{:S(2)}, u32[]{:S(2)}) collective-permute-start(bf16[64,2048]{1,0:T(8,128)(2,1)} %get-tuple-element.396), channel_id=1, source_target_pairs={{0,4},{4,8},{8,12},{12,14},{14,10},{10,6},{6,2},{2,0},{1,5},{5,9},... | collective-permute-start | bytes 786440 | tf_op jit(solution)/shard_map/ppermute | solution.py:69
  444.6 20.6 %collective-permute-start.82 = (bf16[64,2048]{1,0:T(8,128)(2,1)}, bf16[64,2048]{1,0:T(8,128)(2,1)}, u32[]{:S(2)}, u32[]{:S(2)}) collective-permute-start(bf16[64,2048]{1,0:T(8,128)(2,1)} %get-tuple-element.397), channel_id=1, source_target_pairs={{4,0},{8,4},{12,8},{14,12},{10,14},{6,10},{2,6},{0,2},{5,1},{9,5},... | collective-permute-start | bytes 786440 | tf_op jit(solution)/shard_map/ppermute | solution.py:69
  451.5 15.5 %collective-permute-start.77 = (bf16[1024,256]{1,0:T(8,128)(2,1)}, bf16[1024,256]{1,0:T(8,128)(2,1)}, u32[]{:S(2)}, u32[]{:S(2)}) collective-permute-start(bf16[1024,256]{1,0:T(8,128)(2,1)} %collective-permute-done.73.refs_2_), channel_id=1, source_target_pairs={{4,0},{8,4},{12,8},{14,12},{10,14},{6,10},{2,6},{0,2},{5,1},{9,5},... | collective-permute-start | bytes 1572872 | tf_op jit(solution)/shard_map/ppermute | solution.py:69
  452.7 15.5 %collective-permute-start.79 = (bf16[1024,256]{1,0:T(8,128)(2,1)}, bf16[1024,256]{1,0:T(8,128)(2,1)}, u32[]{:S(2)}, u32[]{:S(2)}) collective-permute-start(bf16[1024,256]{1,0:T(8,128)(2,1)} %collective-permute-done.76.refs_1_), channel_id=1, source_target_pairs={{0,4},{4,8},{8,12},{12,14},{14,10},{10,6},{6,2},{2,0},{1,5},{5,9},... | collective-permute-start | bytes 1572872 | tf_op jit(solution)/shard_map/ppermute | solution.py:69
  465.2 9.3 %collective-permute-start.90 = (bf16[512,256]{1,0:T(8,128)(2,1)S(1)}, bf16[512,256]{1,0:T(8,128)(2,1)S(1)}, u32[]{:S(2)}, u32[]{:S(2)}) collective-permute-start(bf16[512,256]{1,0:T(8,128)(2,1)S(1)} %copy-done.22), channel_id=1, source_target_pairs={{0,4},{2,6},{4,0},{6,2},{8,12},{10,14},{12,8},{14,10},{1,5},{3,7},... | collective-permute-start | bytes 786440 | tf_op jit(solution)/shard_map/ppermute | solution.py:69
  468.2 17.6 %collective-permute-start.80 = (bf16[1024,256]{1,0:T(8,128)(2,1)}, bf16[1024,256]{1,0:T(8,128)(2,1)S(1)}, u32[]{:S(2)}, u32[]{:S(2)}) collective-permute-start(bf16[1024,256]{1,0:T(8,128)(2,1)} %collective-permute-done.77.refs_4_), channel_id=1, source_target_pairs={{4,0},{8,4},{12,8},{14,12},{10,14},{6,10},{2,6},{0,2},{5,1},{9,5},... | collective-permute-start | bytes 1572872 | tf_op jit(solution)/shard_map/ppermute | solution.py:69
  469.7 16.2 %collective-permute-start.78 = (bf16[64,2048]{1,0:T(8,128)(2,1)S(1)}, bf16[64,2048]{1,0:T(8,128)(2,1)S(1)}, u32[]{:S(2)}, u32[]{:S(2)}) collective-permute-start(bf16[64,2048]{1,0:T(8,128)(2,1)S(1)} %get-tuple-element.394), channel_id=1, source_target_pairs={{0,4},{4,8},{8,12},{12,14},{14,10},{10,6},{6,2},{2,0},{1,5},{5,9},... | collective-permute-start | bytes 786440 | tf_op jit(solution)/shard_map/ppermute | solution.py:69
  470.4 15.4 %collective-permute-start.83 = (bf16[64,2048]{1,0:T(8,128)(2,1)S(1)}, bf16[64,2048]{1,0:T(8,128)(2,1)S(1)}, u32[]{:S(2)}, u32[]{:S(2)}) collective-permute-start(bf16[64,2048]{1,0:T(8,128)(2,1)S(1)} %get-tuple-element.395), channel_id=1, source_target_pairs={{4,0},{8,4},{12,8},{14,12},{10,14},{6,10},{2,6},{0,2},{5,1},{9,5},... | collective-permute-start | bytes 786440 | tf_op jit(solution)/shard_map/ppermute | solution.py:69
  474.6 11.7 %collective-permute-start.91 = (bf16[256,256]{1,0:T(8,128)(2,1)S(1)}, bf16[256,256]{1,0:T(8,128)(2,1)S(1)}, u32[]{:S(2)}, u32[]{:S(2)}) collective-permute-start(bf16[256,256]{1,0:T(8,128)(2,1)S(1)} %dynamic-slice_convert_fusion.1), channel_id=1, source_target_pairs={{0,2},{2,0},{4,6},{6,4},{8,10},{10,8},{12,14},{14,12},{1,3},{3,1},... | collective-permute-start | bytes 393224 | tf_op jit(solution)/shard_map/ppermute | solution.py:69
  491.3 26.8 %collective-permute-start.93 = (bf16[1280,256]{1,0:T(8,128)(2,1)}, bf16[1280,256]{1,0:T(8,128)(2,1)}, u32[]{:S(2)}, u32[]{:S(2)}) collective-permute-start(bf16[1280,256]{1,0:T(8,128)(2,1)} %pad_maximum_fusion.3.refs_0_.refs_7_), channel_id=1, source_target_pairs={{4,0},{8,4},{12,8},{14,12},{10,14},{6,10},{2,6},{0,2},{5,1},{9,5},... | collective-permute-start | bytes 1966088 | tf_op jit(solution)/shard_map/ppermute | solution.py:69
  492.5 25.6 %collective-permute-start.92 = (bf16[1280,256]{1,0:T(8,128)(2,1)}, bf16[1280,256]{1,0:T(8,128)(2,1)}, u32[]{:S(2)}, u32[]{:S(2)}) collective-permute-start(bf16[1280,256]{1,0:T(8,128)(2,1)} %pad_maximum_fusion.3.refs_0_.refs_7_), channel_id=1, source_target_pairs={{0,4},{4,8},{8,12},{12,14},{14,10},{10,6},{6,2},{2,0},{1,5},{5,9},... | collective-permute-start | bytes 1966088 | tf_op jit(solution)/shard_map/ppermute | solution.py:69
  494.5 12.1 %collective-permute-start.87 = (f32[4352]{0:T(1024)S(1)}, f32[4352]{0:T(1024)S(1)}, u32[]{:S(2)}, u32[]{:S(2)}) collective-permute-start(f32[4352]{0:T(1024)S(1)} %add.328), channel_id=1, source_target_pairs={{0,8},{2,10},{4,12},{6,14},{8,0},{10,2},{12,4},{14,6},{1,9},{3,11}... | collective-permute-start | bytes 52232 | tf_op jit(solution)/shard_map/ppermute | solution.py:69
  505.4 9.4 %collective-permute-start.94 = (bf16[1024,256]{1,0:T(8,128)(2,1)}, bf16[1024,256]{1,0:T(8,128)(2,1)S(1)}, u32[]{:S(2)}, u32[]{:S(2)}) collective-permute-start(bf16[1024,256]{1,0:T(8,128)(2,1)} %collective-permute-done.79.refs_3_), channel_id=1, source_target_pairs={{0,4},{4,8},{8,12},{12,14},{14,10},{10,6},{6,2},{2,0},{1,5},{5,9},... | collective-permute-start | bytes 1572872 | tf_op jit(solution)/shard_map/ppermute | solution.py:69
  511.9 26.0 %collective-permute-start.64 = (bf16[64,2048]{1,0:T(8,128)(2,1)S(1)}, bf16[64,2048]{1,0:T(8,128)(2,1)S(1)}, u32[]{:S(2)}, u32[]{:S(2)}) collective-permute-start(bf16[64,2048]{1,0:T(8,128)(2,1)S(1)} %get-tuple-element.419), channel_id=1, source_target_pairs={{0,1},{1,0},{2,3},{3,2},{4,5},{5,4},{6,7},{7,6},{8,9},{9,8},{10,11... | collective-permute-start | bytes 786440 | tf_op jit(solution)/shard_map/ppermute | solution.py:69
  518.1 20.7 %collective-permute-start.84 = (f32[64,2048]{1,0:T(8,128)S(1)}, f32[64,2048]{1,0:T(8,128)S(1)}, u32[]{:S(2)}, u32[]{:S(2)}) collective-permute-start(f32[64,2048]{1,0:T(8,128)S(1)} %get-tuple-element.418), channel_id=1, source_target_pairs={{0,1},{1,0},{2,3},{3,2},{4,5},{5,4},{6,7},{7,6},{8,9},{9,8},{10,11... | collective-permute-start | bytes 1572872 | tf_op jit(solution)/shard_map/ppermute | solution.py:69
  522.4 18.6 %collective-permute-start.97 = (bf16[1280,256]{1,0:T(8,128)(2,1)}, bf16[1280,256]{1,0:T(8,128)(2,1)S(1)}, u32[]{:S(2)}, u32[]{:S(2)}) collective-permute-start(bf16[1280,256]{1,0:T(8,128)(2,1)} %collective-permute-done.92.refs_1_.refs_8_), channel_id=1, source_target_pairs={{0,4},{4,8},{8,12},{12,14},{14,10},{10,6},{6,2},{2,0},{1,5},{5,9},... | collective-permute-start | bytes 1966088 | tf_op jit(solution)/shard_map/ppermute | solution.py:69
  526.9 13.1 %collective-permute-start.99 = (f32[1024,128]{1,0:T(8,128)}, f32[1024,128]{1,0:T(8,128)S(1)}, u32[]{:S(2)}, u32[]{:S(2)}) collective-permute-start(f32[1024,128]{1,0:T(8,128)} %shard_map.300), channel_id=1, source_target_pairs={{0,16},{16,0},{1,17},{17,1},{2,18},{18,2},{3,19},{19,3},{4,20},{20... | collective-permute-start | bytes 1572872 | tf_op jit(solution)/shard_map/ppermute | solution.py:69
  527.2 13.8 %collective-permute-start.98 = (bf16[1280,256]{1,0:T(8,128)(2,1)}, bf16[1280,256]{1,0:T(8,128)(2,1)S(1)}, u32[]{:S(2)}, u32[]{:S(2)}) collective-permute-start(bf16[1280,256]{1,0:T(8,128)(2,1)} %collective-permute-done.93.refs_2_.refs_9_), channel_id=1, source_target_pairs={{4,0},{8,4},{12,8},{14,12},{10,14},{6,10},{2,6},{0,2},{5,1},{9,5},... | collective-permute-start | bytes 1966088 | tf_op jit(solution)/shard_map/ppermute | solution.py:69
  540.9 17.4 %collective-permute-start.100 = (bf16[1280,256]{1,0:T(8,128)(2,1)S(1)}, bf16[1280,256]{1,0:T(8,128)(2,1)S(1)}, u32[]{:S(2)}, u32[]{:S(2)}) collective-permute-start(bf16[1280,256]{1,0:T(8,128)(2,1)S(1)} %collective-permute-done.97.refs_3_.refs_10_), channel_id=1, source_target_pairs={{0,4},{4,8},{8,12},{12,14},{14,10},{10,6},{6,2},{2,0},{1,5},{5,9},... | collective-permute-start | bytes 1966088 | tf_op jit(solution)/shard_map/ppermute | solution.py:69
  544.2 14.1 %collective-permute-start.101 = (bf16[1280,256]{1,0:T(8,128)(2,1)S(1)}, bf16[1280,256]{1,0:T(8,128)(2,1)S(1)}, u32[]{:S(2)}, u32[]{:S(2)}) collective-permute-start(bf16[1280,256]{1,0:T(8,128)(2,1)S(1)} %collective-permute-done.98.refs_4_.refs_11_), channel_id=1, source_target_pairs={{4,0},{8,4},{12,8},{14,12},{10,14},{6,10},{2,6},{0,2},{5,1},{9,5},... | collective-permute-start | bytes 1966088 | tf_op jit(solution)/shard_map/ppermute | solution.py:69
  558.4 9.2 %collective-permute-start.102 = (bf16[640,256]{1,0:T(8,128)(2,1)S(1)}, bf16[640,256]{1,0:T(8,128)(2,1)S(1)}, u32[]{:S(2)}, u32[]{:S(2)}) collective-permute-start(bf16[640,256]{1,0:T(8,128)(2,1)S(1)} %slice.271), channel_id=1, source_target_pairs={{0,4},{4,8},{8,12},{12,14},{14,10},{10,6},{6,2},{2,0},{1,5},{5,9},... | collective-permute-start | bytes 983048 | tf_op jit(solution)/shard_map/ppermute | solution.py:69
  (88 other events, 703.7 us)

commit v4 on v3

--- a/solution.py
+++ b/solution.py
@@ -1061,7 +1061,9 @@
         layer_parts.append(layer_part(step, ring.ahead, after(weighted, signal), down))
         if step == 1 and pair:
             made["routed"] = (made["grads"], ring.swap_halves(made["grads"]))
-        return tuple([layer_parts[-1]] + across(signal))
+        earlier = their_rows[-1:]
+        across(signal)
+        return tuple([layer_parts[-1]] + earlier)
 
     back_sum = ring.scatter(back_mine, back_other, back_hook)
 
@@ -1090,16 +1092,16 @@
                 jnp.concatenate(part, axis=0) for part in (layer_parts[:middle], layer_parts[middle:])
             ]
             made["layer"] = Fold(ring, *after(halves, walk.ahead))
-            made["layer"].step()
         else:
             made["layer"].step(walk.ahead)
         done.append(made["layer"].ahead)
-        if pair and step == 0:
+        if pair and step == 1:
             rows = jnp.concatenate(after(their_rows, walk.ahead), axis=0)
             made["theirs"] = [rows, ring.swap_halves(rows)]
-            done.append(rows)
-        if pair and step % 2:
-            x, g = after((made["theirs"][step // 2], made["routed"][step // 2]), walk.ahead)
+            done += made["theirs"]
+        if pair and step >= ring.ahead - 2:
+            half = step - (ring.ahead - 2)
+            x, g = after((made["theirs"][half], made["routed"][half]), walk.ahead)
             made["other"].append(
                 other_experts(first, x, g, gate_proj, up_proj, down_proj, router_lanes, picks)
             )
@@ -1109,7 +1111,6 @@
     branch, _ = ring.gather(
         jnp.concatenate([mid_grad.astype(BF16), pad_lanes(logit_grad)], axis=1), other_hook
     )
-    layer_out = ring.join_halves((residual + made["layer"].result()).astype(BF16))
 
     attn_halves = (attn_mine, attn_other)
     out_theirs, out_arrived = ring.send_share(branch, attn_halves, width, BF16)
@@ -1152,6 +1153,8 @@
     def in_hook(step, signal):
         done = []
         if step == 0:
+            made["layer"].step(signal)
+            done.append(made["layer"].ahead)
             share = ring.add_share(out_arrived, after(branch, signal), attn_halves, width)
             made["out_walk"] = ring.walk(share.astype(BF16), True)
         else:
@@ -1167,6 +1170,7 @@
     if qkv_theirs is not None:
         in_mine = after(in_mine, qkv_theirs)
     attn_in_grad = ring.scatter(in_mine, in_other, in_hook)
+    layer_out = ring.join_halves((residual + made["layer"].result()).astype(BF16))
     qkv_share = made["qkv"]
     first_normed_grad = attn_in_grad * attn_gain
     tokens_grad = mid_grad + first_inverse * (

time: 578 us -> 571 us (0.988)
  waiting for transfers between devices: 151 us -> 140 us
    ppermute x104, waiting for transfers between devices: 151 us -> 140 us  [send(): return lax.ppermute(values, axis, pairs)]
    unnamed x131 -> x139, local copies, waits for them, and re-layouts: 28.3 us -> 27.4 us
  transfers between devices with their start and end apart: 104 -> 104, of which waited for: 43 -> 38; matrix products, arithmetic and copies ran while one was open for 12% -> 12% of each run, Pallas kernels for 33% -> 34%
where the time goes in v4:
time: 571 us; the launch traced here: 564 us
  Pallas kernels  228 us (40%)
  waiting for transfers between devices  140 us (25%)
  starting transfers between devices  103 us (18%)
  other arithmetic  46.4 us (8%)
  local copies, waits for them, and re-layouts  43.8 us (8%)
    ppermute x104, waiting for transfers between devices, send(): return lax.ppermute(values, axis, pairs)  140 us
    ppermute x104, starting transfers between devices, send(): return lax.ppermute(values, axis, pairs)  103 us
    pallas_call x1, Pallas kernels, experts(): call(functools.partial(experts_kernel, picks, expert_count), 41, grid_spe...  41.3 us
    pallas_call x3, Pallas kernels, gate_up_grad(): call(gate_up_grad_kernel, 11.7, grid=(width // wide,), in_specs=[pl.Block...  34.7 us
    pallas_call x2, Pallas kernels, other_experts(): call(functools.partial(other_experts_kernel, picks), 15, grid_spec=pltpu....  31.6 us
    unnamed x139, local copies, waits for them, and re-layouts  27.4 us
    pallas_call x6, Pallas kernels, transposed_product(): call(transposed_product_kernel, 4, grid_spec=pltpu.PrefetchScalarGridSpec...  21.7 us
    pallas_call x4, Pallas kernels, layer_part(): call(layer_kernel, 4, grid=(1,), in_specs=[pl.BlockSpec((rows // parts, h...  20.1 us
  transfers between devices with their start and end apart: 104, of which 38 were waited for; matrix products, arithmetic and copies ran while one was open for 12% of the time, Pallas kernels for 34%

profile of v4, /device:TPU:0, one launch (start us, length us, event | category | flops | bytes accessed | tf_op | source)
XLA Modules:
  0.0 564.1 jit_solution(8052274558801410086)
XLA Ops:
  3.2 2.9 collective-permute-start.7
  11.8 3.3 shard_map.281.refs_0_
  16.6 2.0 collective-permute-start.2
  21.8 4.9 collective-permute-done.2
  52.1 2.6 collective-permute-done.13
  54.7 2.0 collective-permute-start.14
  61.8 3.0 collective-permute-done.17
  67.6 3.8 collective-permute-done.18.xo_ref.ao_ref
  71.4 7.3 %shard_map.282 = (f32[1024,384]{1,0:T(8,128)}, bf16[1024,256]{1,0:T(8,128)(2,1)}, bf16[1024,128]{1,0:T(8,128)(2,1)}, bf16[1024,128]{1,0:T(8,128)(2,1)}) custom-call(s32[2]{0:T(128)} %pad_add_fusion.at_ref, bf16[512,2048]{1,0:T(8,128)(2,1)} %constant_dynamic-update-slice_fusion.5.xm_ref.am_ref, bf16[512,2048]{1,0:T(8,128)(2,1)} %collective-permute-done.18.xo_ref.ao_ref, ...), custom_call_target="tpu_custom_call" | custom-call | flops 8049999872 | tf_op jit(solution)/shard_map/pallas_call | solution.py:321
  78.6 7.1 %shard_map.284 = (bf16[512,256]{1,0:T(8,128)(2,1)}, f32[2,512,1]{2,1,0:T(8,128)}, bf16[512,2048]{1,0:T(8,128)(2,1)}) custom-call(s32[2]{0:T(128)} %pad_add_fusion.at_ref, s32[1,1024]{1,0:T(1,128)} %and_select_fusion.1.pos_ref, s32[1024,1]{1,0:T(8,128)} %fusion.14.lim_ref, bf16[1024,256]{1,0:T(8,128)(2,1)} %get-tuple-element.186.ql_ref, ...), custom_call_target="tpu_custom_call" | custom-call | flops 7474999808 | tf_op jit(solution)/shard_map/pallas_call | solution.py:364
  88.3 7.1 %shard_map.283 = (bf16[512,256]{1,0:T(8,128)(2,1)}, f32[2,512,1]{2,1,0:T(8,128)}, bf16[512,2048]{1,0:T(8,128)(2,1)}) custom-call(s32[2]{0:T(128)} %pad_add_fusion.at_ref, s32[1,1024]{1,0:T(1,128)} %and_select_fusion.1.pos_ref, s32[1024,1]{1,0:T(8,128)} %fusion.14.lim_ref, bf16[1024,256]{1,0:T(8,128)(2,1)} %get-tuple-element.186.ql_ref, ...), custom_call_target="tpu_custom_call" | custom-call | flops 7474999808 | tf_op jit(solution)/shard_map/pallas_call | solution.py:364
  96.8 3.0 add_convert_fusion.3
  103.8 5.3 collective-permute-done.20
  115.8 6.2 %collective-permute-done.21 = bf16[64,2048]{1,0:T(8,128)(2,1)} collective-permute-done((bf16[64,2048]{1,0:T(8,128)(2,1)}, bf16[64,2048]{1,0:T(8,128)(2,1)}, u32[]{:S(2)}, u32[]{:S(2)}) %collective-permute-start.21) | collective-permute-done | bytes 262176 | tf_op jit(solution)/shard_map/ppermute | solution.py:69
  125.9 5.0 collective-permute-done.26
  133.8 3.6 collective-permute-done.24
  137.4 2.3 collective-permute-done.27
  143.1 3.7 collective-permute-done.29
  149.2 5.5 collective-permute-done.31
  157.1 7.5 %collective-permute-done.32 = bf16[64,2048]{1,0:T(8,128)(2,1)S(1)} collective-permute-done((bf16[64,2048]{1,0:T(8,128)(2,1)S(1)}, bf16[64,2048]{1,0:T(8,128)(2,1)S(1)}, u32[]{:S(2)}, u32[]{:S(2)}) %collective-permute-start.32) | collective-permute-done | bytes 262176 | tf_op jit(solution)/shard_map/ppermute | solution.py:69
  166.1 4.9 collective-permute-done.34
  172.3 3.0 collective-permute-done.35.xo_ref.x1.ao_ref
  175.4 41.3 %shard_map.285 = (bf16[1024,1152]{1,0:T(8,128)(2,1)}, bf16[1024,2304]{1,0:T(8,128)(2,1)}, f32[1024,128]{1,0:T(8,128)}, bf16[512,2176]{1,0:T(8,128)(2,1)}, bf16[512,2176]{1,0:T(8,128)(2,1)}) custom-call(s32[2]{0:T(128)} %pad_add_fusion.2.first_ref, bf16[512,2048]{1,0:T(8,128)(2,1)} %copy-done.6, bf16[512,2048]{1,0:T(8,128)(2,1)} %collective-permute-done.35.xo_ref.x1.ao_ref, ...), custom_call_target="tpu_custom_call" | custom-call | flops 47149998080 | tf_op jit(solution)/shard_map/pallas_call | solution.py:582
  216.9 5.9 %collective-permute-done.37.g_ref.g2 = bf16[512,2176]{1,0:T(8,128)(2,1)} collective-permute-done((bf16[512,2176]{1,0:T(8,128)(2,1)}, bf16[512,2176]{1,0:T(8,128)(2,1)}, u32[]{:S(2)}, u32[]{:S(2)}) %collective-permute-start.37) | collective-permute-done | bytes 2228256 | tf_op jit(solution)/shard_map/ppermute | solution.py:69
  222.8 2.3 add_convert_fusion
  228.6 5.0 shard_map.286
  239.1 5.0 shard_map.287
  247.5 2.0 collective-permute-start.42
  250.9 5.0 shard_map.288
  259.3 5.0 shard_map.289
  274.5 5.3 collective-permute-done.51
  279.8 4.1 collective-permute-done.55
  291.6 10.5 %collective-permute-done.52 = bf16[64,2048]{1,0:T(8,128)(2,1)S(1)} collective-permute-done((bf16[64,2048]{1,0:T(8,128)(2,1)S(1)}, bf16[64,2048]{1,0:T(8,128)(2,1)S(1)}, u32[]{:S(2)}, u32[]{:S(2)}) %collective-permute-start.52) | collective-permute-done | bytes 262176 | tf_op jit(solution)/shard_map/ppermute | solution.py:69
  302.6 7.4 %collective-permute-done.54 = bf16[64,2176]{1,0:T(8,128)(2,1)S(1)} collective-permute-done((bf16[64,2176]{1,0:T(8,128)(2,1)S(1)}, bf16[64,2176]{1,0:T(8,128)(2,1)S(1)}, u32[]{:S(2)}, u32[]{:S(2)}) %collective-permute-start.54) | collective-permute-done | bytes 278560 | tf_op jit(solution)/shard_map/ppermute | solution.py:69
  315.0 15.7 %shard_map.290 = (bf16[512,1152]{1,0:T(8,128)(2,1)}, bf16[512,2304]{1,0:T(8,128)(2,1)}) custom-call(s32[2]{0:T(128)} %pad_add_fusion.2.first_ref, bf16[512,2048]{1,0:T(8,128)(2,1)} %copy-done.29, bf16[512,2176]{1,0:T(8,128)(2,1)} %collective-permute-done.37.g_ref.g2, bf16[3,2048,384]{2,1,0:T(8,128)(2,1)} %wg_ref.5, bf16[3,2048,384]{2,1,0:T(8,128)(2,1)} %wu_ref.5, ...), custom_call_target="tpu_custom_call" | custom-call | flops 17250000896 | tf_op jit(solution)/shard_map/pallas_call | solution.py:683
  333.7 15.9 %shard_map.291 = (bf16[512,1152]{1,0:T(8,128)(2,1)}, bf16[512,2304]{1,0:T(8,128)(2,1)}) custom-call(s32[2]{0:T(128)} %pad_add_fusion.2.first_ref, bf16[512,2048]{1,0:T(8,128)(2,1)} %copy-done.45, bf16[512,2176]{1,0:T(8,128)(2,1)} %collective-permute-done.62.g_ref.g3, bf16[3,2048,384]{2,1,0:T(8,128)(2,1)} %wg_ref.5, bf16[3,2048,384]{2,1,0:T(8,128)(2,1)} %wu_ref.5, ...), custom_call_target="tpu_custom_call" | custom-call | flops 17250000896 | tf_op jit(solution)/shard_map/pallas_call | solution.py:683
  350.7 4.3 collective-permute-done.63.ao_ref.bo_ref
  356.5 3.3 shard_map.292
  359.8 18.1 %shard_map.293 = (bf16[512,512]{1,0:T(8,128)(2,1)}, bf16[512,512]{1,0:T(8,128)(2,1)}, f32[2,128]{1,0:T(2,128)}, bf16[512,2048]{1,0:T(8,128)(2,1)}, bf16[512,2048]{1,0:T(8,128)(2,1)}) custom-call(s32[2]{0:T(128)} %pad_add_fusion.at_ref, bf16[512,2176]{1,0:T(8,128)(2,1)} %copy-done.38, bf16[512,2176]{1,0:T(8,128)(2,1)} %copy-done.44, ...), custom_call_target="tpu_custom_call" | custom-call | flops 21275000832 | tf_op jit(solution)/shard_map/pallas_call | solution.py:467
  382.8 4.2 shard_map.294
  387.6 2.5 add_convert_fusion.1
  393.0 11.6 %shard_map.296 = (f32[3,2048,384]{2,1,0:T(8,128)}, f32[3,2048,384]{2,1,0:T(8,128)}, f32[8,128]{1,0:T(8,128)}) custom-call(bf16[512,2048]{1,0:T(8,128)(2,1)} %copy-done.6, bf16[512,2048]{1,0:T(8,128)(2,1)} %collective-permute-done.35.xo_ref.x1.ao_ref, bf16[512,2048]{1,0:T(8,128)(2,1)} %copy-done.29, bf16[512,2048]{1,0:T(8,128)(2,1)} %copy-done.45, ...), custom_call_target="tpu_custom_call" | custom-call | flops 13454999552 | tf_op jit(solution)/shard_map/pallas_call | solution.py:748
  404.6 3.4 shard_map.295
  412.2 11.6 %shard_map.298 = (f32[3,2048,384]{2,1,0:T(8,128)}, f32[3,2048,384]{2,1,0:T(8,128)}, f32[8,128]{1,0:T(8,128)}) custom-call(bf16[512,2048]{1,0:T(8,128)(2,1)} %copy-done.6, bf16[512,2048]{1,0:T(8,128)(2,1)} %collective-permute-done.35.xo_ref.x1.ao_ref, bf16[512,2048]{1,0:T(8,128)(2,1)} %copy-done.29, ...), custom_call_target="tpu_custom_call", output_to_operand_aliasing={{0}: (8, {}), {1}: (9, {})} | custom-call | flops 13454999552 | tf_op jit(solution)/shard_map/pallas_call | solution.py:748
  423.8 4.4 shard_map.297
  429.6 2.2 convert_add_fusion
  437.6 5.6 collective-permute-done.76.refs_1_
  445.2 11.6 %shard_map.299 = (f32[3,2048,384]{2,1,0:T(8,128)}, f32[3,2048,384]{2,1,0:T(8,128)}, f32[8,128]{1,0:T(8,128)}) custom-call(bf16[512,2048]{1,0:T(8,128)(2,1)} %copy-done.6, bf16[512,2048]{1,0:T(8,128)(2,1)} %collective-permute-done.35.xo_ref.x1.ao_ref, bf16[512,2048]{1,0:T(8,128)(2,1)} %copy-done.29, ...), custom_call_target="tpu_custom_call", output_to_operand_aliasing={{0}: (8, {}), {1}: (9, {})} | custom-call | flops 13454999552 | tf_op jit(solution)/shard_map/pallas_call | solution.py:748
  463.4 2.8 collective-permute-done.90
  466.8 10.0 %collective-permute-done.83 = bf16[64,2048]{1,0:T(8,128)(2,1)S(1)} collective-permute-done((bf16[64,2048]{1,0:T(8,128)(2,1)S(1)}, bf16[64,2048]{1,0:T(8,128)(2,1)S(1)}, u32[]{:S(2)}, u32[]{:S(2)}) %collective-permute-start.83) | collective-permute-done | bytes 262176 | tf_op jit(solution)/shard_map/ppermute | solution.py:69
  477.3 4.0 collective-permute-done.85
  486.7 9.7 %shard_map.305 = (f32[3,384,2048]{2,1,0:T(8,128)}, f32[8,128]{1,0:T(8,128)}) custom-call(bf16[1024,1152]{1,0:T(8,128)(2,1)} %get-tuple-element.317.w_ref.w0.w1, bf16[1024,1152]{1,0:T(8,128)(2,1)} %get-tuple-element.317.w_ref.w0.w1, bf16[512,2176]{1,0:T(8,128)(2,1)} %constant_dynamic-update-slice_fusion.25.gm_ref.g0, ...), custom_call_target="tpu_custom_call" | custom-call | flops 11155000320 | tf_op jit(solution)/shard_map/pallas_call | solution.py:782
  499.1 2.2 collective-permute-done.88
  503.4 2.4 collective-permute-done.94.refs_5_
  509.1 3.4 collective-permute-done.96.refs_8_
  514.4 3.2 shard_map.300
  520.8 9.7 %shard_map.306 = (f32[3,384,2048]{2,1,0:T(8,128)}, f32[8,128]{1,0:T(8,128)}) custom-call(bf16[1024,1152]{1,0:T(8,128)(2,1)} %get-tuple-element.317.w_ref.w0.w1, bf16[1024,1152]{1,0:T(8,128)(2,1)} %get-tuple-element.317.w_ref.w0.w1, bf16[512,2176]{1,0:T(8,128)(2,1)} %constant_dynamic-update-slice_fusion.25.gm_ref.g0, ...), custom_call_target="tpu_custom_call", output_to_operand_aliasing={{0}: (8, {})} | custom-call | flops 11155000320 | tf_op jit(solution)/shard_map/pallas_call | solution.py:782
  534.1 2.8 collective-permute-start.100
  536.8 3.2 shard_map.301
  541.9 6.0 %shard_map.302 = f32[1024,2048]{1,0:T(8,128)} custom-call(s32[8]{0:T(128)} %get-tuple-element.441.owners_ref, bf16[1024,256]{1,0:T(8,128)(2,1)} %copy-done.14, bf16[1024,256]{1,0:T(8,128)(2,1)} %collective-permute-done.76.refs_1_, bf16[1024,256]{1,0:T(8,128)(2,1)} %collective-permute-done.73.refs_2_, bf16[1024,256]{1,0:T(8,128)(2,1)} %collective-permute-done.79.refs_3_, ...), custom_call_target="tpu_custom_call" | custom-call | flops 4600000000 | tf_op jit(solution)/shard_map/pallas_call | solution.py:824
  548.0 3.0 collective-permute-done.101.refs_6_.refs_13_
  551.0 2.0 collective-permute-start.102
  553.1 7.2 %shard_map.303 = (f32[1024,2048]{1,0:T(8,128)}, f32[1024,256]{1,0:T(8,128)}, f32[1024,256]{1,0:T(8,128)}) custom-call(s32[8]{0:T(128)} %get-tuple-element.441.owners_ref, bf16[1280,256]{1,0:T(8,128)(2,1)} %pad_maximum_fusion.3.refs_0_.refs_7_, bf16[1280,256]{1,0:T(8,128)(2,1)} %collective-permute-done.92.refs_1_.refs_8_, ...), custom_call_target="tpu_custom_call" | custom-call | flops 5750000128 | tf_op jit(solution)/shard_map/pallas_call | solution.py:862
  561.1 2.8 shard_map.304
  (429 shorter events, 178.3 us)
Async XLA Ops:
  3.2 27.5 %collective-permute-start.7 = (bf16[64,2176]{1,0:T(8,128)(2,1)S(1)}, bf16[64,2176]{1,0:T(8,128)(2,1)S(1)}, u32[]{:S(2)}, u32[]{:S(2)}) collective-permute-start(bf16[64,2176]{1,0:T(8,128)(2,1)S(1)} %get-tuple-element.429), channel_id=1, source_target_pairs={{4,0},{8,4},{12,8},{14,12},{10,14},{6,10},{2,6},{0,2},{5,1},{9,5},... | collective-permute-start | bytes 835592 | tf_op jit(solution)/shard_map/ppermute | solution.py:69
  6.2 15.6 %collective-permute-start.3 = (bf16[64,2176]{1,0:T(8,128)(2,1)S(1)}, bf16[64,2176]{1,0:T(8,128)(2,1)}, u32[]{:S(2)}, u32[]{:S(2)}) collective-permute-start(bf16[64,2176]{1,0:T(8,128)(2,1)S(1)} %get-tuple-element.429), channel_id=1, source_target_pairs={{0,4},{4,8},{8,12},{12,14},{14,10},{10,6},{6,2},{2,0},{1,5},{5,9},... | collective-permute-start | bytes 835592 | tf_op jit(solution)/shard_map/ppermute | solution.py:69
  9.2 12.6 %collective-permute-start.1 = (bf16[64,2048]{1,0:T(8,128)(2,1)S(1)}, bf16[64,2048]{1,0:T(8,128)(2,1)}, u32[]{:S(2)}, u32[]{:S(2)}) collective-permute-start(bf16[64,2048]{1,0:T(8,128)(2,1)S(1)} %get-tuple-element.387), channel_id=1, source_target_pairs={{4,0},{8,4},{12,8},{14,12},{10,14},{6,10},{2,6},{0,2},{5,1},{9,5},... | collective-permute-start | bytes 786440 | tf_op jit(solution)/shard_map/ppermute | solution.py:69
  16.6 10.1 %collective-permute-start.2 = (bf16[256,768]{1,0:T(8,128)(2,1)S(1)}, bf16[256,768]{1,0:T(8,128)(2,1)S(1)}, u32[]{:S(2)}, u32[]{:S(2)}) collective-permute-start(bf16[256,768]{1,0:T(8,128)(2,1)S(1)} %get-tuple-element.419), channel_id=1, source_target_pairs={{0,16},{16,0},{1,17},{17,1},{2,18},{18,2},{3,19},{19,3},{4,20},{20... | collective-permute-start | bytes 1179656 | tf_op jit(solution)/shard_map/ppermute | solution.py:69
  28.9 13.4 %collective-permute-start.4 = (bf16[64,2048]{1,0:T(8,128)(2,1)}, bf16[64,2048]{1,0:T(8,128)(2,1)}, u32[]{:S(2)}, u32[]{:S(2)}) collective-permute-start(bf16[64,2048]{1,0:T(8,128)(2,1)} %collective-permute-done), channel_id=1, source_target_pairs={{0,4},{4,8},{8,12},{12,14},{14,10},{10,6},{6,2},{2,0},{1,5},{5,9},... | collective-permute-start | bytes 786440 | tf_op jit(solution)/shard_map/ppermute | solution.py:69
  31.5 10.8 %collective-permute-start.5 = (bf16[64,2048]{1,0:T(8,128)(2,1)}, bf16[64,2048]{1,0:T(8,128)(2,1)}, u32[]{:S(2)}, u32[]{:S(2)}) collective-permute-start(bf16[64,2048]{1,0:T(8,128)(2,1)} %collective-permute-done.1), channel_id=1, source_target_pairs={{4,0},{8,4},{12,8},{14,12},{10,14},{6,10},{2,6},{0,2},{5,1},{9,5},... | collective-permute-start | bytes 786440 | tf_op jit(solution)/shard_map/ppermute | solution.py:69
  31.8 10.5 %collective-permute-start.8 = (bf16[64,2176]{1,0:T(8,128)(2,1)}, bf16[64,2176]{1,0:T(8,128)(2,1)}, u32[]{:S(2)}, u32[]{:S(2)}) collective-permute-start(bf16[64,2176]{1,0:T(8,128)(2,1)} %collective-permute-done.3), channel_id=1, source_target_pairs={{0,4},{4,8},{8,12},{12,14},{14,10},{10,6},{6,2},{2,0},{1,5},{5,9},... | collective-permute-start | bytes 835592 | tf_op jit(solution)/shard_map/ppermute | solution.py:69
  33.6 10.4 %collective-permute-start.12 = (bf16[64,2176]{1,0:T(8,128)(2,1)S(1)}, bf16[64,2176]{1,0:T(8,128)(2,1)}, u32[]{:S(2)}, u32[]{:S(2)}) collective-permute-start(bf16[64,2176]{1,0:T(8,128)(2,1)S(1)} %collective-permute-done.7), channel_id=1, source_target_pairs={{4,0},{8,4},{12,8},{14,12},{10,14},{6,10},{2,6},{0,2},{5,1},{9,5},... | collective-permute-start | bytes 835592 | tf_op jit(solution)/shard_map/ppermute | solution.py:69
  42.4 9.7 %collective-permute-start.9 = (bf16[64,2048]{1,0:T(8,128)(2,1)}, bf16[64,2048]{1,0:T(8,128)(2,1)S(1)}, u32[]{:S(2)}, u32[]{:S(2)}) collective-permute-start(bf16[64,2048]{1,0:T(8,128)(2,1)} %collective-permute-done.4), channel_id=1, source_target_pairs={{0,4},{4,8},{8,12},{12,14},{14,10},{10,6},{6,2},{2,0},{1,5},{5,9},... | collective-permute-start | bytes 786440 | tf_op jit(solution)/shard_map/ppermute | solution.py:69
  44.5 10.2 %collective-permute-start.13 = (bf16[64,2176]{1,0:T(8,128)(2,1)}, bf16[64,2176]{1,0:T(8,128)(2,1)S(1)}, u32[]{:S(2)}, u32[]{:S(2)}) collective-permute-start(bf16[64,2176]{1,0:T(8,128)(2,1)} %collective-permute-done.8), channel_id=1, source_target_pairs={{0,4},{4,8},{8,12},{12,14},{14,10},{10,6},{6,2},{2,0},{1,5},{5,9},... | collective-permute-start | bytes 835592 | tf_op jit(solution)/shard_map/ppermute | solution.py:69
  46.0 10.6 %collective-permute-start.16 = (bf16[64,2176]{1,0:T(8,128)(2,1)}, bf16[64,2176]{1,0:T(8,128)(2,1)S(1)}, u32[]{:S(2)}, u32[]{:S(2)}) collective-permute-start(bf16[64,2176]{1,0:T(8,128)(2,1)} %collective-permute-done.12), channel_id=1, source_target_pairs={{4,0},{8,4},{12,8},{14,12},{10,14},{6,10},{2,6},{0,2},{5,1},{9,5},... | collective-permute-start | bytes 835592 | tf_op jit(solution)/shard_map/ppermute | solution.py:69
  85.8 9.7 %collective-permute-start.19 = (bf16[512,2048]{1,0:T(8,128)(2,1)}, bf16[512,2048]{1,0:T(8,128)(2,1)S(1)}, u32[]{:S(2)}, u32[]{:S(2)}) collective-permute-start(bf16[512,2048]{1,0:T(8,128)(2,1)} %get-tuple-element.190), channel_id=1, source_target_pairs={{0,1},{1,0},{2,3},{3,2},{4,5},{5,4},{6,7},{7,6},{8,9},{9,8},{10,11... | collective-permute-start | bytes 6291464 | tf_op jit(solution)/shard_map/ppermute | solution.py:69
  112.4 9.5 %collective-permute-start.25 = (bf16[64,2048]{1,0:T(8,128)(2,1)}, bf16[64,2048]{1,0:T(8,128)(2,1)}, u32[]{:S(2)}, u32[]{:S(2)}) collective-permute-start(bf16[64,2048]{1,0:T(8,128)(2,1)} %get-tuple-element.415), channel_id=1, source_target_pairs={{4,0},{8,4},{12,8},{14,12},{10,14},{6,10},{2,6},{0,2},{5,1},{9,5},... | collective-permute-start | bytes 786440 | tf_op jit(solution)/shard_map/ppermute | solution.py:69
  143.1 29.3 %collective-permute-start.36 = (bf16[512,2176]{1,0:T(8,128)(2,1)}, bf16[512,2176]{1,0:T(8,128)(2,1)}, u32[]{:S(2)}, u32[]{:S(2)}) collective-permute-start(bf16[512,2176]{1,0:T(8,128)(2,1)} %constant_dynamic-update-slice_fusion.25.gm_ref.g0), channel_id=1, source_target_pairs={{0,1},{1,0},{2,3},{3,2},{4,5},{5,4},{6,7},{7,6},{8,9},{9,8},{10,11... | collective-permute-start | bytes 6684680 | tf_op jit(solution)/shard_map/ppermute | solution.py:69
  154.6 11.5 %collective-permute-start.33 = (bf16[64,2048]{1,0:T(8,128)(2,1)S(1)}, bf16[64,2048]{1,0:T(8,128)(2,1)S(1)}, u32[]{:S(2)}, u32[]{:S(2)}) collective-permute-start(bf16[64,2048]{1,0:T(8,128)(2,1)S(1)} %collective-permute-done.31), channel_id=1, source_target_pairs={{4,0},{8,4},{12,8},{14,12},{10,14},{6,10},{2,6},{0,2},{5,1},{9,5},... | collective-permute-start | bytes 786440 | tf_op jit(solution)/shard_map/ppermute | solution.py:69
  171.8 51.0 %collective-permute-start.37 = (bf16[512,2176]{1,0:T(8,128)(2,1)}, bf16[512,2176]{1,0:T(8,128)(2,1)}, u32[]{:S(2)}, u32[]{:S(2)}) collective-permute-start(bf16[512,2176]{1,0:T(8,128)(2,1)} %constant_dynamic-update-slice_fusion.25.gm_ref.g0), channel_id=1, source_target_pairs={{0,16},{16,0},{1,17},{17,1},{2,18},{18,2},{3,19},{19,3},{4,20},{20... | collective-permute-start | bytes 6684680 | tf_op jit(solution)/shard_map/ppermute | solution.py:69
  226.7 9.4 %collective-permute-start.46 = (bf16[64,2176]{1,0:T(8,128)(2,1)S(1)}, bf16[64,2176]{1,0:T(8,128)(2,1)S(1)}, u32[]{:S(2)}, u32[]{:S(2)}) collective-permute-start(bf16[64,2176]{1,0:T(8,128)(2,1)S(1)} %get-tuple-element.396), channel_id=1, source_target_pairs={{4,0},{8,4},{12,8},{14,12},{10,14},{6,10},{2,6},{0,2},{5,1},{9,5},... | collective-permute-start | bytes 835592 | tf_op jit(solution)/shard_map/ppermute | solution.py:69
  228.1 17.6 %collective-permute-start.41 = (bf16[128,2048]{1,0:T(8,128)(2,1)}, bf16[128,2048]{1,0:T(8,128)(2,1)}, u32[]{:S(2)}, u32[]{:S(2)}) collective-permute-start(bf16[128,2048]{1,0:T(8,128)(2,1)} %slice.230), channel_id=1, source_target_pairs={{0,16},{16,0},{1,17},{17,1},{2,18},{18,2},{3,19},{19,3},{4,20},{20... | collective-permute-start | bytes 1572872 | tf_op jit(solution)/shard_map/ppermute | solution.py:69
  234.4 11.2 %collective-permute-start.40 = (bf16[64,2176]{1,0:T(8,128)(2,1)}, bf16[64,2176]{1,0:T(8,128)(2,1)}, u32[]{:S(2)}, u32[]{:S(2)}) collective-permute-start(bf16[64,2176]{1,0:T(8,128)(2,1)} %add_convert_fusion.9), channel_id=1, source_target_pairs={{0,4},{4,8},{8,12},{12,14},{14,10},{10,6},{6,2},{2,0},{1,5},{5,9},... | collective-permute-start | bytes 835592 | tf_op jit(solution)/shard_map/ppermute | solution.py:69
  237.6 18.6 %collective-permute-start.43 = (bf16[128,2048]{1,0:T(8,128)(2,1)}, bf16[128,2048]{1,0:T(8,128)(2,1)}, u32[]{:S(2)}, u32[]{:S(2)}) collective-permute-start(bf16[128,2048]{1,0:T(8,128)(2,1)} %slice.232), channel_id=1, source_target_pairs={{0,16},{16,0},{1,17},{17,1},{2,18},{18,2},{3,19},{19,3},{4,20},{20... | collective-permute-start | bytes 1572872 | tf_op jit(solution)/shard_map/ppermute | solution.py:69
  250.4 15.4 %collective-permute-start.45 = (bf16[128,2048]{1,0:T(8,128)(2,1)}, bf16[128,2048]{1,0:T(8,128)(2,1)}, u32[]{:S(2)}, u32[]{:S(2)}) collective-permute-start(bf16[128,2048]{1,0:T(8,128)(2,1)} %slice.235), channel_id=1, source_target_pairs={{0,16},{16,0},{1,17},{17,1},{2,18},{18,2},{3,19},{19,3},{4,20},{20... | collective-permute-start | bytes 1572872 | tf_op jit(solution)/shard_map/ppermute | solution.py:69
  269.6 14.4 %collective-permute-start.55 = (bf16[128,2048]{1,0:T(8,128)(2,1)S(1)}, bf16[128,2048]{1,0:T(8,128)(2,1)S(1)}, u32[]{:S(2)}, u32[]{:S(2)}) collective-permute-start(bf16[128,2048]{1,0:T(8,128)(2,1)S(1)} %slice.248), channel_id=1, source_target_pairs={{0,16},{16,0},{1,17},{17,1},{2,18},{18,2},{3,19},{19,3},{4,20},{20... | collective-permute-start | bytes 1572872 | tf_op jit(solution)/shard_map/ppermute | solution.py:69
  287.2 22.7 %collective-permute-start.56 = (bf16[512,2048]{1,0:T(8,128)(2,1)S(1)}, bf16[512,2048]{1,0:T(8,128)(2,1)S(1)}, u32[]{:S(2)}, u32[]{:S(2)}) collective-permute-start(bf16[512,2048]{1,0:T(8,128)(2,1)S(1)} %constant_dynamic-update-slice_fusion.33.x_ref.x2), channel_id=1, source_target_pairs={{0,1},{1,0},{2,3},{3,2},{4,5},{5,4},{6,7},{7,6},{8,9},{9,8},{10,11... | collective-permute-start | bytes 6291464 | tf_op jit(solution)/shard_map/ppermute | solution.py:69
  287.3 45.6 %collective-permute-start.62 = (bf16[512,2176]{1,0:T(8,128)(2,1)}, bf16[512,2176]{1,0:T(8,128)(2,1)}, u32[]{:S(2)}, u32[]{:S(2)}) collective-permute-start(bf16[512,2176]{1,0:T(8,128)(2,1)} %collective-permute-done.37.g_ref.g2), channel_id=1, source_target_pairs={{0,1},{1,0},{2,3},{3,2},{4,5},{5,4},{6,7},{7,6},{8,9},{9,8},{10,11... | collective-permute-start | bytes 6684680 | tf_op jit(solution)/shard_map/ppermute | solution.py:69
  287.8 14.7 %collective-permute-start.53 = (bf16[64,2176]{1,0:T(8,128)(2,1)S(1)}, bf16[64,2176]{1,0:T(8,128)(2,1)S(1)}, u32[]{:S(2)}, u32[]{:S(2)}) collective-permute-start(bf16[64,2176]{1,0:T(8,128)(2,1)S(1)} %collective-permute-done.50), channel_id=1, source_target_pairs={{0,4},{4,8},{8,12},{12,14},{14,10},{10,6},{6,2},{2,0},{1,5},{5,9},... | collective-permute-start | bytes 835592 | tf_op jit(solution)/shard_map/ppermute | solution.py:69
  289.6 12.6 %collective-permute-start.52 = (bf16[64,2048]{1,0:T(8,128)(2,1)S(1)}, bf16[64,2048]{1,0:T(8,128)(2,1)S(1)}, u32[]{:S(2)}, u32[]{:S(2)}) collective-permute-start(bf16[64,2048]{1,0:T(8,128)(2,1)S(1)} %get-tuple-element.216), channel_id=1, source_target_pairs={{0,4},{4,8},{8,12},{12,14},{14,10},{10,6},{6,2},{2,0},{1,5},{5,9},... | collective-permute-start | bytes 786440 | tf_op jit(solution)/shard_map/ppermute | solution.py:69
  290.4 40.3 %collective-permute-start.66 = (bf16[64,2048]{1,0:T(8,128)(2,1)S(1)}, bf16[64,2048]{1,0:T(8,128)(2,1)S(1)}, u32[]{:S(2)}, u32[]{:S(2)}) collective-permute-start(bf16[64,2048]{1,0:T(8,128)(2,1)S(1)} %get-tuple-element.254), channel_id=1, source_target_pairs={{4,0},{8,4},{12,8},{14,12},{10,14},{6,10},{2,6},{0,2},{5,1},{9,5},... | collective-permute-start | bytes 786440 | tf_op jit(solution)/shard_map/ppermute | solution.py:69
  311.3 20.0 %collective-permute-start.58 = (bf16[64,2176]{1,0:T(8,128)(2,1)S(1)}, bf16[64,2176]{1,0:T(8,128)(2,1)S(1)}, u32[]{:S(2)}, u32[]{:S(2)}) collective-permute-start(bf16[64,2176]{1,0:T(8,128)(2,1)S(1)} %collective-permute-done.53), channel_id=1, source_target_pairs={{0,4},{4,8},{8,12},{12,14},{14,10},{10,6},{6,2},{2,0},{1,5},{5,9},... | collective-permute-start | bytes 835592 | tf_op jit(solution)/shard_map/ppermute | solution.py:69
  312.9 17.8 %collective-permute-start.57 = (bf16[64,2048]{1,0:T(8,128)(2,1)S(1)}, bf16[64,2048]{1,0:T(8,128)(2,1)S(1)}, u32[]{:S(2)}, u32[]{:S(2)}) collective-permute-start(bf16[64,2048]{1,0:T(8,128)(2,1)S(1)} %add_convert_fusion.20), channel_id=1, source_target_pairs={{0,4},{4,8},{8,12},{12,14},{14,10},{10,6},{6,2},{2,0},{1,5},{5,9},... | collective-permute-start | bytes 786440 | tf_op jit(solution)/shard_map/ppermute | solution.py:69
  313.7 17.5 %collective-permute-start.59 = (bf16[64,2176]{1,0:T(8,128)(2,1)S(1)}, bf16[64,2176]{1,0:T(8,128)(2,1)S(1)}, u32[]{:S(2)}, u32[]{:S(2)}) collective-permute-start(bf16[64,2176]{1,0:T(8,128)(2,1)S(1)} %collective-permute-done.54), channel_id=1, source_target_pairs={{4,0},{8,4},{12,8},{14,12},{10,14},{6,10},{2,6},{0,2},{5,1},{9,5},... | collective-permute-start | bytes 835592 | tf_op jit(solution)/shard_map/ppermute | solution.py:69
  330.8 18.9 %collective-permute-start.67 = (bf16[64,2048]{1,0:T(8,128)(2,1)S(1)}, bf16[64,2048]{1,0:T(8,128)(2,1)S(1)}, u32[]{:S(2)}, u32[]{:S(2)}) collective-permute-start(bf16[64,2048]{1,0:T(8,128)(2,1)S(1)} %get-tuple-element.255), channel_id=1, source_target_pairs={{4,0},{8,4},{12,8},{14,12},{10,14},{6,10},{2,6},{0,2},{5,1},{9,5},... | collective-permute-start | bytes 786440 | tf_op jit(solution)/shard_map/ppermute | solution.py:69
  331.2 19.3 %collective-permute-start.61 = (bf16[64,2176]{1,0:T(8,128)(2,1)S(1)}, bf16[64,2176]{1,0:T(8,128)(2,1)S(1)}, u32[]{:S(2)}, u32[]{:S(2)}) collective-permute-start(bf16[64,2176]{1,0:T(8,128)(2,1)S(1)} %collective-permute-done.58), channel_id=1, source_target_pairs={{0,4},{4,8},{8,12},{12,14},{14,10},{10,6},{6,2},{2,0},{1,5},{5,9},... | collective-permute-start | bytes 835592 | tf_op jit(solution)/shard_map/ppermute | solution.py:69
  332.9 16.8 %collective-permute-start.60 = (bf16[64,2048]{1,0:T(8,128)(2,1)S(1)}, bf16[64,2048]{1,0:T(8,128)(2,1)S(1)}, u32[]{:S(2)}, u32[]{:S(2)}) collective-permute-start(bf16[64,2048]{1,0:T(8,128)(2,1)S(1)} %get-tuple-element.232), channel_id=1, source_target_pairs={{0,4},{4,8},{8,12},{12,14},{14,10},{10,6},{6,2},{2,0},{1,5},{5,9},... | collective-permute-start | bytes 786440 | tf_op jit(solution)/shard_map/ppermute | solution.py:69
  377.9 9.7 %collective-permute-start.64 = (bf16[512,2048]{1,0:T(8,128)(2,1)}, bf16[512,2048]{1,0:T(8,128)(2,1)}, u32[]{:S(2)}, u32[]{:S(2)}) collective-permute-start(bf16[512,2048]{1,0:T(8,128)(2,1)} %get-tuple-element.252), channel_id=1, source_target_pairs={{0,1},{1,0},{2,3},{3,2},{4,5},{5,4},{6,7},{7,6},{8,9},{9,8},{10,11... | collective-permute-start | bytes 6291464 | tf_op jit(solution)/shard_map/ppermute | solution.py:69
  379.9 121.5 %collective-permute-start.68 = (bf16[64,2048]{1,0:T(8,128)(2,1)}, bf16[64,2048]{1,0:T(8,128)(2,1)}, u32[]{:S(2)}, u32[]{:S(2)}) collective-permute-start(bf16[64,2048]{1,0:T(8,128)(2,1)} %get-tuple-element.256), channel_id=1, source_target_pairs={{4,0},{8,4},{12,8},{14,12},{10,14},{6,10},{2,6},{0,2},{5,1},{9,5},... | collective-permute-start | bytes 786440 | tf_op jit(solution)/shard_map/ppermute | solution.py:69
  381.3 26.7 %collective-permute-start.71 = (bf16[1024,256]{1,0:T(8,128)(2,1)}, bf16[1024,256]{1,0:T(8,128)(2,1)S(1)}, u32[]{:S(2)}, u32[]{:S(2)}) collective-permute-start(bf16[1024,256]{1,0:T(8,128)(2,1)} %shard_map.292), channel_id=1, source_target_pairs={{0,16},{16,0},{1,17},{17,1},{2,18},{18,2},{3,19},{19,3},{4,20},{20... | collective-permute-start | bytes 1572872 | tf_op jit(solution)/shard_map/ppermute | solution.py:69
  387.0 41.2 %collective-permute-start.74 = (bf16[1024,512]{1,0:T(8,128)(2,1)}, bf16[1024,512]{1,0:T(8,128)(2,1)}, u32[]{:S(2)}, u32[]{:S(2)}) collective-permute-start(bf16[1024,512]{1,0:T(8,128)(2,1)} %shard_map.294), channel_id=1, source_target_pairs={{0,16},{16,0},{1,17},{17,1},{2,18},{18,2},{3,19},{19,3},{4,20},{20... | collective-permute-start | bytes 3145736 | tf_op jit(solution)/shard_map/ppermute | solution.py:69
  390.8 19.2 %collective-permute-start.70 = (bf16[64,2048]{1,0:T(8,128)(2,1)S(1)}, bf16[64,2048]{1,0:T(8,128)(2,1)S(1)}, u32[]{:S(2)}, u32[]{:S(2)}) collective-permute-start(bf16[64,2048]{1,0:T(8,128)(2,1)S(1)} %get-tuple-element.403), channel_id=1, source_target_pairs={{0,4},{4,8},{8,12},{12,14},{14,10},{10,6},{6,2},{2,0},{1,5},{5,9},... | collective-permute-start | bytes 786440 | tf_op jit(solution)/shard_map/ppermute | solution.py:69
  391.6 18.4 %collective-permute-start.65 = (bf16[64,2048]{1,0:T(8,128)(2,1)S(1)}, bf16[64,2048]{1,0:T(8,128)(2,1)S(1)}, u32[]{:S(2)}, u32[]{:S(2)}) collective-permute-start(bf16[64,2048]{1,0:T(8,128)(2,1)S(1)} %get-tuple-element.253), channel_id=1, source_target_pairs={{0,4},{4,8},{8,12},{12,14},{14,10},{10,6},{6,2},{2,0},{1,5},{5,9},... | collective-permute-start | bytes 786440 | tf_op jit(solution)/shard_map/ppermute | solution.py:69
  408.0 25.6 %collective-permute-start.81 = (bf16[64,2048]{1,0:T(8,128)(2,1)}, bf16[64,2048]{1,0:T(8,128)(2,1)}, u32[]{:S(2)}, u32[]{:S(2)}) collective-permute-start(bf16[64,2048]{1,0:T(8,128)(2,1)} %get-tuple-element.402), channel_id=1, source_target_pairs={{4,0},{8,4},{12,8},{14,12},{10,14},{6,10},{2,6},{0,2},{5,1},{9,5},... | collective-permute-start | bytes 786440 | tf_op jit(solution)/shard_map/ppermute | solution.py:69
  410.1 23.5 %collective-permute-start.72 = (bf16[64,2048]{1,0:T(8,128)(2,1)S(1)}, bf16[64,2048]{1,0:T(8,128)(2,1)}, u32[]{:S(2)}, u32[]{:S(2)}) collective-permute-start(bf16[64,2048]{1,0:T(8,128)(2,1)S(1)} %add_convert_fusion.14), channel_id=1, source_target_pairs={{0,4},{4,8},{8,12},{12,14},{14,10},{10,6},{6,2},{2,0},{1,5},{5,9},... | collective-permute-start | bytes 786440 | tf_op jit(solution)/shard_map/ppermute | solution.py:69
  411.6 22.1 %collective-permute-start.73 = (bf16[1024,256]{1,0:T(8,128)(2,1)S(1)}, bf16[1024,256]{1,0:T(8,128)(2,1)}, u32[]{:S(2)}, u32[]{:S(2)}) collective-permute-start(bf16[1024,256]{1,0:T(8,128)(2,1)S(1)} %add_convert_fusion.4.refs_0_), channel_id=1, source_target_pairs={{4,0},{8,4},{12,8},{14,12},{10,14},{6,10},{2,6},{0,2},{5,1},{9,5},... | collective-permute-start | bytes 1572872 | tf_op jit(solution)/shard_map/ppermute | solution.py:69
  428.2 15.0 %collective-permute-start.76 = (bf16[1024,256]{1,0:T(8,128)(2,1)S(1)}, bf16[1024,256]{1,0:T(8,128)(2,1)}, u32[]{:S(2)}, u32[]{:S(2)}) collective-permute-start(bf16[1024,256]{1,0:T(8,128)(2,1)S(1)} %add_convert_fusion.4.refs_0_), channel_id=1, source_target_pairs={{0,4},{4,8},{8,12},{12,14},{14,10},{10,6},{6,2},{2,0},{1,5},{5,9},... | collective-permute-start | bytes 1572872 | tf_op jit(solution)/shard_map/ppermute | solution.py:69
  435.6 22.8 %collective-permute-start.75 = (bf16[64,2048]{1,0:T(8,128)(2,1)}, bf16[64,2048]{1,0:T(8,128)(2,1)}, u32[]{:S(2)}, u32[]{:S(2)}) collective-permute-start(bf16[64,2048]{1,0:T(8,128)(2,1)} %get-tuple-element.400), channel_id=1, source_target_pairs={{0,4},{4,8},{8,12},{12,14},{14,10},{10,6},{6,2},{2,0},{1,5},{5,9},... | collective-permute-start | bytes 786440 | tf_op jit(solution)/shard_map/ppermute | solution.py:69
  436.1 20.7 %collective-permute-start.82 = (bf16[64,2048]{1,0:T(8,128)(2,1)}, bf16[64,2048]{1,0:T(8,128)(2,1)}, u32[]{:S(2)}, u32[]{:S(2)}) collective-permute-start(bf16[64,2048]{1,0:T(8,128)(2,1)} %get-tuple-element.401), channel_id=1, source_target_pairs={{4,0},{8,4},{12,8},{14,12},{10,14},{6,10},{2,6},{0,2},{5,1},{9,5},... | collective-permute-start | bytes 786440 | tf_op jit(solution)/shard_map/ppermute | solution.py:69
  443.2 15.2 %collective-permute-start.77 = (bf16[1024,256]{1,0:T(8,128)(2,1)}, bf16[1024,256]{1,0:T(8,128)(2,1)}, u32[]{:S(2)}, u32[]{:S(2)}) collective-permute-start(bf16[1024,256]{1,0:T(8,128)(2,1)} %collective-permute-done.73.refs_2_), channel_id=1, source_target_pairs={{4,0},{8,4},{12,8},{14,12},{10,14},{6,10},{2,6},{0,2},{5,1},{9,5},... | collective-permute-start | bytes 1572872 | tf_op jit(solution)/shard_map/ppermute | solution.py:69
  444.4 15.1 %collective-permute-start.79 = (bf16[1024,256]{1,0:T(8,128)(2,1)}, bf16[1024,256]{1,0:T(8,128)(2,1)}, u32[]{:S(2)}, u32[]{:S(2)}) collective-permute-start(bf16[1024,256]{1,0:T(8,128)(2,1)} %collective-permute-done.76.refs_1_), channel_id=1, source_target_pairs={{0,4},{4,8},{8,12},{12,14},{14,10},{10,6},{6,2},{2,0},{1,5},{5,9},... | collective-permute-start | bytes 1572872 | tf_op jit(solution)/shard_map/ppermute | solution.py:69
  456.9 9.3 %collective-permute-start.90 = (bf16[512,256]{1,0:T(8,128)(2,1)S(1)}, bf16[512,256]{1,0:T(8,128)(2,1)S(1)}, u32[]{:S(2)}, u32[]{:S(2)}) collective-permute-start(bf16[512,256]{1,0:T(8,128)(2,1)S(1)} %copy-done.23), channel_id=1, source_target_pairs={{0,4},{2,6},{4,0},{6,2},{8,12},{10,14},{12,8},{14,10},{1,5},{3,7},... | collective-permute-start | bytes 786440 | tf_op jit(solution)/shard_map/ppermute | solution.py:69
  459.5 17.3 %collective-permute-start.80 = (bf16[1024,256]{1,0:T(8,128)(2,1)}, bf16[1024,256]{1,0:T(8,128)(2,1)S(1)}, u32[]{:S(2)}, u32[]{:S(2)}) collective-permute-start(bf16[1024,256]{1,0:T(8,128)(2,1)} %collective-permute-done.77.refs_4_), channel_id=1, source_target_pairs={{4,0},{8,4},{12,8},{14,12},{10,14},{6,10},{2,6},{0,2},{5,1},{9,5},... | collective-permute-start | bytes 1572872 | tf_op jit(solution)/shard_map/ppermute | solution.py:69
  461.3 15.5 %collective-permute-start.78 = (bf16[64,2048]{1,0:T(8,128)(2,1)S(1)}, bf16[64,2048]{1,0:T(8,128)(2,1)S(1)}, u32[]{:S(2)}, u32[]{:S(2)}) collective-permute-start(bf16[64,2048]{1,0:T(8,128)(2,1)S(1)} %get-tuple-element.398), channel_id=1, source_target_pairs={{0,4},{4,8},{8,12},{12,14},{14,10},{10,6},{6,2},{2,0},{1,5},{5,9},... | collective-permute-start | bytes 786440 | tf_op jit(solution)/shard_map/ppermute | solution.py:69
  461.7 15.1 %collective-permute-start.83 = (bf16[64,2048]{1,0:T(8,128)(2,1)S(1)}, bf16[64,2048]{1,0:T(8,128)(2,1)S(1)}, u32[]{:S(2)}, u32[]{:S(2)}) collective-permute-start(bf16[64,2048]{1,0:T(8,128)(2,1)S(1)} %get-tuple-element.399), channel_id=1, source_target_pairs={{4,0},{8,4},{12,8},{14,12},{10,14},{6,10},{2,6},{0,2},{5,1},{9,5},... | collective-permute-start | bytes 786440 | tf_op jit(solution)/shard_map/ppermute | solution.py:69
  466.3 11.0 %collective-permute-start.91 = (bf16[256,256]{1,0:T(8,128)(2,1)S(1)}, bf16[256,256]{1,0:T(8,128)(2,1)S(1)}, u32[]{:S(2)}, u32[]{:S(2)}) collective-permute-start(bf16[256,256]{1,0:T(8,128)(2,1)S(1)} %dynamic-slice_convert_fusion.1), channel_id=1, source_target_pairs={{0,2},{2,0},{4,6},{6,4},{8,10},{10,8},{12,14},{14,12},{1,3},{3,1},... | collective-permute-start | bytes 393224 | tf_op jit(solution)/shard_map/ppermute | solution.py:69
  482.3 26.8 %collective-permute-start.93 = (bf16[1280,256]{1,0:T(8,128)(2,1)}, bf16[1280,256]{1,0:T(8,128)(2,1)}, u32[]{:S(2)}, u32[]{:S(2)}) collective-permute-start(bf16[1280,256]{1,0:T(8,128)(2,1)} %pad_maximum_fusion.3.refs_0_.refs_7_), channel_id=1, source_target_pairs={{4,0},{8,4},{12,8},{14,12},{10,14},{6,10},{2,6},{0,2},{5,1},{9,5},... | collective-permute-start | bytes 1966088 | tf_op jit(solution)/shard_map/ppermute | solution.py:69
  483.6 25.5 %collective-permute-start.92 = (bf16[1280,256]{1,0:T(8,128)(2,1)}, bf16[1280,256]{1,0:T(8,128)(2,1)}, u32[]{:S(2)}, u32[]{:S(2)}) collective-permute-start(bf16[1280,256]{1,0:T(8,128)(2,1)} %pad_maximum_fusion.3.refs_0_.refs_7_), channel_id=1, source_target_pairs={{0,4},{4,8},{8,12},{12,14},{14,10},{10,6},{6,2},{2,0},{1,5},{5,9},... | collective-permute-start | bytes 1966088 | tf_op jit(solution)/shard_map/ppermute | solution.py:69
  485.2 12.3 %collective-permute-start.87 = (f32[4352]{0:T(1024)S(1)}, f32[4352]{0:T(1024)S(1)}, u32[]{:S(2)}, u32[]{:S(2)}) collective-permute-start(f32[4352]{0:T(1024)S(1)} %add.328), channel_id=1, source_target_pairs={{0,8},{2,10},{4,12},{6,14},{8,0},{10,2},{12,4},{14,6},{1,9},{3,11}... | collective-permute-start | bytes 52232 | tf_op jit(solution)/shard_map/ppermute | solution.py:69
  496.4 9.5 %collective-permute-start.94 = (bf16[1024,256]{1,0:T(8,128)(2,1)}, bf16[1024,256]{1,0:T(8,128)(2,1)S(1)}, u32[]{:S(2)}, u32[]{:S(2)}) collective-permute-start(bf16[1024,256]{1,0:T(8,128)(2,1)} %collective-permute-done.79.refs_3_), channel_id=1, source_target_pairs={{0,4},{4,8},{8,12},{12,14},{14,10},{10,6},{6,2},{2,0},{1,5},{5,9},... | collective-permute-start | bytes 1572872 | tf_op jit(solution)/shard_map/ppermute | solution.py:69
  502.9 27.6 %collective-permute-start.69 = (bf16[64,2048]{1,0:T(8,128)(2,1)S(1)}, bf16[64,2048]{1,0:T(8,128)(2,1)S(1)}, u32[]{:S(2)}, u32[]{:S(2)}) collective-permute-start(bf16[64,2048]{1,0:T(8,128)(2,1)S(1)} %get-tuple-element.423), channel_id=1, source_target_pairs={{0,1},{1,0},{2,3},{3,2},{4,5},{5,4},{6,7},{7,6},{8,9},{9,8},{10,11... | collective-permute-start | bytes 786440 | tf_op jit(solution)/shard_map/ppermute | solution.py:69
  509.1 22.3 %collective-permute-start.84 = (f32[64,2048]{1,0:T(8,128)S(1)}, f32[64,2048]{1,0:T(8,128)S(1)}, u32[]{:S(2)}, u32[]{:S(2)}) collective-permute-start(f32[64,2048]{1,0:T(8,128)S(1)} %get-tuple-element.422), channel_id=1, source_target_pairs={{0,1},{1,0},{2,3},{3,2},{4,5},{5,4},{6,7},{7,6},{8,9},{9,8},{10,11... | collective-permute-start | bytes 1572872 | tf_op jit(solution)/shard_map/ppermute | solution.py:69
  513.6 20.5 %collective-permute-start.97 = (bf16[1280,256]{1,0:T(8,128)(2,1)}, bf16[1280,256]{1,0:T(8,128)(2,1)S(1)}, u32[]{:S(2)}, u32[]{:S(2)}) collective-permute-start(bf16[1280,256]{1,0:T(8,128)(2,1)} %collective-permute-done.92.refs_1_.refs_8_), channel_id=1, source_target_pairs={{0,4},{4,8},{8,12},{12,14},{14,10},{10,6},{6,2},{2,0},{1,5},{5,9},... | collective-permute-start | bytes 1966088 | tf_op jit(solution)/shard_map/ppermute | solution.py:69
  517.6 15.0 %collective-permute-start.99 = (f32[1024,128]{1,0:T(8,128)}, f32[1024,128]{1,0:T(8,128)S(1)}, u32[]{:S(2)}, u32[]{:S(2)}) collective-permute-start(f32[1024,128]{1,0:T(8,128)} %shard_map.300), channel_id=1, source_target_pairs={{0,16},{16,0},{1,17},{17,1},{2,18},{18,2},{3,19},{19,3},{4,20},{20... | collective-permute-start | bytes 1572872 | tf_op jit(solution)/shard_map/ppermute | solution.py:69
  519.5 14.6 %collective-permute-start.98 = (bf16[1280,256]{1,0:T(8,128)(2,1)}, bf16[1280,256]{1,0:T(8,128)(2,1)S(1)}, u32[]{:S(2)}, u32[]{:S(2)}) collective-permute-start(bf16[1280,256]{1,0:T(8,128)(2,1)} %collective-permute-done.93.refs_2_.refs_9_), channel_id=1, source_target_pairs={{4,0},{8,4},{12,8},{14,12},{10,14},{6,10},{2,6},{0,2},{5,1},{9,5},... | collective-permute-start | bytes 1966088 | tf_op jit(solution)/shard_map/ppermute | solution.py:69
  534.1 16.9 %collective-permute-start.100 = (bf16[1280,256]{1,0:T(8,128)(2,1)S(1)}, bf16[1280,256]{1,0:T(8,128)(2,1)S(1)}, u32[]{:S(2)}, u32[]{:S(2)}) collective-permute-start(bf16[1280,256]{1,0:T(8,128)(2,1)S(1)} %collective-permute-done.97.refs_3_.refs_10_), channel_id=1, source_target_pairs={{0,4},{4,8},{8,12},{12,14},{14,10},{10,6},{6,2},{2,0},{1,5},{5,9},... | collective-permute-start | bytes 1966088 | tf_op jit(solution)/shard_map/ppermute | solution.py:69
  536.8 14.1 %collective-permute-start.101 = (bf16[1280,256]{1,0:T(8,128)(2,1)S(1)}, bf16[1280,256]{1,0:T(8,128)(2,1)S(1)}, u32[]{:S(2)}, u32[]{:S(2)}) collective-permute-start(bf16[1280,256]{1,0:T(8,128)(2,1)S(1)} %collective-permute-done.98.refs_4_.refs_11_), channel_id=1, source_target_pairs={{4,0},{8,4},{12,8},{14,12},{10,14},{6,10},{2,6},{0,2},{5,1},{9,5},... | collective-permute-start | bytes 1966088 | tf_op jit(solution)/shard_map/ppermute | solution.py:69
  551.0 9.2 %collective-permute-start.102 = (bf16[640,256]{1,0:T(8,128)(2,1)S(1)}, bf16[640,256]{1,0:T(8,128)(2,1)S(1)}, u32[]{:S(2)}, u32[]{:S(2)}) collective-permute-start(bf16[640,256]{1,0:T(8,128)(2,1)S(1)} %slice.271), channel_id=1, source_target_pairs={{0,4},{4,8},{8,12},{12,14},{14,10},{10,6},{6,2},{2,0},{1,5},{5,9},... | collective-permute-start | bytes 983048 | tf_op jit(solution)/shard_map/ppermute | solution.py:69
  (92 other events, 729.7 us)

commit v5 on v4

--- a/solution.py
+++ b/solution.py
@@ -137,7 +137,7 @@
         return theirs, self.swap_halves(theirs)
 
     def sum_all(self, values):
-        for axis in ("ep", "fsdp", "tp"):
+        for axis in ("tp", "fsdp", "ep"):
             step = 1
             while step < lax.axis_size(axis):
                 pairs = [(i, i ^ step) for i in range(lax.axis_size(axis))]
@@ -1193,6 +1193,7 @@
         kv_share = kept + ring.send(sent.astype(BF16), pairs).astype(F32)
         step //= 2
     own_share = jnp.concatenate([qkv_share[:, :q_cols], kv_share], axis=0).astype(BF16)
+    own_share = after(own_share, made["out_walk"].found[-1])
 
     last = ring.ahead - 1
     lanes_at = width // LANES

time: 571 us -> 569 us (level)
    unnamed x139 -> x133, local copies, waits for them, and re-layouts: 27.4 us -> 26.4 us
  transfers between devices with their start and end apart: 104 -> 104, of which waited for: 38 -> 41; matrix products, arithmetic and copies ran while one was open for 12% -> 11% of each run, Pallas kernels for 34% -> 34%
where the time goes in v5:
time: 569 us; the launch traced here: 562 us
  Pallas kernels  228 us (40%)
  waiting for transfers between devices  142 us (25%)
  starting transfers between devices  100 us (18%)
  other arithmetic  46.6 us (8%)
  local copies, waits for them, and re-layouts  42.8 us (8%)
    ppermute x104, waiting for transfers between devices, send(): return lax.ppermute(values, axis, pairs)  142 us
    ppermute x104, starting transfers between devices, send(): return lax.ppermute(values, axis, pairs)  100 us
    pallas_call x1, Pallas kernels, experts(): call(functools.partial(experts_kernel, picks, expert_count), 41, grid_spe...  41.3 us
    pallas_call x3, Pallas kernels, gate_up_grad(): call(gate_up_grad_kernel, 11.7, grid=(width // wide,), in_specs=[pl.Block...  34.8 us
    pallas_call x2, Pallas kernels, other_experts(): call(functools.partial(other_experts_kernel, picks), 15, grid_spec=pltpu....  31.6 us
    unnamed x133, local copies, waits for them, and re-layouts  26.4 us
    pallas_call x6, Pallas kernels, transposed_product(): call(transposed_product_kernel, 4, grid_spec=pltpu.PrefetchScalarGridSpec...  21.7 us
    pallas_call x4, Pallas kernels, layer_part(): call(layer_kernel, 4, grid=(1,), in_specs=[pl.BlockSpec((rows // parts, h...  20.2 us
  transfers between devices with their start and end apart: 104, of which 41 were waited for; matrix products, arithmetic and copies ran while one was open for 11% of the time, Pallas kernels for 34%

profile of v5, /device:TPU:0, one launch (start us, length us, event | category | flops | bytes accessed | tf_op | source)
XLA Modules:
  0.0 562.1 jit_solution(5710478609613141282)
XLA Ops:
  3.6 3.0 collective-permute-start
  8.5 2.0 collective-permute-start.3
  11.1 3.3 shard_map.281.refs_0_
  15.9 2.0 collective-permute-start.2
  21.1 4.9 collective-permute-done.2
  34.9 1.9 fusion.17
  52.2 4.3 collective-permute-done.10
  63.0 3.0 collective-permute-done.17
  68.1 3.8 collective-permute-done.18.xo_ref.ao_ref
  71.9 7.3 %shard_map.282 = (f32[1024,384]{1,0:T(8,128)}, bf16[1024,256]{1,0:T(8,128)(2,1)}, bf16[1024,128]{1,0:T(8,128)(2,1)}, bf16[1024,128]{1,0:T(8,128)(2,1)}) custom-call(s32[2]{0:T(128)} %pad_add_fusion.at_ref, bf16[512,2048]{1,0:T(8,128)(2,1)} %constant_dynamic-update-slice_fusion.5.xm_ref.am_ref, bf16[512,2048]{1,0:T(8,128)(2,1)} %collective-permute-done.18.xo_ref.ao_ref, ...), custom_call_target="tpu_custom_call" | custom-call | flops 8049999872 | tf_op jit(solution)/shard_map/pallas_call | solution.py:321
  79.2 7.1 %shard_map.284 = (bf16[512,256]{1,0:T(8,128)(2,1)}, f32[2,512,1]{2,1,0:T(8,128)}, bf16[512,2048]{1,0:T(8,128)(2,1)}) custom-call(s32[2]{0:T(128)} %pad_add_fusion.at_ref, s32[1,1024]{1,0:T(1,128)} %and_select_fusion.1.pos_ref, s32[1024,1]{1,0:T(8,128)} %fusion.14.lim_ref, bf16[1024,256]{1,0:T(8,128)(2,1)} %get-tuple-element.187.ql_ref, ...), custom_call_target="tpu_custom_call" | custom-call | flops 7474999808 | tf_op jit(solution)/shard_map/pallas_call | solution.py:364
  88.8 7.1 %shard_map.283 = (bf16[512,256]{1,0:T(8,128)(2,1)}, f32[2,512,1]{2,1,0:T(8,128)}, bf16[512,2048]{1,0:T(8,128)(2,1)}) custom-call(s32[2]{0:T(128)} %pad_add_fusion.at_ref, s32[1,1024]{1,0:T(1,128)} %and_select_fusion.1.pos_ref, s32[1024,1]{1,0:T(8,128)} %fusion.14.lim_ref, bf16[1024,256]{1,0:T(8,128)(2,1)} %get-tuple-element.187.ql_ref, ...), custom_call_target="tpu_custom_call" | custom-call | flops 7474999808 | tf_op jit(solution)/shard_map/pallas_call | solution.py:364
  97.3 3.0 add_convert_fusion.3
  104.0 5.7 %collective-permute-done.20 = bf16[64,2048]{1,0:T(8,128)(2,1)S(1)} collective-permute-done((bf16[64,2048]{1,0:T(8,128)(2,1)S(1)}, bf16[64,2048]{1,0:T(8,128)(2,1)S(1)}, u32[]{:S(2)}, u32[]{:S(2)}) %collective-permute-start.20) | collective-permute-done | bytes 262176 | tf_op jit(solution)/shard_map/ppermute | solution.py:69
  116.9 4.8 collective-permute-done.21
  125.7 3.6 collective-permute-done.26
  133.8 4.5 collective-permute-done.24
  142.0 3.7 collective-permute-done.28
  148.1 5.5 collective-permute-done.30
  156.0 6.7 %collective-permute-done.32 = bf16[64,2048]{1,0:T(8,128)(2,1)S(1)} collective-permute-done((bf16[64,2048]{1,0:T(8,128)(2,1)S(1)}, bf16[64,2048]{1,0:T(8,128)(2,1)S(1)}, u32[]{:S(2)}, u32[]{:S(2)}) %collective-permute-start.32) | collective-permute-done | bytes 262176 | tf_op jit(solution)/shard_map/ppermute | solution.py:69
  164.3 5.0 collective-permute-done.34
  170.6 3.0 collective-permute-done.35.xo_ref.x1.ao_ref
  173.7 41.3 %shard_map.285 = (bf16[1024,1152]{1,0:T(8,128)(2,1)}, bf16[1024,2304]{1,0:T(8,128)(2,1)}, f32[1024,128]{1,0:T(8,128)}, bf16[512,2176]{1,0:T(8,128)(2,1)}, bf16[512,2176]{1,0:T(8,128)(2,1)}) custom-call(s32[2]{0:T(128)} %pad_add_fusion.2.first_ref, bf16[512,2048]{1,0:T(8,128)(2,1)} %copy-done.6, bf16[512,2048]{1,0:T(8,128)(2,1)} %collective-permute-done.35.xo_ref.x1.ao_ref, ...), custom_call_target="tpu_custom_call" | custom-call | flops 47149998080 | tf_op jit(solution)/shard_map/pallas_call | solution.py:582
  215.2 6.0 %collective-permute-done.37.g_ref.g2 = bf16[512,2176]{1,0:T(8,128)(2,1)} collective-permute-done((bf16[512,2176]{1,0:T(8,128)(2,1)}, bf16[512,2176]{1,0:T(8,128)(2,1)}, u32[]{:S(2)}, u32[]{:S(2)}) %collective-permute-start.37) | collective-permute-done | bytes 2228256 | tf_op jit(solution)/shard_map/ppermute | solution.py:69
  221.1 2.3 add_convert_fusion
  226.9 5.0 shard_map.286
  236.4 5.0 shard_map.287
  247.5 5.0 shard_map.288
  252.6 1.9 add_convert_fusion.5
  256.5 5.1 shard_map.289
  271.8 5.3 collective-permute-done.50
  278.7 2.6 collective-permute-done.55
  289.1 10.5 %collective-permute-done.52 = bf16[64,2048]{1,0:T(8,128)(2,1)S(1)} collective-permute-done((bf16[64,2048]{1,0:T(8,128)(2,1)S(1)}, bf16[64,2048]{1,0:T(8,128)(2,1)S(1)}, u32[]{:S(2)}, u32[]{:S(2)}) %collective-permute-start.52) | collective-permute-done | bytes 262176 | tf_op jit(solution)/shard_map/ppermute | solution.py:69
  304.3 15.7 %shard_map.290 = (bf16[512,1152]{1,0:T(8,128)(2,1)}, bf16[512,2304]{1,0:T(8,128)(2,1)}) custom-call(s32[2]{0:T(128)} %pad_add_fusion.2.first_ref, bf16[512,2048]{1,0:T(8,128)(2,1)} %copy-done.27, bf16[512,2176]{1,0:T(8,128)(2,1)} %collective-permute-done.37.g_ref.g2, bf16[3,2048,384]{2,1,0:T(8,128)(2,1)} %wg_ref.5, bf16[3,2048,384]{2,1,0:T(8,128)(2,1)} %wu_ref.5, ...), custom_call_target="tpu_custom_call" | custom-call | flops 17250000896 | tf_op jit(solution)/shard_map/pallas_call | solution.py:683
  323.5 15.9 %shard_map.291 = (bf16[512,1152]{1,0:T(8,128)(2,1)}, bf16[512,2304]{1,0:T(8,128)(2,1)}) custom-call(s32[2]{0:T(128)} %pad_add_fusion.2.first_ref, bf16[512,2048]{1,0:T(8,128)(2,1)} %copy-done.43, bf16[512,2176]{1,0:T(8,128)(2,1)} %collective-permute-done.62.g_ref.g3, bf16[3,2048,384]{2,1,0:T(8,128)(2,1)} %wg_ref.5, bf16[3,2048,384]{2,1,0:T(8,128)(2,1)} %wu_ref.5, ...), custom_call_target="tpu_custom_call" | custom-call | flops 17250000896 | tf_op jit(solution)/shard_map/pallas_call | solution.py:683
  340.5 4.3 collective-permute-done.63.ao_ref.bo_ref
  346.3 3.3 shard_map.292
  349.6 18.1 %shard_map.293 = (bf16[512,512]{1,0:T(8,128)(2,1)}, bf16[512,512]{1,0:T(8,128)(2,1)}, f32[2,128]{1,0:T(2,128)}, bf16[512,2048]{1,0:T(8,128)(2,1)}, bf16[512,2048]{1,0:T(8,128)(2,1)}) custom-call(s32[2]{0:T(128)} %pad_add_fusion.at_ref, bf16[512,2176]{1,0:T(8,128)(2,1)} %copy-done.36, bf16[512,2176]{1,0:T(8,128)(2,1)} %copy-done.42, ...), custom_call_target="tpu_custom_call" | custom-call | flops 21275000832 | tf_op jit(solution)/shard_map/pallas_call | solution.py:467
  372.1 4.2 shard_map.294
  376.8 2.5 add_convert_fusion.1
  383.0 11.6 %shard_map.296 = (f32[3,2048,384]{2,1,0:T(8,128)}, f32[3,2048,384]{2,1,0:T(8,128)}, f32[8,128]{1,0:T(8,128)}) custom-call(bf16[512,2048]{1,0:T(8,128)(2,1)} %copy-done.6, bf16[512,2048]{1,0:T(8,128)(2,1)} %collective-permute-done.35.xo_ref.x1.ao_ref, bf16[512,2048]{1,0:T(8,128)(2,1)} %copy-done.27, bf16[512,2048]{1,0:T(8,128)(2,1)} %copy-done.43, ...), custom_call_target="tpu_custom_call" | custom-call | flops 13454999552 | tf_op jit(solution)/shard_map/pallas_call | solution.py:748
  394.6 3.4 shard_map.295
  401.9 11.6 %shard_map.298 = (f32[3,2048,384]{2,1,0:T(8,128)}, f32[3,2048,384]{2,1,0:T(8,128)}, f32[8,128]{1,0:T(8,128)}) custom-call(bf16[512,2048]{1,0:T(8,128)(2,1)} %copy-done.6, bf16[512,2048]{1,0:T(8,128)(2,1)} %collective-permute-done.35.xo_ref.x1.ao_ref, bf16[512,2048]{1,0:T(8,128)(2,1)} %copy-done.27, ...), custom_call_target="tpu_custom_call", output_to_operand_aliasing={{0}: (8, {}), {1}: (9, {})} | custom-call | flops 13454999552 | tf_op jit(solution)/shard_map/pallas_call | solution.py:748
  413.5 4.4 shard_map.297
  419.7 2.2 convert_add_fusion
  423.7 1.9 add_convert_fusion.13
  427.6 5.3 collective-permute-done.76.refs_1_
  435.0 11.6 %shard_map.299 = (f32[3,2048,384]{2,1,0:T(8,128)}, f32[3,2048,384]{2,1,0:T(8,128)}, f32[8,128]{1,0:T(8,128)}) custom-call(bf16[512,2048]{1,0:T(8,128)(2,1)} %copy-done.6, bf16[512,2048]{1,0:T(8,128)(2,1)} %collective-permute-done.35.xo_ref.x1.ao_ref, bf16[512,2048]{1,0:T(8,128)(2,1)} %copy-done.27, ...), custom_call_target="tpu_custom_call", output_to_operand_aliasing={{0}: (8, {}), {1}: (9, {})} | custom-call | flops 13454999552 | tf_op jit(solution)/shard_map/pallas_call | solution.py:748
  452.7 3.2 collective-permute-done.90
  456.1 10.5 %collective-permute-done.83 = bf16[64,2048]{1,0:T(8,128)(2,1)S(1)} collective-permute-done((bf16[64,2048]{1,0:T(8,128)(2,1)S(1)}, bf16[64,2048]{1,0:T(8,128)(2,1)S(1)}, u32[]{:S(2)}, u32[]{:S(2)}) %collective-permute-start.83) | collective-permute-done | bytes 262176 | tf_op jit(solution)/shard_map/ppermute | solution.py:69
  470.8 2.2 collective-permute-start.92
  473.1 4.9 collective-permute-done.94.refs_5_
  480.2 9.7 %shard_map.305 = (f32[3,384,2048]{2,1,0:T(8,128)}, f32[8,128]{1,0:T(8,128)}) custom-call(bf16[1024,1152]{1,0:T(8,128)(2,1)} %get-tuple-element.319.w_ref.w0.w1, bf16[1024,1152]{1,0:T(8,128)(2,1)} %get-tuple-element.319.w_ref.w0.w1, bf16[512,2176]{1,0:T(8,128)(2,1)} %constant_dynamic-update-slice_fusion.25.gm_ref.g0, ...), custom_call_target="tpu_custom_call" | custom-call | flops 11155000320 | tf_op jit(solution)/shard_map/pallas_call | solution.py:782
  489.9 6.2 %collective-permute-done.87 = f32[4352]{0:T(1024)S(1)} collective-permute-done((f32[4352]{0:T(1024)S(1)}, f32[4352]{0:T(1024)S(1)}, u32[]{:S(2)}, u32[]{:S(2)}) %collective-permute-start.87) | collective-permute-done | bytes 17440 | tf_op jit(solution)/shard_map/ppermute | solution.py:69
  496.1 3.9 collective-permute-done.88
  502.8 3.2 collective-permute-done.89
  512.2 3.2 shard_map.300
  518.1 9.7 %shard_map.306 = (f32[3,384,2048]{2,1,0:T(8,128)}, f32[8,128]{1,0:T(8,128)}) custom-call(bf16[1024,1152]{1,0:T(8,128)(2,1)} %get-tuple-element.319.w_ref.w0.w1, bf16[1024,1152]{1,0:T(8,128)(2,1)} %get-tuple-element.319.w_ref.w0.w1, bf16[512,2176]{1,0:T(8,128)(2,1)} %constant_dynamic-update-slice_fusion.25.gm_ref.g0, ...), custom_call_target="tpu_custom_call", output_to_operand_aliasing={{0}: (8, {})} | custom-call | flops 11155000320 | tf_op jit(solution)/shard_map/pallas_call | solution.py:782
  529.2 4.1 collective-permute-done.98.refs_4_.refs_11_
  535.4 3.2 shard_map.301
  540.5 6.0 %shard_map.302 = f32[1024,2048]{1,0:T(8,128)} custom-call(s32[8]{0:T(128)} %get-tuple-element.443.owners_ref, bf16[1024,256]{1,0:T(8,128)(2,1)} %copy-done.14, bf16[1024,256]{1,0:T(8,128)(2,1)} %collective-permute-done.76.refs_1_, bf16[1024,256]{1,0:T(8,128)(2,1)} %collective-permute-done.73.refs_2_, bf16[1024,256]{1,0:T(8,128)(2,1)} %collective-permute-done.79.refs_3_, ...), custom_call_target="tpu_custom_call" | custom-call | flops 4600000000 | tf_op jit(solution)/shard_map/pallas_call | solution.py:824
  546.5 2.2 collective-permute-done.100.refs_5_.refs_12_
  551.2 7.2 %shard_map.303 = (f32[1024,2048]{1,0:T(8,128)}, f32[1024,256]{1,0:T(8,128)}, f32[1024,256]{1,0:T(8,128)}) custom-call(s32[8]{0:T(128)} %get-tuple-element.443.owners_ref, bf16[1280,256]{1,0:T(8,128)(2,1)} %pad_maximum_fusion.3.refs_0_.refs_7_, bf16[1280,256]{1,0:T(8,128)(2,1)} %collective-permute-done.92.refs_1_.refs_8_, ...), custom_call_target="tpu_custom_call" | custom-call | flops 5750000128 | tf_op jit(solution)/shard_map/pallas_call | solution.py:862
  559.2 2.7 shard_map.304
  (423 shorter events, 176.7 us)
Async XLA Ops:
  3.6 15.8 %collective-permute-start = (bf16[64,2048]{1,0:T(8,128)(2,1)S(1)}, bf16[64,2048]{1,0:T(8,128)(2,1)}, u32[]{:S(2)}, u32[]{:S(2)}) collective-permute-start(bf16[64,2048]{1,0:T(8,128)(2,1)S(1)} %get-tuple-element.389), channel_id=1, source_target_pairs={{0,4},{4,8},{8,12},{12,14},{14,10},{10,6},{6,2},{2,0},{1,5},{5,9},... | collective-permute-start | bytes 786440 | tf_op jit(solution)/shard_map/ppermute | solution.py:69
  6.6 14.5 %collective-permute-start.1 = (bf16[64,2048]{1,0:T(8,128)(2,1)S(1)}, bf16[64,2048]{1,0:T(8,128)(2,1)}, u32[]{:S(2)}, u32[]{:S(2)}) collective-permute-start(bf16[64,2048]{1,0:T(8,128)(2,1)S(1)} %get-tuple-element.389), channel_id=1, source_target_pairs={{4,0},{8,4},{12,8},{14,12},{10,14},{6,10},{2,6},{0,2},{5,1},{9,5},... | collective-permute-start | bytes 786440 | tf_op jit(solution)/shard_map/ppermute | solution.py:69
  8.5 12.6 %collective-permute-start.3 = (bf16[64,2176]{1,0:T(8,128)(2,1)S(1)}, bf16[64,2176]{1,0:T(8,128)(2,1)S(1)}, u32[]{:S(2)}, u32[]{:S(2)}) collective-permute-start(bf16[64,2176]{1,0:T(8,128)(2,1)S(1)} %get-tuple-element.431), channel_id=1, source_target_pairs={{0,4},{4,8},{8,12},{12,14},{14,10},{10,6},{6,2},{2,0},{1,5},{5,9},... | collective-permute-start | bytes 835592 | tf_op jit(solution)/shard_map/ppermute | solution.py:69
  10.5 19.4 %collective-permute-start.7 = (bf16[64,2176]{1,0:T(8,128)(2,1)S(1)}, bf16[64,2176]{1,0:T(8,128)(2,1)}, u32[]{:S(2)}, u32[]{:S(2)}) collective-permute-start(bf16[64,2176]{1,0:T(8,128)(2,1)S(1)} %get-tuple-element.431), channel_id=1, source_target_pairs={{4,0},{8,4},{12,8},{14,12},{10,14},{6,10},{2,6},{0,2},{5,1},{9,5},... | collective-permute-start | bytes 835592 | tf_op jit(solution)/shard_map/ppermute | solution.py:69
  15.9 10.1 %collective-permute-start.2 = (bf16[256,768]{1,0:T(8,128)(2,1)S(1)}, bf16[256,768]{1,0:T(8,128)(2,1)S(1)}, u32[]{:S(2)}, u32[]{:S(2)}) collective-permute-start(bf16[256,768]{1,0:T(8,128)(2,1)S(1)} %get-tuple-element.421), channel_id=1, source_target_pairs={{0,16},{16,0},{1,17},{17,1},{2,18},{18,2},{3,19},{19,3},{4,20},{20... | collective-permute-start | bytes 1179656 | tf_op jit(solution)/shard_map/ppermute | solution.py:69
  26.0 15.7 %collective-permute-start.4 = (bf16[64,2048]{1,0:T(8,128)(2,1)}, bf16[64,2048]{1,0:T(8,128)(2,1)}, u32[]{:S(2)}, u32[]{:S(2)}) collective-permute-start(bf16[64,2048]{1,0:T(8,128)(2,1)} %collective-permute-done), channel_id=1, source_target_pairs={{0,4},{4,8},{8,12},{12,14},{14,10},{10,6},{6,2},{2,0},{1,5},{5,9},... | collective-permute-start | bytes 786440 | tf_op jit(solution)/shard_map/ppermute | solution.py:69
  30.0 13.3 %collective-permute-start.8 = (bf16[64,2176]{1,0:T(8,128)(2,1)S(1)}, bf16[64,2176]{1,0:T(8,128)(2,1)}, u32[]{:S(2)}, u32[]{:S(2)}) collective-permute-start(bf16[64,2176]{1,0:T(8,128)(2,1)S(1)} %collective-permute-done.3), channel_id=1, source_target_pairs={{0,4},{4,8},{8,12},{12,14},{14,10},{10,6},{6,2},{2,0},{1,5},{5,9},... | collective-permute-start | bytes 835592 | tf_op jit(solution)/shard_map/ppermute | solution.py:69
  31.6 13.3 %collective-permute-start.12 = (bf16[64,2176]{1,0:T(8,128)(2,1)}, bf16[64,2176]{1,0:T(8,128)(2,1)}, u32[]{:S(2)}, u32[]{:S(2)}) collective-permute-start(bf16[64,2176]{1,0:T(8,128)(2,1)} %collective-permute-done.7), channel_id=1, source_target_pairs={{4,0},{8,4},{12,8},{14,12},{10,14},{6,10},{2,6},{0,2},{5,1},{9,5},... | collective-permute-start | bytes 835592 | tf_op jit(solution)/shard_map/ppermute | solution.py:69
  32.1 11.3 %collective-permute-start.6 = (bf16[256,768]{1,0:T(8,128)(2,1)S(1)}, bf16[256,768]{1,0:T(8,128)(2,1)S(1)}, u32[]{:S(2)}, u32[]{:S(2)}) collective-permute-start(bf16[256,768]{1,0:T(8,128)(2,1)S(1)} %get-tuple-element.173), channel_id=1, source_target_pairs={{0,16},{16,0},{1,17},{17,1},{2,18},{18,2},{3,19},{19,3},{4,20},{20... | collective-permute-start | bytes 1179656 | tf_op jit(solution)/shard_map/ppermute | solution.py:69
  33.6 9.7 %collective-permute-start.5 = (bf16[64,2048]{1,0:T(8,128)(2,1)}, bf16[64,2048]{1,0:T(8,128)(2,1)}, u32[]{:S(2)}, u32[]{:S(2)}) collective-permute-start(bf16[64,2048]{1,0:T(8,128)(2,1)} %collective-permute-done.1), channel_id=1, source_target_pairs={{4,0},{8,4},{12,8},{14,12},{10,14},{6,10},{2,6},{0,2},{5,1},{9,5},... | collective-permute-start | bytes 786440 | tf_op jit(solution)/shard_map/ppermute | solution.py:69
  43.3 13.2 %collective-permute-start.9 = (bf16[64,2048]{1,0:T(8,128)(2,1)}, bf16[64,2048]{1,0:T(8,128)(2,1)S(1)}, u32[]{:S(2)}, u32[]{:S(2)}) collective-permute-start(bf16[64,2048]{1,0:T(8,128)(2,1)} %collective-permute-done.4), channel_id=1, source_target_pairs={{0,4},{4,8},{8,12},{12,14},{14,10},{10,6},{6,2},{2,0},{1,5},{5,9},... | collective-permute-start | bytes 786440 | tf_op jit(solution)/shard_map/ppermute | solution.py:69
  44.9 11.6 %collective-permute-start.13 = (bf16[64,2176]{1,0:T(8,128)(2,1)}, bf16[64,2176]{1,0:T(8,128)(2,1)S(1)}, u32[]{:S(2)}, u32[]{:S(2)}) collective-permute-start(bf16[64,2176]{1,0:T(8,128)(2,1)} %collective-permute-done.8), channel_id=1, source_target_pairs={{0,4},{4,8},{8,12},{12,14},{14,10},{10,6},{6,2},{2,0},{1,5},{5,9},... | collective-permute-start | bytes 835592 | tf_op jit(solution)/shard_map/ppermute | solution.py:69
  46.4 10.7 %collective-permute-start.16 = (bf16[64,2176]{1,0:T(8,128)(2,1)}, bf16[64,2176]{1,0:T(8,128)(2,1)S(1)}, u32[]{:S(2)}, u32[]{:S(2)}) collective-permute-start(bf16[64,2176]{1,0:T(8,128)(2,1)} %collective-permute-done.12), channel_id=1, source_target_pairs={{4,0},{8,4},{12,8},{14,12},{10,14},{6,10},{2,6},{0,2},{5,1},{9,5},... | collective-permute-start | bytes 835592 | tf_op jit(solution)/shard_map/ppermute | solution.py:69
  46.9 9.6 %collective-permute-start.11 = (bf16[256,768]{1,0:T(8,128)(2,1)S(1)}, bf16[256,768]{1,0:T(8,128)(2,1)S(1)}, u32[]{:S(2)}, u32[]{:S(2)}) collective-permute-start(bf16[256,768]{1,0:T(8,128)(2,1)S(1)} %get-tuple-element.178), channel_id=1, source_target_pairs={{0,16},{16,0},{1,17},{17,1},{2,18},{18,2},{3,19},{19,3},{4,20},{20... | collective-permute-start | bytes 1179656 | tf_op jit(solution)/shard_map/ppermute | solution.py:69
  86.3 9.7 %collective-permute-start.19 = (bf16[512,2048]{1,0:T(8,128)(2,1)}, bf16[512,2048]{1,0:T(8,128)(2,1)S(1)}, u32[]{:S(2)}, u32[]{:S(2)}) collective-permute-start(bf16[512,2048]{1,0:T(8,128)(2,1)} %get-tuple-element.191), channel_id=1, source_target_pairs={{0,1},{1,0},{2,3},{3,2},{4,5},{5,4},{6,7},{7,6},{8,9},{9,8},{10,11... | collective-permute-start | bytes 6291464 | tf_op jit(solution)/shard_map/ppermute | solution.py:69
  142.0 28.7 %collective-permute-start.36 = (bf16[512,2176]{1,0:T(8,128)(2,1)}, bf16[512,2176]{1,0:T(8,128)(2,1)}, u32[]{:S(2)}, u32[]{:S(2)}) collective-permute-start(bf16[512,2176]{1,0:T(8,128)(2,1)} %constant_dynamic-update-slice_fusion.25.gm_ref.g0), channel_id=1, source_target_pairs={{0,1},{1,0},{2,3},{3,2},{4,5},{5,4},{6,7},{7,6},{8,9},{9,8},{10,11... | collective-permute-start | bytes 6684680 | tf_op jit(solution)/shard_map/ppermute | solution.py:69
  170.1 51.0 %collective-permute-start.37 = (bf16[512,2176]{1,0:T(8,128)(2,1)}, bf16[512,2176]{1,0:T(8,128)(2,1)}, u32[]{:S(2)}, u32[]{:S(2)}) collective-permute-start(bf16[512,2176]{1,0:T(8,128)(2,1)} %constant_dynamic-update-slice_fusion.25.gm_ref.g0), channel_id=1, source_target_pairs={{0,16},{16,0},{1,17},{17,1},{2,18},{18,2},{3,19},{19,3},{4,20},{20... | collective-permute-start | bytes 6684680 | tf_op jit(solution)/shard_map/ppermute | solution.py:69
  225.7 17.2 %collective-permute-start.41 = (bf16[128,2048]{1,0:T(8,128)(2,1)}, bf16[128,2048]{1,0:T(8,128)(2,1)}, u32[]{:S(2)}, u32[]{:S(2)}) collective-permute-start(bf16[128,2048]{1,0:T(8,128)(2,1)} %slice.230), channel_id=1, source_target_pairs={{0,16},{16,0},{1,17},{17,1},{2,18},{18,2},{3,19},{19,3},{4,20},{20... | collective-permute-start | bytes 1572872 | tf_op jit(solution)/shard_map/ppermute | solution.py:69
  226.2 15.2 %collective-permute-start.46 = (bf16[64,2176]{1,0:T(8,128)(2,1)S(1)}, bf16[64,2176]{1,0:T(8,128)(2,1)}, u32[]{:S(2)}, u32[]{:S(2)}) collective-permute-start(bf16[64,2176]{1,0:T(8,128)(2,1)S(1)} %get-tuple-element.398), channel_id=1, source_target_pairs={{4,0},{8,4},{12,8},{14,12},{10,14},{6,10},{2,6},{0,2},{5,1},{9,5},... | collective-permute-start | bytes 835592 | tf_op jit(solution)/shard_map/ppermute | solution.py:69
  232.7 10.2 %collective-permute-start.40 = (bf16[64,2176]{1,0:T(8,128)(2,1)}, bf16[64,2176]{1,0:T(8,128)(2,1)}, u32[]{:S(2)}, u32[]{:S(2)}) collective-permute-start(bf16[64,2176]{1,0:T(8,128)(2,1)} %add_convert_fusion.9), channel_id=1, source_target_pairs={{0,4},{4,8},{8,12},{12,14},{14,10},{10,6},{6,2},{2,0},{1,5},{5,9},... | collective-permute-start | bytes 835592 | tf_op jit(solution)/shard_map/ppermute | solution.py:69
  234.9 17.7 %collective-permute-start.43 = (bf16[128,2048]{1,0:T(8,128)(2,1)}, bf16[128,2048]{1,0:T(8,128)(2,1)}, u32[]{:S(2)}, u32[]{:S(2)}) collective-permute-start(bf16[128,2048]{1,0:T(8,128)(2,1)} %slice.232), channel_id=1, source_target_pairs={{0,16},{16,0},{1,17},{17,1},{2,18},{18,2},{3,19},{19,3},{4,20},{20... | collective-permute-start | bytes 1572872 | tf_op jit(solution)/shard_map/ppermute | solution.py:69
  247.0 16.0 %collective-permute-start.45 = (bf16[128,2048]{1,0:T(8,128)(2,1)}, bf16[128,2048]{1,0:T(8,128)(2,1)}, u32[]{:S(2)}, u32[]{:S(2)}) collective-permute-start(bf16[128,2048]{1,0:T(8,128)(2,1)} %slice.235), channel_id=1, source_target_pairs={{0,16},{16,0},{1,17},{17,1},{2,18},{18,2},{3,19},{19,3},{4,20},{20... | collective-permute-start | bytes 1572872 | tf_op jit(solution)/shard_map/ppermute | solution.py:69
  266.9 14.4 %collective-permute-start.55 = (bf16[128,2048]{1,0:T(8,128)(2,1)S(1)}, bf16[128,2048]{1,0:T(8,128)(2,1)S(1)}, u32[]{:S(2)}, u32[]{:S(2)}) collective-permute-start(bf16[128,2048]{1,0:T(8,128)(2,1)S(1)} %slice.248), channel_id=1, source_target_pairs={{0,16},{16,0},{1,17},{17,1},{2,18},{18,2},{3,19},{19,3},{4,20},{20... | collective-permute-start | bytes 1572872 | tf_op jit(solution)/shard_map/ppermute | solution.py:69
  284.6 15.9 %collective-permute-start.56 = (bf16[512,2048]{1,0:T(8,128)(2,1)S(1)}, bf16[512,2048]{1,0:T(8,128)(2,1)S(1)}, u32[]{:S(2)}, u32[]{:S(2)}) collective-permute-start(bf16[512,2048]{1,0:T(8,128)(2,1)S(1)} %constant_dynamic-update-slice_fusion.33.x_ref.x2), channel_id=1, source_target_pairs={{0,1},{1,0},{2,3},{3,2},{4,5},{5,4},{6,7},{7,6},{8,9},{9,8},{10,11... | collective-permute-start | bytes 6291464 | tf_op jit(solution)/shard_map/ppermute | solution.py:69
  284.7 37.5 %collective-permute-start.62 = (bf16[512,2176]{1,0:T(8,128)(2,1)}, bf16[512,2176]{1,0:T(8,128)(2,1)}, u32[]{:S(2)}, u32[]{:S(2)}) collective-permute-start(bf16[512,2176]{1,0:T(8,128)(2,1)} %collective-permute-done.37.g_ref.g2), channel_id=1, source_target_pairs={{0,1},{1,0},{2,3},{3,2},{4,5},{5,4},{6,7},{7,6},{8,9},{9,8},{10,11... | collective-permute-start | bytes 6684680 | tf_op jit(solution)/shard_map/ppermute | solution.py:69
  285.2 15.2 %collective-permute-start.53 = (bf16[64,2176]{1,0:T(8,128)(2,1)S(1)}, bf16[64,2176]{1,0:T(8,128)(2,1)S(1)}, u32[]{:S(2)}, u32[]{:S(2)}) collective-permute-start(bf16[64,2176]{1,0:T(8,128)(2,1)S(1)} %collective-permute-done.50), channel_id=1, source_target_pairs={{0,4},{4,8},{8,12},{12,14},{14,10},{10,6},{6,2},{2,0},{1,5},{5,9},... | collective-permute-start | bytes 835592 | tf_op jit(solution)/shard_map/ppermute | solution.py:69
  287.0 12.5 %collective-permute-start.52 = (bf16[64,2048]{1,0:T(8,128)(2,1)S(1)}, bf16[64,2048]{1,0:T(8,128)(2,1)S(1)}, u32[]{:S(2)}, u32[]{:S(2)}) collective-permute-start(bf16[64,2048]{1,0:T(8,128)(2,1)S(1)} %get-tuple-element.217), channel_id=1, source_target_pairs={{0,4},{4,8},{8,12},{12,14},{14,10},{10,6},{6,2},{2,0},{1,5},{5,9},... | collective-permute-start | bytes 786440 | tf_op jit(solution)/shard_map/ppermute | solution.py:69
  288.7 11.8 %collective-permute-start.54 = (bf16[64,2176]{1,0:T(8,128)(2,1)S(1)}, bf16[64,2176]{1,0:T(8,128)(2,1)S(1)}, u32[]{:S(2)}, u32[]{:S(2)}) collective-permute-start(bf16[64,2176]{1,0:T(8,128)(2,1)S(1)} %collective-permute-done.51), channel_id=1, source_target_pairs={{4,0},{8,4},{12,8},{14,12},{10,14},{6,10},{2,6},{0,2},{5,1},{9,5},... | collective-permute-start | bytes 835592 | tf_op jit(solution)/shard_map/ppermute | solution.py:69
  299.5 20.5 %collective-permute-start.66 = (bf16[64,2048]{1,0:T(8,128)(2,1)S(1)}, bf16[64,2048]{1,0:T(8,128)(2,1)S(1)}, u32[]{:S(2)}, u32[]{:S(2)}) collective-permute-start(bf16[64,2048]{1,0:T(8,128)(2,1)S(1)} %get-tuple-element.255), channel_id=1, source_target_pairs={{4,0},{8,4},{12,8},{14,12},{10,14},{6,10},{2,6},{0,2},{5,1},{9,5},... | collective-permute-start | bytes 786440 | tf_op jit(solution)/shard_map/ppermute | solution.py:69
  300.6 20.4 %collective-permute-start.58 = (bf16[64,2176]{1,0:T(8,128)(2,1)S(1)}, bf16[64,2176]{1,0:T(8,128)(2,1)S(1)}, u32[]{:S(2)}, u32[]{:S(2)}) collective-permute-start(bf16[64,2176]{1,0:T(8,128)(2,1)S(1)} %collective-permute-done.53), channel_id=1, source_target_pairs={{0,4},{4,8},{8,12},{12,14},{14,10},{10,6},{6,2},{2,0},{1,5},{5,9},... | collective-permute-start | bytes 835592 | tf_op jit(solution)/shard_map/ppermute | solution.py:69
  301.8 18.2 %collective-permute-start.57 = (bf16[64,2048]{1,0:T(8,128)(2,1)S(1)}, bf16[64,2048]{1,0:T(8,128)(2,1)S(1)}, u32[]{:S(2)}, u32[]{:S(2)}) collective-permute-start(bf16[64,2048]{1,0:T(8,128)(2,1)S(1)} %add_convert_fusion.20), channel_id=1, source_target_pairs={{0,4},{4,8},{8,12},{12,14},{14,10},{10,6},{6,2},{2,0},{1,5},{5,9},... | collective-permute-start | bytes 786440 | tf_op jit(solution)/shard_map/ppermute | solution.py:69
  303.6 17.4 %collective-permute-start.59 = (bf16[64,2176]{1,0:T(8,128)(2,1)S(1)}, bf16[64,2176]{1,0:T(8,128)(2,1)S(1)}, u32[]{:S(2)}, u32[]{:S(2)}) collective-permute-start(bf16[64,2176]{1,0:T(8,128)(2,1)S(1)} %collective-permute-done.54), channel_id=1, source_target_pairs={{4,0},{8,4},{12,8},{14,12},{10,14},{6,10},{2,6},{0,2},{5,1},{9,5},... | collective-permute-start | bytes 835592 | tf_op jit(solution)/shard_map/ppermute | solution.py:69
  320.1 19.4 %collective-permute-start.67 = (bf16[64,2048]{1,0:T(8,128)(2,1)S(1)}, bf16[64,2048]{1,0:T(8,128)(2,1)S(1)}, u32[]{:S(2)}, u32[]{:S(2)}) collective-permute-start(bf16[64,2048]{1,0:T(8,128)(2,1)S(1)} %get-tuple-element.256), channel_id=1, source_target_pairs={{4,0},{8,4},{12,8},{14,12},{10,14},{6,10},{2,6},{0,2},{5,1},{9,5},... | collective-permute-start | bytes 786440 | tf_op jit(solution)/shard_map/ppermute | solution.py:69
  321.0 19.4 %collective-permute-start.61 = (bf16[64,2176]{1,0:T(8,128)(2,1)S(1)}, bf16[64,2176]{1,0:T(8,128)(2,1)S(1)}, u32[]{:S(2)}, u32[]{:S(2)}) collective-permute-start(bf16[64,2176]{1,0:T(8,128)(2,1)S(1)} %collective-permute-done.58), channel_id=1, source_target_pairs={{0,4},{4,8},{8,12},{12,14},{14,10},{10,6},{6,2},{2,0},{1,5},{5,9},... | collective-permute-start | bytes 835592 | tf_op jit(solution)/shard_map/ppermute | solution.py:69
  322.2 17.3 %collective-permute-start.60 = (bf16[64,2048]{1,0:T(8,128)(2,1)S(1)}, bf16[64,2048]{1,0:T(8,128)(2,1)S(1)}, u32[]{:S(2)}, u32[]{:S(2)}) collective-permute-start(bf16[64,2048]{1,0:T(8,128)(2,1)S(1)} %get-tuple-element.233), channel_id=1, source_target_pairs={{0,4},{4,8},{8,12},{12,14},{14,10},{10,6},{6,2},{2,0},{1,5},{5,9},... | collective-permute-start | bytes 786440 | tf_op jit(solution)/shard_map/ppermute | solution.py:69
  369.6 130.5 %collective-permute-start.68 = (bf16[64,2048]{1,0:T(8,128)(2,1)}, bf16[64,2048]{1,0:T(8,128)(2,1)}, u32[]{:S(2)}, u32[]{:S(2)}) collective-permute-start(bf16[64,2048]{1,0:T(8,128)(2,1)} %get-tuple-element.257), channel_id=1, source_target_pairs={{4,0},{8,4},{12,8},{14,12},{10,14},{6,10},{2,6},{0,2},{5,1},{9,5},... | collective-permute-start | bytes 786440 | tf_op jit(solution)/shard_map/ppermute | solution.py:69
  370.5 27.5 %collective-permute-start.71 = (bf16[1024,256]{1,0:T(8,128)(2,1)}, bf16[1024,256]{1,0:T(8,128)(2,1)S(1)}, u32[]{:S(2)}, u32[]{:S(2)}) collective-permute-start(bf16[1024,256]{1,0:T(8,128)(2,1)} %shard_map.292), channel_id=1, source_target_pairs={{0,16},{16,0},{1,17},{17,1},{2,18},{18,2},{3,19},{19,3},{4,20},{20... | collective-permute-start | bytes 1572872 | tf_op jit(solution)/shard_map/ppermute | solution.py:69
  376.3 41.7 %collective-permute-start.74 = (bf16[1024,512]{1,0:T(8,128)(2,1)}, bf16[1024,512]{1,0:T(8,128)(2,1)}, u32[]{:S(2)}, u32[]{:S(2)}) collective-permute-start(bf16[1024,512]{1,0:T(8,128)(2,1)} %shard_map.294), channel_id=1, source_target_pairs={{0,16},{16,0},{1,17},{17,1},{2,18},{18,2},{3,19},{19,3},{4,20},{20... | collective-permute-start | bytes 3145736 | tf_op jit(solution)/shard_map/ppermute | solution.py:69
  380.1 19.7 %collective-permute-start.70 = (bf16[64,2048]{1,0:T(8,128)(2,1)S(1)}, bf16[64,2048]{1,0:T(8,128)(2,1)S(1)}, u32[]{:S(2)}, u32[]{:S(2)}) collective-permute-start(bf16[64,2048]{1,0:T(8,128)(2,1)S(1)} %get-tuple-element.405), channel_id=1, source_target_pairs={{0,4},{4,8},{8,12},{12,14},{14,10},{10,6},{6,2},{2,0},{1,5},{5,9},... | collective-permute-start | bytes 786440 | tf_op jit(solution)/shard_map/ppermute | solution.py:69
  381.3 18.4 %collective-permute-start.65 = (bf16[64,2048]{1,0:T(8,128)(2,1)S(1)}, bf16[64,2048]{1,0:T(8,128)(2,1)S(1)}, u32[]{:S(2)}, u32[]{:S(2)}) collective-permute-start(bf16[64,2048]{1,0:T(8,128)(2,1)S(1)} %get-tuple-element.254), channel_id=1, source_target_pairs={{0,4},{4,8},{8,12},{12,14},{14,10},{10,6},{6,2},{2,0},{1,5},{5,9},... | collective-permute-start | bytes 786440 | tf_op jit(solution)/shard_map/ppermute | solution.py:69
  398.0 25.6 %collective-permute-start.81 = (bf16[64,2048]{1,0:T(8,128)(2,1)}, bf16[64,2048]{1,0:T(8,128)(2,1)}, u32[]{:S(2)}, u32[]{:S(2)}) collective-permute-start(bf16[64,2048]{1,0:T(8,128)(2,1)} %get-tuple-element.404), channel_id=1, source_target_pairs={{4,0},{8,4},{12,8},{14,12},{10,14},{6,10},{2,6},{0,2},{5,1},{9,5},... | collective-permute-start | bytes 786440 | tf_op jit(solution)/shard_map/ppermute | solution.py:69
  399.8 23.8 %collective-permute-start.72 = (bf16[64,2048]{1,0:T(8,128)(2,1)S(1)}, bf16[64,2048]{1,0:T(8,128)(2,1)}, u32[]{:S(2)}, u32[]{:S(2)}) collective-permute-start(bf16[64,2048]{1,0:T(8,128)(2,1)S(1)} %add_convert_fusion.14), channel_id=1, source_target_pairs={{0,4},{4,8},{8,12},{12,14},{14,10},{10,6},{6,2},{2,0},{1,5},{5,9},... | collective-permute-start | bytes 786440 | tf_op jit(solution)/shard_map/ppermute | solution.py:69
  401.6 22.1 %collective-permute-start.73 = (bf16[1024,256]{1,0:T(8,128)(2,1)S(1)}, bf16[1024,256]{1,0:T(8,128)(2,1)}, u32[]{:S(2)}, u32[]{:S(2)}) collective-permute-start(bf16[1024,256]{1,0:T(8,128)(2,1)S(1)} %add_convert_fusion.4.refs_0_), channel_id=1, source_target_pairs={{4,0},{8,4},{12,8},{14,12},{10,14},{6,10},{2,6},{0,2},{5,1},{9,5},... | collective-permute-start | bytes 1572872 | tf_op jit(solution)/shard_map/ppermute | solution.py:69
  418.0 15.0 %collective-permute-start.76 = (bf16[1024,256]{1,0:T(8,128)(2,1)S(1)}, bf16[1024,256]{1,0:T(8,128)(2,1)}, u32[]{:S(2)}, u32[]{:S(2)}) collective-permute-start(bf16[1024,256]{1,0:T(8,128)(2,1)S(1)} %add_convert_fusion.4.refs_0_), channel_id=1, source_target_pairs={{0,4},{4,8},{8,12},{12,14},{14,10},{10,6},{6,2},{2,0},{1,5},{5,9},... | collective-permute-start | bytes 1572872 | tf_op jit(solution)/shard_map/ppermute | solution.py:69
  425.6 21.0 %collective-permute-start.82 = (bf16[64,2048]{1,0:T(8,128)(2,1)}, bf16[64,2048]{1,0:T(8,128)(2,1)}, u32[]{:S(2)}, u32[]{:S(2)}) collective-permute-start(bf16[64,2048]{1,0:T(8,128)(2,1)} %get-tuple-element.403), channel_id=1, source_target_pairs={{4,0},{8,4},{12,8},{14,12},{10,14},{6,10},{2,6},{0,2},{5,1},{9,5},... | collective-permute-start | bytes 786440 | tf_op jit(solution)/shard_map/ppermute | solution.py:69
  426.0 22.4 %collective-permute-start.75 = (bf16[64,2048]{1,0:T(8,128)(2,1)}, bf16[64,2048]{1,0:T(8,128)(2,1)}, u32[]{:S(2)}, u32[]{:S(2)}) collective-permute-start(bf16[64,2048]{1,0:T(8,128)(2,1)} %get-tuple-element.402), channel_id=1, source_target_pairs={{0,4},{4,8},{8,12},{12,14},{14,10},{10,6},{6,2},{2,0},{1,5},{5,9},... | collective-permute-start | bytes 786440 | tf_op jit(solution)/shard_map/ppermute | solution.py:69
  432.9 15.4 %collective-permute-start.77 = (bf16[1024,256]{1,0:T(8,128)(2,1)}, bf16[1024,256]{1,0:T(8,128)(2,1)}, u32[]{:S(2)}, u32[]{:S(2)}) collective-permute-start(bf16[1024,256]{1,0:T(8,128)(2,1)} %collective-permute-done.73.refs_2_), channel_id=1, source_target_pairs={{4,0},{8,4},{12,8},{14,12},{10,14},{6,10},{2,6},{0,2},{5,1},{9,5},... | collective-permute-start | bytes 1572872 | tf_op jit(solution)/shard_map/ppermute | solution.py:69
  433.7 15.9 %collective-permute-start.79 = (bf16[1024,256]{1,0:T(8,128)(2,1)}, bf16[1024,256]{1,0:T(8,128)(2,1)}, u32[]{:S(2)}, u32[]{:S(2)}) collective-permute-start(bf16[1024,256]{1,0:T(8,128)(2,1)} %collective-permute-done.76.refs_1_), channel_id=1, source_target_pairs={{0,4},{4,8},{8,12},{12,14},{14,10},{10,6},{6,2},{2,0},{1,5},{5,9},... | collective-permute-start | bytes 1572872 | tf_op jit(solution)/shard_map/ppermute | solution.py:69
  449.6 17.0 %collective-permute-start.80 = (bf16[1024,256]{1,0:T(8,128)(2,1)}, bf16[1024,256]{1,0:T(8,128)(2,1)S(1)}, u32[]{:S(2)}, u32[]{:S(2)}) collective-permute-start(bf16[1024,256]{1,0:T(8,128)(2,1)} %collective-permute-done.77.refs_4_), channel_id=1, source_target_pairs={{4,0},{8,4},{12,8},{14,12},{10,14},{6,10},{2,6},{0,2},{5,1},{9,5},... | collective-permute-start | bytes 1572872 | tf_op jit(solution)/shard_map/ppermute | solution.py:69
  450.6 16.0 %collective-permute-start.78 = (bf16[64,2048]{1,0:T(8,128)(2,1)S(1)}, bf16[64,2048]{1,0:T(8,128)(2,1)S(1)}, u32[]{:S(2)}, u32[]{:S(2)}) collective-permute-start(bf16[64,2048]{1,0:T(8,128)(2,1)S(1)} %get-tuple-element.400), channel_id=1, source_target_pairs={{0,4},{4,8},{8,12},{12,14},{14,10},{10,6},{6,2},{2,0},{1,5},{5,9},... | collective-permute-start | bytes 786440 | tf_op jit(solution)/shard_map/ppermute | solution.py:69
  451.8 14.8 %collective-permute-start.83 = (bf16[64,2048]{1,0:T(8,128)(2,1)S(1)}, bf16[64,2048]{1,0:T(8,128)(2,1)S(1)}, u32[]{:S(2)}, u32[]{:S(2)}) collective-permute-start(bf16[64,2048]{1,0:T(8,128)(2,1)S(1)} %get-tuple-element.401), channel_id=1, source_target_pairs={{4,0},{8,4},{12,8},{14,12},{10,14},{6,10},{2,6},{0,2},{5,1},{9,5},... | collective-permute-start | bytes 786440 | tf_op jit(solution)/shard_map/ppermute | solution.py:69
  456.0 11.0 %collective-permute-start.91 = (bf16[256,256]{1,0:T(8,128)(2,1)S(1)}, bf16[256,256]{1,0:T(8,128)(2,1)S(1)}, u32[]{:S(2)}, u32[]{:S(2)}) collective-permute-start(bf16[256,256]{1,0:T(8,128)(2,1)S(1)} %dynamic-slice_convert_fusion.1), channel_id=1, source_target_pairs={{0,2},{2,0},{4,6},{6,4},{8,10},{10,8},{12,14},{14,12},{1,3},{3,1},... | collective-permute-start | bytes 393224 | tf_op jit(solution)/shard_map/ppermute | solution.py:69
  466.6 11.4 %collective-permute-start.94 = (bf16[1024,256]{1,0:T(8,128)(2,1)}, bf16[1024,256]{1,0:T(8,128)(2,1)S(1)}, u32[]{:S(2)}, u32[]{:S(2)}) collective-permute-start(bf16[1024,256]{1,0:T(8,128)(2,1)} %collective-permute-done.79.refs_3_), channel_id=1, source_target_pairs={{0,4},{4,8},{8,12},{12,14},{14,10},{10,6},{6,2},{2,0},{1,5},{5,9},... | collective-permute-start | bytes 1572872 | tf_op jit(solution)/shard_map/ppermute | solution.py:69
  468.2 9.8 %collective-permute-start.86 = (f32[4352]{0:T(1024)S(1)}, f32[4352]{0:T(1024)S(1)}, u32[]{:S(2)}, u32[]{:S(2)}) collective-permute-start(f32[4352]{0:T(1024)S(1)} %fusion.25), channel_id=1, source_target_pairs={{0,16},{16,0},{1,17},{17,1},{2,18},{18,2},{3,19},{19,3},{4,20},{20... | collective-permute-start | bytes 52232 | tf_op jit(solution)/shard_map/ppermute | solution.py:69
  470.8 39.8 %collective-permute-start.92 = (bf16[1280,256]{1,0:T(8,128)(2,1)}, bf16[1280,256]{1,0:T(8,128)(2,1)}, u32[]{:S(2)}, u32[]{:S(2)}) collective-permute-start(bf16[1280,256]{1,0:T(8,128)(2,1)} %pad_maximum_fusion.3.refs_0_.refs_7_), channel_id=1, source_target_pairs={{0,4},{4,8},{8,12},{12,14},{14,10},{10,6},{6,2},{2,0},{1,5},{5,9},... | collective-permute-start | bytes 1966088 | tf_op jit(solution)/shard_map/ppermute | solution.py:69
  473.0 38.3 %collective-permute-start.93 = (bf16[1280,256]{1,0:T(8,128)(2,1)}, bf16[1280,256]{1,0:T(8,128)(2,1)}, u32[]{:S(2)}, u32[]{:S(2)}) collective-permute-start(bf16[1280,256]{1,0:T(8,128)(2,1)} %pad_maximum_fusion.3.refs_0_.refs_7_), channel_id=1, source_target_pairs={{4,0},{8,4},{12,8},{14,12},{10,14},{6,10},{2,6},{0,2},{5,1},{9,5},... | collective-permute-start | bytes 1966088 | tf_op jit(solution)/shard_map/ppermute | solution.py:69
  478.0 32.6 %collective-permute-start.95 = (bf16[512,256]{1,0:T(8,128)(2,1)S(1)}, bf16[512,256]{1,0:T(8,128)(2,1)}, u32[]{:S(2)}, u32[]{:S(2)}) collective-permute-start(bf16[512,256]{1,0:T(8,128)(2,1)S(1)} %slice.269), channel_id=1, source_target_pairs={{0,4},{4,8},{8,12},{12,14},{14,10},{10,6},{6,2},{2,0},{1,5},{5,9},... | collective-permute-start | bytes 786440 | tf_op jit(solution)/shard_map/ppermute | solution.py:69
  478.8 17.3 %collective-permute-start.87 = (f32[4352]{0:T(1024)S(1)}, f32[4352]{0:T(1024)S(1)}, u32[]{:S(2)}, u32[]{:S(2)}) collective-permute-start(f32[4352]{0:T(1024)S(1)} %add.328), channel_id=1, source_target_pairs={{0,2},{2,0},{4,6},{6,4},{8,10},{10,8},{12,14},{14,12},{1,3},{3,1},... | collective-permute-start | bytes 52232 | tf_op jit(solution)/shard_map/ppermute | solution.py:69
  500.1 10.5 %collective-permute-start.96 = (bf16[512,256]{1,0:T(8,128)(2,1)S(1)}, bf16[512,256]{1,0:T(8,128)(2,1)S(1)}, u32[]{:S(2)}, u32[]{:S(2)}) collective-permute-start(bf16[512,256]{1,0:T(8,128)(2,1)S(1)} %slice.270), channel_id=1, source_target_pairs={{4,0},{8,4},{12,8},{14,12},{10,14},{6,10},{2,6},{0,2},{5,1},{9,5},... | collective-permute-start | bytes 786440 | tf_op jit(solution)/shard_map/ppermute | solution.py:69
  511.3 17.9 %collective-permute-start.97 = (bf16[1280,256]{1,0:T(8,128)(2,1)}, bf16[1280,256]{1,0:T(8,128)(2,1)S(1)}, u32[]{:S(2)}, u32[]{:S(2)}) collective-permute-start(bf16[1280,256]{1,0:T(8,128)(2,1)} %collective-permute-done.92.refs_1_.refs_8_), channel_id=1, source_target_pairs={{0,4},{4,8},{8,12},{12,14},{14,10},{10,6},{6,2},{2,0},{1,5},{5,9},... | collective-permute-start | bytes 1966088 | tf_op jit(solution)/shard_map/ppermute | solution.py:69
  515.3 13.9 %collective-permute-start.99 = (f32[1024,128]{1,0:T(8,128)}, f32[1024,128]{1,0:T(8,128)S(1)}, u32[]{:S(2)}, u32[]{:S(2)}) collective-permute-start(f32[1024,128]{1,0:T(8,128)} %shard_map.300), channel_id=1, source_target_pairs={{0,16},{16,0},{1,17},{17,1},{2,18},{18,2},{3,19},{19,3},{4,20},{20... | collective-permute-start | bytes 1572872 | tf_op jit(solution)/shard_map/ppermute | solution.py:69
  516.9 16.4 %collective-permute-start.98 = (bf16[1280,256]{1,0:T(8,128)(2,1)}, bf16[1280,256]{1,0:T(8,128)(2,1)S(1)}, u32[]{:S(2)}, u32[]{:S(2)}) collective-permute-start(bf16[1280,256]{1,0:T(8,128)(2,1)} %collective-permute-done.93.refs_2_.refs_9_), channel_id=1, source_target_pairs={{4,0},{8,4},{12,8},{14,12},{10,14},{6,10},{2,6},{0,2},{5,1},{9,5},... | collective-permute-start | bytes 1966088 | tf_op jit(solution)/shard_map/ppermute | solution.py:69
  533.4 15.3 %collective-permute-start.100 = (bf16[1280,256]{1,0:T(8,128)(2,1)S(1)}, bf16[1280,256]{1,0:T(8,128)(2,1)S(1)}, u32[]{:S(2)}, u32[]{:S(2)}) collective-permute-start(bf16[1280,256]{1,0:T(8,128)(2,1)S(1)} %collective-permute-done.97.refs_3_.refs_10_), channel_id=1, source_target_pairs={{0,4},{4,8},{8,12},{12,14},{14,10},{10,6},{6,2},{2,0},{1,5},{5,9},... | collective-permute-start | bytes 1966088 | tf_op jit(solution)/shard_map/ppermute | solution.py:69
  533.6 15.3 %collective-permute-start.101 = (bf16[1280,256]{1,0:T(8,128)(2,1)S(1)}, bf16[1280,256]{1,0:T(8,128)(2,1)S(1)}, u32[]{:S(2)}, u32[]{:S(2)}) collective-permute-start(bf16[1280,256]{1,0:T(8,128)(2,1)S(1)} %collective-permute-done.98.refs_4_.refs_11_), channel_id=1, source_target_pairs={{4,0},{8,4},{12,8},{14,12},{10,14},{6,10},{2,6},{0,2},{5,1},{9,5},... | collective-permute-start | bytes 1966088 | tf_op jit(solution)/shard_map/ppermute | solution.py:69
  (89 other events, 722.9 us)
